TPU v7x, 32 devices: a whole 2x2x4 slice. The times are simulated.
32 devices in a mesh: seq: 8 (over z, x), ctx: 4 (over y, core).
Axes of the slice: x: 2, y: 2, z: 4, core: 2. Of those that a mesh axis runs over, the one named last changes fastest.
Arguments:
- inputs: bfloat16 [2, 8, 4, 128, 2048], P(None, 'seq', None, 'ctx'), may hold values from -6 to 6
- doc_ids: int32 [2, 8, 4, 128], P(None, 'seq', None, 'ctx'), may hold values from 0 to 8, as said below
- cotangent: bfloat16 [2, 8, 4, 128, 2048], P(None, 'seq', None, 'ctx'), may hold values from -11 to 11
- weight_qkv: float32 [2048, 3, 2048], P('seq', None, 'ctx'), may hold values from -0.110485435 to 0.110485435
- moment_qkv: float32 [2048, 3, 2048], P('seq', None, 'ctx'), may hold values from -2.8076172e-05 to 2.8076172e-05
- second_qkv: float32 [2048, 3, 2048], P('seq', None, 'ctx'), may hold values from 1.9520521e-10 to 7.852912e-10
- weight_out: float32 [2048, 2048], P('seq', 'ctx'), may hold values from -0.5 to 0.5
- moment_out: float32 [2048, 2048], P('seq', 'ctx'), may hold values from -5.493164e-05 to 5.493164e-05
- second_out: float32 [2048, 2048], P('seq', 'ctx'), may hold values from 7.838011e-10 to 3.1381845e-09
- weight_mlp: float32 [2048, 2, 8192], P('seq', None, 'ctx'), may hold values from -0.176776695 to 0.176776695
- moment_mlp: float32 [2048, 2, 8192], P('seq', None, 'ctx'), may hold values from -5.493164e-05 to 5.493164e-05
- second_mlp: float32 [2048, 2, 8192], P('seq', None, 'ctx'), may hold values from 7.838011e-10 to 3.1381845e-09
- weight_down: float32 [2048, 8192], P('seq', 'ctx'), may hold values from -0.0625 to 0.0625
- moment_down: float32 [2048, 8192], P('seq', 'ctx'), may hold values from -5.493164e-05 to 5.493164e-05
- second_down: float32 [2048, 8192], P('seq', 'ctx'), may hold values from 7.838011e-10 to 3.1381845e-09
- norm_gains: float32 [2, 2048], replicated, may hold values from 0.4 to 2.5
- moment_gains: float32 [2, 2048], replicated, may hold values from -0.00021972656 to 0.00021972656
- second_gains: float32 [2, 2048], replicated, may hold values from 1.2546778e-08 to 5.021691e-08
- gate_logit: float32 [16], replicated, may hold values from -2 to 2
- moment_gate: float32 [16], replicated, may hold values from -0.0004394531 to 0.0004394531
- second_gate: float32 [16], replicated, may hold values from 5.00679e-08 to 2.0116568e-07
Outputs:
- block_out: bfloat16 [2, 8, 4, 128, 2048], P(None, 'seq', None, 'ctx')
- input_grad: bfloat16 [2, 8, 4, 128, 2048], P(None, 'seq', None, 'ctx')
- grad_norm: float32 [], replicated
- qkv_moment: float32 [2048, 3, 2048], P('seq', None, 'ctx')
- qkv_second: float32 [2048, 3, 2048], P('seq', None, 'ctx')
- qkv_weight: float32 [2048, 3, 2048], P('seq', None, 'ctx')
- out_moment: float32 [2048, 2048], P('seq', 'ctx')
- out_second: float32 [2048, 2048], P('seq', 'ctx')
- out_weight: float32 [2048, 2048], P('seq', 'ctx')
- mlp_moment: float32 [2048, 2, 8192], P('seq', None, 'ctx')
- mlp_second: float32 [2048, 2, 8192], P('seq', None, 'ctx')
- mlp_weight: float32 [2048, 2, 8192], P('seq', None, 'ctx')
- down_moment: float32 [2048, 8192], P('seq', 'ctx')
- down_second: float32 [2048, 8192], P('seq', 'ctx')
- down_weight: float32 [2048, 8192], P('seq', 'ctx')
- gains_moment: float32 [2, 2048], replicated
- gains_second: float32 [2, 2048], replicated
- gains_weight: float32 [2, 2048], replicated
- gate_moment: float32 [16], replicated
- gate_second: float32 [16], replicated
- gate_weight: float32 [16], replicated
Inputs may be any that keep to these rules, and one draw needn't show every extreme that they name: `doc_ids`: within each sequence (512 tokens) the ids are 0 at its first token and rise by 0 or 1 from token to token, ending at 8 in every sequence; in every sequence some whole segment after the first belongs to the document of the token just before it.
All inputs are finite; a program needn't handle non-finite values.
Results may differ from a plain program's by a relative error of at most 0.025.
Values may be sent and summed in bfloat16 or wider, within the bound.
No kernel may reach another device: no remote copies, remote signals or barrier semaphores. Data moves between devices by JAX's collectives and lax.ppermute only.
A program may use at most 320 MiB of HBM per device.

v0:
```python
import jax
import jax.numpy as jnp
from jax import lax
from jax.sharding import PartitionSpec as P

D = 2048
HEADS = 16
HEAD_DIM = 128
FF = 8192
STEP_COUNT = 10


EPS = 1e-06
NEG = -1e30
CLIP = 1.0
BETA1 = 0.9
BETA2 = 0.95
ADAM_EPS = 1e-08
DECAY = 0.1
HIGH = lax.Precision.HIGHEST


def elu_one(tensor):
    return jnp.where(tensor > 0, tensor + 1.0, jnp.exp(jnp.minimum(tensor, 0.0)))


def rms_norm(tensor, scaling):
    return tensor * lax.rsqrt(jnp.mean(tensor * tensor, axis=-1, keepdims=True) + EPS) * scaling


def memory_read(queries, keys_in, values_in, doc_rows):
    head_count = queries.shape[2]
    feat_width = queries.shape[3]

    def advance(state_in, segment):
        memory, normer, previous = state_in
        query_seg, key_seg, value_seg, doc_seg = segment
        query_pos = elu_one(query_seg)
        key_pos = elu_one(key_seg)
        reading = (doc_seg == previous).astype(jnp.float32)[:, None, None]
        numerator = jnp.einsum("lhe,hef->lhf", query_pos, memory, precision=HIGH)
        denominator = 1.0 + jnp.einsum("lhe,he->lh", query_pos, normer, precision=HIGH)
        recalled = reading * numerator / denominator[:, :, None]
        last_id = doc_seg[-1]
        keeping = (last_id == previous).astype(jnp.float32)
        base_memory = keeping * memory
        base_norm = keeping * normer
        key_denom = 1.0 + jnp.einsum("lhe,he->lh", key_pos, base_norm, precision=HIGH)
        before = jnp.einsum("lhe,hef->lhf", key_pos, base_memory, precision=HIGH)
        change = value_seg - before / key_denom[:, :, None]
        writing = key_pos * (doc_seg == last_id).astype(jnp.float32)[:, None, None]
        memory = base_memory + jnp.einsum("lhe,lhf->hef", writing, change, precision=HIGH)
        normer = base_norm + jnp.sum(writing, axis=0)
        return ((memory, normer, last_id), recalled)

    initial = (
        jnp.zeros((head_count, feat_width, feat_width), jnp.float32),
        jnp.zeros((head_count, feat_width), jnp.float32),
        jnp.array(-1, jnp.int32),
    )
    ignored, recalled = lax.scan(advance, initial, (queries, keys_in, values_in, doc_rows))
    return recalled


def adam_update(weight, moment, second, gradient, factor, step_rate, decay):
    clipped = gradient * factor
    moment = BETA1 * moment + (1.0 - BETA1) * clipped
    second = BETA2 * second + (1.0 - BETA2) * clipped * clipped
    fixed_first = moment / (1.0 - BETA1**STEP_COUNT)
    fixed_second = second / (1.0 - BETA2**STEP_COUNT)
    updated = weight - step_rate * (
        fixed_first / (jnp.sqrt(fixed_second) + ADAM_EPS) + decay * weight
    )
    return (moment, second, updated)


def softmax_rows(queries, keys_in, doc_rows, scaling):
    seg_len = doc_rows.shape[1]
    position = jnp.arange(seg_len)
    allowed = (position[:, None] >= position[None, :])[None] & (
        doc_rows[:, :, None] == doc_rows[:, None, :]
    )
    scores = (
        jnp.einsum("rlhe,rmhe->rhlm", queries, keys_in, preferred_element_type=jnp.float32)
        * scaling
    )
    return jnp.where(allowed[:, None], scores, NEG)


def on_device(
    inputs,
    doc_ids,
    cotangent,
    weight_qkv,
    moment_qkv,
    second_qkv,
    weight_out,
    moment_out,
    second_out,
    weight_mlp,
    moment_mlp,
    second_mlp,
    weight_down,
    moment_down,
    second_down,
    norm_gains,
    moment_gains,
    second_gains,
    gate_logit,
    moment_gate,
    second_gate,
):
    bf_type = jnp.bfloat16
    micro_count = inputs.shape[0]
    local_width = weight_qkv.shape[2]
    local_heads = local_width // HEAD_DIM
    head_start = lax.axis_index("ctx") * local_heads
    gate_local = lax.dynamic_slice_in_dim(gate_logit, head_start, local_heads)
    mixing = jax.nn.sigmoid(gate_local)[:, None]
    scaling = HEAD_DIM ** (-0.5)
    shards = (
        weight_qkv.astype(bf_type),
        weight_out.astype(bf_type),
        weight_mlp.astype(bf_type),
        weight_down.astype(bf_type),
    )

    def fetch_weights():
        return (
            lax.all_gather(shards[0], "seq", axis=0, tiled=True),
            lax.all_gather(shards[1], "seq", axis=0, tiled=True),
            lax.all_gather(shards[2], "seq", axis=0, tiled=True),
            lax.all_gather(shards[3], "seq", axis=0, tiled=True),
        )

    def reduce_rows(partial_term):
        return lax.psum_scatter(partial_term, "ctx", scatter_dimension=1, tiled=True)

    def spread_rows(grad_rows):
        return lax.all_gather(grad_rows, "ctx", axis=1, tiled=True)

    def collect_rows(partial_term):
        return lax.psum_scatter(partial_term, "ctx", scatter_dimension=1, tiled=True)

    grad_qkv = jnp.zeros((D, 3, local_width), jnp.float32)
    grad_out = jnp.zeros((D, local_width), jnp.float32)
    grad_mlp = jnp.zeros((D, 2, weight_mlp.shape[2]), jnp.float32)
    grad_down = jnp.zeros((D, weight_down.shape[1]), jnp.float32)
    gain_grad = jnp.zeros(norm_gains.shape, jnp.float32)
    gate_grad = jnp.zeros((local_heads,), jnp.float32)
    out_list = []
    grad_rows_list = []
    for micro_index in range(micro_count):
        gathered = fetch_weights()
        full_qkv, full_out, full_mlp, full_down = gathered
        token_rows = inputs[micro_index, 0].astype(jnp.float32)
        own_ids = doc_ids[micro_index, 0]
        normed_att = rms_norm(token_rows, norm_gains[0]).astype(bf_type)
        att_rows, doc_rows = (
            lax.all_gather(normed_att, "ctx", axis=1, tiled=True),
            lax.all_gather(own_ids, "ctx", axis=1, tiled=True),
        )
        seg_count = doc_rows.shape[0]
        seg_len = doc_rows.shape[1]
        projected = jnp.einsum(
            "rld,dcj->rlcj", att_rows, full_qkv, preferred_element_type=jnp.float32
        ).astype(bf_type)
        shaped = projected.reshape(seg_count, seg_len, 3, local_heads, HEAD_DIM)
        queries = shaped[:, :, 0]
        keys_in = shaped[:, :, 1]
        values_in = shaped[:, :, 2]
        scores = softmax_rows(queries, keys_in, doc_rows, scaling)
        row_peak = jnp.max(scores, axis=-1, keepdims=True)
        exponent = jnp.exp(scores - row_peak)
        row_total = jnp.sum(exponent, axis=-1, keepdims=True)
        log_total = row_peak + jnp.log(row_total)
        prob_low = (exponent / row_total).astype(bf_type)
        local_out = jnp.einsum(
            "rhlm,rmhe->rlhe", prob_low, values_in, preferred_element_type=jnp.float32
        )
        recalled, memory_back = jax.vjp(
            lambda a, b, c: memory_read(a, b, c, doc_rows),
            queries.astype(jnp.float32),
            keys_in.astype(jnp.float32),
            values_in.astype(jnp.float32),
        )
        combined = (
            (mixing * recalled + (1.0 - mixing) * local_out)
            .astype(bf_type)
            .reshape(seg_count, seg_len, local_width)
        )
        attended = reduce_rows(
            jnp.einsum("rlj,dj->rld", combined, full_out, preferred_element_type=jnp.float32)
        )
        hidden = token_rows + attended
        normed_mlp = rms_norm(hidden, norm_gains[1]).astype(bf_type)
        mlp_rows = lax.all_gather(normed_mlp, "ctx", axis=1, tiled=True)
        gate_up = jnp.einsum(
            "rld,dcf->rlcf", mlp_rows, full_mlp, preferred_element_type=jnp.float32
        )
        active = (jax.nn.gelu(gate_up[:, :, 0]) * gate_up[:, :, 1]).astype(bf_type)
        mlp_out = reduce_rows(
            jnp.einsum("rlf,df->rld", active, full_down, preferred_element_type=jnp.float32)
        )
        out_list.append((hidden + mlp_out).astype(bf_type))
        gathered = fetch_weights()
        full_qkv, full_out, full_mlp, full_down = gathered
        back_rows = cotangent[micro_index, 0].astype(jnp.float32)
        mlp_grads = spread_rows(back_rows.astype(bf_type))
        d_active = jnp.einsum(
            "rld,df->rlf", mlp_grads, full_down, preferred_element_type=jnp.float32
        )
        grad_down = grad_down + jnp.einsum(
            "rld,rlf->df", mlp_grads, active, preferred_element_type=jnp.float32
        )
        ignored, gelu_back = jax.vjp(
            lambda a, b: jax.nn.gelu(a) * b, gate_up[:, :, 0], gate_up[:, :, 1]
        )
        d_gate, d_up = gelu_back(d_active)
        d_gate_up = jnp.stack([d_gate, d_up], axis=2).astype(bf_type)
        grad_mlp = grad_mlp + jnp.einsum(
            "rld,rlcf->dcf", mlp_rows, d_gate_up, preferred_element_type=jnp.float32
        )
        d_normed_mlp = collect_rows(
            jnp.einsum("rlcf,dcf->rld", d_gate_up, full_mlp, preferred_element_type=jnp.float32)
        )
        ignored, norm_back = jax.vjp(rms_norm, hidden, norm_gains[1])
        d_hidden_norm, d_gain_mlp = norm_back(d_normed_mlp)
        d_hidden = back_rows + d_hidden_norm
        att_grads = spread_rows(d_hidden.astype(bf_type))
        d_combined = jnp.einsum(
            "rld,dj->rlj", att_grads, full_out, preferred_element_type=jnp.float32
        )
        grad_out = grad_out + jnp.einsum(
            "rld,rlj->dj", att_grads, combined, preferred_element_type=jnp.float32
        )
        d_combined = d_combined.reshape(seg_count, seg_len, local_heads, HEAD_DIM)
        gate_grad = (
            gate_grad
            + jnp.sum(d_combined * (recalled - local_out), axis=(0, 1, 3))
            * (mixing * (1.0 - mixing))[:, 0]
        )
        d_recalled = mixing * d_combined
        d_local = ((1.0 - mixing) * d_combined).astype(bf_type)
        scores = softmax_rows(queries, keys_in, doc_rows, scaling)
        probs = jnp.exp(scores - log_total)
        prob_low = probs.astype(bf_type)
        d_prob = jnp.einsum(
            "rlhe,rmhe->rhlm", d_local, values_in, preferred_element_type=jnp.float32
        )
        d_values = jnp.einsum(
            "rhlm,rlhe->rmhe", prob_low, d_local, preferred_element_type=jnp.float32
        )
        d_scores = (probs * (d_prob - jnp.sum(d_prob * probs, axis=-1, keepdims=True))).astype(
            bf_type
        )
        d_queries = (
            jnp.einsum("rhlm,rmhe->rlhe", d_scores, keys_in, preferred_element_type=jnp.float32)
            * scaling
        )
        d_keys = (
            jnp.einsum("rhlm,rlhe->rmhe", d_scores, queries, preferred_element_type=jnp.float32)
            * scaling
        )
        memory_q, memory_k, memory_v = memory_back(d_recalled)
        d_projected = jnp.stack(
            [d_queries + memory_q, d_keys + memory_k, d_values + memory_v], axis=2
        )
        d_projected = d_projected.reshape(seg_count, seg_len, 3, local_width).astype(bf_type)
        grad_qkv = grad_qkv + jnp.einsum(
            "rld,rlcj->dcj", att_rows, d_projected, preferred_element_type=jnp.float32
        )
        d_normed_att = collect_rows(
            jnp.einsum("rlcj,dcj->rld", d_projected, full_qkv, preferred_element_type=jnp.float32)
        )
        ignored, norm_first = jax.vjp(rms_norm, token_rows, norm_gains[0])
        d_rows_norm, d_gain_att = norm_first(d_normed_att)
        grad_rows_list.append((d_hidden + d_rows_norm).astype(bf_type))
        gain_grad = gain_grad + jnp.stack([d_gain_att, d_gain_mlp], axis=0)
    own_qkv, own_out, own_mlp, own_down = (
        lax.psum_scatter(
            grad_qkv.astype(jnp.bfloat16), "seq", scatter_dimension=0, tiled=True
        ).astype(jnp.float32),
        lax.psum_scatter(
            grad_out.astype(jnp.bfloat16), "seq", scatter_dimension=0, tiled=True
        ).astype(jnp.float32),
        lax.psum_scatter(
            grad_mlp.astype(jnp.bfloat16), "seq", scatter_dimension=0, tiled=True
        ).astype(jnp.float32),
        lax.psum_scatter(
            grad_down.astype(jnp.bfloat16), "seq", scatter_dimension=0, tiled=True
        ).astype(jnp.float32),
    )
    gate_padded = lax.dynamic_update_slice(
        jnp.zeros(gate_logit.shape, jnp.float32), gate_grad, (head_start,)
    )
    owned = (
        jnp.sum(own_qkv * own_qkv)
        + jnp.sum(own_out * own_out)
        + jnp.sum(own_mlp * own_mlp)
        + jnp.sum(own_down * own_down)
    )
    gains_total, gate_total = lax.psum((gain_grad, gate_padded), ("seq", "ctx"))
    owned_total = lax.psum(owned, ("seq", "ctx"))
    squares = owned_total + jnp.sum(gains_total * gains_total) + jnp.sum(gate_total * gate_total)
    grad_norm = jnp.sqrt(squares)
    factor = jnp.minimum(1.0, CLIP / (grad_norm + 1e-06))
    qkv_new = adam_update(weight_qkv, moment_qkv, second_qkv, own_qkv, factor, D ** (-0.5), DECAY)
    out_new = adam_update(
        weight_out,
        moment_out,
        second_out,
        own_out,
        factor,
        4.0 * (HEADS * HEAD_DIM) ** (-0.5),
        DECAY,
    )
    mlp_new = adam_update(weight_mlp, moment_mlp, second_mlp, own_mlp, factor, D ** (-0.5), DECAY)
    down_new = adam_update(
        weight_down, moment_down, second_down, own_down, factor, FF ** (-0.5), DECAY
    )
    gains_new = adam_update(norm_gains, moment_gains, second_gains, gains_total, factor, 0.5, 0.0)
    gate_new = adam_update(gate_logit, moment_gate, second_gate, gate_total, factor, 1.0, 0.0)
    block_out = jnp.stack(out_list, axis=0)[:, None]
    input_grad = jnp.stack(grad_rows_list, axis=0)[:, None]
    return (
        block_out,
        input_grad,
        grad_norm,
        qkv_new[0],
        qkv_new[1],
        qkv_new[2],
        out_new[0],
        out_new[1],
        out_new[2],
        mlp_new[0],
        mlp_new[1],
        mlp_new[2],
        down_new[0],
        down_new[1],
        down_new[2],
        gains_new[0],
        gains_new[1],
        gains_new[2],
        gate_new[0],
        gate_new[1],
        gate_new[2],
    )


def solution(mesh):
    placed = (
        P(None, "seq", None, "ctx", None),
        P(None, "seq", None, "ctx"),
        P(None, "seq", None, "ctx", None),
        P("seq", None, "ctx"),
        P("seq", None, "ctx"),
        P("seq", None, "ctx"),
        P("seq", "ctx"),
        P("seq", "ctx"),
        P("seq", "ctx"),
        P("seq", None, "ctx"),
        P("seq", None, "ctx"),
        P("seq", None, "ctx"),
        P("seq", "ctx"),
        P("seq", "ctx"),
        P("seq", "ctx"),
        P(),
        P(),
        P(),
        P(),
        P(),
        P(),
    )
    return jax.shard_map(
        on_device,
        mesh=mesh,
        in_specs=placed,
        out_specs=(
            P(None, "seq", None, "ctx", None),
            P(None, "seq", None, "ctx", None),
            P(),
            P("seq", None, "ctx"),
            P("seq", None, "ctx"),
            P("seq", None, "ctx"),
            P("seq", "ctx"),
            P("seq", "ctx"),
            P("seq", "ctx"),
            P("seq", None, "ctx"),
            P("seq", None, "ctx"),
            P("seq", None, "ctx"),
            P("seq", "ctx"),
            P("seq", "ctx"),
            P("seq", "ctx"),
            P(),
            P(),
            P(),
            P(),
            P(),
            P(),
        ),
        check_vma=False,
    )
```

profile of v0, /device:TPU:0, one launch (start us, length us, event | category | flops | bytes accessed | tf_op | source)
XLA Modules:
  0.0 2057.8 jit_solution(5936296835686708693)
XLA Ops:
  38.6 101.8 %all-gather.19.cloned.1.call-done = bf16[2048,3,512]{2,0,1:T(8,128)(2,1)} async-done(((bf16[256,3,512]{2,0,1:T(8,128)(2,1)}), bf16[2048,3,512]{2,0,1:T(8,128)(2,1)}) %all-gather.19.cloned.1.call-update) | async-done | bytes 6291472 | tf_op jit(solution)/shard_map/all_gather | solution.py:130
  174.4 82.3 %while.172 = (s32[]{:T(128)}, f32[4,128,128]{2,1,0:T(8,128)S(1)}, f32[4,128]{1,0:T(4,128)}, s32[]{:T(128)}, f32[4,128,4,128]{1,3,2,0:T(8,128)}, /*index=5*/f32[4...) while((s32[]{:T(128)}, f32[4,128,128]{2,1,0:T(8,128)S(1)}, ...), condition=%wide.region_3.4_spmd.clone, body=%wide.region_1.0_spmd.clone.sunk | while | flops 307173376 | bytes 14824450 | solution.py:61
  288.3 85.3 %while.173 = (s32[]{:T(128)}, f32[4,128,128]{2,1,0:T(8,128)S(1)}, f32[4,128]{1,0:T(4,128)}, s32[]{:T(128)}, f32[4,128,4,128]{1,3,2,0:T(8,128)}, /*index=5*/f32[4...) while((s32[]{:T(128)}, f32[4,128,128]{2,1,0:T(8,128)S(1)}, ...), condition=%wide.region_12.13_spmd.clone, body=%wide.region_10.12_spmd.clone.sunk | while | flops 307173376 | bytes 14824450 | solution.py:61
  390.8 38.0 %reduce-scatter.13.cloned.1.call-done = f32[4,32,2048]{2,1,0:T(8,128)} async-done(((f32[4,128,2048]{2,1,0:T(8,128)}), f32[4,32,2048]{2,1,0:T(8,128)}) %reduce-scatter.13.cloned.1.call-update) | async-done | bytes 1048592 | tf_op jit(solution)/shard_map/reduce_scatter | solution.py:137
  428.7 47.7 %reduce-scatter.17.cloned.1.call-done = f32[4,32,2048]{2,1,0:T(8,128)} async-done(((f32[4,128,2048]{2,1,0:T(8,128)}), f32[4,32,2048]{2,1,0:T(8,128)}) %reduce-scatter.17.cloned.1.call-update) | async-done | bytes 1048592 | tf_op jit(solution)/shard_map/reduce_scatter | solution.py:137
  489.7 12.6 all-gather.23.cloned.1.call-done
  502.3 230.4 %all-gather.25.cloned.1.call-done = bf16[2048,2,2048]{2,0,1:T(8,128)(2,1)} async-done(((bf16[256,2,2048]{2,0,1:T(8,128)(2,1)}), bf16[2048,2,2048]{2,0,1:T(8,128)(2,1)}) %all-gather.25.cloned.1.call-update) | async-done | bytes 16777232 | tf_op jit(solution)/shard_map/all_gather | solution.py:132
  732.6 15.1 fusion.196
  755.6 127.5 %all-gather.27.cloned.1.call-done = bf16[2048,2048]{1,0:T(8,128)(2,1)} async-done(((bf16[256,2048]{1,0:T(8,128)(2,1)}), bf16[2048,2048]{1,0:T(8,128)(2,1)}) %all-gather.27.cloned.1.call-update) | async-done | bytes 8388624 | tf_op jit(solution)/shard_map/all_gather | solution.py:133
  883.1 12.5 fusion.277
  897.6 13.8 fusion.241
  911.5 42.8 %reduce-scatter.21.cloned.1.call-done = f32[4,32,2048]{2,1,0:T(8,128)} async-done(((f32[4,128,2048]{2,1,0:T(8,128)}), f32[4,32,2048]{2,1,0:T(8,128)}) %reduce-scatter.21.cloned.1.call-update) | async-done | bytes 1048592 | tf_op jit(solution)/shard_map/reduce_scatter | solution.py:143
  958.0 22.0 %all-gather.31.cloned.1.call-done = bf16[4,128,2048]{2,1,0:T(8,128)(2,1)} async-done(((bf16[4,32,2048]{2,1,0:T(8,128)(2,1)}), bf16[4,128,2048]{2,1,0:T(8,128)(2,1)}) %all-gather.31.cloned.1.call-update) | async-done | bytes 2097168 | tf_op jit(solution)/shard_map/all_gather | solution.py:197
  980.0 15.3 fusion.194
  1004.8 13.1 fusion.276
  1019.9 13.8 fusion.244
  1033.9 10.6 fusion.203
  1044.5 33.8 %reduce-scatter.25.cloned.1.call-done = f32[4,32,2048]{2,1,0:T(8,128)} async-done(((f32[4,128,2048]{2,1,0:T(8,128)}), f32[4,32,2048]{2,1,0:T(8,128)}) %reduce-scatter.25.cloned.1.call-update) | async-done | bytes 1048592 | tf_op jit(solution)/shard_map/reduce_scatter | solution.py:143
  1080.3 45.4 %reduce-scatter.19.cloned.1.call-done = f32[4,32,2048]{2,1,0:T(8,128)} async-done(((f32[4,128,2048]{2,1,0:T(8,128)}), f32[4,32,2048]{2,1,0:T(8,128)}) %reduce-scatter.19.cloned.1.call-update) | async-done | bytes 1048592 | tf_op jit(solution)/shard_map/reduce_scatter | solution.py:137
  1130.0 22.1 %all-gather.33.cloned.1.call-done = bf16[4,128,2048]{2,1,0:T(8,128)(2,1)} async-done(((bf16[4,32,2048]{2,1,0:T(8,128)(2,1)}), bf16[4,128,2048]{2,1,0:T(8,128)(2,1)}) %all-gather.33.cloned.1.call-update) | async-done | bytes 2097168 | tf_op jit(solution)/shard_map/all_gather | solution.py:140
  1157.1 19.7 all-gather.35.cloned.1.call-done
  1182.6 9.9 fusion.262
  1192.5 10.4 fusion.207
  1214.0 90.1 %while.174 = (s32[]{:T(128)}, f32[4,128,128]{2,1,0:T(8,128)S(1)}, f32[4,128]{1,0:T(4,128)S(1)}, f32[4,128,4,128]{3,1,2,0:T(8,128)}, f32[4,128,4,128]{3,1,2,0:T(8...) while((s32[]{:T(128)}, f32[4,128,128]{2,1,0:T(8,128)S(1)}, ...), condition=%wide.region_24.25_spmd.clone, body=%wide.region_21.24_spmd.clone.sunk | while | flops 608045056 | bytes 9658237 | solution.py:61
  1326.7 89.7 %while.175 = (s32[]{:T(128)}, f32[4,128,128]{2,1,0:T(8,128)S(1)}, f32[4,128]{1,0:T(4,128)S(1)}, f32[4,128,4,128]{3,1,2,0:T(8,128)}, f32[4,128,4,128]{3,1,2,0:T(8...) while((s32[]{:T(128)}, f32[4,128,128]{2,1,0:T(8,128)S(1)}, ...), condition=%wide.region_33.34_spmd.clone, body=%wide.region_30.33_spmd.clone.sunk | while | flops 608045056 | bytes 9658237 | solution.py:61
  1462.9 18.5 fusion.247
  1481.3 19.1 fusion.188
  1520.5 24.2 %reduce-scatter.15.cloned.1.call-done = f32[4,32,2048]{2,1,0:T(8,128)} async-done(((f32[4,128,2048]{2,1,0:T(8,128)}), f32[4,32,2048]{2,1,0:T(8,128)}) %reduce-scatter.15.cloned.1.call-update) | async-done | bytes 1048592 | tf_op jit(solution)/shard_map/reduce_scatter | solution.py:137
  1550.0 117.2 %reduce-scatter.29.cloned.1.call-done = bf16[256,3,512]{2,0,1:T(8,128)(2,1)} async-done(((bf16[2048,3,512]{2,0,1:T(8,128)(2,1)}), bf16[256,3,512]{2,0,1:T(8,128)(2,1)}) %reduce-scatter.29.cloned.1.call-update) | async-done | bytes 786448 | tf_op jit(solution)/shard_map/reduce_scatter | solution.py:281
  1670.6 281.9 %reduce-scatter.33.cloned.1.call-done = bf16[256,2,2048]{2,0,1:T(8,128)(2,1)} async-done(((bf16[2048,2,2048]{2,0,1:T(8,128)(2,1)}), bf16[256,2,2048]{2,0,1:T(8,128)(2,1)}) %reduce-scatter.33.cloned.1.call-update) | async-done | bytes 2097168 | tf_op jit(solution)/shard_map/reduce_scatter | solution.py:287
  1958.3 39.2 %all-reduce = (f32[]{:T(128)}, f32[2,2048]{1,0:T(2,128)S(1)}, f32[16]{0:T(128)S(1)}) all-reduce(f32[]{:T(128)S(6)} %add.417, f32[2,2048]{1,0:T(2,128)S(1)} %maximum_add_fusion, f32[16]{0:T(128)S(1)} %multiply_dynamic-update-slice_fusion.2), channel_id=1, replica_groups=mesh['seq'=8,'ctx'=4] {'seq','ctx'}, use_global_device_ids=true, to_apply=%region_44.45 | all-reduce | flops 4113 | bytes 32904 | tf_op jit(solution)/shard_map/psum | solution.py:304
  2000.7 13.4 multiply_subtract_fusion
  (899 shorter events, 652.7 us)
Async XLA Ops:
  7.2 31.4 %all-gather.17.cloned.1.call-start = ((), (), s32[]{:S(2)}) async-start(), calls=%async_computation.12 | async-start | bytes 2621440 | tf_op jit(solution)/shard_map/all_gather | solution.py:160
  8.1 1117.7 %copy-start.72 = (f32[1,2048]{1,0:T(1,128)}, f32[1,2048]{1,0:T(1,128)S(1)}, u32[]{:S(2)}) copy-start(f32[1,2048]{1,0:T(1,128)S(1)} %get-tuple-element.2830) | copy-start | bytes 24580
  12.8 127.6 %all-gather.19.cloned.1.call-start = ((), (), s32[]{:S(2)}) async-start(), calls=%async_computation.13 | async-start | bytes 7077888 | tf_op jit(solution)/shard_map/all_gather | solution.py:130
  13.9 243.6 %all-gather.29.cloned.1.call-start = ((), (), s32[]{:S(2)}) async-start(), calls=%async_computation.20 | async-start | bytes 2621440 | tf_op jit(solution)/shard_map/all_gather | solution.py:160
  14.6 365.4 %all-gather.21.cloned.1.call-start = ((), (), s32[]{:S(2)}) async-start(), calls=%async_computation.14 | async-start | bytes 2359296 | tf_op jit(solution)/shard_map/all_gather | solution.py:131
  15.5 413.3 %reduce-scatter.13.cloned.1.call-start = ((), (), s32[]{:S(2)}) async-start(), calls=%async_computation.15 | async-start | bytes 5242880 | tf_op jit(solution)/shard_map/reduce_scatter | solution.py:137
  265.4 108.3 %copy-start.37 = (bf16[4,128,1,4,128]{4,3,1,2,0:T(4,128)(2,1)}, bf16[4,128,1,4,128]{4,3,1,2,0:T(4,128)(2,1)S(1)}, u32[]{:S(2)}) copy-start(bf16[4,128,1,4,128]{4,3,1,2,0:T(4,128)(2,1)S(1)} %get-tuple-element.2815) | copy-start | bytes 1572868
  385.8 90.7 %reduce-scatter.17.cloned.1.call-start = ((), (), s32[]{:S(2)}) async-start(), calls=%async_computation.21 | async-start | bytes 5242880 | tf_op jit(solution)/shard_map/reduce_scatter | solution.py:137
  390.7 111.6 %all-gather.23.cloned.1.call-start = ((), (), s32[]{:S(2)}) async-start(), calls=%async_computation.16 | async-start | bytes 2621440 | tf_op jit(solution)/shard_map/all_gather | solution.py:197
  478.3 647.4 %copy-start.2 = (f32[4,32,2048]{2,1,0:T(8,128)}, f32[4,32,2048]{2,1,0:T(8,128)S(1)}, u32[]{:S(2)}) copy-start(f32[4,32,2048]{2,1,0:T(8,128)S(1)} %get-tuple-element.2827) | copy-start | bytes 3145732
  478.3 647.4 %copy-start.4 = (f32[4,32,2048]{2,1,0:T(8,128)}, f32[4,32,2048]{2,1,0:T(8,128)S(1)}, u32[]{:S(2)}) copy-start(f32[4,32,2048]{2,1,0:T(8,128)S(1)} %get-tuple-element.2728) | copy-start | bytes 3145732
  478.3 647.4 %copy-start.83 = (f32[4,32]{1,0:T(4,128)}, f32[4,32]{1,0:T(4,128)S(1)}, u32[]{:S(2)}) copy-start(f32[4,32]{1,0:T(4,128)S(1)} %fusion.362) | copy-start | bytes 1540
  479.5 253.1 %all-gather.25.cloned.1.call-start = ((), (), s32[]{:S(2)}) async-start(), calls=%async_computation.17 | async-start | bytes 18874368 | tf_op jit(solution)/shard_map/all_gather | solution.py:132
  485.4 270.2 %all-gather.37.cloned.1.call-start = ((), (), s32[]{:S(2)}) async-start(), calls=%async_computation.34 | async-start | bytes 2621440 | tf_op jit(solution)/shard_map/all_gather | solution.py:140
  486.5 396.6 %all-gather.27.cloned.1.call-start = ((), (), s32[]{:S(2)}) async-start(), calls=%async_computation.18 | async-start | bytes 9437184 | tf_op jit(solution)/shard_map/all_gather | solution.py:133
  489.7 464.6 %reduce-scatter.21.cloned.1.call-start = ((), (), s32[]{:S(2)}) async-start(), calls=%async_computation.24 | async-start | bytes 5242880 | tf_op jit(solution)/shard_map/reduce_scatter | solution.py:143
  911.4 68.6 %all-gather.31.cloned.1.call-start = ((), (), s32[]{:S(2)}) async-start(), calls=%async_computation.22 | async-start | bytes 2621440 | tf_op jit(solution)/shard_map/all_gather | solution.py:197
  911.5 214.3 %copy-start.85 = (f32[4,32]{1,0:T(4,128)}, f32[4,32]{1,0:T(4,128)S(1)}, u32[]{:S(2)}) copy-start(f32[4,32]{1,0:T(4,128)S(1)} %fusion.364) | copy-start | bytes 1540
  957.2 47.6 %all-gather.39.cloned.1.call-start = ((), (), s32[]{:S(2)}) async-start(), calls=%async_computation.35 | async-start | bytes 2621440 | tf_op jit(solution)/shard_map/all_gather | solution.py:140
  958.0 120.3 %reduce-scatter.25.cloned.1.call-start = ((), (), s32[]{:S(2)}) async-start(), calls=%async_computation.27 | async-start | bytes 5242880 | tf_op jit(solution)/shard_map/reduce_scatter | solution.py:143
  1033.6 92.1 %reduce-scatter.19.cloned.1.call-start = ((), (), s32[]{:S(2)}) async-start(), calls=%async_computation.23 | async-start | bytes 5242880 | tf_op jit(solution)/shard_map/reduce_scatter | solution.py:137
  1044.4 107.7 %all-gather.33.cloned.1.call-start = ((), (), s32[]{:S(2)}) async-start(), calls=%async_computation.25 | async-start | bytes 2621440 | tf_op jit(solution)/shard_map/all_gather | solution.py:140
  1129.4 47.4 %all-gather.35.cloned.1.call-start = ((), (), s32[]{:S(2)}) async-start(), calls=%async_computation.28 | async-start | bytes 2621440 | tf_op jit(solution)/shard_map/all_gather | solution.py:140
  1130.0 383.6 %reduce-scatter.31.cloned.1.call-start = ((), (), s32[]{:S(2)}) async-start(), calls=%async_computation.31 | async-start | bytes 2359296 | tf_op jit(solution)/shard_map/reduce_scatter | solution.py:284
  1182.3 333.0 %reduce-scatter.35.cloned.1.call-start = ((), (), s32[]{:S(2)}) async-start(), calls=%async_computation.33 | async-start | bytes 9437184 | tf_op jit(solution)/shard_map/reduce_scatter | solution.py:290
  1203.0 314.7 %reduce-scatter.23.cloned.1.call-start = ((), (), s32[]{:S(2)}) async-start(), calls=%async_computation.26 | async-start | bytes 5242880 | tf_op jit(solution)/shard_map/reduce_scatter | solution.py:143
  1214.0 90.1 %copy-start.106 = (f32[4]{0:T(128)S(1)}, f32[4]{0:T(128)}, u32[]{:S(2)}) copy-start(f32[4]{0:T(128)} %get-tuple-element.2731) | copy-start | bytes 52
  1323.4 194.3 %reduce-scatter.27.cloned.1.call-start = ((), (), s32[]{:S(2)}) async-start(), calls=%async_computation.29 | async-start | bytes 5242880 | tf_op jit(solution)/shard_map/reduce_scatter | solution.py:143
  1437.3 107.5 %reduce-scatter.15.cloned.1.call-start = ((), (), s32[]{:S(2)}) async-start(), calls=%async_computation.19 | async-start | bytes 5242880 | tf_op jit(solution)/shard_map/reduce_scatter | solution.py:137
  1448.4 218.8 %reduce-scatter.29.cloned.1.call-start = ((), (), s32[]{:S(2)}) async-start(), calls=%async_computation.30 | async-start | bytes 7077888 | tf_op jit(solution)/shard_map/reduce_scatter | solution.py:281
  1460.8 491.7 %reduce-scatter.33.cloned.1.call-start = ((), (), s32[]{:S(2)}) async-start(), calls=%async_computation.32 | async-start | bytes 18874368 | tf_op jit(solution)/shard_map/reduce_scatter | solution.py:287
  1549.4 407.8 %copy-start.55 = (bf16[1,4,32,2048]{3,2,1,0:T(8,128)(2,1)S(1)}, bf16[1,4,32,2048]{3,2,1,0:T(8,128)(2,1)}, u32[]{:S(2)}) copy-start(bf16[1,4,32,2048]{3,2,1,0:T(8,128)(2,1)} %get-tuple-element.2822) | copy-start | bytes 1572868
  (142 other events, 1361.7 us)
Sparse Core Ops, SparseCore 0:
  12.9 25.6 all-gather.16
  41.4 99.0 all-gather.18
  142.6 20.7 all-gather.28
  165.9 49.4 all-gather.20
  385.9 42.8 reduce-scatter.12
  431.9 44.5 reduce-scatter.16
  479.6 22.5 all-gather.22
  505.0 227.5 all-gather.24
  734.8 20.7 all-gather.36
  758.1 124.9 all-gather.26
  911.5 42.6 reduce-scatter.20
  957.3 22.5 all-gather.30
  982.2 22.5 all-gather.38
  1033.8 44.4 reduce-scatter.24
  1081.2 44.4 reduce-scatter.18
  1129.5 22.5 all-gather.32
  1154.2 22.5 all-gather.34
  1182.4 67.8 reduce-scatter.30
  1254.4 148.3 reduce-scatter.34
  1405.8 43.4 reduce-scatter.22
  1452.6 44.4 reduce-scatter.26
  1500.2 44.4 reduce-scatter.14
  1548.8 118.3 reduce-scatter.28
  1671.3 281.1 reduce-scatter.32
where the time goes:
time: 2070 us; the launch traced here: 2060 us
  waiting for transfers between devices  1190 us (57%)
  matrix products  394 us (19%)
  local copies, waits for them, and re-layouts  211 us (10%)
  other arithmetic  172 us (8%)
  blocking collectives  51.1 us (2%)
  between operations  21.8 us (1%)
    reduce_scatter x1, waiting for transfers between devices, on_device(): lax.psum_scatter(grad_mlp.astype(jnp.bfloat16), 'seq', scatter_dimension=...  282 us
    all_gather x1, waiting for transfers between devices, fetch_weights(): lax.all_gather(shards[2], 'seq', axis=0, tiled=True)  230 us
    reduce_scatter x4, waiting for transfers between devices, reduce_rows(): lax.psum_scatter(partial_term, 'ctx', scatter_dimension=1, tiled=True)  155 us
    all_gather x1, waiting for transfers between devices, fetch_weights(): lax.all_gather(shards[3], 'seq', axis=0, tiled=True)  128 us
    reduce_scatter x1, waiting for transfers between devices, on_device(): lax.psum_scatter(grad_qkv.astype(jnp.bfloat16), 'seq', scatter_dimension=...  117 us
    all_gather x1, waiting for transfers between devices, fetch_weights(): lax.all_gather(shards[0], 'seq', axis=0, tiled=True)  102 us
    reduce_scatter x4, waiting for transfers between devices, collect_rows(): lax.psum_scatter(partial_term, 'ctx', scatter_dimension=1, tiled=True)  76.5 us
    dynamic_update_slice x64, other arithmetic, memory_read(): lax.scan(advance, initial, (queries, keys_in, values_in, doc_rows))  70.8 us
  transfers between devices with their start and end apart: 24, of which 18 were waited for; matrix products, arithmetic and copies ran while one was open for 30% of the time, Pallas kernels for 0%

commit v1 on v0

v1 whole, which is shorter than its diff:
```python
import functools

import jax
import jax.numpy as jnp
from jax import lax
from jax.experimental import pallas as pl
from jax.experimental.pallas import tpu as pltpu
from jax.sharding import Mesh
from jax.sharding import PartitionSpec as P

D = 2048
HEADS = 16
HEAD_DIM = 128
FF = 8192
STEP_COUNT = 10
CHUNKS = 2

EPS = 1e-06
NEG = -1e30
CLIP = 1.0
BETA1 = 0.9
BETA2 = 0.95
ADAM_EPS = 1e-08
DECAY = 0.1
BF = jnp.bfloat16
F32 = jnp.float32
SCALING = HEAD_DIM ** (-0.5)
VMEM_LIMIT = 48 * 1024 * 1024


def rms_norm(tensor, scaling):
    return tensor * lax.rsqrt(jnp.mean(tensor * tensor, axis=-1, keepdims=True) + EPS) * scaling


def adam_update(weight, moment, second, gradient, factor, step_rate, decay):
    clipped = gradient * factor
    moment = BETA1 * moment + (1.0 - BETA1) * clipped
    second = BETA2 * second + (1.0 - BETA2) * clipped * clipped
    fixed_first = moment / (1.0 - BETA1**STEP_COUNT)
    fixed_second = second / (1.0 - BETA2**STEP_COUNT)
    updated = weight - step_rate * (
        fixed_first / (jnp.sqrt(fixed_second) + ADAM_EPS) + decay * weight
    )
    return (moment, second, updated)


def swap(tensor, axis):
    return lax.ppermute(tensor, axis, [(0, 1), (1, 0)])


def gather_tokens(own, outer, inner):
    by_inner = swap(own, inner)
    by_outer = swap(own, outer)
    by_both = swap(by_inner, outer)
    pieces = [own, by_inner, by_outer, by_both]
    pieces = pieces + [swap(p, "c") for p in pieces]
    return jnp.concatenate([p[None] for p in pieces], axis=0)


def scatter_tokens(partial, outer, inner):
    half = partial[:4].astype(F32) + swap(partial[4:], "c").astype(F32)
    low = half.astype(BF)
    half = half[:2] + swap(low[2:], outer).astype(F32)
    low = half.astype(BF)
    return half[0] + swap(low[1], inner).astype(F32)


def mm(a, b, dims):
    return lax.dot_general(a, b, (dims, ((), ())), preferred_element_type=F32)


NN = ((1,), (0,))
NT = ((1,), (1,))
TN = ((0,), (0,))


def mm_mem(a, b, dims):
    return mm(a.astype(BF), b.astype(BF), dims)


def elu_one(tensor):
    return jnp.where(tensor > 0, tensor + 1.0, jnp.exp(jnp.minimum(tensor, 0.0)))


def elu_slope(tensor):
    low = jnp.where(tensor == 0, 0.5, jnp.exp(jnp.minimum(tensor, 0.0)))
    return jnp.where(tensor > 0, 1.0, low)


def segment_of(ref, r, part):
    block = ref[:, :, r, :, part * HEAD_DIM : (part + 1) * HEAD_DIM]
    return block.reshape(-1, HEAD_DIM)


def memory_forward(qs, ks, vs, cols):
    seg_count = len(qs)
    saved = []
    memory = normer = None
    for r in range(seg_count):
        reading, writing, keep = cols[r]
        sq = elu_one(qs[r].astype(F32))
        sk = elu_one(ks[r].astype(F32))
        value = vs[r].astype(F32)
        rows = sq.shape[0]
        item = dict(sq=sq, sk=sk)
        if r == 0:
            item["recalled"] = jnp.zeros_like(sq)
            change = value
        else:
            both = mm_mem(jnp.concatenate([sq, sk], axis=0), memory, NN)
            num = both[:rows]
            den = 1.0 + jnp.sum(sq * normer, axis=-1, keepdims=True)
            item["recalled"] = reading * num / den
            before = keep * both[rows:]
            kden = 1.0 + keep * jnp.sum(sk * normer, axis=-1, keepdims=True)
            change = value - before / kden
            item.update(num=num, den=den, before=before, kden=kden, memory=memory, normer=normer)
        item["change"] = change
        if r < seg_count - 1:
            write = sk * writing
            fresh = mm_mem(write, change, TN)
            fresh_norm = jnp.sum(write, axis=0, keepdims=True)
            memory = fresh if r == 0 else keep * memory + fresh
            normer = fresh_norm if r == 0 else keep[:1] * normer + fresh_norm
        saved.append(item)
    return saved


def local_probs(query, key, allowed):
    scores = jnp.where(allowed > 0, mm(query, key, NT) * SCALING, NEG)
    exponent = jnp.exp(scores - jnp.max(scores, axis=-1, keepdims=True))
    return exponent / jnp.sum(exponent, axis=-1, keepdims=True)


def columns_of(cols_ref, r):
    cols = cols_ref[r]
    return cols[:, 0:1], cols[:, 1:2], cols[:, 2:3]


def attention_fwd_kernel(heads, proj_ref, mask_ref, cols_ref, gate_ref, out_ref):
    seg_count = mask_ref.shape[0]
    cols = [columns_of(cols_ref, r) for r in range(seg_count)]
    for h in range(heads):
        qs = [segment_of(proj_ref, r, h) for r in range(seg_count)]
        ks = [segment_of(proj_ref, r, heads + h) for r in range(seg_count)]
        vs = [segment_of(proj_ref, r, 2 * heads + h) for r in range(seg_count)]
        saved = memory_forward(qs, ks, vs, cols)
        mixing = gate_ref[h : h + 1]
        for r in range(seg_count):
            prob_low = local_probs(qs[r], ks[r], mask_ref[r]).astype(BF)
            local_out = mm(prob_low, vs[r], NN)
            combined = mixing * saved[r]["recalled"] + (1.0 - mixing) * local_out
            out_ref[:, :, r, :, h * HEAD_DIM : (h + 1) * HEAD_DIM] = combined.astype(BF).reshape(
                out_ref.shape[0], out_ref.shape[1], out_ref.shape[3], HEAD_DIM
            )


def attention_bwd_kernel(
    heads, proj_ref, grad_ref, mask_ref, cols_ref, gate_ref, out_ref, gate_out_ref
):
    seg_count = mask_ref.shape[0]
    cols = [columns_of(cols_ref, r) for r in range(seg_count)]

    def put(r, part, value):
        out_ref[:, :, r, :, part * HEAD_DIM : (part + 1) * HEAD_DIM] = value.astype(BF).reshape(
            out_ref.shape[0], out_ref.shape[1], out_ref.shape[3], HEAD_DIM
        )

    for h in range(heads):
        qs = [segment_of(proj_ref, r, h) for r in range(seg_count)]
        ks = [segment_of(proj_ref, r, heads + h) for r in range(seg_count)]
        vs = [segment_of(proj_ref, r, 2 * heads + h) for r in range(seg_count)]
        saved = memory_forward(qs, ks, vs, cols)
        mixing = gate_ref[h : h + 1]
        gate_sum = jnp.zeros((1, HEAD_DIM), F32)
        d_memory = d_normer = None
        for r in reversed(range(seg_count)):
            reading, writing, keep = cols[r]
            item = saved[r]
            sq, sk = item["sq"], item["sk"]
            rows = sq.shape[0]
            d_combined = segment_of(grad_ref, r, h).astype(F32)
            d_recalled = mixing * d_combined
            d_local = ((1.0 - mixing) * d_combined).astype(BF)
            probs = local_probs(qs[r], ks[r], mask_ref[r])
            prob_low = probs.astype(BF)
            local_out = mm(prob_low, vs[r], NN)
            gate_sum = gate_sum + jnp.sum(
                d_combined * (item["recalled"] - local_out), axis=0, keepdims=True
            )
            d_prob = mm(d_local, vs[r], NT)
            d_value = mm(prob_low, d_local, TN)
            d_scores = (
                probs * (d_prob - jnp.sum(d_prob * probs, axis=-1, keepdims=True))
            ).astype(BF)
            d_query = mm(d_scores, ks[r], NN) * SCALING
            d_key = mm(d_scores, qs[r], TN) * SCALING
            d_sk = None
            d_before = d_kden = None
            if r < seg_count - 1:
                d_change = writing * mm_mem(sk, d_memory, NN)
                d_sk = writing * (mm_mem(item["change"], d_memory, NT) + d_normer)
                d_value = d_value + d_change
                if r > 0:
                    d_before = keep * (-d_change / item["kden"])
                    d_kden = keep * (
                        jnp.sum(d_change * item["before"], axis=-1, keepdims=True)
                        / (item["kden"] * item["kden"])
                    )
            if r > 0:
                d_num = reading * d_recalled / item["den"]
                d_den = -reading * (
                    jnp.sum(d_recalled * item["num"], axis=-1, keepdims=True)
                    / (item["den"] * item["den"])
                )
                if d_before is None:
                    d_sq = mm_mem(d_num, item["memory"], NT) + d_den * item["normer"]
                    new_memory = mm_mem(sq, d_num, TN)
                    new_normer = jnp.sum(sq * d_den, axis=0, keepdims=True)
                else:
                    stacked = jnp.concatenate([d_num, d_before], axis=0)
                    both = mm_mem(stacked, item["memory"], NT)
                    d_sq = both[:rows] + d_den * item["normer"]
                    d_sk = d_sk + both[rows:] + d_kden * item["normer"]
                    new_memory = keep * d_memory + mm_mem(
                        jnp.concatenate([sq, sk], axis=0), stacked, TN
                    )
                    new_normer = keep[:1] * d_normer + jnp.sum(
                        sq * d_den + sk * d_kden, axis=0, keepdims=True
                    )
                d_memory, d_normer = new_memory, new_normer
                d_query = d_query + d_sq * elu_slope(qs[r].astype(F32))
            if d_sk is not None:
                d_key = d_key + d_sk * elu_slope(ks[r].astype(F32))
            put(r, h, d_query)
            put(r, heads + h, d_key)
            put(r, 2 * heads + h, d_value)
        gate_out_ref[h : h + 1] = gate_sum


def block_spec(shape, where):
    dims = list(shape)
    dims[where] = None

    def index(s):
        place = [0] * len(dims)
        place[where] = s
        return tuple(place)

    return pl.BlockSpec(tuple(dims), index)


def attention_fwd(projected, mask, cols, gate_rows, where):
    heads = gate_rows.shape[0]
    out_shape = projected.shape[:-1] + (heads * HEAD_DIM,)
    return pl.pallas_call(
        functools.partial(attention_fwd_kernel, heads),
        grid=(projected.shape[where],),
        in_specs=[
            block_spec(projected.shape, where),
            pl.BlockSpec((None,) + mask.shape[1:], lambda s: (s, 0, 0, 0)),
            pl.BlockSpec((None,) + cols.shape[1:], lambda s: (s, 0, 0, 0)),
            pl.BlockSpec(gate_rows.shape, lambda s: (0, 0)),
        ],
        out_specs=block_spec(out_shape, where),
        out_shape=jax.ShapeDtypeStruct(out_shape, BF),
        compiler_params=pltpu.CompilerParams(vmem_limit_bytes=VMEM_LIMIT),
        cost_estimate=pl.CostEstimate(
            flops=400_000_000 * 50, bytes_accessed=6_000_000, transcendentals=0
        ),
        name="attention_forward",
    )(projected, mask, cols, gate_rows)


def attention_bwd(projected, d_combined, mask, cols, gate_rows, where):
    heads = gate_rows.shape[0]
    seqs = projected.shape[where]
    return pl.pallas_call(
        functools.partial(attention_bwd_kernel, heads),
        grid=(seqs,),
        in_specs=[
            block_spec(projected.shape, where),
            block_spec(d_combined.shape, where),
            pl.BlockSpec((None,) + mask.shape[1:], lambda s: (s, 0, 0, 0)),
            pl.BlockSpec((None,) + cols.shape[1:], lambda s: (s, 0, 0, 0)),
            pl.BlockSpec(gate_rows.shape, lambda s: (0, 0)),
        ],
        out_specs=[
            block_spec(projected.shape, where),
            pl.BlockSpec((None, heads, HEAD_DIM), lambda s: (s, 0, 0)),
        ],
        out_shape=[
            jax.ShapeDtypeStruct(projected.shape, BF),
            jax.ShapeDtypeStruct((seqs, heads, HEAD_DIM), F32),
        ],
        compiler_params=pltpu.CompilerParams(vmem_limit_bytes=VMEM_LIMIT),
        cost_estimate=pl.CostEstimate(
            flops=1_000_000_000 * 50, bytes_accessed=10_000_000, transcendentals=0
        ),
        name="attention_backward",
    )(projected, d_combined, mask, cols, gate_rows)


GELU_A = 0.7978845608028654
GELU_B = 0.044715


def ff_kernel(width, x_ref, g_ref, w_ref, act_ref, grad_ref):
    weights = w_ref[...]
    gate_up = mm(x_ref[...], weights[:, : 2 * width], NN)
    d_active = mm(g_ref[...], weights[:, 2 * width :], NN)
    gate = gate_up[:, :width]
    up = gate_up[:, width:]
    square = gate * gate
    tanh = jnp.tanh(GELU_A * gate * (1.0 + GELU_B * square))
    half = 0.5 * (1.0 + tanh)
    gelu = gate * half
    slope = half + 0.5 * gate * (1.0 - tanh * tanh) * GELU_A * (1.0 + 3.0 * GELU_B * square)
    act_ref[...] = (gelu * up).astype(BF)
    grad_ref[:, :width] = (d_active * up * slope).astype(BF)
    grad_ref[:, width:] = (d_active * gelu).astype(BF)


def feed_forward(rows, grads, weights):
    tokens = rows.shape[0]
    width = weights.shape[1] // 3
    tile = 256
    return pl.pallas_call(
        functools.partial(ff_kernel, width),
        grid=(tokens // tile,),
        in_specs=[
            pl.BlockSpec((tile, D), lambda i: (i, 0)),
            pl.BlockSpec((tile, D), lambda i: (i, 0)),
            pl.BlockSpec(weights.shape, lambda i: (0, 0)),
        ],
        out_specs=[
            pl.BlockSpec((tile, width), lambda i: (i, 0)),
            pl.BlockSpec((tile, 2 * width), lambda i: (i, 0)),
        ],
        out_shape=[
            jax.ShapeDtypeStruct((tokens, width), BF),
            jax.ShapeDtypeStruct((tokens, 2 * width), BF),
        ],
        compiler_params=pltpu.CompilerParams(vmem_limit_bytes=VMEM_LIMIT),
        cost_estimate=pl.CostEstimate(
            flops=2 * tokens * D * 3 * width,
            bytes_accessed=2 * (2 * tokens * D + 3 * D * width + 3 * tokens * width),
            transcendentals=tokens * width,
        ),
        name="feed_forward",
    )(rows, grads, weights)


def on_device(
    inputs,
    doc_ids,
    cotangent,
    weight_qkv,
    moment_qkv,
    second_qkv,
    weight_out,
    moment_out,
    second_out,
    weight_mlp,
    moment_mlp,
    second_mlp,
    weight_down,
    moment_down,
    second_down,
    norm_gains,
    moment_gains,
    second_gains,
    gate_logit,
    moment_gate,
    second_gate,
):
    micro_count, _, seg_count, own_len, _ = inputs.shape
    own_tokens = seg_count * own_len
    x_place = lax.axis_index("x")
    y_place = lax.axis_index("y")
    c_place = lax.axis_index("c")
    is_low = x_place == 0
    orders = [("x", "y") if m % 2 == 0 else ("y", "x") for m in range(micro_count)]

    def half_columns(weight, which):
        width = weight.shape[-1] // 2
        return lax.dynamic_slice_in_dim(weight, which * width, width, axis=weight.ndim - 1)

    def by_place(own, other, axis):
        return jnp.where(
            is_low,
            jnp.concatenate([own, other], axis=axis),
            jnp.concatenate([other, own], axis=axis),
        )

    def exchange_weight(weight):
        low = weight.astype(BF)
        mine = half_columns(low, x_place)
        theirs = swap(half_columns(low, 1 - x_place), "x")
        return by_place(mine, theirs, 0)

    def fetch(block):
        return lax.all_gather(block, "z", axis=0, tiled=True)

    shard_qkv = exchange_weight(weight_qkv)
    heads = shard_qkv.shape[2] // HEAD_DIM
    width_att = shard_qkv.shape[2]
    full_qkv = fetch(shard_qkv.reshape(-1, 3 * width_att))
    full_out = fetch(exchange_weight(weight_out))
    shard_mlp = exchange_weight(weight_mlp)
    shard_down = exchange_weight(weight_down)
    width_ff = shard_down.shape[1]
    width = width_ff // CHUNKS
    full_ff = []
    for k in range(CHUNKS):
        part = slice(k * width, (k + 1) * width)
        full_ff.append(
            fetch(
                jnp.concatenate(
                    [shard_mlp[:, 0, part], shard_mlp[:, 1, part], shard_down[:, part]], axis=1
                )
            )
        )

    head_start = (y_place * 2 + c_place) * (2 * heads) + x_place * heads
    gate_local = lax.dynamic_slice_in_dim(gate_logit, head_start, heads)
    mixing = jax.nn.sigmoid(gate_local)
    gate_rows = jnp.broadcast_to(mixing[:, None], (heads, HEAD_DIM))

    token_rows = [
        inputs[m, 0].reshape(own_tokens, D).astype(F32) for m in range(micro_count)
    ]
    back_low = [cotangent[m, 0].reshape(own_tokens, D) for m in range(micro_count)]

    normed_att = [rms_norm(t, norm_gains[0]).astype(BF) for t in token_rows]
    att_rows = [
        gather_tokens(normed_att[m], *orders[m]).reshape(8 * own_tokens, D)
        for m in range(micro_count)
    ]
    gathered_ids = [gather_tokens(doc_ids[m, 0], *orders[m]) for m in range(micro_count)]
    all_back = jnp.concatenate(
        [gather_tokens(back_low[m], *orders[m]).reshape(8 * own_tokens, D) for m in range(micro_count)],
        axis=0,
    )

    rel_c = jnp.arange(2)[:, None, None] ^ c_place
    rel_y = jnp.arange(2)[None, :, None] ^ y_place
    places = ((rel_y * 2 + rel_c) * own_len + jnp.arange(own_len)).reshape(-1)
    causal = places[:, None] >= places[None, :]
    masks = []
    columns = []
    for m in range(micro_count):
        ids = gathered_ids[m].reshape(2, 2, 2, seg_count, own_len)
        where = 1 if orders[m][0] == "x" else 2
        ids = jnp.moveaxis(ids, where, 0)
        ids = jnp.moveaxis(ids, 3, 1).reshape(2, seg_count, -1)
        same = ids[:, :, :, None] == ids[:, :, None, :]
        masks.append((same & causal).astype(F32))
        last = jnp.max(ids, axis=2)
        previous = jnp.concatenate([jnp.full((2, 1), -1, last.dtype), last[:, :-1]], axis=1)
        reading = ids == previous[:, :, None]
        writing = ids == last[:, :, None]
        keep = jnp.broadcast_to((last == previous)[:, :, None], ids.shape)
        columns.append(jnp.stack([reading, writing, keep], axis=-1).astype(F32))

    slots = (2, 2, 2, seg_count, own_len)
    projected = []
    combined = []
    hidden = []
    normed_mlp = []
    for m in range(micro_count):
        where = 1 if orders[m][0] == "x" else 2
        proj = mm(att_rows[m], full_qkv, NN).astype(BF)
        projected.append(proj.reshape(slots + (3 * width_att,)))
        comb = attention_fwd(projected[m], masks[m], columns[m], gate_rows, where)
        combined.append(comb.reshape(8 * own_tokens, width_att))
        partial = mm(combined[m], full_out, NT).astype(BF)
        attended = scatter_tokens(partial.reshape(8, own_tokens, D), *orders[m])
        hidden.append(token_rows[m] + attended)
        normed_mlp.append(rms_norm(hidden[m], norm_gains[1]).astype(BF))
    mlp_rows = jnp.concatenate(
        [
            gather_tokens(normed_mlp[m], *orders[m]).reshape(8 * own_tokens, D)
            for m in range(micro_count)
        ],
        axis=0,
    )

    def reduce_rows(partial):
        return lax.psum_scatter(partial, "z", scatter_dimension=0, tiled=True)

    active = []
    d_gate_up = []
    own_ff = []
    for k in range(CHUNKS):
        act, grad = feed_forward(mlp_rows, all_back, full_ff[k])
        active.append(act)
        d_gate_up.append(grad)
        grad_ff = jnp.concatenate(
            [mm(mlp_rows, grad, TN).astype(BF), mm(all_back, act, TN).astype(BF)], axis=1
        )
        own_ff.append(reduce_rows(grad_ff))
    d_partial = sum(mm(d_gate_up[k], full_ff[k][:, : 2 * width], NT) for k in range(CHUNKS)).astype(BF)
    out_partial = sum(mm(active[k], full_ff[k][:, 2 * width :], NT) for k in range(CHUNKS)).astype(BF)
    d_partial = d_partial.reshape(micro_count, 8, own_tokens, D)
    out_partial = out_partial.reshape(micro_count, 8, own_tokens, D)

    gain_grad_att = jnp.zeros((D,), F32)
    gain_grad_mlp = jnp.zeros((D,), F32)
    d_hidden = []
    for m in range(micro_count):
        d_normed = scatter_tokens(d_partial[m], *orders[m])
        ignored, norm_back = jax.vjp(rms_norm, hidden[m], norm_gains[1])
        d_norm, d_gain = norm_back(d_normed)
        gain_grad_mlp = gain_grad_mlp + d_gain
        d_hidden.append(back_low[m].astype(F32) + d_norm)

    gate_sum = jnp.zeros((heads,), F32)
    grad_qkv = jnp.zeros((D, 3 * width_att), F32)
    grad_out = jnp.zeros((D, width_att), F32)
    grad_rows = []
    for m in range(micro_count):
        where = 1 if orders[m][0] == "x" else 2
        att_grads = gather_tokens(d_hidden[m].astype(BF), *orders[m]).reshape(8 * own_tokens, D)
        d_combined = mm(att_grads, full_out, NN)
        grad_out = grad_out + mm(att_grads, combined[m], TN)
        d_proj, gate_part = attention_bwd(
            projected[m],
            d_combined.reshape(slots + (width_att,)),
            masks[m],
            columns[m],
            gate_rows,
            where,
        )
        gate_sum = gate_sum + jnp.sum(gate_part, axis=(0, 2))
        d_proj = d_proj.reshape(8 * own_tokens, 3 * width_att)
        grad_qkv = grad_qkv + mm(att_rows[m], d_proj, TN)
        partial = mm(d_proj, full_qkv, NT).astype(BF).reshape(8, own_tokens, D)
        d_normed = scatter_tokens(partial, *orders[m])
        ignored, norm_first = jax.vjp(rms_norm, token_rows[m], norm_gains[0])
        d_norm, d_gain = norm_first(d_normed)
        gain_grad_att = gain_grad_att + d_gain
        grad_rows.append((d_hidden[m] + d_norm).astype(BF))
    own_out = reduce_rows(grad_out.astype(BF))
    own_qkv = reduce_rows(grad_qkv.astype(BF))

    block_out = []
    for m in range(micro_count):
        mlp_out = scatter_tokens(out_partial[m], *orders[m])
        block_out.append((hidden[m] + mlp_out).astype(BF))

    def exchange_grad(grad):
        rows = grad.shape[0] // 2
        mine = lax.dynamic_slice_in_dim(grad, x_place * rows, rows, axis=0)
        theirs = swap(lax.dynamic_slice_in_dim(grad, (1 - x_place) * rows, rows, axis=0), "x")
        return mine, theirs

    def join(mine, theirs):
        return by_place(mine, theirs, mine.ndim - 1).astype(F32)

    parts = [exchange_grad(g) for g in own_ff]
    rows = weight_qkv.shape[0]
    sides = []
    for side in range(2):
        stacked = jnp.stack([p[side].reshape(rows, 3, width) for p in parts], axis=2)
        sides.append(stacked.reshape(rows, 3, width_ff))
    ff_grad = join(*sides)
    own_mlp, own_down = ff_grad[:, :2], ff_grad[:, 2]
    own_out = join(*exchange_grad(own_out))
    mine, theirs = exchange_grad(own_qkv)
    own_qkv = join(mine.reshape(rows, 3, width_att), theirs.reshape(rows, 3, width_att))

    gate_grad = gate_sum * mixing * (1.0 - mixing)
    gate_padded = lax.dynamic_update_slice(
        jnp.zeros(gate_logit.shape, F32), gate_grad, (head_start,)
    )
    owned = (
        jnp.sum(own_qkv * own_qkv)
        + jnp.sum(own_out * own_out)
        + jnp.sum(own_mlp * own_mlp)
        + jnp.sum(own_down * own_down)
    )
    everywhere = ("z", "x", "y", "c")
    gain_grad = jnp.stack([gain_grad_att, gain_grad_mlp], axis=0)
    gains_total, gate_total, owned_total = lax.psum((gain_grad, gate_padded, owned), everywhere)
    squares = owned_total + jnp.sum(gains_total * gains_total) + jnp.sum(gate_total * gate_total)
    grad_norm = jnp.sqrt(squares)
    factor = jnp.minimum(1.0, CLIP / (grad_norm + 1e-06))
    qkv_new = adam_update(weight_qkv, moment_qkv, second_qkv, own_qkv, factor, D ** (-0.5), DECAY)
    out_new = adam_update(
        weight_out, moment_out, second_out, own_out, factor, 4.0 * (HEADS * HEAD_DIM) ** (-0.5), DECAY
    )
    mlp_new = adam_update(weight_mlp, moment_mlp, second_mlp, own_mlp, factor, D ** (-0.5), DECAY)
    down_new = adam_update(
        weight_down, moment_down, second_down, own_down, factor, FF ** (-0.5), DECAY
    )
    gains_new = adam_update(norm_gains, moment_gains, second_gains, gains_total, factor, 0.5, 0.0)
    gate_new = adam_update(gate_logit, moment_gate, second_gate, gate_total, factor, 1.0, 0.0)
    shape = (micro_count, 1, seg_count, own_len, D)
    return (
        jnp.stack(block_out, axis=0).reshape(shape),
        jnp.stack(grad_rows, axis=0).reshape(shape),
        grad_norm,
        *qkv_new,
        *out_new,
        *mlp_new,
        *down_new,
        *gains_new,
        *gate_new,
    )


def solution(mesh):
    seq_count, ctx_count = mesh.devices.shape
    inner = Mesh(
        mesh.devices.reshape(seq_count // 2, 2, ctx_count // 2, 2), ("z", "x", "y", "c")
    )
    seq, ctx = ("z", "x"), ("y", "c")
    rows = P(None, seq, None, ctx, None)
    wide = P(seq, None, ctx)
    flat = P(seq, ctx)
    weights = (wide,) * 3 + (flat,) * 3 + (wide,) * 3 + (flat,) * 3 + (P(),) * 6
    return jax.shard_map(
        on_device,
        mesh=inner,
        in_specs=(rows, P(None, seq, None, ctx), rows) + weights,
        out_specs=(rows, rows, P()) + weights,
        check_vma=False,
    )
```

time: 2070 us -> 1090 us (0.53)
  waiting for transfers between devices: 1190 us -> 429 us
  matrix products: 394 us -> 139 us
  Pallas kernels: 0 us -> 79.6 us
  starting transfers between devices: 1.58 us -> 65 us
  other arithmetic: 172 us -> 115 us
    all_gather x12 -> x4, waiting for transfers between devices: 561 us -> 0.01 us  [fetch(): return lax.all_gather(block, 'z', axis=0, tiled=True)]
    reduce_scatter x12 -> x4, waiting for transfers between devices: 631 us -> 131 us  [reduce_rows(): return lax.psum_scatter(partial, 'z', scatter_dimension=0, tiled=True)]
    ppermute x0 -> x102, waiting for transfers between devices: none -> 298 us  [swap(): return lax.ppermute(tensor, axis, [(0, 1), (1, 0)])]
    dot_general x140 -> x20, matrix products: 394 us -> 139 us  [mm(): return lax.dot_general(a, b, (dims, ((), ())), preferred_element_type=F32)]
    unnamed x268 -> x294, local copies, waits for them, and re-layouts: 59 us -> 149 us
    pallas_call x0 -> x6, Pallas kernels: none -> 79.6 us  [the longest x2 40.6 us: feed_forward(): pl.pallas_call(functools.partial(ff_kernel, width), grid=(tokens // tile,...]
    dynamic_update_slice x65 -> x1, other arithmetic: 71.3 us -> 0.16 us  [on_device(): lax.dynamic_update_slice(jnp.zeros(gate_logit.shape, F32), gate_grad, (he...]
    ppermute x0 -> x102, starting transfers between devices: none -> 64 us  [swap(): return lax.ppermute(tensor, axis, [(0, 1), (1, 0)])]
  transfers between devices with their start and end apart: 24 -> 110, of which waited for: 18 -> 45; matrix products, arithmetic and copies ran while one was open for 30% -> 28% of each run, Pallas kernels for 0% -> 5%
where the time goes in v1:
time: 1090 us
  waiting for transfers between devices  429 us (39%)
  local copies, waits for them, and re-layouts  194 us (18%)
  matrix products  139 us (13%)
  other arithmetic  115 us (11%)
  Pallas kernels  79.6 us (7%)
  starting transfers between devices  65 us (6%)
  blocking collectives  41.5 us (4%)
  between operations  22.2 us (2%)
    ppermute x102, waiting for transfers between devices, swap(): return lax.ppermute(tensor, axis, [(0, 1), (1, 0)])  298 us
    unnamed x294, local copies, waits for them, and re-layouts  149 us
    dot_general x20, matrix products, mm(): return lax.dot_general(a, b, (dims, ((), ())), preferred_element_type=F32)  139 us
    reduce_scatter x4, waiting for transfers between devices, reduce_rows(): return lax.psum_scatter(partial, 'z', scatter_dimension=0, tiled=True)  131 us
    ppermute x102, starting transfers between devices, swap(): return lax.ppermute(tensor, axis, [(0, 1), (1, 0)])  64 us
    psum x1, blocking collectives, on_device(): lax.psum((gain_grad, gate_padded, owned), everywhere)  41.5 us
    pallas_call x2, Pallas kernels, feed_forward(): pl.pallas_call(functools.partial(ff_kernel, width), grid=(tokens // tile,...  40.6 us
    sub x6, other arithmetic, adam_update(): weight - step_rate * (fixed_first / (jnp.sqrt(fixed_second) + ADAM_EPS) +...  26.7 us
  transfers between devices with their start and end apart: 110, of which 45 were waited for; matrix products, arithmetic and copies ran while one was open for 28% of the time, Pallas kernels for 5%

profile of v1, /device:TPU:0, one launch (start us, length us, event | category | flops | bytes accessed | tf_op | source)
XLA Modules:
  0.0 1085.1 jit_solution(10833907898203309767)
XLA Ops:
  13.3 9.3 collective-permute-done.7
  49.4 21.7 %collective-permute-done.65 = bf16[256,1024]{1,0:T(8,128)(2,1)} collective-permute-done((bf16[256,1024]{1,0:T(8,128)(2,1)}, bf16[256,1024]{1,0:T(8,128)(2,1)}, u32[]{:S(2)}, u32[]{:S(2)}) %collective-permute-start.65) | collective-permute-done | bytes 524320 | tf_op jit(solution)/shard_map/ppermute | solution.py:48
  87.3 10.4 collective-permute-done.10
  138.5 9.2 collective-permute-done.57
  153.7 10.5 collective-permute-done.28
  170.7 11.9 %collective-permute-done.2 = bf16[128,2048]{1,0:T(8,128)(2,1)S(1)} collective-permute-done((bf16[128,2048]{1,0:T(8,128)(2,1)}, bf16[128,2048]{1,0:T(8,128)(2,1)S(1)}, u32[]{:S(2)}, u32[]{:S(2)}) %collective-permute-start.2) | collective-permute-done | bytes 524320 | tf_op jit(solution)/shard_map/ppermute | solution.py:48
  188.0 9.8 collective-permute-done.52
  252.9 20.7 %collective-permute-done.41 = bf16[2,128,2048]{2,1,0:T(8,128)(2,1)S(1)} collective-permute-done((bf16[2,128,2048]{2,1,0:T(8,128)(2,1)S(1)}, bf16[2,128,2048]{2,1,0:T(8,128)(2,1)S(1)}, u32[]{:S(2)}, u32[]{:S(2)}) %collective-permute-start.41) | collective-permute-done | bytes 1048608 | tf_op jit(solution)/shard_map/ppermute | solution.py:48
  320.7 8.6 collective-permute-done.21
  334.0 9.0 collective-permute-done.45
  357.8 20.1 %feed_forward.3 = (bf16[2048,512]{1,0:T(8,128)(2,1)S(1)}, bf16[2048,1024]{1,0:T(8,128)(2,1)}) custom-call(bf16[2048,2048]{1,0:T(8,128)(2,1)} %pad_maximum_fusion.x_ref, bf16[2048,2048]{1,0:T(8,128)(2,1)} %pad_maximum_fusion.1.g_ref, bf16[2048,1536]{1,0:T(8,128)(2,1)} %all-gather.11.cloned.1.call-done.w_ref), custom_call_target="tpu_custom_call" | custom-call | flops 12884901888 | bytes 29360128 | tf_op jit(solution)/shard_map/feed_forward/pallas_call | solution.py:328
  379.2 20.5 %feed_forward.2 = (bf16[2048,512]{1,0:T(8,128)(2,1)S(1)}, bf16[2048,1024]{1,0:T(8,128)(2,1)}) custom-call(bf16[2048,2048]{1,0:T(8,128)(2,1)} %pad_maximum_fusion.x_ref, bf16[2048,2048]{1,0:T(8,128)(2,1)} %pad_maximum_fusion.1.g_ref, bf16[2048,1536]{1,0:T(8,128)(2,1)} %all-gather.9.cloned.1.call-done.w_ref), custom_call_target="tpu_custom_call" | custom-call | flops 12884901888 | bytes 29360128 | tf_op jit(solution)/shard_map/feed_forward/pallas_call | solution.py:328
  399.8 14.8 %fusion.2 = f32[2048,2048]{1,0:T(8,128)} fusion(bf16[2048,1024]{1,0:T(8,128)(2,1)} %get-tuple-element.31, bf16[2048,1536]{1,0:T(8,128)(2,1)S(1)} %copy-done.101), kind=kOutput, calls=%fused_computation.10 | convolution fusion | flops 8589934592 | bytes 25165824 | tf_op jit(solution)/shard_map/dot_general | solution.py:69
  414.5 15.3 %add_convert_fusion = bf16[2048,2048]{1,0:T(8,128)(2,1)} fusion(f32[2048,2048]{1,0:T(8,128)} %fusion.2, bf16[2048,1024]{1,0:T(8,128)(2,1)S(1)} %copy-done.104, bf16[2048,1536]{1,0:T(8,128)(2,1)} %all-gather.11.cloned.1.call-done.w_ref), kind=kOutput, calls=%fused_computation | convolution fusion | flops 8598323200 | bytes 33554432 | tf_op jit(solution)/shard_map/dot_general | solution.py:69
  436.3 9.9 fusion.8
  446.2 11.0 %add_convert_fusion.1 = bf16[2048,2048]{1,0:T(8,128)(2,1)} fusion(f32[2048,2048]{1,0:T(8,128)} %fusion.8, bf16[2048,512]{1,0:T(8,128)(2,1)S(1)} %copy-done.16, bf16[2048,1536]{1,0:T(8,128)(2,1)} %all-gather.11.cloned.1.call-done.w_ref), kind=kOutput, calls=%fused_computation.1 | convolution fusion | flops 4303355904 | bytes 29360128 | tf_op jit(solution)/shard_map/dot_general | solution.py:69
  473.3 17.3 %collective-permute-done.86 = bf16[2,128,2048]{2,1,0:T(8,128)(2,1)S(1)} collective-permute-done((bf16[2,128,2048]{2,1,0:T(8,128)(2,1)S(1)}, bf16[2,128,2048]{2,1,0:T(8,128)(2,1)S(1)}, u32[]{:S(2)}, u32[]{:S(2)}) %collective-permute-start.86) | collective-permute-done | bytes 1048608 | tf_op jit(solution)/shard_map/ppermute | solution.py:48
  495.7 17.3 %collective-permute-done.70 = bf16[2,128,2048]{2,1,0:T(8,128)(2,1)S(1)} collective-permute-done((bf16[2,128,2048]{2,1,0:T(8,128)(2,1)S(1)}, bf16[2,128,2048]{2,1,0:T(8,128)(2,1)S(1)}, u32[]{:S(2)}, u32[]{:S(2)}) %collective-permute-start.70) | collective-permute-done | bytes 1048608 | tf_op jit(solution)/shard_map/ppermute | solution.py:48
  518.2 10.3 collective-permute-done.87
  529.9 8.7 collective-permute-done.71
  546.3 10.6 collective-permute-done.88
  559.0 10.6 collective-permute-done.75
  579.8 10.2 collective-permute-done.77
  595.2 12.8 %attention_backward.3 = (bf16[2,2,2,4,32,768]{5,4,3,2,1,0:T(8,128)(2,1)S(1)}, f32[2,2,128]{2,1,0:T(2,128)S(1)}) custom-call(bf16[2,2,2,4,32,768]{5,4,3,2,1,0:T(8,128)(2,1)S(1)} %bitcast.427, f32[2,2,2,4,32,256]{5,4,3,2,1,0:T(8,128)S(1)} %fusion.35.grad_ref, f32[2,4,128,128]{3,2,1,0:T(8,128)S(1)} %get-tuple-element.244.mask_ref, ...), custom_call_target="tpu_custom_call" | custom-call | flops 49999998976 | bytes 10000000 | tf_op jit(solution)/shard_map/attention_backward/pallas_call | solution.py:278
  621.9 12.5 %attention_backward.2 = (bf16[2,2,2,4,32,768]{5,4,3,2,1,0:T(8,128)(2,1)S(1)}, f32[2,2,128]{2,1,0:T(2,128)S(1)}) custom-call(bf16[2,2,2,4,32,768]{5,4,3,2,1,0:T(8,128)(2,1)S(1)} %bitcast.425, f32[2,2,2,4,32,256]{5,4,3,2,1,0:T(8,128)S(1)} %fusion.37.grad_ref, f32[2,4,128,128]{3,2,1,0:T(8,128)S(1)} %get-tuple-element.243.mask_ref, ...), custom_call_target="tpu_custom_call" | custom-call | flops 49999998976 | bytes 10000000 | tf_op jit(solution)/shard_map/attention_backward/pallas_call | solution.py:278
  654.7 11.4 %convolution_convert_fusion.5 = bf16[2048,1024]{0,1:T(8,128)(2,1)S(1)} fusion(bf16[2048,1024]{1,0:T(8,128)(2,1)} %get-tuple-element.31, bf16[1024,2048]{1,0:T(8,128)(2,1)S(1)} %bitcast.443, bf16[1024,2048]{1,0:T(8,128)(2,1)S(1)} %bitcast.446), kind=kOutput, calls=%fused_computation.30 | convolution fusion | flops 8608808960 | bytes 16777216 | tf_op jit(solution)/shard_map/dot_general | solution.py:69
  679.5 11.5 %convolution_convert_fusion.4 = bf16[2048,1024]{0,1:T(8,128)(2,1)S(1)} fusion(bf16[2048,1024]{1,0:T(8,128)(2,1)} %get-tuple-element.32, bf16[1024,2048]{1,0:T(8,128)(2,1)S(1)} %bitcast.444, bf16[1024,2048]{1,0:T(8,128)(2,1)S(1)} %bitcast.447), kind=kOutput, calls=%fused_computation.29 | convolution fusion | flops 8608808960 | bytes 16777216 | tf_op jit(solution)/shard_map/dot_general | solution.py:69
  756.0 21.5 %collective-permute-done.83 = bf16[2,128,2048]{2,1,0:T(8,128)(2,1)S(1)} collective-permute-done((bf16[2,128,2048]{2,1,0:T(8,128)(2,1)S(1)}, bf16[2,128,2048]{2,1,0:T(8,128)(2,1)S(1)}, u32[]{:S(2)}, u32[]{:S(2)}) %collective-permute-start.83) | collective-permute-done | bytes 1048608 | tf_op jit(solution)/shard_map/ppermute | solution.py:48
  798.3 20.9 %reduce-scatter.9.cloned.1.call-done = bf16[512,1536]{0,1:T(8,128)(2,1)} async-done(((bf16[2048,1536]{0,1:T(8,128)(2,1)}), bf16[512,1536]{0,1:T(8,128)(2,1)}) %reduce-scatter.9.cloned.1.call-update) | async-done | bytes 1572880 | tf_op jit(solution)/shard_map/reduce_scatter | solution.py:490
  823.3 109.6 %reduce-scatter.11.cloned.1.call-done = bf16[512,1536]{0,1:T(8,128)(2,1)} async-done(((bf16[2048,1536]{0,1:T(8,128)(2,1)}), bf16[512,1536]{0,1:T(8,128)(2,1)}) %reduce-scatter.11.cloned.1.call-update) | async-done | bytes 1572880 | tf_op jit(solution)/shard_map/reduce_scatter | solution.py:490
  969.0 41.5 %all-reduce.2 = (f32[]{:T(128)}, f32[2,2048]{1,0:T(2,128)S(1)}, f32[16]{0:T(128)S(1)}) all-reduce(f32[]{:T(128)S(6)} %add.448, f32[2,2048]{1,0:T(2,128)} %pad_maximum_fusion.10, f32[16]{0:T(128)} %copy-done.96), channel_id=1, replica_groups=mesh['z'=4,'x'=2,'y'=2,'c'=2] {'z','x','y','c'}, use_global_device_ids=true, to_apply=%region_18.19 | all-reduce | flops 4113 | bytes 32904 | tf_op jit(solution)/shard_map/psum | solution.py:585
  1028.0 11.4 %multiply_subtract_fusion = (f32[256,2,2048]{0,2,1:T(8,128)}, f32[256,2,2048]{0,2,1:T(8,128)}, f32[256,2,2048]{0,2,1:T(8,128)}) fusion(f32[256,2,2048]{0,2,1:T(8,128)} %copy.167, f32[]{:T(128)S(6)} %min.3, f32[256,3,2048]{0,2,1:T(8,128)} %fusion.4, f32[256,2,2048]{0,2,1:T(8,128)} %copy.165, f32[256,2,2048]{0,2,1:T(8,128)} %copy.164), kind=kLoop, calls=%fused_computation.21 | loop fusion | flops 16777216 | bytes 29360132 | tf_op jit(solution)/shard_map/sub | solution.py:41
  (666 shorter events, 512.0 us)
Async XLA Ops:
  7.2 198.2 %all-gather.5.cloned.1.call-start = ((), (), s32[]{:S(2)}) async-start(), calls=%async_computation.4 | async-start | bytes 3932160 | tf_op jit(solution)/shard_map/all_gather | solution.py:403
  23.7 196.3 %all-gather.7.cloned.1.call-start = ((), (), s32[]{:S(2)}) async-start(), calls=%async_computation.5 | async-start | bytes 1310720 | tf_op jit(solution)/shard_map/all_gather | solution.py:403
  24.3 58.0 %collective-permute-start.8 = (s32[4,32]{1,0:T(4,128)}, s32[4,32]{1,0:T(4,128)}, u32[]{:S(2)}, u32[]{:S(2)}) collective-permute-start(s32[4,32]{1,0:T(4,128)} %get-tuple-element.253), channel_id=1, source_target_pairs={{0,2},{2,0},{1,3},{3,1},{4,6},{6,4},{5,7},{7,5},{8,10},{10,8},{9,1... | collective-permute-start | bytes 1544 | tf_op jit(solution)/shard_map/ppermute | solution.py:48
  26.1 56.9 %collective-permute-start.9 = (s32[4,32]{1,0:T(4,128)}, s32[4,32]{1,0:T(4,128)}, u32[]{:S(2)}, u32[]{:S(2)}) collective-permute-start(s32[4,32]{1,0:T(4,128)} %get-tuple-element.253), channel_id=1, source_target_pairs={{0,4},{4,0},{1,5},{5,1},{2,6},{6,2},{3,7},{7,3},{8,12},{12,8},{9,1... | collective-permute-start | bytes 1544 | tf_op jit(solution)/shard_map/ppermute | solution.py:48
  27.6 70.1 %collective-permute-start.11 = (s32[4,32]{1,0:T(4,128)}, s32[4,32]{1,0:T(4,128)}, u32[]{:S(2)}, u32[]{:S(2)}) collective-permute-start(s32[4,32]{1,0:T(4,128)} %get-tuple-element.253), channel_id=1, source_target_pairs={{0,1},{1,0},{2,3},{3,2},{4,5},{5,4},{6,7},{7,6},{8,9},{9,8},{10,11... | collective-permute-start | bytes 1544 | tf_op jit(solution)/shard_map/ppermute | solution.py:48
  34.3 40.8 %collective-permute-start.64 = (bf16[256,2,1024]{2,0,1:T(8,128)(2,1)}, bf16[256,2,1024]{2,0,1:T(8,128)(2,1)}, u32[]{:S(2)}, u32[]{:S(2)}) collective-permute-start(bf16[256,2,1024]{2,0,1:T(8,128)(2,1)} %get-tuple-element.208), channel_id=1, source_target_pairs={{0,4},{4,0},{1,5},{5,1},{2,6},{6,2},{3,7},{7,3},{8,12},{12,8},{9,1... | collective-permute-start | bytes 3145736 | tf_op jit(solution)/shard_map/ppermute | solution.py:48
  46.7 311.2 %all-gather.11.cloned.1.call-start = ((), (), s32[]{:S(2)}) async-start(), calls=%async_computation.7 | async-start | bytes 7864320 | tf_op jit(solution)/shard_map/all_gather | solution.py:403
  80.6 298.6 %all-gather.9.cloned.1.call-start = ((), (), s32[]{:S(2)}) async-start(), calls=%async_computation.6 | async-start | bytes 7864320 | tf_op jit(solution)/shard_map/all_gather | solution.py:403
  97.7 68.5 %collective-permute-start.29 = (bf16[128,2048]{1,0:T(8,128)(2,1)}, bf16[128,2048]{1,0:T(8,128)(2,1)}, u32[]{:S(2)}, u32[]{:S(2)}) collective-permute-start(bf16[128,2048]{1,0:T(8,128)(2,1)} %get-tuple-element.216), channel_id=1, source_target_pairs={{0,1},{1,0},{2,3},{3,2},{4,5},{5,4},{6,7},{7,6},{8,9},{9,8},{10,11... | collective-permute-start | bytes 1572872 | tf_op jit(solution)/shard_map/ppermute | solution.py:48
  114.6 68.8 %collective-permute-start.3 = (bf16[128,2048]{1,0:T(8,128)(2,1)}, bf16[128,2048]{1,0:T(8,128)(2,1)}, u32[]{:S(2)}, u32[]{:S(2)}) collective-permute-start(bf16[128,2048]{1,0:T(8,128)(2,1)} %get-tuple-element.215), channel_id=1, source_target_pairs={{0,1},{1,0},{2,3},{3,2},{4,5},{5,4},{6,7},{7,6},{8,9},{9,8},{10,11... | collective-permute-start | bytes 1572872 | tf_op jit(solution)/shard_map/ppermute | solution.py:48
  126.0 73.1 %collective-permute-start.53 = (bf16[128,2048]{1,0:T(8,128)(2,1)S(1)}, bf16[128,2048]{1,0:T(8,128)(2,1)}, u32[]{:S(2)}, u32[]{:S(2)}) collective-permute-start(bf16[128,2048]{1,0:T(8,128)(2,1)S(1)} %bitcast.451), channel_id=1, source_target_pairs={{0,1},{1,0},{2,3},{3,2},{4,5},{5,4},{6,7},{7,6},{8,9},{9,8},{10,11... | collective-permute-start | bytes 1572872 | tf_op jit(solution)/shard_map/ppermute | solution.py:48
  147.7 94.3 %collective-permute-start.60 = (bf16[128,2048]{1,0:T(8,128)(2,1)}, bf16[128,2048]{1,0:T(8,128)(2,1)}, u32[]{:S(2)}, u32[]{:S(2)}) collective-permute-start(bf16[128,2048]{1,0:T(8,128)(2,1)} %bitcast.87), channel_id=1, source_target_pairs={{0,1},{1,0},{2,3},{3,2},{4,5},{5,4},{6,7},{7,6},{8,9},{9,8},{10,11... | collective-permute-start | bytes 1572872 | tf_op jit(solution)/shard_map/ppermute | solution.py:48
  153.6 629.3 %reduce-scatter.7.cloned.1.call-start = ((), (), s32[]{:S(2)}) async-start(), calls=%async_computation.9 | async-start | bytes 1310720 | tf_op jit(solution)/shard_map/reduce_scatter | solution.py:490
  197.7 42.2 %collective-permute-start.59 = (bf16[128,2048]{1,0:T(8,128)(2,1)}, bf16[128,2048]{1,0:T(8,128)(2,1)}, u32[]{:S(2)}, u32[]{:S(2)}) collective-permute-start(bf16[128,2048]{1,0:T(8,128)(2,1)} %collective-permute-done.57), channel_id=1, source_target_pairs={{0,2},{2,0},{1,3},{3,1},{4,6},{6,4},{5,7},{7,5},{8,10},{10,8},{9,1... | collective-permute-start | bytes 1572872 | tf_op jit(solution)/shard_map/ppermute | solution.py:48
  199.1 45.4 %collective-permute-start.61 = (bf16[128,2048]{1,0:T(8,128)(2,1)}, bf16[128,2048]{1,0:T(8,128)(2,1)S(1)}, u32[]{:S(2)}, u32[]{:S(2)}) collective-permute-start(bf16[128,2048]{1,0:T(8,128)(2,1)} %collective-permute-done.57), channel_id=1, source_target_pairs={{0,1},{1,0},{2,3},{3,2},{4,5},{5,4},{6,7},{7,6},{8,9},{9,8},{10,11... | collective-permute-start | bytes 1572872 | tf_op jit(solution)/shard_map/ppermute | solution.py:48
  203.3 46.4 %collective-permute-start.62 = (bf16[128,2048]{1,0:T(8,128)(2,1)}, bf16[128,2048]{1,0:T(8,128)(2,1)}, u32[]{:S(2)}, u32[]{:S(2)}) collective-permute-start(bf16[128,2048]{1,0:T(8,128)(2,1)} %collective-permute-done.58), channel_id=1, source_target_pairs={{0,1},{1,0},{2,3},{3,2},{4,5},{5,4},{6,7},{7,6},{8,9},{9,8},{10,11... | collective-permute-start | bytes 1572872 | tf_op jit(solution)/shard_map/ppermute | solution.py:48
  242.0 37.0 %collective-permute-start.56 = (bf16[128,2048]{1,0:T(8,128)(2,1)S(1)}, bf16[128,2048]{1,0:T(8,128)(2,1)S(1)}, u32[]{:S(2)}, u32[]{:S(2)}) collective-permute-start(bf16[128,2048]{1,0:T(8,128)(2,1)S(1)} %copy-done.66), channel_id=1, source_target_pairs={{0,1},{1,0},{2,3},{3,2},{4,5},{5,4},{6,7},{7,6},{8,9},{9,8},{10,11... | collective-permute-start | bytes 1572872 | tf_op jit(solution)/shard_map/ppermute | solution.py:48
  244.5 35.3 %collective-permute-start.63 = (bf16[128,2048]{1,0:T(8,128)(2,1)}, bf16[128,2048]{1,0:T(8,128)(2,1)S(1)}, u32[]{:S(2)}, u32[]{:S(2)}) collective-permute-start(bf16[128,2048]{1,0:T(8,128)(2,1)} %collective-permute-done.59), channel_id=1, source_target_pairs={{0,1},{1,0},{2,3},{3,2},{4,5},{5,4},{6,7},{7,6},{8,9},{9,8},{10,11... | collective-permute-start | bytes 1572872 | tf_op jit(solution)/shard_map/ppermute | solution.py:48
  306.9 38.3 %collective-permute-start.46 = (bf16[128,2048]{1,0:T(8,128)(2,1)S(1)}, bf16[128,2048]{1,0:T(8,128)(2,1)S(1)}, u32[]{:S(2)}, u32[]{:S(2)}) collective-permute-start(bf16[128,2048]{1,0:T(8,128)(2,1)S(1)} %get-tuple-element.252), channel_id=1, source_target_pairs={{0,1},{1,0},{2,3},{3,2},{4,5},{5,4},{6,7},{7,6},{8,9},{9,8},{10,11... | collective-permute-start | bytes 1572872 | tf_op jit(solution)/shard_map/ppermute | solution.py:48
  471.2 41.9 %collective-permute-start.70 = (bf16[2,128,2048]{2,1,0:T(8,128)(2,1)S(1)}, bf16[2,128,2048]{2,1,0:T(8,128)(2,1)S(1)}, u32[]{:S(2)}, u32[]{:S(2)}) collective-permute-start(bf16[2,128,2048]{2,1,0:T(8,128)(2,1)S(1)} %slice.548), channel_id=1, source_target_pairs={{0,2},{2,0},{1,3},{3,1},{4,6},{6,4},{5,7},{7,5},{8,10},{10,8},{9,1... | collective-permute-start | bytes 3145736 | tf_op jit(solution)/shard_map/ppermute | solution.py:48
  472.9 44.5 %collective-permute-start.67 = (bf16[2,128,2048]{2,1,0:T(8,128)(2,1)S(1)}, bf16[2,128,2048]{2,1,0:T(8,128)(2,1)S(1)}, u32[]{:S(2)}, u32[]{:S(2)}) collective-permute-start(bf16[2,128,2048]{2,1,0:T(8,128)(2,1)S(1)} %slice.549), channel_id=1, source_target_pairs={{0,4},{4,0},{1,5},{5,1},{2,6},{6,2},{3,7},{7,3},{8,12},{12,8},{9,1... | collective-permute-start | bytes 3145736 | tf_op jit(solution)/shard_map/ppermute | solution.py:48
  491.0 37.5 %collective-permute-start.87 = (bf16[128,2048]{1,0:T(8,128)(2,1)S(1)}, bf16[128,2048]{1,0:T(8,128)(2,1)S(1)}, u32[]{:S(2)}, u32[]{:S(2)}) collective-permute-start(bf16[128,2048]{1,0:T(8,128)(2,1)S(1)} %fusion.65), channel_id=1, source_target_pairs={{0,4},{4,0},{1,5},{5,1},{2,6},{6,2},{3,7},{7,3},{8,12},{12,8},{9,1... | collective-permute-start | bytes 1572872 | tf_op jit(solution)/shard_map/ppermute | solution.py:48
  544.1 35.0 %collective-permute-start.91 = (bf16[128,2048]{1,0:T(8,128)(2,1)S(1)}, bf16[128,2048]{1,0:T(8,128)(2,1)S(1)}, u32[]{:S(2)}, u32[]{:S(2)}) collective-permute-start(bf16[128,2048]{1,0:T(8,128)(2,1)S(1)} %get-tuple-element.176), channel_id=1, source_target_pairs={{0,1},{1,0},{2,3},{3,2},{4,5},{5,4},{6,7},{7,6},{8,9},{9,8},{10,11... | collective-permute-start | bytes 1572872 | tf_op jit(solution)/shard_map/ppermute | solution.py:48
  556.9 33.8 %collective-permute-start.78 = (bf16[128,2048]{1,0:T(8,128)(2,1)S(1)}, bf16[128,2048]{1,0:T(8,128)(2,1)S(1)}, u32[]{:S(2)}, u32[]{:S(2)}) collective-permute-start(bf16[128,2048]{1,0:T(8,128)(2,1)S(1)} %get-tuple-element.178), channel_id=1, source_target_pairs={{0,1},{1,0},{2,3},{3,2},{4,5},{5,4},{6,7},{7,6},{8,9},{9,8},{10,11... | collective-permute-start | bytes 1572872 | tf_op jit(solution)/shard_map/ppermute | solution.py:48
  616.6 178.8 %reduce-scatter.5.cloned.1.call-start = ((), (), s32[]{:S(2)}) async-start(), calls=%async_computation.8 | async-start | bytes 3932160 | tf_op jit(solution)/shard_map/reduce_scatter | solution.py:490
  646.0 173.2 %reduce-scatter.9.cloned.1.call-start = ((), (), s32[]{:S(2)}) async-start(), calls=%async_computation.10 | async-start | bytes 7864320 | tf_op jit(solution)/shard_map/reduce_scatter | solution.py:490
  669.6 263.3 %reduce-scatter.11.cloned.1.call-start = ((), (), s32[]{:S(2)}) async-start(), calls=%async_computation.11 | async-start | bytes 7864320 | tf_op jit(solution)/shard_map/reduce_scatter | solution.py:490
  710.1 38.6 %collective-permute-start.82 = (bf16[4,128,2048]{2,1,0:T(8,128)(2,1)}, bf16[4,128,2048]{2,1,0:T(8,128)(2,1)}, u32[]{:S(2)}, u32[]{:S(2)}) collective-permute-start(bf16[4,128,2048]{2,1,0:T(8,128)(2,1)} %bitcast.127), channel_id=1, source_target_pairs={{0,1},{1,0},{2,3},{3,2},{4,5},{5,4},{6,7},{7,6},{8,9},{9,8},{10,11... | collective-permute-start | bytes 6291464 | tf_op jit(solution)/shard_map/ppermute | solution.py:48
  713.3 38.9 %collective-permute-start.96 = (bf16[2,128,2048]{2,1,0:T(8,128)(2,1)S(1)}, bf16[2,128,2048]{2,1,0:T(8,128)(2,1)}, u32[]{:S(2)}, u32[]{:S(2)}) collective-permute-start(bf16[2,128,2048]{2,1,0:T(8,128)(2,1)S(1)} %slice.544), channel_id=1, source_target_pairs={{0,2},{2,0},{1,3},{3,1},{4,6},{6,4},{5,7},{7,5},{8,10},{10,8},{9,1... | collective-permute-start | bytes 3145736 | tf_op jit(solution)/shard_map/ppermute | solution.py:48
  754.6 37.0 %collective-permute-start.97 = (bf16[128,2048]{1,0:T(8,128)(2,1)}, bf16[128,2048]{1,0:T(8,128)(2,1)}, u32[]{:S(2)}, u32[]{:S(2)}) collective-permute-start(bf16[128,2048]{1,0:T(8,128)(2,1)} %fusion.66), channel_id=1, source_target_pairs={{0,4},{4,0},{1,5},{5,1},{2,6},{6,2},{3,7},{7,3},{8,12},{12,8},{9,1... | collective-permute-start | bytes 1572872 | tf_op jit(solution)/shard_map/ppermute | solution.py:48
  797.5 145.2 %collective-permute-start.98 = (bf16[256,768]{1,0:T(8,128)(2,1)}, bf16[256,768]{1,0:T(8,128)(2,1)}, u32[]{:S(2)}, u32[]{:S(2)}) collective-permute-start(bf16[256,768]{1,0:T(8,128)(2,1)} %get-tuple-element.231), channel_id=1, source_target_pairs={{0,4},{4,0},{1,5},{5,1},{2,6},{6,2},{3,7},{7,3},{8,12},{12,8},{9,1... | collective-permute-start | bytes 1179656 | tf_op jit(solution)/shard_map/ppermute | solution.py:48
  821.8 126.0 %collective-permute-start.100 = (bf16[256,1536]{0,1:T(8,128)(2,1)}, bf16[256,1536]{0,1:T(8,128)(2,1)}, u32[]{:S(2)}, u32[]{:S(2)}) collective-permute-start(bf16[256,1536]{0,1:T(8,128)(2,1)} %get-tuple-element.210), channel_id=1, source_target_pairs={{0,4},{4,0},{1,5},{5,1},{2,6},{6,2},{3,7},{7,3},{8,12},{12,8},{9,1... | collective-permute-start | bytes 2359304 | tf_op jit(solution)/shard_map/ppermute | solution.py:48
  (183 other events, 2477.1 us)
Sparse Core Ops, SparseCore 0:
  23.8 64.9 all-gather.4
  90.9 26.6 all-gather.6
  119.7 114.8 all-gather.10
  236.6 113.5 all-gather.8
  616.8 26.6 reduce-scatter.6
  646.2 59.7 reduce-scatter.4
  708.4 110.7 reduce-scatter.8
  821.6 111.2 reduce-scatter.10

commit v2 on v1

--- a/solution.py
+++ b/solution.py
@@ -48,21 +48,35 @@
     return lax.ppermute(tensor, axis, [(0, 1), (1, 0)])
 
 
+def tie(tensor, *earlier):
+    return lax.optimization_barrier((tensor,) + earlier)[0]
+
+
 def gather_tokens(own, outer, inner):
     by_inner = swap(own, inner)
     by_outer = swap(own, outer)
     by_both = swap(by_inner, outer)
-    pieces = [own, by_inner, by_outer, by_both]
-    pieces = pieces + [swap(p, "c") for p in pieces]
-    return jnp.concatenate([p[None] for p in pieces], axis=0)
-
-
-def scatter_tokens(partial, outer, inner):
+    mine = jnp.concatenate([own, by_inner, by_outer, by_both], axis=0)
+    return mine, swap(mine, "c")
+
+
+def scatter_tokens(partial, outer, inner, *earlier):
     half = partial[:4].astype(F32) + swap(partial[4:], "c").astype(F32)
     low = half.astype(BF)
     half = half[:2] + swap(low[2:], outer).astype(F32)
-    low = half.astype(BF)
-    return half[0] + swap(low[1], inner).astype(F32)
+    low = tie(half[1].astype(BF), *earlier)
+    return half[0] + swap(low, inner).astype(F32)
+
+
+def sum_everywhere(tensor, z_count, beside):
+    reach = 1
+    while reach < z_count:
+        tensor = tensor + lax.ppermute(tensor, "z", [(i, i ^ reach) for i in range(z_count)])
+        reach *= 2
+    tensor = tie(tensor + swap(tensor, "c"), beside)
+    for axis in ("y", "x"):
+        tensor = tensor + swap(tensor, axis)
+    return tensor
 
 
 def mm(a, b, dims):
@@ -266,7 +280,7 @@
         out_shape=jax.ShapeDtypeStruct(out_shape, BF),
         compiler_params=pltpu.CompilerParams(vmem_limit_bytes=VMEM_LIMIT),
         cost_estimate=pl.CostEstimate(
-            flops=400_000_000 * 50, bytes_accessed=6_000_000, transcendentals=0
+            flops=400_000_000, bytes_accessed=3_000_000, transcendentals=0
         ),
         name="attention_forward",
     )(projected, mask, cols, gate_rows)
@@ -295,7 +309,7 @@
         ],
         compiler_params=pltpu.CompilerParams(vmem_limit_bytes=VMEM_LIMIT),
         cost_estimate=pl.CostEstimate(
-            flops=1_000_000_000 * 50, bytes_accessed=10_000_000, transcendentals=0
+            flops=1_000_000_000, bytes_accessed=5_000_000, transcendentals=0
         ),
         name="attention_backward",
     )(projected, d_combined, mask, cols, gate_rows)
@@ -305,7 +319,19 @@
 GELU_B = 0.044715
 
 
-def ff_kernel(width, x_ref, g_ref, w_ref, act_ref, grad_ref):
+def ff_kernel(width, half, mine_ref, other_ref, g_ref, w_ref, act_ref, grad_ref):
+    step = pl.program_id(0)
+
+    @pl.when(step < half)
+    def first():
+        ff_tile(width, mine_ref, g_ref, w_ref, act_ref, grad_ref)
+
+    @pl.when(step >= half)
+    def second():
+        ff_tile(width, other_ref, g_ref, w_ref, act_ref, grad_ref)
+
+
+def ff_tile(width, x_ref, g_ref, w_ref, act_ref, grad_ref):
     weights = w_ref[...]
     gate_up = mm(x_ref[...], weights[:, : 2 * width], NN)
     d_active = mm(g_ref[...], weights[:, 2 * width :], NN)
@@ -322,16 +348,18 @@
 
 
 def feed_forward(rows, grads, weights):
-    tokens = rows.shape[0]
+    tokens = grads.shape[0]
     width = weights.shape[1] // 3
     tile = 256
+    half = tokens // (2 * tile)
     return pl.pallas_call(
-        functools.partial(ff_kernel, width),
+        functools.partial(ff_kernel, width, half),
         grid=(tokens // tile,),
         in_specs=[
+            pl.BlockSpec((tile, D), lambda i: (jnp.minimum(i, half - 1), 0)),
+            pl.BlockSpec((tile, D), lambda i: (jnp.maximum(i - half, 0), 0)),
             pl.BlockSpec((tile, D), lambda i: (i, 0)),
-            pl.BlockSpec((tile, D), lambda i: (i, 0)),
-            pl.BlockSpec(weights.shape, lambda i: (0, 0)),
+            pl.BlockSpec(weights.shape, lambda i: (0, 0), pipeline_mode=pl.Buffered(1)),
         ],
         out_specs=[
             pl.BlockSpec((tile, width), lambda i: (i, 0)),
@@ -343,12 +371,149 @@
         ],
         compiler_params=pltpu.CompilerParams(vmem_limit_bytes=VMEM_LIMIT),
         cost_estimate=pl.CostEstimate(
-            flops=2 * tokens * D * 3 * width,
-            bytes_accessed=2 * (2 * tokens * D + 3 * D * width + 3 * tokens * width),
-            transcendentals=tokens * width,
+            flops=tokens * D * width, bytes_accessed=tokens * D, transcendentals=0
         ),
         name="feed_forward",
-    )(rows, grads, weights)
+    )(*rows, grads, weights)
+
+
+def grads_kernel(count, *refs):
+    rows, grads, by_rows, by_grads = (refs[k * count : (k + 1) * count] for k in range(4))
+    out_ref = refs[4 * count]
+    split = by_rows[0].shape[1]
+
+    def total(left, right):
+        acc = None
+        for a, b in zip(left, right):
+            term = mm(a[...], b[...], TN)
+            acc = term if acc is None else acc + term
+        return acc
+
+    out_ref[:, :split] = total(rows, by_rows).astype(BF)
+    out_ref[:, split:] = total(grads, by_grads).astype(BF)
+
+
+def weight_grads(rows, grads, by_rows, by_grads):
+    def halves(arrays):
+        parts = []
+        for a in arrays:
+            parts += [(a[0], 0), (a[1], 0)] if isinstance(a, tuple) else [(a, 0), (a, 1)]
+        return parts
+
+    groups = [halves(a) for a in (rows, grads, by_rows, by_grads)]
+    count = len(groups[0])
+    tokens = by_rows[0].shape[0] // 2
+    first, second = by_rows[0].shape[1], by_grads[0].shape[1]
+    tile = 512
+
+    def tall(half):
+        return pl.BlockSpec((tokens, tile), lambda i: (half, i))
+
+    def whole(width, half):
+        return pl.BlockSpec((tokens, width), lambda i: (half, 0), pipeline_mode=pl.Buffered(1))
+
+    return pl.pallas_call(
+        functools.partial(grads_kernel, count),
+        grid=(D // tile,),
+        in_specs=[tall(half) for _, half in groups[0] + groups[1]]
+        + [whole(first, half) for _, half in groups[2]]
+        + [whole(second, half) for _, half in groups[3]],
+        out_specs=pl.BlockSpec((tile, first + second), lambda i: (i, 0)),
+        out_shape=jax.ShapeDtypeStruct((D, first + second), BF),
+        compiler_params=pltpu.CompilerParams(vmem_limit_bytes=VMEM_LIMIT),
+        cost_estimate=pl.CostEstimate(
+            flops=tokens * D * (first + second), bytes_accessed=tokens * D, transcendentals=0
+        ),
+        name="weight_grads",
+    )(*[a for group in groups for a, _ in group])
+
+
+RATE_QKV = D ** (-0.5)
+RATE_OUT = 4.0 * (HEADS * HEAD_DIM) ** (-0.5)
+RATE_DOWN = FF ** (-0.5)
+
+
+def clip_factor(small):
+    row = lax.broadcasted_iota(jnp.int32, small.shape, 0)
+    lane = lax.broadcasted_iota(jnp.int32, small.shape, 1)
+    summed = (row == small.shape[0] - 1) & (lane >= HEADS)
+    squares = jnp.sum(jnp.where(summed, small, small * small), axis=(0, 1), keepdims=True)
+    grad_norm = jnp.sqrt(squares)
+    return grad_norm, jnp.minimum(1.0, CLIP / (grad_norm + 1e-06))
+
+
+def adam_kernel(place_ref, small_ref, *refs):
+    ins, grads, outs = refs[:12], refs[12:16], refs[16:]
+    factor = clip_factor(small_ref[...])[1]
+    is_low = place_ref[0] == 0
+
+    def put(number, place, gradient, rate):
+        weight, moment, second = (r[place] for r in ins[3 * number : 3 * number + 3])
+        new = adam_update(weight, moment, second, gradient.astype(F32), factor, rate, DECAY)
+        for ref, value in zip(outs[3 * number : 3 * number + 3], new):
+            ref[place] = value
+
+    mine, theirs = grads[0][...], grads[1][...]
+    sides = (jnp.where(is_low, mine, theirs), jnp.where(is_low, theirs, mine))
+    width = mine.shape[1] // 4
+    everything = slice(None)
+    for s, side in enumerate(sides):
+        cols = slice(s * width, (s + 1) * width)
+        for part in range(3):
+            put(0, (part, everything, cols), side[:, part * width : (part + 1) * width], RATE_QKV)
+        put(1, (everything, cols), side[:, 3 * width :], RATE_OUT)
+    put(2, (everything, everything), grads[2][...], RATE_QKV)
+    put(2 + 1, (everything, everything), grads[3][...], RATE_DOWN)
+
+
+def mlp_view(t):
+    rows, _, width_ff = t.shape
+    return t.reshape(rows, 2, width_ff // 128, 128).transpose(0, 2, 1, 3).reshape(-1, 128)
+
+
+def adam_all(small, x_place, arrays, att_mine, att_theirs, grad_mlp, grad_down):
+    rows, _, width_ff = arrays[6].shape
+    lanes = width_ff // 128
+
+    def qkv_view(t):
+        return jnp.transpose(t, (1, 0, 2))
+
+    def mlp_back(t):
+        return t.reshape(rows, lanes, 2, 128).transpose(0, 2, 1, 3).reshape(rows, 2, width_ff)
+
+    views = [qkv_view(t) for t in arrays[:3]] + list(arrays[3:6])
+    views += [mlp_view(t) for t in arrays[6:9]] + list(arrays[9:])
+    grads = [att_mine, att_theirs, grad_mlp, grad_down]
+    steps = 8
+
+    def spec(t):
+        axis = t.ndim - 2
+        block = list(t.shape)
+        block[axis] //= steps
+        return pl.BlockSpec(tuple(block), lambda i: (0,) * axis + (i, 0))
+
+    new = pl.pallas_call(
+        adam_kernel,
+        grid=(steps,),
+        in_specs=[
+            pl.BlockSpec(memory_space=pltpu.SMEM),
+            pl.BlockSpec(small.shape, lambda i: (0, 0)),
+        ]
+        + [spec(t) for t in views + grads],
+        out_specs=[spec(t) for t in views],
+        out_shape=[jax.ShapeDtypeStruct(t.shape, F32) for t in views],
+        compiler_params=pltpu.CompilerParams(vmem_limit_bytes=VMEM_LIMIT),
+        cost_estimate=pl.CostEstimate(
+            flops=20 * sum(t.size for t in views) // 3,
+            bytes_accessed=8 * sum(t.size for t in views),
+            transcendentals=0,
+        ),
+        name="adam",
+    )(x_place[None], small, *views, *grads)
+    new = list(new)
+    return (
+        [qkv_view(t) for t in new[:3]] + new[3:6] + [mlp_back(t) for t in new[6:9]] + new[9:]
+    )
 
 
 def on_device(
@@ -382,6 +547,8 @@
     is_low = x_place == 0
     orders = [("x", "y") if m % 2 == 0 else ("y", "x") for m in range(micro_count)]
 
+    z_count = D // (2 * weight_qkv.shape[0])
+
     def half_columns(weight, which):
         width = weight.shape[-1] // 2
         return lax.dynamic_slice_in_dim(weight, which * width, width, axis=weight.ndim - 1)
@@ -393,55 +560,63 @@
             jnp.concatenate([other, own], axis=axis),
         )
 
-    def exchange_weight(weight):
-        low = weight.astype(BF)
-        mine = half_columns(low, x_place)
-        theirs = swap(half_columns(low, 1 - x_place), "x")
-        return by_place(mine, theirs, 0)
+    def exchange_rows(columns_for, *earlier):
+        theirs = swap(tie(columns_for(1 - x_place), *earlier), "x")
+        mine = columns_for(x_place)
+        both = jnp.zeros((2 * rows, mine.shape[1]), BF)
+        both = lax.dynamic_update_slice_in_dim(both, mine, x_place * rows, axis=0)
+        return lax.dynamic_update_slice_in_dim(both, theirs, (1 - x_place) * rows, axis=0)
 
     def fetch(block):
         return lax.all_gather(block, "z", axis=0, tiled=True)
 
-    shard_qkv = exchange_weight(weight_qkv)
-    heads = shard_qkv.shape[2] // HEAD_DIM
-    width_att = shard_qkv.shape[2]
-    full_qkv = fetch(shard_qkv.reshape(-1, 3 * width_att))
-    full_out = fetch(exchange_weight(weight_out))
-    shard_mlp = exchange_weight(weight_mlp)
-    shard_down = exchange_weight(weight_down)
-    width_ff = shard_down.shape[1]
+    rows = weight_qkv.shape[0]
+    heads = weight_qkv.shape[2] // (2 * HEAD_DIM)
+    width_att = heads * HEAD_DIM
+    width_ff = weight_down.shape[1] // 2
     width = width_ff // CHUNKS
-    full_ff = []
-    for k in range(CHUNKS):
-        part = slice(k * width, (k + 1) * width)
-        full_ff.append(
-            fetch(
-                jnp.concatenate(
-                    [shard_mlp[:, 0, part], shard_mlp[:, 1, part], shard_down[:, part]], axis=1
-                )
-            )
-        )
+
+    def att_columns(which):
+        qkv = half_columns(weight_qkv, which).astype(BF).reshape(rows, -1)
+        return jnp.concatenate([qkv, half_columns(weight_out, which).astype(BF)], axis=1)
+
+    def ff_columns(k, which):
+        start = which * width_ff + k * width
+        mlp = lax.dynamic_slice_in_dim(weight_mlp, start, width, axis=2).astype(BF)
+        down = lax.dynamic_slice_in_dim(weight_down, start, width, axis=1).astype(BF)
+        return jnp.concatenate([mlp[:, 0], mlp[:, 1], down], axis=1)
+
+    shard_att = exchange_rows(att_columns)
+    full_att = fetch(shard_att)
+    full_qkv = full_att[:, : 3 * width_att]
+    full_out = full_att[:, 3 * width_att :]
 
     head_start = (y_place * 2 + c_place) * (2 * heads) + x_place * heads
     gate_local = lax.dynamic_slice_in_dim(gate_logit, head_start, heads)
     mixing = jax.nn.sigmoid(gate_local)
     gate_rows = jnp.broadcast_to(mixing[:, None], (heads, HEAD_DIM))
 
-    token_rows = [
-        inputs[m, 0].reshape(own_tokens, D).astype(F32) for m in range(micro_count)
+    micros = range(micro_count)
+    tokens = 8 * own_tokens
+    token_rows = [inputs[m, 0].reshape(own_tokens, D).astype(F32) for m in micros]
+    back_low = [cotangent[m, 0].reshape(own_tokens, D) for m in micros]
+    normed_att = [rms_norm(t, norm_gains[0]).astype(BF) for t in token_rows]
+    att_pairs = [gather_tokens(normed_att[m], *orders[m]) for m in micros]
+    att_rows = [jnp.concatenate(pair, axis=0) for pair in att_pairs]
+    all_ids = doc_ids[:, 0]
+    for axis in ("y", "x", "c"):
+        all_ids = jnp.stack([all_ids, swap(all_ids, axis)], axis=0)
+
+    shard_ff = [exchange_rows(functools.partial(ff_columns, 0), *att_rows)]
+    full_ff = [fetch(shard_ff[0])]
+    back_rows = [
+        jnp.concatenate(gather_tokens(tie(back_low[m], *att_rows), *orders[m]), axis=0)
+        for m in micros
     ]
-    back_low = [cotangent[m, 0].reshape(own_tokens, D) for m in range(micro_count)]
-
-    normed_att = [rms_norm(t, norm_gains[0]).astype(BF) for t in token_rows]
-    att_rows = [
-        gather_tokens(normed_att[m], *orders[m]).reshape(8 * own_tokens, D)
-        for m in range(micro_count)
-    ]
-    gathered_ids = [gather_tokens(doc_ids[m, 0], *orders[m]) for m in range(micro_count)]
-    all_back = jnp.concatenate(
-        [gather_tokens(back_low[m], *orders[m]).reshape(8 * own_tokens, D) for m in range(micro_count)],
-        axis=0,
-    )
+    for k in range(1, CHUNKS):
+        shard = exchange_rows(functools.partial(ff_columns, k), shard_ff[-1])
+        shard_ff.append(shard)
+        full_ff.append(fetch(shard))
 
     rel_c = jnp.arange(2)[:, None, None] ^ c_place
     rel_y = jnp.arange(2)[None, :, None] ^ y_place
@@ -449,11 +624,8 @@
     causal = places[:, None] >= places[None, :]
     masks = []
     columns = []
-    for m in range(micro_count):
-        ids = gathered_ids[m].reshape(2, 2, 2, seg_count, own_len)
-        where = 1 if orders[m][0] == "x" else 2
-        ids = jnp.moveaxis(ids, where, 0)
-        ids = jnp.moveaxis(ids, 3, 1).reshape(2, seg_count, -1)
+    for m in micros:
+        ids = jnp.transpose(all_ids[:, :, :, m], (1, 3, 0, 2, 4)).reshape(2, seg_count, -1)
         same = ids[:, :, :, None] == ids[:, :, None, :]
         masks.append((same & causal).astype(F32))
         last = jnp.max(ids, axis=2)
@@ -464,27 +636,22 @@
         columns.append(jnp.stack([reading, writing, keep], axis=-1).astype(F32))
 
     slots = (2, 2, 2, seg_count, own_len)
+    wheres = [1 if orders[m][0] == "x" else 2 for m in micros]
     projected = []
     combined = []
     hidden = []
-    normed_mlp = []
-    for m in range(micro_count):
-        where = 1 if orders[m][0] == "x" else 2
-        proj = mm(att_rows[m], full_qkv, NN).astype(BF)
+    mlp_rows = []
+    for m in micros:
+        rows_in = att_rows[m] if m == 0 else tie(att_rows[m], *back_rows, *shard_ff)
+        proj = mm(rows_in, full_qkv, NN).astype(BF)
         projected.append(proj.reshape(slots + (3 * width_att,)))
-        comb = attention_fwd(projected[m], masks[m], columns[m], gate_rows, where)
-        combined.append(comb.reshape(8 * own_tokens, width_att))
+        comb = attention_fwd(projected[m], masks[m], columns[m], gate_rows, wheres[m])
+        combined.append(comb.reshape(tokens, width_att))
         partial = mm(combined[m], full_out, NT).astype(BF)
         attended = scatter_tokens(partial.reshape(8, own_tokens, D), *orders[m])
         hidden.append(token_rows[m] + attended)
-        normed_mlp.append(rms_norm(hidden[m], norm_gains[1]).astype(BF))
-    mlp_rows = jnp.concatenate(
-        [
-            gather_tokens(normed_mlp[m], *orders[m]).reshape(8 * own_tokens, D)
-            for m in range(micro_count)
-        ],
-        axis=0,
-    )
+        normed_mlp = rms_norm(hidden[m], norm_gains[1]).astype(BF)
+        mlp_rows.append(gather_tokens(normed_mlp, *orders[m]))
 
     def reduce_rows(partial):
         return lax.psum_scatter(partial, "z", scatter_dimension=0, tiled=True)
@@ -492,108 +659,135 @@
     active = []
     d_gate_up = []
     own_ff = []
+    d_total = [None] * micro_count
+    out_total = [None] * micro_count
     for k in range(CHUNKS):
-        act, grad = feed_forward(mlp_rows, all_back, full_ff[k])
-        active.append(act)
-        d_gate_up.append(grad)
-        grad_ff = jnp.concatenate(
-            [mm(mlp_rows, grad, TN).astype(BF), mm(all_back, act, TN).astype(BF)], axis=1
-        )
-        own_ff.append(reduce_rows(grad_ff))
-    d_partial = sum(mm(d_gate_up[k], full_ff[k][:, : 2 * width], NT) for k in range(CHUNKS)).astype(BF)
-    out_partial = sum(mm(active[k], full_ff[k][:, 2 * width :], NT) for k in range(CHUNKS)).astype(BF)
-    d_partial = d_partial.reshape(micro_count, 8, own_tokens, D)
-    out_partial = out_partial.reshape(micro_count, 8, own_tokens, D)
+        active.append([])
+        d_gate_up.append([])
+        for m in micros:
+            rows_in = mlp_rows[m]
+            if k == CHUNKS - 1 and m > 0:
+                rows_in = (tie(rows_in[0], d_total[m - 1]), rows_in[1])
+            act, grad = feed_forward(rows_in, back_rows[m], full_ff[k])
+            active[k].append(act)
+            d_gate_up[k].append(grad)
+            d_term = mm(grad, full_ff[k][:, : 2 * width], NT)
+            d_total[m] = d_term if k == 0 else d_total[m] + d_term
+            if k < CHUNKS - 1:
+                out_term = mm(act, full_ff[k][:, 2 * width :], NT)
+                out_total[m] = out_term if k == 0 else out_total[m] + out_term
+            else:
+                d_total[m] = d_total[m].astype(BF)
+        if k < CHUNKS - 1:
+            grad_ff = weight_grads(mlp_rows, back_rows, d_gate_up[k], active[k])
+            own_ff.append(reduce_rows(grad_ff))
+            full_ff[k + 1] = tie(full_ff[k + 1], grad_ff, *d_total, *out_total)
+    d_partial = [t.reshape(8, own_tokens, D) for t in d_total]
 
     gain_grad_att = jnp.zeros((D,), F32)
     gain_grad_mlp = jnp.zeros((D,), F32)
     d_hidden = []
-    for m in range(micro_count):
-        d_normed = scatter_tokens(d_partial[m], *orders[m])
+    att_grads = []
+    last_active = [tie(active[-1][m], *d_partial) for m in micros]
+    grad_ff = weight_grads(mlp_rows, back_rows, d_gate_up[-1], last_active)
+    for m in micros:
+        d_normed = scatter_tokens(d_partial[m], *orders[m], grad_ff)
         ignored, norm_back = jax.vjp(rms_norm, hidden[m], norm_gains[1])
         d_norm, d_gain = norm_back(d_normed)
         gain_grad_mlp = gain_grad_mlp + d_gain
         d_hidden.append(back_low[m].astype(F32) + d_norm)
+        d_hidden_low = d_hidden[m].astype(BF)
+        att_grads.append(gather_tokens(d_hidden_low, *orders[m]))
+
+    own_ff.append(reduce_rows(grad_ff))
+    for m in micros:
+        act = tie(last_active[m], d_hidden[m])
+        out_total[m] = out_total[m] + mm(act, full_ff[-1][:, 2 * width :], NT)
 
     gate_sum = jnp.zeros((heads,), F32)
-    grad_qkv = jnp.zeros((D, 3 * width_att), F32)
-    grad_out = jnp.zeros((D, width_att), F32)
-    grad_rows = []
-    for m in range(micro_count):
-        where = 1 if orders[m][0] == "x" else 2
-        att_grads = gather_tokens(d_hidden[m].astype(BF), *orders[m]).reshape(8 * own_tokens, D)
-        d_combined = mm(att_grads, full_out, NN)
-        grad_out = grad_out + mm(att_grads, combined[m], TN)
+    d_projs = []
+    for m in micros:
+        other = att_grads[m][1] if m > 0 else tie(att_grads[m][1], own_ff[0])
+        d_combined = jnp.concatenate(
+            [mm(att_grads[m][0], full_out, NN), mm(other, full_out, NN)], axis=0
+        )
         d_proj, gate_part = attention_bwd(
             projected[m],
             d_combined.reshape(slots + (width_att,)),
             masks[m],
             columns[m],
             gate_rows,
-            where,
+            wheres[m],
         )
         gate_sum = gate_sum + jnp.sum(gate_part, axis=(0, 2))
-        d_proj = d_proj.reshape(8 * own_tokens, 3 * width_att)
-        grad_qkv = grad_qkv + mm(att_rows[m], d_proj, TN)
-        partial = mm(d_proj, full_qkv, NT).astype(BF).reshape(8, own_tokens, D)
-        d_normed = scatter_tokens(partial, *orders[m])
+        d_projs.append(d_proj.reshape(tokens, 3 * width_att))
+    grad_att = weight_grads(att_rows, att_grads, d_projs, combined)
+    own_att = reduce_rows(grad_att)
+
+    grad_rows = []
+    for m in micros:
+        partial = mm(tie(d_projs[m], grad_att), full_qkv, NT).astype(BF)
+        d_normed = scatter_tokens(partial.reshape(8, own_tokens, D), *orders[m], own_ff[-1])
         ignored, norm_first = jax.vjp(rms_norm, token_rows[m], norm_gains[0])
         d_norm, d_gain = norm_first(d_normed)
         gain_grad_att = gain_grad_att + d_gain
         grad_rows.append((d_hidden[m] + d_norm).astype(BF))
-    own_out = reduce_rows(grad_out.astype(BF))
-    own_qkv = reduce_rows(grad_qkv.astype(BF))
 
     block_out = []
-    for m in range(micro_count):
-        mlp_out = scatter_tokens(out_partial[m], *orders[m])
+    for m in micros:
+        partial = tie(out_total[m].astype(BF), *[pair[1] for pair in att_grads])
+        mlp_out = scatter_tokens(partial.reshape(8, own_tokens, D), *orders[m])
         block_out.append((hidden[m] + mlp_out).astype(BF))
 
     def exchange_grad(grad):
-        rows = grad.shape[0] // 2
         mine = lax.dynamic_slice_in_dim(grad, x_place * rows, rows, axis=0)
         theirs = swap(lax.dynamic_slice_in_dim(grad, (1 - x_place) * rows, rows, axis=0), "x")
         return mine, theirs
 
-    def join(mine, theirs):
-        return by_place(mine, theirs, mine.ndim - 1).astype(F32)
-
-    parts = [exchange_grad(g) for g in own_ff]
-    rows = weight_qkv.shape[0]
-    sides = []
-    for side in range(2):
-        stacked = jnp.stack([p[side].reshape(rows, 3, width) for p in parts], axis=2)
-        sides.append(stacked.reshape(rows, 3, width_ff))
-    ff_grad = join(*sides)
-    own_mlp, own_down = ff_grad[:, :2], ff_grad[:, 2]
-    own_out = join(*exchange_grad(own_out))
-    mine, theirs = exchange_grad(own_qkv)
-    own_qkv = join(mine.reshape(rows, 3, width_att), theirs.reshape(rows, 3, width_att))
+    def squares_of(grad):
+        wide = grad.astype(F32)
+        return jnp.sum(wide * wide)
+
+    pairs = [exchange_grad(g) for g in own_ff]
+
+    def ff_part(start, stop):
+        low = jnp.concatenate([p[0][:, start * width : stop * width] for p in pairs], axis=1)
+        high = jnp.concatenate([p[1][:, start * width : stop * width] for p in pairs], axis=1)
+        return by_place(low, high, 1)
+
+    grad_mlp = mlp_view(jnp.stack([ff_part(0, 1), ff_part(1, 2)], axis=1))
+    grad_down = ff_part(2, 3)
+    att_mine, att_theirs = exchange_grad(own_att)
 
     gate_grad = gate_sum * mixing * (1.0 - mixing)
     gate_padded = lax.dynamic_update_slice(
         jnp.zeros(gate_logit.shape, F32), gate_grad, (head_start,)
     )
-    owned = (
-        jnp.sum(own_qkv * own_qkv)
-        + jnp.sum(own_out * own_out)
-        + jnp.sum(own_mlp * own_mlp)
-        + jnp.sum(own_down * own_down)
-    )
-    everywhere = ("z", "x", "y", "c")
-    gain_grad = jnp.stack([gain_grad_att, gain_grad_mlp], axis=0)
-    gains_total, gate_total, owned_total = lax.psum((gain_grad, gate_padded, owned), everywhere)
-    squares = owned_total + jnp.sum(gains_total * gains_total) + jnp.sum(gate_total * gate_total)
-    grad_norm = jnp.sqrt(squares)
-    factor = jnp.minimum(1.0, CLIP / (grad_norm + 1e-06))
-    qkv_new = adam_update(weight_qkv, moment_qkv, second_qkv, own_qkv, factor, D ** (-0.5), DECAY)
-    out_new = adam_update(
-        weight_out, moment_out, second_out, own_out, factor, 4.0 * (HEADS * HEAD_DIM) ** (-0.5), DECAY
-    )
-    mlp_new = adam_update(weight_mlp, moment_mlp, second_mlp, own_mlp, factor, D ** (-0.5), DECAY)
-    down_new = adam_update(
-        weight_down, moment_down, second_down, own_down, factor, FF ** (-0.5), DECAY
-    )
+    ff_owned = tie(sum(squares_of(g) for g in own_ff), grad_mlp, grad_down)
+    owned = squares_of(own_att) + ff_owned
+    small = jnp.concatenate(
+        [gain_grad_att, gain_grad_mlp, gate_padded, owned[None], jnp.zeros((111,), F32)]
+    ).reshape(-1, 128)
+    small = sum_everywhere(small, z_count, att_theirs)
+    grad_norm, factor = (t.reshape(()) for t in clip_factor(small))
+    flat = small.reshape(-1)
+    gains_total = flat[: 2 * D].reshape(2, D)
+    gate_total = flat[2 * D : 2 * D + HEADS]
+    arrays = [
+        weight_qkv,
+        moment_qkv,
+        second_qkv,
+        weight_out,
+        moment_out,
+        second_out,
+        weight_mlp,
+        moment_mlp,
+        second_mlp,
+        weight_down,
+        moment_down,
+        second_down,
+    ]
+    new = adam_all(small, x_place, arrays, att_mine, att_theirs, grad_mlp, grad_down)
     gains_new = adam_update(norm_gains, moment_gains, second_gains, gains_total, factor, 0.5, 0.0)
     gate_new = adam_update(gate_logit, moment_gate, second_gate, gate_total, factor, 1.0, 0.0)
     shape = (micro_count, 1, seg_count, own_len, D)
@@ -601,10 +795,7 @@
         jnp.stack(block_out, axis=0).reshape(shape),
         jnp.stack(grad_rows, axis=0).reshape(shape),
         grad_norm,
-        *qkv_new,
-        *out_new,
-        *mlp_new,
-        *down_new,
+        *new,
         *gains_new,
         *gate_new,
     )

time: 1090 us -> 814 us (0.75)
  waiting for transfers between devices: 429 us -> 289 us
  local copies, waits for them, and re-layouts: 194 us -> 114 us
  Pallas kernels: 79.6 us -> 159 us
  matrix products: 139 us -> 91.7 us
  other arithmetic: 115 us -> 72.1 us
  blocking collectives: 41.5 us -> 0 us
    reduce_scatter x4 -> x3, waiting for transfers between devices: 131 us -> 0.02 us  [reduce_rows(): return lax.psum_scatter(partial, 'z', scatter_dimension=0, tiled=True)]
    unnamed x294 -> x262, local copies, waits for them, and re-layouts: 149 us -> 44 us
    pallas_call x2 -> x8, Pallas kernels: 40.6 us -> 121 us  [the longest x3 50.1 us: weight_grads(): pl.pallas_call(functools.partial(grads_kernel, count), grid=(D // tile,),...]
    dot_general x20 -> x18, matrix products: 139 us -> 91.7 us  [mm(): return lax.dot_general(a, b, (dims, ((), ())), preferred_element_type=F32)]
    psum x1 -> x0, blocking collectives: 41.5 us -> none  [on_device(): lax.psum((gain_grad, gate_padded, owned), everywhere)]
    sub x6 -> x2, other arithmetic: 26.7 us -> 1.22 us  [adam_update(): weight - step_rate * (fixed_first / (jnp.sqrt(fixed_second) + ADAM_EPS) +...]
    ppermute x102 -> x68, waiting for transfers between devices: 298 us -> 286 us  [swap(): return lax.ppermute(tensor, axis, [(0, 1), (1, 0)])]
    concatenate x6 -> x13, other arithmetic: 26.4 us -> 15.9 us  [the longest x8 12 us: gather_tokens(): mine = jnp.concatenate([own, by_inner, by_outer, by_both], axis=0)]
  transfers between devices with their start and end apart: 110 -> 76, of which waited for: 45 -> 40; matrix products, arithmetic and copies ran while one was open for 28% -> 30% of each run, Pallas kernels for 5% -> 17%
where the time goes in v2:
time: 814 us; the launch traced here: 807 us
  waiting for transfers between devices  289 us (36%)
  Pallas kernels  159 us (20%)
  local copies, waits for them, and re-layouts  114 us (14%)
  matrix products  91.7 us (11%)
  other arithmetic  72.1 us (9%)
  starting transfers between devices  60.9 us (7%)
  between operations  20.3 us (2%)
    ppermute x68, waiting for transfers between devices, swap(): return lax.ppermute(tensor, axis, [(0, 1), (1, 0)])  286 us
    dot_general x18, matrix products, mm(): return lax.dot_general(a, b, (dims, ((), ())), preferred_element_type=F32)  91.7 us
    ppermute x68, starting transfers between devices, swap(): return lax.ppermute(tensor, axis, [(0, 1), (1, 0)])  57 us
    pallas_call x3, Pallas kernels, weight_grads(): pl.pallas_call(functools.partial(grads_kernel, count), grid=(D // tile,),...  50.1 us
    pallas_call x4, Pallas kernels, feed_forward(): pl.pallas_call(functools.partial(ff_kernel, width, half), grid=(tokens //...  47 us
    unnamed x262, local copies, waits for them, and re-layouts  44 us
    pallas_call x2, Pallas kernels, attention_bwd(): pl.pallas_call(functools.partial(attention_bwd_kernel, heads), grid=(seqs...  25.1 us
    pallas_call x1, Pallas kernels, adam_all(): pl.pallas_call(adam_kernel, grid=(steps,), in_specs=[pl.BlockSpec(memory_...  23.5 us
  transfers between devices with their start and end apart: 76, of which 40 were waited for; matrix products, arithmetic and copies ran while one was open for 30% of the time, Pallas kernels for 17%

profile of v2, /device:TPU:0, one launch (start us, length us, event | category | flops | bytes accessed | tf_op | source)
XLA Modules:
  0.0 807.1 jit_solution(7615447038548391410)
XLA Ops:
  34.4 14.6 %collective-permute-done.4 = bf16[256,1024]{0,1:T(8,128)(2,1)} collective-permute-done((bf16[256,1024]{0,1:T(8,128)(2,1)}, bf16[256,1024]{0,1:T(8,128)(2,1)}, u32[]{:S(2)}, u32[]{:S(2)}) %collective-permute-start.4) | collective-permute-done | bytes 524320 | tf_op jit(solution)/shard_map/ppermute | solution.py:48
  61.7 10.5 %collective-permute-done.17 = bf16[128,2048]{1,0:T(8,128)(2,1)S(1)} collective-permute-done((bf16[128,2048]{1,0:T(8,128)(2,1)}, bf16[128,2048]{1,0:T(8,128)(2,1)S(1)}, u32[]{:S(2)}, u32[]{:S(2)}) %collective-permute-start.17) | collective-permute-done | bytes 524320 | tf_op jit(solution)/shard_map/ppermute | solution.py:48
  88.7 16.0 %collective-permute-done.23 = bf16[256,1536]{1,0:T(8,128)(2,1)} collective-permute-done((bf16[256,1536]{1,0:T(8,128)(2,1)}, bf16[256,1536]{1,0:T(8,128)(2,1)}, u32[]{:S(2)}, u32[]{:S(2)}) %collective-permute-start.23) | collective-permute-done | bytes 786464 | tf_op jit(solution)/shard_map/ppermute | solution.py:48
  113.7 8.4 %collective-permute-done.25 = bf16[128,2048]{1,0:T(8,128)(2,1)} collective-permute-done((bf16[128,2048]{1,0:T(8,128)(2,1)S(1)}, bf16[128,2048]{1,0:T(8,128)(2,1)}, u32[]{:S(2)}, u32[]{:S(2)}) %collective-permute-start.25) | collective-permute-done | bytes 524320 | tf_op jit(solution)/shard_map/ppermute | solution.py:48
  128.4 8.8 %collective-permute-done.26 = bf16[128,2048]{1,0:T(8,128)(2,1)S(1)} collective-permute-done((bf16[128,2048]{1,0:T(8,128)(2,1)S(1)}, bf16[128,2048]{1,0:T(8,128)(2,1)S(1)}, u32[]{:S(2)}, u32[]{:S(2)}) %collective-permute-start.26) | collective-permute-done | bytes 524320 | tf_op jit(solution)/shard_map/ppermute | solution.py:48
  137.2 10.5 %collective-permute-done.27 = bf16[128,2048]{1,0:T(8,128)(2,1)S(1)} collective-permute-done((bf16[128,2048]{1,0:T(8,128)(2,1)}, bf16[128,2048]{1,0:T(8,128)(2,1)S(1)}, u32[]{:S(2)}, u32[]{:S(2)}) %collective-permute-start.27) | collective-permute-done | bytes 524320 | tf_op jit(solution)/shard_map/ppermute | solution.py:48
  160.4 15.0 %collective-permute-done.24 = bf16[256,1536]{1,0:T(8,128)(2,1)S(1)} collective-permute-done((bf16[256,1536]{1,0:T(8,128)(2,1)S(1)}, bf16[256,1536]{1,0:T(8,128)(2,1)S(1)}, u32[]{:S(2)}, u32[]{:S(2)}) %collective-permute-start.24) | collective-permute-done | bytes 786464 | tf_op jit(solution)/shard_map/ppermute | solution.py:48
  226.7 20.8 %collective-permute-done.30 = bf16[2,128,2048]{2,1,0:T(8,128)(2,1)S(1)} collective-permute-done((bf16[2,128,2048]{2,1,0:T(8,128)(2,1)S(1)}, bf16[2,128,2048]{2,1,0:T(8,128)(2,1)S(1)}, u32[]{:S(2)}, u32[]{:S(2)}) %collective-permute-start.30) | collective-permute-done | bytes 1048608 | tf_op jit(solution)/shard_map/ppermute | solution.py:48
  253.1 9.1 %collective-permute-done.31 = bf16[128,2048]{1,0:T(8,128)(2,1)S(1)} collective-permute-done((bf16[128,2048]{1,0:T(8,128)(2,1)S(1)}, bf16[128,2048]{1,0:T(8,128)(2,1)S(1)}, u32[]{:S(2)}, u32[]{:S(2)}) %collective-permute-start.31) | collective-permute-done | bytes 524320 | tf_op jit(solution)/shard_map/ppermute | solution.py:48
  268.6 8.8 %collective-permute-done.11 = bf16[128,2048]{1,0:T(8,128)(2,1)S(1)} collective-permute-done((bf16[128,2048]{1,0:T(8,128)(2,1)S(1)}, bf16[128,2048]{1,0:T(8,128)(2,1)S(1)}, u32[]{:S(2)}, u32[]{:S(2)}) %collective-permute-start.11) | collective-permute-done | bytes 524320 | tf_op jit(solution)/shard_map/ppermute | solution.py:48
  282.4 10.3 %collective-permute-done.12 = bf16[128,2048]{1,0:T(8,128)(2,1)S(1)} collective-permute-done((bf16[128,2048]{1,0:T(8,128)(2,1)S(1)}, bf16[128,2048]{1,0:T(8,128)(2,1)S(1)}, u32[]{:S(2)}, u32[]{:S(2)}) %collective-permute-start.12) | collective-permute-done | bytes 524320 | tf_op jit(solution)/shard_map/ppermute | solution.py:48
  304.9 11.6 %feed_forward.4 = (bf16[1024,512]{1,0:T(8,128)(2,1)S(1)}, bf16[1024,1024]{1,0:T(8,128)(2,1)S(1)}) custom-call(bf16[512,2048]{1,0:T(8,128)(2,1)S(1)} %pad_maximum_fusion.1.mine_ref.refs_0_, bf16[512,2048]{1,0:T(8,128)(2,1)} %collective-permute-done.14.other_ref.refs_1_, bf16[1024,2048]{1,0:T(8,128)(2,1)} %constant_dynamic-update-slice_fusion.10.g_ref.refs_4_.refs_5_, ...), custom_call_target="tpu_custom_call" | custom-call | flops 1073741824 | bytes 2097152 | tf_op jit(solution)/shard_map/feed_forward/pallas_call | solution.py:355
  317.8 11.8 %feed_forward.5 = (bf16[1024,512]{1,0:T(8,128)(2,1)S(1)}, bf16[1024,1024]{1,0:T(8,128)(2,1)S(1)}) custom-call(bf16[512,2048]{1,0:T(8,128)(2,1)} %pad_maximum_fusion.5.mine_ref.refs_2_, bf16[512,2048]{1,0:T(8,128)(2,1)} %collective-permute-done.35.other_ref.refs_3_, bf16[1024,2048]{1,0:T(8,128)(2,1)} %constant_dynamic-update-slice_fusion.15.g_ref.refs_6_.refs_7_, ...), custom_call_target="tpu_custom_call" | custom-call | flops 1073741824 | bytes 2097152 | tf_op jit(solution)/shard_map/feed_forward/pallas_call | solution.py:355
  330.9 18.5 %weight_grads.3 = bf16[2048,1536]{1,0:T(8,128)(2,1)} custom-call(bf16[512,2048]{1,0:T(8,128)(2,1)S(1)} %pad_maximum_fusion.1.mine_ref.refs_0_, bf16[512,2048]{1,0:T(8,128)(2,1)} %collective-permute-done.14.other_ref.refs_1_, bf16[512,2048]{1,0:T(8,128)(2,1)} %pad_maximum_fusion.5.mine_ref.refs_2_, ...), custom_call_target="tpu_custom_call" | custom-call | flops 1610612736 | bytes 1048576 | tf_op jit(solution)/shard_map/weight_grads/pallas_call | solution.py:415
  358.0 9.4 %fusion = f32[1024,2048]{1,0:T(8,128)} fusion(bf16[1024,1024]{1,0:T(8,128)(2,1)S(1)} %copy-done.9, bf16[2048,1536]{1,0:T(8,128)(2,1)} %all-gather.6.cloned.1.call-done.w_ref), kind=kOutput, calls=%fused_computation.16 | convolution fusion | flops 4294967296 | bytes 14680064 | tf_op jit(solution)/shard_map/dot_general | solution.py:83
  380.5 11.5 %feed_forward.6 = (bf16[1024,512]{1,0:T(8,128)(2,1)S(1)}, bf16[1024,1024]{1,0:T(8,128)(2,1)S(1)}) custom-call(bf16[512,2048]{1,0:T(8,128)(2,1)S(1)} %pad_maximum_fusion.1.mine_ref.refs_0_, bf16[512,2048]{1,0:T(8,128)(2,1)} %collective-permute-done.14.other_ref.refs_1_, bf16[1024,2048]{1,0:T(8,128)(2,1)} %constant_dynamic-update-slice_fusion.10.g_ref.refs_4_.refs_5_, ...), custom_call_target="tpu_custom_call" | custom-call | flops 1073741824 | bytes 2097152 | tf_op jit(solution)/shard_map/feed_forward/pallas_call | solution.py:355
  392.1 9.5 %add_convert_fusion.3 = bf16[1024,2048]{1,0:T(8,128)(2,1)} fusion(f32[1024,2048]{1,0:T(8,128)} %fusion.2, bf16[1024,1024]{1,0:T(8,128)(2,1)S(1)} %get-tuple-element.78.refs_8_.refs_9_, bf16[2048,1536]{1,0:T(8,128)(2,1)S(1)} %copy-done.44), kind=kOutput, calls=%fused_computation.3 | convolution fusion | flops 4299161600 | bytes 18874368 | tf_op jit(solution)/shard_map/dot_general | solution.py:83
  401.6 12.1 %feed_forward.7 = (bf16[1024,512]{1,0:T(8,128)(2,1)S(1)}, bf16[1024,1024]{1,0:T(8,128)(2,1)S(1)}) custom-call(bf16[512,2048]{1,0:T(8,128)(2,1)} %pad_maximum_fusion.5.mine_ref.refs_2_, bf16[512,2048]{1,0:T(8,128)(2,1)} %collective-permute-done.35.other_ref.refs_3_, bf16[1024,2048]{1,0:T(8,128)(2,1)} %constant_dynamic-update-slice_fusion.15.g_ref.refs_6_.refs_7_, ...), custom_call_target="tpu_custom_call" | custom-call | flops 1073741824 | bytes 2097152 | tf_op jit(solution)/shard_map/feed_forward/pallas_call | solution.py:355
  413.7 9.1 %add_convert_fusion.2 = bf16[1024,2048]{1,0:T(8,128)(2,1)S(1)} fusion(f32[1024,2048]{1,0:T(8,128)} %fusion, bf16[1024,1024]{1,0:T(8,128)(2,1)S(1)} %get-tuple-element.80.refs_10_.refs_11_, bf16[2048,1536]{1,0:T(8,128)(2,1)} %all-gather.8.cloned.1.call-done.w_ref), kind=kOutput, calls=%fused_computation.2 | convolution fusion | flops 4299161600 | bytes 18874368 | tf_op jit(solution)/shard_map/dot_general | solution.py:83
  432.9 18.7 %weight_grads.4 = bf16[2048,1536]{1,0:T(8,128)(2,1)} custom-call(bf16[512,2048]{1,0:T(8,128)(2,1)S(1)} %pad_maximum_fusion.1.mine_ref.refs_0_, bf16[512,2048]{1,0:T(8,128)(2,1)} %collective-permute-done.14.other_ref.refs_1_, bf16[512,2048]{1,0:T(8,128)(2,1)} %pad_maximum_fusion.5.mine_ref.refs_2_, ...), custom_call_target="tpu_custom_call" | custom-call | flops 1610612736 | bytes 1048576 | tf_op jit(solution)/shard_map/weight_grads/pallas_call | solution.py:415
  460.4 20.7 %collective-permute-done.37 = bf16[2,128,2048]{2,1,0:T(8,128)(2,1)S(1)} collective-permute-done((bf16[2,128,2048]{2,1,0:T(8,128)(2,1)S(1)}, bf16[2,128,2048]{2,1,0:T(8,128)(2,1)S(1)}, u32[]{:S(2)}, u32[]{:S(2)}) %collective-permute-start.37) | collective-permute-done | bytes 1048608 | tf_op jit(solution)/shard_map/ppermute | solution.py:48
  482.6 8.9 %collective-permute-done.45 = bf16[128,2048]{1,0:T(8,128)(2,1)S(1)} collective-permute-done((bf16[128,2048]{1,0:T(8,128)(2,1)S(1)}, bf16[128,2048]{1,0:T(8,128)(2,1)S(1)}, u32[]{:S(2)}, u32[]{:S(2)}) %collective-permute-start.45) | collective-permute-done | bytes 524320 | tf_op jit(solution)/shard_map/ppermute | solution.py:48
  499.7 9.5 %collective-permute-done.46 = bf16[128,2048]{1,0:T(8,128)(2,1)S(1)} collective-permute-done((bf16[128,2048]{1,0:T(8,128)(2,1)S(1)}, bf16[128,2048]{1,0:T(8,128)(2,1)S(1)}, u32[]{:S(2)}, u32[]{:S(2)}) %collective-permute-start.46) | collective-permute-done | bytes 524320 | tf_op jit(solution)/shard_map/ppermute | solution.py:48
  514.2 9.6 %collective-permute-done.47 = bf16[128,2048]{1,0:T(8,128)(2,1)S(1)} collective-permute-done((bf16[128,2048]{1,0:T(8,128)(2,1)S(1)}, bf16[128,2048]{1,0:T(8,128)(2,1)S(1)}, u32[]{:S(2)}, u32[]{:S(2)}) %collective-permute-start.47) | collective-permute-done | bytes 524320 | tf_op jit(solution)/shard_map/ppermute | solution.py:48
  560.2 12.7 %attention_backward.3 = (bf16[2,2,2,4,32,768]{5,4,3,2,1,0:T(8,128)(2,1)S(1)}, f32[2,2,128]{2,1,0:T(2,128)S(1)}) custom-call(bf16[2,2,2,4,32,768]{5,4,3,2,1,0:T(8,128)(2,1)S(1)} %bitcast.287, f32[2,2,2,4,32,256]{5,4,3,2,1,0:T(8,128)S(1)} %bitcast.289, f32[2,4,128,128]{3,2,1,0:T(8,128)S(1)} %copy-done.23, f32[2,4,128,3]{3,2,1,0:T(8,128)S(1)} %copy-done.19, ...), custom_call_target="tpu_custom_call" | custom-call | flops 1000000000 | bytes 5000000 | tf_op jit(solution)/shard_map/attention_backward/pallas_call | solution.py:292
  582.2 20.2 %collective-permute-done.54 = bf16[2,128,2048]{2,1,0:T(8,128)(2,1)S(1)} collective-permute-done((bf16[2,128,2048]{2,1,0:T(8,128)(2,1)S(1)}, bf16[2,128,2048]{2,1,0:T(8,128)(2,1)S(1)}, u32[]{:S(2)}, u32[]{:S(2)}) %collective-permute-start.54) | collective-permute-done | bytes 1048608 | tf_op jit(solution)/shard_map/ppermute | solution.py:48
  603.4 9.6 %collective-permute-done.52 = bf16[128,2048]{1,0:T(8,128)(2,1)S(1)} collective-permute-done((bf16[128,2048]{1,0:T(8,128)(2,1)S(1)}, bf16[128,2048]{1,0:T(8,128)(2,1)S(1)}, u32[]{:S(2)}, u32[]{:S(2)}) %collective-permute-start.52) | collective-permute-done | bytes 524320 | tf_op jit(solution)/shard_map/ppermute | solution.py:48
  620.8 12.3 %attention_backward.2 = (bf16[2,2,2,4,32,768]{5,4,3,2,1,0:T(8,128)(2,1)S(1)}, f32[2,2,128]{2,1,0:T(2,128)S(1)}) custom-call(bf16[2,2,2,4,32,768]{5,4,3,2,1,0:T(8,128)(2,1)S(1)} %bitcast.285, f32[2,2,2,4,32,256]{5,4,3,2,1,0:T(8,128)S(1)} %bitcast.288, f32[2,4,128,128]{3,2,1,0:T(8,128)S(1)} %copy-done.21, f32[2,4,128,3]{3,2,1,0:T(8,128)S(1)} %copy-done.17, ...), custom_call_target="tpu_custom_call" | custom-call | flops 1000000000 | bytes 5000000 | tf_op jit(solution)/shard_map/attention_backward/pallas_call | solution.py:292
  633.1 12.9 %weight_grads.5 = bf16[2048,1024]{1,0:T(8,128)(2,1)} custom-call(bf16[1024,2048]{1,0:T(8,128)(2,1)} %copy-done.47, bf16[1024,2048]{1,0:T(8,128)(2,1)} %copy-done.47, bf16[1024,2048]{1,0:T(8,128)(2,1)} %copy-done.46, bf16[1024,2048]{1,0:T(8,128)(2,1)} %copy-done.46, bf16[512,2048]{1,0:T(8,128)(2,1)} %pad_maximum_fusion.6.refs_4_, ...), custom_call_target="tpu_custom_call" | custom-call | flops 1073741824 | bytes 1048576 | tf_op jit(solution)/shard_map/weight_grads/pallas_call | solution.py:415
  705.8 10.0 %collective-permute-done.60 = bf16[2,128,2048]{2,1,0:T(8,128)(2,1)S(1)} collective-permute-done((bf16[2,128,2048]{2,1,0:T(8,128)(2,1)}, bf16[2,128,2048]{2,1,0:T(8,128)(2,1)S(1)}, u32[]{:S(2)}, u32[]{:S(2)}) %collective-permute-start.60) | collective-permute-done | bytes 1048608 | tf_op jit(solution)/shard_map/ppermute | solution.py:48
  717.7 13.4 %collective-permute-done.57 = bf16[2,128,2048]{2,1,0:T(8,128)(2,1)S(1)} collective-permute-done((bf16[2,128,2048]{2,1,0:T(8,128)(2,1)S(1)}, bf16[2,128,2048]{2,1,0:T(8,128)(2,1)S(1)}, u32[]{:S(2)}, u32[]{:S(2)}) %collective-permute-start.57) | collective-permute-done | bytes 1048608 | tf_op jit(solution)/shard_map/ppermute | solution.py:48
  775.5 23.5 %adam.1 = (f32[3,256,512]{2,1,0:T(8,128)}, f32[3,256,512]{2,1,0:T(8,128)}, f32[3,256,512]{2,1,0:T(8,128)}, f32[256,512]{1,0:T(8,128)}, f32[256,512]{1,0:T(8,128)...) custom-call(s32[1]{0:T(128)} %bitcast.79.place_ref, ...), custom_call_target="tpu_custom_call" | custom-call | flops 41943040 | bytes 50331648 | tf_op jit(solution)/shard_map/adam/pallas_call | solution.py:495
  (586 shorter events, 378.3 us)
Async XLA Ops:
  7.2 175.5 %all-gather.4.cloned.1.call-start = ((), (), s32[]{:S(2)}) async-start(), calls=%async_computation.3 | async-start | bytes 5242880 | tf_op jit(solution)/shard_map/all_gather | solution.py:571
  11.4 48.0 %collective-permute-start.15 = (bf16[128,2048]{1,0:T(8,128)(2,1)S(1)}, bf16[128,2048]{1,0:T(8,128)(2,1)}, u32[]{:S(2)}, u32[]{:S(2)}) collective-permute-start(bf16[128,2048]{1,0:T(8,128)(2,1)S(1)} %get-tuple-element.180), channel_id=1, source_target_pairs={{0,4},{4,0},{1,5},{5,1},{2,6},{6,2},{3,7},{7,3},{8,12},{12,8},{9,1... | collective-permute-start | bytes 1572872 | tf_op jit(solution)/shard_map/ppermute | solution.py:48
  14.4 47.3 %collective-permute-start.16 = (bf16[128,2048]{1,0:T(8,128)(2,1)S(1)}, bf16[128,2048]{1,0:T(8,128)(2,1)}, u32[]{:S(2)}, u32[]{:S(2)}) collective-permute-start(bf16[128,2048]{1,0:T(8,128)(2,1)S(1)} %get-tuple-element.180), channel_id=1, source_target_pairs={{0,2},{2,0},{1,3},{3,1},{4,6},{6,4},{5,7},{7,5},{8,10},{10,8},{9,1... | collective-permute-start | bytes 1572872 | tf_op jit(solution)/shard_map/ppermute | solution.py:48
  15.9 43.8 %collective-permute-start = (bf16[128,2048]{1,0:T(8,128)(2,1)S(1)}, bf16[128,2048]{1,0:T(8,128)(2,1)}, u32[]{:S(2)}, u32[]{:S(2)}) collective-permute-start(bf16[128,2048]{1,0:T(8,128)(2,1)S(1)} %get-tuple-element.179), channel_id=1, source_target_pairs={{0,2},{2,0},{1,3},{3,1},{4,6},{6,4},{5,7},{7,5},{8,10},{10,8},{9,1... | collective-permute-start | bytes 1572872 | tf_op jit(solution)/shard_map/ppermute | solution.py:48
  16.4 57.3 %collective-permute-start.1 = (bf16[128,2048]{1,0:T(8,128)(2,1)S(1)}, bf16[128,2048]{1,0:T(8,128)(2,1)}, u32[]{:S(2)}, u32[]{:S(2)}) collective-permute-start(bf16[128,2048]{1,0:T(8,128)(2,1)S(1)} %get-tuple-element.179), channel_id=1, source_target_pairs={{0,4},{4,0},{1,5},{5,1},{2,6},{6,2},{3,7},{7,3},{8,12},{12,8},{9,1... | collective-permute-start | bytes 1572872 | tf_op jit(solution)/shard_map/ppermute | solution.py:48
  19.5 29.4 %collective-permute-start.4 = (bf16[256,1024]{0,1:T(8,128)(2,1)}, bf16[256,1024]{0,1:T(8,128)(2,1)}, u32[]{:S(2)}, u32[]{:S(2)}) collective-permute-start(bf16[256,1024]{0,1:T(8,128)(2,1)} %pad_maximum_fusion.14), channel_id=1, source_target_pairs={{0,4},{4,0},{1,5},{5,1},{2,6},{6,2},{3,7},{7,3},{8,12},{12,8},{9,1... | collective-permute-start | bytes 1572872 | tf_op jit(solution)/shard_map/ppermute | solution.py:48
  48.9 38.2 %collective-permute-start.5 = (s32[2,4,32]{2,1,0:T(4,128)S(1)}, s32[2,4,32]{2,1,0:T(4,128)S(1)}, u32[]{:S(2)}, u32[]{:S(2)}) collective-permute-start(s32[2,4,32]{2,1,0:T(4,128)S(1)} %bitcast.336), channel_id=1, source_target_pairs={{0,2},{2,0},{1,3},{3,1},{4,6},{6,4},{5,7},{7,5},{8,10},{10,8},{9,1... | collective-permute-start | bytes 3080 | tf_op jit(solution)/shard_map/ppermute | solution.py:48
  52.6 250.1 %all-gather.6.cloned.1.call-start = ((), (), s32[]{:S(2)}) async-start(), calls=%async_computation.4 | async-start | bytes 7864320 | tf_op jit(solution)/shard_map/all_gather | solution.py:571
  107.1 273.4 %all-gather.8.cloned.1.call-start = ((), (), s32[]{:S(2)}) async-start(), calls=%async_computation.5 | async-start | bytes 7864320 | tf_op jit(solution)/shard_map/all_gather | solution.py:571
  112.1 25.1 %collective-permute-start.26 = (bf16[128,2048]{1,0:T(8,128)(2,1)S(1)}, bf16[128,2048]{1,0:T(8,128)(2,1)S(1)}, u32[]{:S(2)}, u32[]{:S(2)}) collective-permute-start(bf16[128,2048]{1,0:T(8,128)(2,1)S(1)} %bitcast.303), channel_id=1, source_target_pairs={{0,2},{2,0},{1,3},{3,1},{4,6},{6,4},{5,7},{7,5},{8,10},{10,8},{9,1... | collective-permute-start | bytes 1572872 | tf_op jit(solution)/shard_map/ppermute | solution.py:48
  122.1 25.6 %collective-permute-start.27 = (bf16[128,2048]{1,0:T(8,128)(2,1)}, bf16[128,2048]{1,0:T(8,128)(2,1)S(1)}, u32[]{:S(2)}, u32[]{:S(2)}) collective-permute-start(bf16[128,2048]{1,0:T(8,128)(2,1)} %collective-permute-done.25), channel_id=1, source_target_pairs={{0,2},{2,0},{1,3},{3,1},{4,6},{6,4},{5,7},{7,5},{8,10},{10,8},{9,1... | collective-permute-start | bytes 1572872 | tf_op jit(solution)/shard_map/ppermute | solution.py:48
  123.2 27.1 %collective-permute-start.20 = (bf16[128,2048]{1,0:T(8,128)(2,1)S(1)}, bf16[128,2048]{1,0:T(8,128)(2,1)S(1)}, u32[]{:S(2)}, u32[]{:S(2)}) collective-permute-start(bf16[128,2048]{1,0:T(8,128)(2,1)S(1)} %bitcast.307), channel_id=1, source_target_pairs={{0,4},{4,0},{1,5},{5,1},{2,6},{6,2},{3,7},{7,3},{8,12},{12,8},{9,1... | collective-permute-start | bytes 1572872 | tf_op jit(solution)/shard_map/ppermute | solution.py:48
  150.3 26.0 %collective-permute-start.28 = (bf16[512,2048]{1,0:T(8,128)(2,1)}, bf16[512,2048]{1,0:T(8,128)(2,1)}, u32[]{:S(2)}, u32[]{:S(2)}) collective-permute-start(bf16[512,2048]{1,0:T(8,128)(2,1)} %pad_maximum_fusion.4), channel_id=1, source_target_pairs={{0,1},{1,0},{2,3},{3,2},{4,5},{5,4},{6,7},{7,6},{8,9},{9,8},{10,11... | collective-permute-start | bytes 6291464 | tf_op jit(solution)/shard_map/ppermute | solution.py:48
  151.9 27.6 %collective-permute-start.22 = (bf16[512,2048]{1,0:T(8,128)(2,1)}, bf16[512,2048]{1,0:T(8,128)(2,1)}, u32[]{:S(2)}, u32[]{:S(2)}) collective-permute-start(bf16[512,2048]{1,0:T(8,128)(2,1)} %pad_maximum_fusion.3), channel_id=1, source_target_pairs={{0,1},{1,0},{2,3},{3,2},{4,5},{5,4},{6,7},{7,6},{8,9},{9,8},{10,11... | collective-permute-start | bytes 6291464 | tf_op jit(solution)/shard_map/ppermute | solution.py:48
  218.7 398.2 %reduce-scatter.4.cloned.1.call-start = ((), (), s32[]{:S(2)}) async-start(), calls=%async_computation.6 | async-start | bytes 7864320 | tf_op jit(solution)/shard_map/reduce_scatter | solution.py:657
  221.9 25.6 %collective-permute-start.30 = (bf16[2,128,2048]{2,1,0:T(8,128)(2,1)S(1)}, bf16[2,128,2048]{2,1,0:T(8,128)(2,1)S(1)}, u32[]{:S(2)}, u32[]{:S(2)}) collective-permute-start(bf16[2,128,2048]{2,1,0:T(8,128)(2,1)S(1)} %slice.649), channel_id=1, source_target_pairs={{0,2},{2,0},{1,3},{3,1},{4,6},{6,4},{5,7},{7,5},{8,10},{10,8},{9,1... | collective-permute-start | bytes 3145736 | tf_op jit(solution)/shard_map/ppermute | solution.py:48
  225.7 25.6 %collective-permute-start.9 = (bf16[2,128,2048]{2,1,0:T(8,128)(2,1)S(1)}, bf16[2,128,2048]{2,1,0:T(8,128)(2,1)S(1)}, u32[]{:S(2)}, u32[]{:S(2)}) collective-permute-start(bf16[2,128,2048]{2,1,0:T(8,128)(2,1)S(1)} %slice.650), channel_id=1, source_target_pairs={{0,4},{4,0},{1,5},{5,1},{2,6},{6,2},{3,7},{7,3},{8,12},{12,8},{9,1... | collective-permute-start | bytes 3145736 | tf_op jit(solution)/shard_map/ppermute | solution.py:48
  267.7 25.0 %collective-permute-start.12 = (bf16[128,2048]{1,0:T(8,128)(2,1)S(1)}, bf16[128,2048]{1,0:T(8,128)(2,1)S(1)}, u32[]{:S(2)}, u32[]{:S(2)}) collective-permute-start(bf16[128,2048]{1,0:T(8,128)(2,1)S(1)} %get-tuple-element.219), channel_id=1, source_target_pairs={{0,4},{4,0},{1,5},{5,1},{2,6},{6,2},{3,7},{7,3},{8,12},{12,8},{9,1... | collective-permute-start | bytes 1572872 | tf_op jit(solution)/shard_map/ppermute | solution.py:48
  350.4 320.9 %reduce-scatter.6.cloned.1.call-start = ((), (), s32[]{:S(2)}) async-start(), calls=%async_computation.7 | async-start | bytes 7864320 | tf_op jit(solution)/shard_map/reduce_scatter | solution.py:657
  431.8 25.8 %collective-permute-start.44 = (bf16[2,128,2048]{2,1,0:T(8,128)(2,1)}, bf16[2,128,2048]{2,1,0:T(8,128)(2,1)}, u32[]{:S(2)}, u32[]{:S(2)}) collective-permute-start(bf16[2,128,2048]{2,1,0:T(8,128)(2,1)} %slice.647), channel_id=1, source_target_pairs={{0,2},{2,0},{1,3},{3,1},{4,6},{6,4},{5,7},{7,5},{8,10},{10,8},{9,1... | collective-permute-start | bytes 3145736 | tf_op jit(solution)/shard_map/ppermute | solution.py:48
  455.0 26.1 %collective-permute-start.37 = (bf16[2,128,2048]{2,1,0:T(8,128)(2,1)S(1)}, bf16[2,128,2048]{2,1,0:T(8,128)(2,1)S(1)}, u32[]{:S(2)}, u32[]{:S(2)}) collective-permute-start(bf16[2,128,2048]{2,1,0:T(8,128)(2,1)S(1)} %slice.648), channel_id=1, source_target_pairs={{0,4},{4,0},{1,5},{5,1},{2,6},{6,2},{3,7},{7,3},{8,12},{12,8},{9,1... | collective-permute-start | bytes 3145736 | tf_op jit(solution)/shard_map/ppermute | solution.py:48
  459.2 32.3 %collective-permute-start.45 = (bf16[128,2048]{1,0:T(8,128)(2,1)S(1)}, bf16[128,2048]{1,0:T(8,128)(2,1)S(1)}, u32[]{:S(2)}, u32[]{:S(2)}) collective-permute-start(bf16[128,2048]{1,0:T(8,128)(2,1)S(1)} %fusion.59), channel_id=1, source_target_pairs={{0,4},{4,0},{1,5},{5,1},{2,6},{6,2},{3,7},{7,3},{8,12},{12,8},{9,1... | collective-permute-start | bytes 1572872 | tf_op jit(solution)/shard_map/ppermute | solution.py:48
  497.6 246.6 %reduce-scatter.8.cloned.1.call-start = ((), (), s32[]{:S(2)}) async-start(), calls=%async_computation.8 | async-start | bytes 5242880 | tf_op jit(solution)/shard_map/reduce_scatter | solution.py:657
  554.7 25.8 %collective-permute-start.51 = (bf16[2,128,2048]{2,1,0:T(8,128)(2,1)}, bf16[2,128,2048]{2,1,0:T(8,128)(2,1)S(1)}, u32[]{:S(2)}, u32[]{:S(2)}) collective-permute-start(bf16[2,128,2048]{2,1,0:T(8,128)(2,1)} %slice.646), channel_id=1, source_target_pairs={{0,4},{4,0},{1,5},{5,1},{2,6},{6,2},{3,7},{7,3},{8,12},{12,8},{9,1... | collective-permute-start | bytes 3145736 | tf_op jit(solution)/shard_map/ppermute | solution.py:48
  576.4 26.1 %collective-permute-start.54 = (bf16[2,128,2048]{2,1,0:T(8,128)(2,1)S(1)}, bf16[2,128,2048]{2,1,0:T(8,128)(2,1)S(1)}, u32[]{:S(2)}, u32[]{:S(2)}) collective-permute-start(bf16[2,128,2048]{2,1,0:T(8,128)(2,1)S(1)} %slice.645), channel_id=1, source_target_pairs={{0,2},{2,0},{1,3},{3,1},{4,6},{6,4},{5,7},{7,5},{8,10},{10,8},{9,1... | collective-permute-start | bytes 3145736 | tf_op jit(solution)/shard_map/ppermute | solution.py:48
  580.9 32.1 %collective-permute-start.52 = (bf16[128,2048]{1,0:T(8,128)(2,1)S(1)}, bf16[128,2048]{1,0:T(8,128)(2,1)S(1)}, u32[]{:S(2)}, u32[]{:S(2)}) collective-permute-start(bf16[128,2048]{1,0:T(8,128)(2,1)S(1)} %fusion.60), channel_id=1, source_target_pairs={{0,2},{2,0},{1,3},{3,1},{4,6},{6,4},{5,7},{7,5},{8,10},{10,8},{9,1... | collective-permute-start | bytes 1572872 | tf_op jit(solution)/shard_map/ppermute | solution.py:48
  648.1 32.6 %collective-permute-start.62 = (bf16[256,1536]{1,0:T(8,128)(2,1)}, bf16[256,1536]{1,0:T(8,128)(2,1)}, u32[]{:S(2)}, u32[]{:S(2)}) collective-permute-start(bf16[256,1536]{1,0:T(8,128)(2,1)} %constant_dynamic-slice_fusion.5), channel_id=1, source_target_pairs={{0,4},{4,0},{1,5},{5,1},{2,6},{6,2},{3,7},{7,3},{8,12},{12,8},{9,1... | collective-permute-start | bytes 2359304 | tf_op jit(solution)/shard_map/ppermute | solution.py:48
  657.5 26.7 %collective-permute-start.59 = (bf16[4,128,2048]{2,1,0:T(8,128)(2,1)}, bf16[4,128,2048]{2,1,0:T(8,128)(2,1)}, u32[]{:S(2)}, u32[]{:S(2)}) collective-permute-start(bf16[4,128,2048]{2,1,0:T(8,128)(2,1)} %bitcast.71), channel_id=1, source_target_pairs={{0,1},{1,0},{2,3},{3,2},{4,5},{5,4},{6,7},{7,6},{8,9},{9,8},{10,11... | collective-permute-start | bytes 6291464 | tf_op jit(solution)/shard_map/ppermute | solution.py:48
  669.6 32.7 %collective-permute-start.56 = (bf16[4,128,2048]{2,1,0:T(8,128)(2,1)}, bf16[4,128,2048]{2,1,0:T(8,128)(2,1)}, u32[]{:S(2)}, u32[]{:S(2)}) collective-permute-start(bf16[4,128,2048]{2,1,0:T(8,128)(2,1)} %bitcast.66), channel_id=1, source_target_pairs={{0,1},{1,0},{2,3},{3,2},{4,5},{5,4},{6,7},{7,6},{8,9},{9,8},{10,11... | collective-permute-start | bytes 6291464 | tf_op jit(solution)/shard_map/ppermute | solution.py:48
  690.4 25.5 %collective-permute-start.60 = (bf16[2,128,2048]{2,1,0:T(8,128)(2,1)}, bf16[2,128,2048]{2,1,0:T(8,128)(2,1)S(1)}, u32[]{:S(2)}, u32[]{:S(2)}) collective-permute-start(bf16[2,128,2048]{2,1,0:T(8,128)(2,1)} %slice.643), channel_id=1, source_target_pairs={{0,2},{2,0},{1,3},{3,1},{4,6},{6,4},{5,7},{7,5},{8,10},{10,8},{9,1... | collective-permute-start | bytes 3145736 | tf_op jit(solution)/shard_map/ppermute | solution.py:48
  705.0 26.1 %collective-permute-start.57 = (bf16[2,128,2048]{2,1,0:T(8,128)(2,1)S(1)}, bf16[2,128,2048]{2,1,0:T(8,128)(2,1)S(1)}, u32[]{:S(2)}, u32[]{:S(2)}) collective-permute-start(bf16[2,128,2048]{2,1,0:T(8,128)(2,1)S(1)} %slice.644), channel_id=1, source_target_pairs={{0,4},{4,0},{1,5},{5,1},{2,6},{6,2},{3,7},{7,3},{8,12},{12,8},{9,1... | collective-permute-start | bytes 3145736 | tf_op jit(solution)/shard_map/ppermute | solution.py:48
  716.3 24.7 %collective-permute-start.61 = (bf16[128,2048]{1,0:T(8,128)(2,1)S(1)}, bf16[128,2048]{1,0:T(8,128)(2,1)S(1)}, u32[]{:S(2)}, u32[]{:S(2)}) collective-permute-start(bf16[128,2048]{1,0:T(8,128)(2,1)S(1)} %fusion.63), channel_id=1, source_target_pairs={{0,4},{4,0},{1,5},{5,1},{2,6},{6,2},{3,7},{7,3},{8,12},{12,8},{9,1... | collective-permute-start | bytes 1572872 | tf_op jit(solution)/shard_map/ppermute | solution.py:48
  (163 other events, 1964.1 us)
Sparse Core Ops, SparseCore 0:
  52.7 81.0 all-gather.3
  135.9 113.8 all-gather.5
  252.0 113.5 all-gather.7
  367.8 108.9 reduce-scatter.3
  497.7 111.5 reduce-scatter.5
  649.3 76.8 reduce-scatter.7

commit v3 on v2

--- a/solution.py
+++ b/solution.py
@@ -52,20 +52,45 @@
     return lax.optimization_barrier((tensor,) + earlier)[0]
 
 
-def gather_tokens(own, outer, inner):
-    by_inner = swap(own, inner)
-    by_outer = swap(own, outer)
-    by_both = swap(by_inner, outer)
-    mine = jnp.concatenate([own, by_inner, by_outer, by_both], axis=0)
+def gather_start(own, outer, inner, *before_x):
+    start = {"x": tie(own, *before_x), "y": own}
+    return own, swap(start[inner], inner), swap(start[outer], outer)
+
+
+def gather_across(state, outer):
+    return state + (swap(state[1], outer),)
+
+
+def gather_core(state):
+    mine = jnp.concatenate(state, axis=0)
     return mine, swap(mine, "c")
 
 
-def scatter_tokens(partial, outer, inner, *earlier):
-    half = partial[:4].astype(F32) + swap(partial[4:], "c").astype(F32)
-    low = half.astype(BF)
-    half = half[:2] + swap(low[2:], outer).astype(F32)
-    low = tie(half[1].astype(BF), *earlier)
-    return half[0] + swap(low, inner).astype(F32)
+def gather_tokens(own, outer, inner, *before_x):
+    return gather_core(gather_across(gather_start(own, outer, inner, *before_x), outer))
+
+
+def scatter_core(mine, other, units):
+    came = swap(other, "c").reshape(4, units, -1)
+    mine = mine.reshape(4, units, -1)
+    send = (mine[2:].astype(F32) + came[2:].astype(F32)).astype(BF)
+    return mine[:2].astype(F32) + came[:2].astype(F32), send
+
+
+def scatter_outer(state, outer):
+    keep, send = state
+    came = swap(send, outer)
+    send = (keep[1] + came[1].astype(F32)).astype(BF)
+    return keep[0] + came[0].astype(F32), send
+
+
+def scatter_inner(state, inner):
+    keep, send = state
+    return keep + swap(send, inner).astype(F32)
+
+
+def tie_send(state, *earlier):
+    return state[0], tie(state[1], *earlier)
 
 
 def sum_everywhere(tensor, z_count, beside):
@@ -319,16 +344,16 @@
 GELU_B = 0.044715
 
 
-def ff_kernel(width, half, mine_ref, other_ref, g_ref, w_ref, act_ref, grad_ref):
+def ff_kernel(width, half, x_mine, x_other, g_mine, g_other, w_ref, *outs):
     step = pl.program_id(0)
 
     @pl.when(step < half)
     def first():
-        ff_tile(width, mine_ref, g_ref, w_ref, act_ref, grad_ref)
+        ff_tile(width, x_mine, g_mine, w_ref, outs[0], outs[2])
 
     @pl.when(step >= half)
     def second():
-        ff_tile(width, other_ref, g_ref, w_ref, act_ref, grad_ref)
+        ff_tile(width, x_other, g_other, w_ref, outs[1], outs[3])
 
 
 def ff_tile(width, x_ref, g_ref, w_ref, act_ref, grad_ref):
@@ -348,33 +373,33 @@
 
 
 def feed_forward(rows, grads, weights):
-    tokens = grads.shape[0]
+    tokens = rows[0].shape[0]
     width = weights.shape[1] // 3
     tile = 256
-    half = tokens // (2 * tile)
-    return pl.pallas_call(
+    half = tokens // tile
+
+    def first(columns):
+        return pl.BlockSpec((tile, columns), lambda i: (jnp.minimum(i, half - 1), 0))
+
+    def second(columns):
+        return pl.BlockSpec((tile, columns), lambda i: (jnp.maximum(i - half, 0), 0))
+
+    whole = pl.BlockSpec(weights.shape, lambda i: (0, 0), pipeline_mode=pl.Buffered(1))
+    act = jax.ShapeDtypeStruct((tokens, width), BF)
+    grad = jax.ShapeDtypeStruct((tokens, 2 * width), BF)
+    out = pl.pallas_call(
         functools.partial(ff_kernel, width, half),
-        grid=(tokens // tile,),
-        in_specs=[
-            pl.BlockSpec((tile, D), lambda i: (jnp.minimum(i, half - 1), 0)),
-            pl.BlockSpec((tile, D), lambda i: (jnp.maximum(i - half, 0), 0)),
-            pl.BlockSpec((tile, D), lambda i: (i, 0)),
-            pl.BlockSpec(weights.shape, lambda i: (0, 0), pipeline_mode=pl.Buffered(1)),
-        ],
-        out_specs=[
-            pl.BlockSpec((tile, width), lambda i: (i, 0)),
-            pl.BlockSpec((tile, 2 * width), lambda i: (i, 0)),
-        ],
-        out_shape=[
-            jax.ShapeDtypeStruct((tokens, width), BF),
-            jax.ShapeDtypeStruct((tokens, 2 * width), BF),
-        ],
+        grid=(2 * half,),
+        in_specs=[first(D), second(D), first(D), second(D), whole],
+        out_specs=[first(width), second(width), first(2 * width), second(2 * width)],
+        out_shape=[act, act, grad, grad],
         compiler_params=pltpu.CompilerParams(vmem_limit_bytes=VMEM_LIMIT),
         cost_estimate=pl.CostEstimate(
             flops=tokens * D * width, bytes_accessed=tokens * D, transcendentals=0
         ),
         name="feed_forward",
-    )(*rows, grads, weights)
+    )(*rows, *grads, weights)
+    return (out[0], out[1]), (out[2], out[3])
 
 
 def grads_kernel(count, *refs):
@@ -402,8 +427,8 @@
 
     groups = [halves(a) for a in (rows, grads, by_rows, by_grads)]
     count = len(groups[0])
-    tokens = by_rows[0].shape[0] // 2
-    first, second = by_rows[0].shape[1], by_grads[0].shape[1]
+    tokens = groups[0][0][0].shape[0] // (1 if isinstance(rows[0], tuple) else 2)
+    first, second = groups[2][0][0].shape[1], groups[3][0][0].shape[1]
     tile = 512
 
     def tall(half):
@@ -422,7 +447,9 @@
         out_shape=jax.ShapeDtypeStruct((D, first + second), BF),
         compiler_params=pltpu.CompilerParams(vmem_limit_bytes=VMEM_LIMIT),
         cost_estimate=pl.CostEstimate(
-            flops=tokens * D * (first + second), bytes_accessed=tokens * D, transcendentals=0
+            flops=2 * count * tokens * D * (first + second),
+            bytes_accessed=2 * (2 * count * tokens * D + (count * tokens + D) * (first + second)),
+            transcendentals=0,
         ),
         name="weight_grads",
     )(*[a for group in groups for a, _ in group])
@@ -560,8 +587,8 @@
             jnp.concatenate([other, own], axis=axis),
         )
 
-    def exchange_rows(columns_for, *earlier):
-        theirs = swap(tie(columns_for(1 - x_place), *earlier), "x")
+    def exchange_rows(columns_for, send, *earlier):
+        theirs = swap(tie(send, *earlier), "x")
         mine = columns_for(x_place)
         both = jnp.zeros((2 * rows, mine.shape[1]), BF)
         both = lax.dynamic_update_slice_in_dim(both, mine, x_place * rows, axis=0)
@@ -586,7 +613,8 @@
         down = lax.dynamic_slice_in_dim(weight_down, start, width, axis=1).astype(BF)
         return jnp.concatenate([mlp[:, 0], mlp[:, 1], down], axis=1)
 
-    shard_att = exchange_rows(att_columns)
+    send_att = att_columns(1 - x_place)
+    shard_att = exchange_rows(att_columns, send_att)
     full_att = fetch(shard_att)
     full_qkv = full_att[:, : 3 * width_att]
     full_out = full_att[:, 3 * width_att :]
@@ -598,25 +626,24 @@
 
     micros = range(micro_count)
     tokens = 8 * own_tokens
-    token_rows = [inputs[m, 0].reshape(own_tokens, D).astype(F32) for m in micros]
+    token_rows = [
+        tie(inputs[m, 0], send_att).reshape(own_tokens, D).astype(F32) for m in micros
+    ]
     back_low = [cotangent[m, 0].reshape(own_tokens, D) for m in micros]
     normed_att = [rms_norm(t, norm_gains[0]).astype(BF) for t in token_rows]
-    att_pairs = [gather_tokens(normed_att[m], *orders[m]) for m in micros]
+    att_pairs = [gather_tokens(normed_att[m], *orders[m], shard_att) for m in micros]
     att_rows = [jnp.concatenate(pair, axis=0) for pair in att_pairs]
     all_ids = doc_ids[:, 0]
     for axis in ("y", "x", "c"):
         all_ids = jnp.stack([all_ids, swap(all_ids, axis)], axis=0)
 
-    shard_ff = [exchange_rows(functools.partial(ff_columns, 0), *att_rows)]
-    full_ff = [fetch(shard_ff[0])]
-    back_rows = [
-        jnp.concatenate(gather_tokens(tie(back_low[m], *att_rows), *orders[m]), axis=0)
-        for m in micros
-    ]
-    for k in range(1, CHUNKS):
-        shard = exchange_rows(functools.partial(ff_columns, k), shard_ff[-1])
-        shard_ff.append(shard)
-        full_ff.append(fetch(shard))
+    shard_ff = []
+    full_ff = []
+    for k in range(CHUNKS):
+        columns_for = functools.partial(ff_columns, k)
+        earlier = [p[0] for p in att_pairs] if k == 0 else [shard_ff[-1]]
+        shard_ff.append(exchange_rows(columns_for, columns_for(1 - x_place), *earlier))
+        full_ff.append(fetch(shard_ff[-1]))
 
     rel_c = jnp.arange(2)[:, None, None] ^ c_place
     rel_y = jnp.arange(2)[None, :, None] ^ y_place
@@ -641,72 +668,95 @@
     combined = []
     hidden = []
     mlp_rows = []
+    back_states = [
+        gather_start(tie(back_low[m], *[p[0] for p in att_pairs]), *orders[m], shard_ff[0])
+        for m in micros
+    ]
     for m in micros:
-        rows_in = att_rows[m] if m == 0 else tie(att_rows[m], *back_rows, *shard_ff)
+        rows_in = att_rows[m]
+        if m == 0:
+            rows_in = tie(rows_in, *[t for state in back_states for t in state])
         proj = mm(rows_in, full_qkv, NN).astype(BF)
         projected.append(proj.reshape(slots + (3 * width_att,)))
         comb = attention_fwd(projected[m], masks[m], columns[m], gate_rows, wheres[m])
         combined.append(comb.reshape(tokens, width_att))
-        partial = mm(combined[m], full_out, NT).astype(BF)
-        attended = scatter_tokens(partial.reshape(8, own_tokens, D), *orders[m])
-        hidden.append(token_rows[m] + attended)
+    half = tokens // 2
+    back_states = [gather_across(back_states[m], orders[m][0]) for m in micros]
+    back_rows = [gather_core(state) for state in back_states]
+    for m in micros:
+        ready = combined[m]
+        if m > 0:
+            ready = tie(ready, *shard_ff, *[state[-1] for state in back_states])
+        other = mm(ready[half:], full_out, NT).astype(BF)
+        mine = mm(ready[:half], full_out, NT).astype(BF)
+        state = scatter_outer(scatter_core(mine, other, own_tokens), orders[m][0])
+        hidden.append(token_rows[m] + scatter_inner(state, orders[m][1]))
         normed_mlp = rms_norm(hidden[m], norm_gains[1]).astype(BF)
         mlp_rows.append(gather_tokens(normed_mlp, *orders[m]))
 
     def reduce_rows(partial):
         return lax.psum_scatter(partial, "z", scatter_dimension=0, tiled=True)
+
+    def products(left, right, totals, dtype):
+        terms = [mm(left[p], right, NT) for p in (1, 0)][::-1]
+        if totals is not None:
+            terms = [a + b for a, b in zip(totals, terms)]
+        return tuple(t.astype(dtype) for t in terms)
 
     active = []
     d_gate_up = []
     own_ff = []
     d_total = [None] * micro_count
     out_total = [None] * micro_count
+    states = [None] * micro_count
     for k in range(CHUNKS):
         active.append([])
         d_gate_up.append([])
+        last = k == CHUNKS - 1
         for m in micros:
             rows_in = mlp_rows[m]
-            if k == CHUNKS - 1 and m > 0:
-                rows_in = (tie(rows_in[0], d_total[m - 1]), rows_in[1])
+            if last and m > 0:
+                rows_in = (tie(rows_in[0], *d_total[m - 1]), rows_in[1])
             act, grad = feed_forward(rows_in, back_rows[m], full_ff[k])
             active[k].append(act)
             d_gate_up[k].append(grad)
-            d_term = mm(grad, full_ff[k][:, : 2 * width], NT)
-            d_total[m] = d_term if k == 0 else d_total[m] + d_term
-            if k < CHUNKS - 1:
-                out_term = mm(act, full_ff[k][:, 2 * width :], NT)
-                out_total[m] = out_term if k == 0 else out_total[m] + out_term
+            if last and m > 0:
+                grad = (grad[0], tie(grad[1], states[m - 1][1]))
+            dtype = BF if last else F32
+            d_total[m] = products(grad, full_ff[k][:, : 2 * width], d_total[m], dtype)
+            if last:
+                states[m] = scatter_core(*d_total[m], own_tokens)
             else:
-                d_total[m] = d_total[m].astype(BF)
-        if k < CHUNKS - 1:
+                out_total[m] = products(act, full_ff[k][:, 2 * width :], out_total[m], F32)
+        if not last:
             grad_ff = weight_grads(mlp_rows, back_rows, d_gate_up[k], active[k])
             own_ff.append(reduce_rows(grad_ff))
-            full_ff[k + 1] = tie(full_ff[k + 1], grad_ff, *d_total, *out_total)
-    d_partial = [t.reshape(8, own_tokens, D) for t in d_total]
+            terms = [t for pair in d_total + out_total for t in pair]
+            full_ff[k + 1] = tie(full_ff[k + 1], grad_ff, *terms)
+
+    last_active = [(active[-1][m][0], tie(active[-1][m][1], states[-1][1])) for m in micros]
+    grad_ff = weight_grads(mlp_rows, back_rows, d_gate_up[-1], last_active)
+    own_ff.append(reduce_rows(grad_ff))
 
     gain_grad_att = jnp.zeros((D,), F32)
     gain_grad_mlp = jnp.zeros((D,), F32)
     d_hidden = []
     att_grads = []
-    last_active = [tie(active[-1][m], *d_partial) for m in micros]
-    grad_ff = weight_grads(mlp_rows, back_rows, d_gate_up[-1], last_active)
     for m in micros:
-        d_normed = scatter_tokens(d_partial[m], *orders[m], grad_ff)
+        state = tie_send(scatter_outer(states[m], orders[m][0]), grad_ff)
+        d_normed = scatter_inner(state, orders[m][1])
         ignored, norm_back = jax.vjp(rms_norm, hidden[m], norm_gains[1])
         d_norm, d_gain = norm_back(d_normed)
         gain_grad_mlp = gain_grad_mlp + d_gain
         d_hidden.append(back_low[m].astype(F32) + d_norm)
-        d_hidden_low = d_hidden[m].astype(BF)
-        att_grads.append(gather_tokens(d_hidden_low, *orders[m]))
-
-    own_ff.append(reduce_rows(grad_ff))
-    for m in micros:
-        act = tie(last_active[m], d_hidden[m])
-        out_total[m] = out_total[m] + mm(act, full_ff[-1][:, 2 * width :], NT)
+        att_grads.append(gather_tokens(d_hidden[m].astype(BF), *orders[m]))
 
     gate_sum = jnp.zeros((heads,), F32)
     d_projs = []
+    out_states = []
     for m in micros:
+        act = (last_active[m][0], tie(last_active[m][1], d_hidden[m]))
+        out_total[m] = products(act, full_ff[-1][:, 2 * width :], out_total[m], BF)
         other = att_grads[m][1] if m > 0 else tie(att_grads[m][1], own_ff[0])
         d_combined = jnp.concatenate(
             [mm(att_grads[m][0], full_out, NN), mm(other, full_out, NN)], axis=0
@@ -721,49 +771,59 @@
         )
         gate_sum = gate_sum + jnp.sum(gate_part, axis=(0, 2))
         d_projs.append(d_proj.reshape(tokens, 3 * width_att))
+    for m in micros:
+        mine, other = out_total[m]
+        other = tie(other, *[pair[1] for pair in att_grads])
+        out_states.append(tie_send(scatter_core(mine, other, own_tokens), d_projs[0]))
     grad_att = weight_grads(att_rows, att_grads, d_projs, combined)
     own_att = reduce_rows(grad_att)
 
+    def exchange_grad(grad):
+        mine = lax.dynamic_slice_in_dim(grad, x_place * rows, rows, axis=0)
+        theirs = swap(lax.dynamic_slice_in_dim(grad, (1 - x_place) * rows, rows, axis=0), "x")
+        return mine, theirs
+
+    def squares_of(grad):
+        wide = grad.astype(F32)
+        return jnp.sum(wide * wide)
+
+    pairs = [exchange_grad(g) for g in own_ff]
+
+    def ff_part(start, stop):
+        low = jnp.concatenate([p[0][:, start * width : stop * width] for p in pairs], axis=1)
+        high = jnp.concatenate([p[1][:, start * width : stop * width] for p in pairs], axis=1)
+        return by_place(low, high, 1)
+
+    grad_mlp = mlp_view(jnp.stack([ff_part(0, 1), ff_part(1, 2)], axis=1))
+    grad_down = ff_part(2, 3)
+    ff_owned = sum(squares_of(g) for g in own_ff)
+
     grad_rows = []
+    block_out = []
+    in_states = []
     for m in micros:
-        partial = mm(tie(d_projs[m], grad_att), full_qkv, NT).astype(BF)
-        d_normed = scatter_tokens(partial.reshape(8, own_tokens, D), *orders[m], own_ff[-1])
+        d_proj = tie(d_projs[m], grad_att)
+        other = mm(d_proj[half:], full_qkv, NT).astype(BF)
+        mine = mm(d_proj[:half], full_qkv, NT).astype(BF)
+        in_states.append(scatter_core(mine, other, own_tokens))
+    for m in micros:
+        state = tie_send(scatter_outer(in_states[m], orders[m][0]), own_ff[-1])
+        d_normed = scatter_inner(state, orders[m][1])
         ignored, norm_first = jax.vjp(rms_norm, token_rows[m], norm_gains[0])
         d_norm, d_gain = norm_first(d_normed)
         gain_grad_att = gain_grad_att + d_gain
         grad_rows.append((d_hidden[m] + d_norm).astype(BF))
-
-    block_out = []
     for m in micros:
-        partial = tie(out_total[m].astype(BF), *[pair[1] for pair in att_grads])
-        mlp_out = scatter_tokens(partial.reshape(8, own_tokens, D), *orders[m])
-        block_out.append((hidden[m] + mlp_out).astype(BF))
-
-    def exchange_grad(grad):
-        mine = lax.dynamic_slice_in_dim(grad, x_place * rows, rows, axis=0)
-        theirs = swap(lax.dynamic_slice_in_dim(grad, (1 - x_place) * rows, rows, axis=0), "x")
-        return mine, theirs
-
-    def squares_of(grad):
-        wide = grad.astype(F32)
-        return jnp.sum(wide * wide)
-
-    pairs = [exchange_grad(g) for g in own_ff]
-
-    def ff_part(start, stop):
-        low = jnp.concatenate([p[0][:, start * width : stop * width] for p in pairs], axis=1)
-        high = jnp.concatenate([p[1][:, start * width : stop * width] for p in pairs], axis=1)
-        return by_place(low, high, 1)
-
-    grad_mlp = mlp_view(jnp.stack([ff_part(0, 1), ff_part(1, 2)], axis=1))
-    grad_down = ff_part(2, 3)
+        state = tie_send(scatter_outer(out_states[m], orders[m][0]), in_states[-1][1])
+        block_out.append((hidden[m] + scatter_inner(state, orders[m][1])).astype(BF))
+
     att_mine, att_theirs = exchange_grad(own_att)
 
     gate_grad = gate_sum * mixing * (1.0 - mixing)
     gate_padded = lax.dynamic_update_slice(
         jnp.zeros(gate_logit.shape, F32), gate_grad, (head_start,)
     )
-    ff_owned = tie(sum(squares_of(g) for g in own_ff), grad_mlp, grad_down)
+    ff_owned = tie(ff_owned, grad_mlp, grad_down)
     owned = squares_of(own_att) + ff_owned
     small = jnp.concatenate(
         [gain_grad_att, gain_grad_mlp, gate_padded, owned[None], jnp.zeros((111,), F32)]

time: 814 us -> 809 us (level)
  local copies, waits for them, and re-layouts: 114 us -> 87.4 us
  matrix products: 91.7 us -> 108 us
  waiting for transfers between devices: 289 us -> 274 us
  starting transfers between devices: 60.9 us -> 70.5 us
    convert_element_type x3 -> x16, other arithmetic: 2.76 us -> 29.5 us  [the longest x5 15.6 us: scatter_core(): send = (mine[2:].astype(F32) + came[2:].astype(F32)).astype(BF)]
    slice x16 -> x1, local copies, waits for them, and re-layouts: 21.6 us -> 0.04 us  [on_device(): mine = mm(ready[:half], full_out, NT).astype(BF)]
    dot_general x18 -> x30, matrix products: 91.7 us -> 108 us  [mm(): return lax.dot_general(a, b, (dims, ((), ())), preferred_element_type=F32)]
    ppermute x68, waiting for transfers between devices: 286 us -> 272 us  [swap(): return lax.ppermute(tensor, axis, [(0, 1), (1, 0)])]
    add x16 -> x3, other arithmetic: 22.7 us -> 9.79 us  [scatter_core(): return (mine[:2].astype(F32) + came[:2].astype(F32), send)]
    ppermute x68, starting transfers between devices: 57 us -> 65.5 us  [swap(): return lax.ppermute(tensor, axis, [(0, 1), (1, 0)])]
    unnamed x262 -> x306, local copies, waits for them, and re-layouts: 44 us -> 38.3 us
  transfers between devices with their start and end apart: 76 -> 76, of which waited for: 40 -> 37; matrix products, arithmetic and copies ran while one was open for 30% -> 31% of each run, Pallas kernels for 17% -> 17%
where the time goes in v3:
time: 809 us; the launch traced here: 803 us
  waiting for transfers between devices  274 us (34%)
  Pallas kernels  162 us (20%)
  matrix products  108 us (13%)
  local copies, waits for them, and re-layouts  87.4 us (11%)
  other arithmetic  79.9 us (10%)
  starting transfers between devices  70.5 us (9%)
  between operations  20.2 us (2%)
    ppermute x68, waiting for transfers between devices, swap(): return lax.ppermute(tensor, axis, [(0, 1), (1, 0)])  272 us
    dot_general x30, matrix products, mm(): return lax.dot_general(a, b, (dims, ((), ())), preferred_element_type=F32)  108 us
    ppermute x68, starting transfers between devices, swap(): return lax.ppermute(tensor, axis, [(0, 1), (1, 0)])  65.5 us
    pallas_call x4, Pallas kernels, feed_forward(): pl.pallas_call(functools.partial(ff_kernel, width, half), grid=(2 * half,...  50.8 us
    pallas_call x3, Pallas kernels, weight_grads(): pl.pallas_call(functools.partial(grads_kernel, count), grid=(D // tile,),...  49.6 us
    unnamed x306, local copies, waits for them, and re-layouts  38.3 us
    pallas_call x2, Pallas kernels, attention_bwd(): pl.pallas_call(functools.partial(attention_bwd_kernel, heads), grid=(seqs...  24.9 us
    pallas_call x1, Pallas kernels, adam_all(): pl.pallas_call(adam_kernel, grid=(steps,), in_specs=[pl.BlockSpec(memory_...  23.5 us
  transfers between devices with their start and end apart: 76, of which 37 were waited for; matrix products, arithmetic and copies ran while one was open for 31% of the time, Pallas kernels for 17%

profile of v3, /device:TPU:0, one launch (start us, length us, event | category | flops | bytes accessed | tf_op | source)
XLA Modules:
  0.0 802.9 jit_solution(16009552071245666534)
XLA Ops:
  12.6 11.5 %collective-permute-done.1 = bf16[256,1024]{0,1:T(8,128)(2,1)S(1)} collective-permute-done((bf16[256,1024]{0,1:T(8,128)(2,1)S(1)}, bf16[256,1024]{0,1:T(8,128)(2,1)S(1)}, u32[]{:S(2)}, u32[]{:S(2)}) %collective-permute-start.1) | collective-permute-done | bytes 524320 | tf_op jit(solution)/shard_map/ppermute | solution.py:48
  49.9 8.6 %collective-permute-done.2 = bf16[128,2048]{1,0:T(8,128)(2,1)} collective-permute-done((bf16[128,2048]{1,0:T(8,128)(2,1)S(1)}, bf16[128,2048]{1,0:T(8,128)(2,1)}, u32[]{:S(2)}, u32[]{:S(2)}) %collective-permute-start.2) | collective-permute-done | bytes 524320 | tf_op jit(solution)/shard_map/ppermute | solution.py:48
  58.5 8.3 %collective-permute-done.3 = bf16[128,2048]{1,0:T(8,128)(2,1)} collective-permute-done((bf16[128,2048]{1,0:T(8,128)(2,1)}, bf16[128,2048]{1,0:T(8,128)(2,1)}, u32[]{:S(2)}, u32[]{:S(2)}) %collective-permute-start.3) | collective-permute-done | bytes 524320 | tf_op jit(solution)/shard_map/ppermute | solution.py:48
  75.4 14.0 %collective-permute-done.9 = bf16[256,1536]{1,0:T(8,128)(2,1)S(1)} collective-permute-done((bf16[256,1536]{1,0:T(8,128)(2,1)S(1)}, bf16[256,1536]{1,0:T(8,128)(2,1)S(1)}, u32[]{:S(2)}, u32[]{:S(2)}) %collective-permute-start.9) | collective-permute-done | bytes 786464 | tf_op jit(solution)/shard_map/ppermute | solution.py:48
  136.0 9.4 %collective-permute-done.11 = bf16[128,2048]{1,0:T(8,128)(2,1)} collective-permute-done((bf16[128,2048]{1,0:T(8,128)(2,1)S(1)}, bf16[128,2048]{1,0:T(8,128)(2,1)}, u32[]{:S(2)}, u32[]{:S(2)}) %collective-permute-start.11) | collective-permute-done | bytes 524320 | tf_op jit(solution)/shard_map/ppermute | solution.py:48
  146.6 10.0 %collective-permute-done.10 = bf16[128,2048]{1,0:T(8,128)(2,1)S(1)} collective-permute-done((bf16[128,2048]{1,0:T(8,128)(2,1)S(1)}, bf16[128,2048]{1,0:T(8,128)(2,1)S(1)}, u32[]{:S(2)}, u32[]{:S(2)}) %collective-permute-start.10) | collective-permute-done | bytes 524320 | tf_op jit(solution)/shard_map/ppermute | solution.py:48
  161.4 6.6 convolution_convert_fusion.9
  168.1 6.8 attention_forward.2
  182.7 6.6 attention_forward.3
  203.6 18.0 %collective-permute-done.17 = bf16[2,128,2048]{2,1,0:T(8,128)(2,1)S(1)} collective-permute-done((bf16[2,128,2048]{2,1,0:T(8,128)(2,1)S(1)}, bf16[2,128,2048]{2,1,0:T(8,128)(2,1)S(1)}, u32[]{:S(2)}, u32[]{:S(2)}) %collective-permute-start.17) | collective-permute-done | bytes 1048608 | tf_op jit(solution)/shard_map/ppermute | solution.py:48
  229.2 8.9 %collective-permute-done.18 = bf16[128,2048]{1,0:T(8,128)(2,1)S(1)} collective-permute-done((bf16[128,2048]{1,0:T(8,128)(2,1)S(1)}, bf16[128,2048]{1,0:T(8,128)(2,1)S(1)}, u32[]{:S(2)}, u32[]{:S(2)}) %collective-permute-start.18) | collective-permute-done | bytes 524320 | tf_op jit(solution)/shard_map/ppermute | solution.py:48
  260.4 8.9 %collective-permute-done.32 = bf16[128,2048]{1,0:T(8,128)(2,1)S(1)} collective-permute-done((bf16[128,2048]{1,0:T(8,128)(2,1)S(1)}, bf16[128,2048]{1,0:T(8,128)(2,1)S(1)}, u32[]{:S(2)}, u32[]{:S(2)}) %collective-permute-start.32) | collective-permute-done | bytes 524320 | tf_op jit(solution)/shard_map/ppermute | solution.py:48
  269.3 7.8 collective-permute-done.33
  281.7 12.7 %feed_forward.5 = (bf16[512,512]{1,0:T(8,128)(2,1)S(1)}, bf16[512,512]{1,0:T(8,128)(2,1)S(1)}, bf16[512,1024]{1,0:T(8,128)(2,1)S(1)}, bf16[512,1024]{1,0:T(8,128)(2,1)S(1)}) custom-call(bf16[512,2048]{1,0:T(8,128)(2,1)S(1)} %pad_maximum_fusion.3.x_mine.refs_2_, bf16[512,2048]{1,0:T(8,128)(2,1)} %collective-permute-done.34.x_other.refs_3_, ...), custom_call_target="tpu_custom_call" | custom-call | flops 536870912 | bytes 1048576 | tf_op jit(solution)/shard_map/feed_forward/pallas_call | solution.py:390
  295.4 12.8 %feed_forward.4 = (bf16[512,512]{1,0:T(8,128)(2,1)S(1)}, bf16[512,512]{1,0:T(8,128)(2,1)S(1)}, bf16[512,1024]{1,0:T(8,128)(2,1)S(1)}, bf16[512,1024]{1,0:T(8,128)(2,1)S(1)}) custom-call(bf16[512,2048]{1,0:T(8,128)(2,1)} %pad_maximum_fusion.2.x_mine.refs_0_, bf16[512,2048]{1,0:T(8,128)(2,1)} %collective-permute-done.22.x_other.refs_1_, ...), custom_call_target="tpu_custom_call" | custom-call | flops 536870912 | bytes 1048576 | tf_op jit(solution)/shard_map/feed_forward/pallas_call | solution.py:390
  308.3 18.1 %weight_grads.3 = bf16[2048,1536]{1,0:T(8,128)(2,1)} custom-call(bf16[512,2048]{1,0:T(8,128)(2,1)} %pad_maximum_fusion.2.x_mine.refs_0_, bf16[512,2048]{1,0:T(8,128)(2,1)} %collective-permute-done.22.x_other.refs_1_, bf16[512,2048]{1,0:T(8,128)(2,1)} %copy-done, bf16[512,2048]{1,0:T(8,128)(2,1)} %collective-permute-done.34.x_other.refs_3_, ...), custom_call_target="tpu_custom_call" | custom-call | flops 12884901888 | bytes 29360128 | tf_op jit(solution)/shard_map/weight_grads/pallas_call | solution.py:440
  363.9 12.6 %feed_forward.6 = (bf16[512,512]{1,0:T(8,128)(2,1)S(1)}, bf16[512,512]{1,0:T(8,128)(2,1)S(1)}, bf16[512,1024]{1,0:T(8,128)(2,1)S(1)}, bf16[512,1024]{1,0:T(8,128)(2,1)S(1)}) custom-call(bf16[512,2048]{1,0:T(8,128)(2,1)} %pad_maximum_fusion.2.x_mine.refs_0_, bf16[512,2048]{1,0:T(8,128)(2,1)} %collective-permute-done.22.x_other.refs_1_, ...), custom_call_target="tpu_custom_call" | custom-call | flops 536870912 | bytes 1048576 | tf_op jit(solution)/shard_map/feed_forward/pallas_call | solution.py:390
  376.6 6.0 add_convert_fusion.5
  386.4 12.6 %feed_forward.7 = (bf16[512,512]{1,0:T(8,128)(2,1)S(1)}, bf16[512,512]{1,0:T(8,128)(2,1)S(1)}, bf16[512,1024]{1,0:T(8,128)(2,1)S(1)}, bf16[512,1024]{1,0:T(8,128)(2,1)S(1)}) custom-call(bf16[512,2048]{1,0:T(8,128)(2,1)S(1)} %copy-done.1, bf16[512,2048]{1,0:T(8,128)(2,1)} %collective-permute-done.34.x_other.refs_3_, bf16[512,2048]{1,0:T(8,128)(2,1)} %copy-done.55, ...), custom_call_target="tpu_custom_call" | custom-call | flops 536870912 | bytes 1048576 | tf_op jit(solution)/shard_map/feed_forward/pallas_call | solution.py:390
  415.7 18.1 %weight_grads.4 = bf16[2048,1536]{1,0:T(8,128)(2,1)} custom-call(bf16[512,2048]{1,0:T(8,128)(2,1)} %pad_maximum_fusion.2.x_mine.refs_0_, bf16[512,2048]{1,0:T(8,128)(2,1)} %collective-permute-done.22.x_other.refs_1_, bf16[512,2048]{1,0:T(8,128)(2,1)} %copy-done, bf16[512,2048]{1,0:T(8,128)(2,1)} %collective-permute-done.34.x_other.refs_3_, ...), custom_call_target="tpu_custom_call" | custom-call | flops 12884901888 | bytes 29360128 | tf_op jit(solution)/shard_map/weight_grads/pallas_call | solution.py:440
  439.9 20.3 %collective-permute-done.44 = bf16[2,128,2048]{2,1,0:T(8,128)(2,1)S(1)} collective-permute-done((bf16[2,128,2048]{2,1,0:T(8,128)(2,1)}, bf16[2,128,2048]{2,1,0:T(8,128)(2,1)S(1)}, u32[]{:S(2)}, u32[]{:S(2)}) %collective-permute-start.44) | collective-permute-done | bytes 1048608 | tf_op jit(solution)/shard_map/ppermute | solution.py:48
  462.9 8.0 collective-permute-done.39
  483.7 9.3 %collective-permute-done.46 = bf16[128,2048]{1,0:T(8,128)(2,1)S(1)} collective-permute-done((bf16[128,2048]{1,0:T(8,128)(2,1)S(1)}, bf16[128,2048]{1,0:T(8,128)(2,1)S(1)}, u32[]{:S(2)}, u32[]{:S(2)}) %collective-permute-start.46) | collective-permute-done | bytes 524320 | tf_op jit(solution)/shard_map/ppermute | solution.py:48
  497.7 10.1 %collective-permute-done.47 = bf16[128,2048]{1,0:T(8,128)(2,1)S(1)} collective-permute-done((bf16[128,2048]{1,0:T(8,128)(2,1)S(1)}, bf16[128,2048]{1,0:T(8,128)(2,1)S(1)}, u32[]{:S(2)}, u32[]{:S(2)}) %collective-permute-start.47) | collective-permute-done | bytes 524320 | tf_op jit(solution)/shard_map/ppermute | solution.py:48
  507.7 8.0 %collective-permute-done.48 = bf16[128,2048]{1,0:T(8,128)(2,1)S(1)} collective-permute-done((bf16[128,2048]{1,0:T(8,128)(2,1)S(1)}, bf16[128,2048]{1,0:T(8,128)(2,1)S(1)}, u32[]{:S(2)}, u32[]{:S(2)}) %collective-permute-start.48) | collective-permute-done | bytes 524320 | tf_op jit(solution)/shard_map/ppermute | solution.py:48
  542.1 12.5 %attention_backward.3 = (bf16[2,2,2,4,32,768]{5,4,3,2,1,0:T(8,128)(2,1)S(1)}, f32[2,2,128]{2,1,0:T(2,128)S(1)}) custom-call(bf16[2,2,2,4,32,768]{5,4,3,2,1,0:T(8,128)(2,1)S(1)} %bitcast.451, f32[2,2,2,4,32,256]{5,4,3,2,1,0:T(8,128)S(1)} %bitcast.453, f32[2,4,128,128]{3,2,1,0:T(8,128)S(1)} %copy-done.12, f32[2,4,128,3]{3,2,1,0:T(8,128)S(1)} %add_convert_fusion.17.cols_ref, ...), custom_call_target="tpu_custom_call" | custom-call | flops 1000000000 | bytes 5000000 | tf_op jit(solution)/shard_map/attention_backward/pallas_call | solution.py:317
  567.5 12.3 %attention_backward.2 = (bf16[2,2,2,4,32,768]{5,4,3,2,1,0:T(8,128)(2,1)S(1)}, f32[2,2,128]{2,1,0:T(2,128)S(1)}) custom-call(bf16[2,2,2,4,32,768]{5,4,3,2,1,0:T(8,128)(2,1)S(1)} %bitcast.449, f32[2,2,2,4,32,256]{5,4,3,2,1,0:T(8,128)S(1)} %bitcast.452, f32[2,4,128,128]{3,2,1,0:T(8,128)S(1)} %copy-done.10, f32[2,4,128,3]{3,2,1,0:T(8,128)S(1)} %copy-done.8, ...), custom_call_target="tpu_custom_call" | custom-call | flops 1000000000 | bytes 5000000 | tf_op jit(solution)/shard_map/attention_backward/pallas_call | solution.py:317
  579.9 13.4 %weight_grads.5 = bf16[2048,1024]{1,0:T(8,128)(2,1)} custom-call(bf16[1024,2048]{1,0:T(8,128)(2,1)} %constant_dynamic-update-slice_fusion.refs_0_.refs_1_, bf16[1024,2048]{1,0:T(8,128)(2,1)} %constant_dynamic-update-slice_fusion.refs_0_.refs_1_, bf16[1024,2048]{1,0:T(8,128)(2,1)} %constant_dynamic-update-slice_fusion.9.refs_2_.refs_3_, ...), custom_call_target="tpu_custom_call" | custom-call | flops 8589934592 | bytes 25165824 | tf_op jit(solution)/shard_map/weight_grads/pallas_call | solution.py:440
  622.1 17.0 %collective-permute-done.51 = bf16[2,128,2048]{2,1,0:T(8,128)(2,1)} collective-permute-done((bf16[2,128,2048]{2,1,0:T(8,128)(2,1)}, bf16[2,128,2048]{2,1,0:T(8,128)(2,1)}, u32[]{:S(2)}, u32[]{:S(2)}) %collective-permute-start.51) | collective-permute-done | bytes 1048608 | tf_op jit(solution)/shard_map/ppermute | solution.py:48
  650.6 29.6 %collective-permute-done.53 = bf16[128,2048]{1,0:T(8,128)(2,1)S(1)} collective-permute-done((bf16[128,2048]{1,0:T(8,128)(2,1)S(1)}, bf16[128,2048]{1,0:T(8,128)(2,1)S(1)}, u32[]{:S(2)}, u32[]{:S(2)}) %collective-permute-start.53) | collective-permute-done | bytes 524320 | tf_op jit(solution)/shard_map/ppermute | solution.py:48
  702.4 17.3 %collective-permute-done.61 = bf16[128,2048]{1,0:T(8,128)(2,1)S(1)} collective-permute-done((bf16[128,2048]{1,0:T(8,128)(2,1)}, bf16[128,2048]{1,0:T(8,128)(2,1)S(1)}, u32[]{:S(2)}, u32[]{:S(2)}) %collective-permute-start.61) | collective-permute-done | bytes 524320 | tf_op jit(solution)/shard_map/ppermute | solution.py:48
  771.2 23.5 %adam.1 = (f32[3,256,512]{2,1,0:T(8,128)}, f32[3,256,512]{2,1,0:T(8,128)}, f32[3,256,512]{2,1,0:T(8,128)}, f32[256,512]{1,0:T(8,128)}, f32[256,512]{1,0:T(8,128)...) custom-call(s32[1]{0:T(128)} %bitcast.89.place_ref, ...), custom_call_target="tpu_custom_call" | custom-call | flops 41943040 | bytes 50331648 | tf_op jit(solution)/shard_map/adam/pallas_call | solution.py:522
  (621 shorter events, 382.7 us)
Async XLA Ops:
  7.2 154.2 %all-gather.4.cloned.1.call-start = ((), (), s32[]{:S(2)}) async-start(), calls=%async_computation.3 | async-start | bytes 5242880 | tf_op jit(solution)/shard_map/all_gather | solution.py:598
  25.1 254.4 %all-gather.6.cloned.1.call-start = ((), (), s32[]{:S(2)}) async-start(), calls=%async_computation.4 | async-start | bytes 7864320 | tf_op jit(solution)/shard_map/all_gather | solution.py:598
  30.3 39.5 %collective-permute-start.6 = (bf16[128,2048]{1,0:T(8,128)(2,1)S(1)}, bf16[128,2048]{1,0:T(8,128)(2,1)S(1)}, u32[]{:S(2)}, u32[]{:S(2)}) collective-permute-start(bf16[128,2048]{1,0:T(8,128)(2,1)S(1)} %get-tuple-element.90), channel_id=1, source_target_pairs={{0,2},{2,0},{1,3},{3,1},{4,6},{6,4},{5,7},{7,5},{8,10},{10,8},{9,1... | collective-permute-start | bytes 1572872 | tf_op jit(solution)/shard_map/ppermute | solution.py:48
  30.6 67.9 %collective-permute-start.13 = (s32[2,4,32]{2,1,0:T(4,128)S(1)}, s32[2,4,32]{2,1,0:T(4,128)S(1)}, u32[]{:S(2)}, u32[]{:S(2)}) collective-permute-start(s32[2,4,32]{2,1,0:T(4,128)S(1)} %bitcast.497), channel_id=1, source_target_pairs={{0,2},{2,0},{1,3},{3,1},{4,6},{6,4},{5,7},{7,5},{8,10},{10,8},{9,1... | collective-permute-start | bytes 3080 | tf_op jit(solution)/shard_map/ppermute | solution.py:48
  90.6 273.3 %all-gather.8.cloned.1.call-start = ((), (), s32[]{:S(2)}) async-start(), calls=%async_computation.5 | async-start | bytes 7864320 | tf_op jit(solution)/shard_map/all_gather | solution.py:598
  105.9 52.4 %collective-permute-start.26 = (bf16[512,2048]{1,0:T(8,128)(2,1)}, bf16[512,2048]{1,0:T(8,128)(2,1)}, u32[]{:S(2)}, u32[]{:S(2)}) collective-permute-start(bf16[512,2048]{1,0:T(8,128)(2,1)} %pad_maximum_fusion.1), channel_id=1, source_target_pairs={{0,1},{1,0},{2,3},{3,2},{4,5},{5,4},{6,7},{7,6},{8,9},{9,8},{10,11... | collective-permute-start | bytes 6291464 | tf_op jit(solution)/shard_map/ppermute | solution.py:48
  113.7 42.9 %collective-permute-start.25 = (bf16[256,1536]{1,0:T(8,128)(2,1)S(1)}, bf16[256,1536]{1,0:T(8,128)(2,1)S(1)}, u32[]{:S(2)}, u32[]{:S(2)}) collective-permute-start(bf16[256,1536]{1,0:T(8,128)(2,1)S(1)} %copy-done.99), channel_id=1, source_target_pairs={{0,4},{4,0},{1,5},{5,1},{2,6},{6,2},{3,7},{7,3},{8,12},{12,8},{9,1... | collective-permute-start | bytes 2359304 | tf_op jit(solution)/shard_map/ppermute | solution.py:48
  125.3 31.3 %collective-permute-start.10 = (bf16[128,2048]{1,0:T(8,128)(2,1)S(1)}, bf16[128,2048]{1,0:T(8,128)(2,1)S(1)}, u32[]{:S(2)}, u32[]{:S(2)}) collective-permute-start(bf16[128,2048]{1,0:T(8,128)(2,1)S(1)} %bitcast.465), channel_id=1, source_target_pairs={{0,4},{4,0},{1,5},{5,1},{2,6},{6,2},{3,7},{7,3},{8,12},{12,8},{9,1... | collective-permute-start | bytes 1572872 | tf_op jit(solution)/shard_map/ppermute | solution.py:48
  134.6 54.8 %collective-permute-start.23 = (bf16[128,2048]{1,0:T(8,128)(2,1)}, bf16[128,2048]{1,0:T(8,128)(2,1)}, u32[]{:S(2)}, u32[]{:S(2)}) collective-permute-start(bf16[128,2048]{1,0:T(8,128)(2,1)} %collective-permute-done.8), channel_id=1, source_target_pairs={{0,4},{4,0},{1,5},{5,1},{2,6},{6,2},{3,7},{7,3},{8,12},{12,8},{9,1... | collective-permute-start | bytes 1572872 | tf_op jit(solution)/shard_map/ppermute | solution.py:48
  145.4 43.9 %collective-permute-start.27 = (bf16[128,2048]{1,0:T(8,128)(2,1)}, bf16[128,2048]{1,0:T(8,128)(2,1)}, u32[]{:S(2)}, u32[]{:S(2)}) collective-permute-start(bf16[128,2048]{1,0:T(8,128)(2,1)} %collective-permute-done.11), channel_id=1, source_target_pairs={{0,2},{2,0},{1,3},{3,1},{4,6},{6,4},{5,7},{7,5},{8,10},{10,8},{9,1... | collective-permute-start | bytes 1572872 | tf_op jit(solution)/shard_map/ppermute | solution.py:48
  191.9 371.7 %reduce-scatter.4.cloned.1.call-start = ((), (), s32[]{:S(2)}) async-start(), calls=%async_computation.6 | async-start | bytes 7864320 | tf_op jit(solution)/shard_map/reduce_scatter | solution.py:698
  196.4 25.1 %collective-permute-start.17 = (bf16[2,128,2048]{2,1,0:T(8,128)(2,1)S(1)}, bf16[2,128,2048]{2,1,0:T(8,128)(2,1)S(1)}, u32[]{:S(2)}, u32[]{:S(2)}) collective-permute-start(bf16[2,128,2048]{2,1,0:T(8,128)(2,1)S(1)} %bitcast.480), channel_id=1, source_target_pairs={{0,4},{4,0},{1,5},{5,1},{2,6},{6,2},{3,7},{7,3},{8,12},{12,8},{9,1... | collective-permute-start | bytes 3145736 | tf_op jit(solution)/shard_map/ppermute | solution.py:48
  201.9 26.1 %collective-permute-start.29 = (bf16[2,128,2048]{2,1,0:T(8,128)(2,1)S(1)}, bf16[2,128,2048]{2,1,0:T(8,128)(2,1)S(1)}, u32[]{:S(2)}, u32[]{:S(2)}) collective-permute-start(bf16[2,128,2048]{2,1,0:T(8,128)(2,1)S(1)} %bitcast.481), channel_id=1, source_target_pairs={{0,2},{2,0},{1,3},{3,1},{4,6},{6,4},{5,7},{7,5},{8,10},{10,8},{9,1... | collective-permute-start | bytes 3145736 | tf_op jit(solution)/shard_map/ppermute | solution.py:48
  247.2 48.2 %collective-permute-start.24 = (bf16[512,2048]{1,0:T(8,128)(2,1)}, bf16[512,2048]{1,0:T(8,128)(2,1)}, u32[]{:S(2)}, u32[]{:S(2)}) collective-permute-start(bf16[512,2048]{1,0:T(8,128)(2,1)} %constant_dynamic-update-slice_fusion.5.g_mine.refs_4_), channel_id=1, source_target_pairs={{0,1},{1,0},{2,3},{3,2},{4,5},{5,4},{6,7},{7,6},{8,9},{9,8},{10,11... | collective-permute-start | bytes 6291464 | tf_op jit(solution)/shard_map/ppermute | solution.py:48
  328.4 360.0 %reduce-scatter.6.cloned.1.call-start = ((), (), s32[]{:S(2)}) async-start(), calls=%async_computation.7 | async-start | bytes 7864320 | tf_op jit(solution)/shard_map/reduce_scatter | solution.py:698
  411.9 25.5 %collective-permute-start.38 = (bf16[2,128,2048]{2,1,0:T(8,128)(2,1)}, bf16[2,128,2048]{2,1,0:T(8,128)(2,1)}, u32[]{:S(2)}, u32[]{:S(2)}) collective-permute-start(bf16[2,128,2048]{2,1,0:T(8,128)(2,1)} %bitcast.46), channel_id=1, source_target_pairs={{0,4},{4,0},{1,5},{5,1},{2,6},{6,2},{3,7},{7,3},{8,12},{12,8},{9,1... | collective-permute-start | bytes 3145736 | tf_op jit(solution)/shard_map/ppermute | solution.py:48
  433.8 304.0 %reduce-scatter.8.cloned.1.call-start = ((), (), s32[]{:S(2)}) async-start(), calls=%async_computation.8 | async-start | bytes 5242880 | tf_op jit(solution)/shard_map/reduce_scatter | solution.py:698
  434.0 26.3 %collective-permute-start.44 = (bf16[2,128,2048]{2,1,0:T(8,128)(2,1)}, bf16[2,128,2048]{2,1,0:T(8,128)(2,1)S(1)}, u32[]{:S(2)}, u32[]{:S(2)}) collective-permute-start(bf16[2,128,2048]{2,1,0:T(8,128)(2,1)} %bitcast.478), channel_id=1, source_target_pairs={{0,2},{2,0},{1,3},{3,1},{4,6},{6,4},{5,7},{7,5},{8,10},{10,8},{9,1... | collective-permute-start | bytes 3145736 | tf_op jit(solution)/shard_map/ppermute | solution.py:48
  439.0 32.0 %collective-permute-start.39 = (bf16[128,2048]{1,0:T(8,128)(2,1)S(1)}, bf16[128,2048]{1,0:T(8,128)(2,1)S(1)}, u32[]{:S(2)}, u32[]{:S(2)}) collective-permute-start(bf16[128,2048]{1,0:T(8,128)(2,1)S(1)} %fusion.100), channel_id=1, source_target_pairs={{0,2},{2,0},{1,3},{3,1},{4,6},{6,4},{5,7},{7,5},{8,10},{10,8},{9,1... | collective-permute-start | bytes 1572872 | tf_op jit(solution)/shard_map/ppermute | solution.py:48
  529.7 25.1 %collective-permute-start.50 = (bf16[512,2048]{1,0:T(8,128)(2,1)}, bf16[512,2048]{1,0:T(8,128)(2,1)}, u32[]{:S(2)}, u32[]{:S(2)}) collective-permute-start(bf16[512,2048]{1,0:T(8,128)(2,1)} %add_convert_fusion.2), channel_id=1, source_target_pairs={{0,1},{1,0},{2,3},{3,2},{4,5},{5,4},{6,7},{7,6},{8,9},{9,8},{10,11... | collective-permute-start | bytes 6291464 | tf_op jit(solution)/shard_map/ppermute | solution.py:48
  532.5 27.2 %collective-permute-start.54 = (bf16[512,2048]{1,0:T(8,128)(2,1)}, bf16[512,2048]{1,0:T(8,128)(2,1)}, u32[]{:S(2)}, u32[]{:S(2)}) collective-permute-start(bf16[512,2048]{1,0:T(8,128)(2,1)} %add_convert_fusion), channel_id=1, source_target_pairs={{0,1},{1,0},{2,3},{3,2},{4,5},{5,4},{6,7},{7,6},{8,9},{9,8},{10,11... | collective-permute-start | bytes 6291464 | tf_op jit(solution)/shard_map/ppermute | solution.py:48
  603.1 38.6 %collective-permute-start.52 = (bf16[512,2048]{1,0:T(8,128)(2,1)}, bf16[512,2048]{1,0:T(8,128)(2,1)}, u32[]{:S(2)}, u32[]{:S(2)}) collective-permute-start(bf16[512,2048]{1,0:T(8,128)(2,1)} %convolution_convert_fusion.6), channel_id=1, source_target_pairs={{0,1},{1,0},{2,3},{3,2},{4,5},{5,4},{6,7},{7,6},{8,9},{9,8},{10,11... | collective-permute-start | bytes 6291464 | tf_op jit(solution)/shard_map/ppermute | solution.py:48
  606.5 39.8 %collective-permute-start.57 = (bf16[512,2048]{1,0:T(8,128)(2,1)}, bf16[512,2048]{1,0:T(8,128)(2,1)}, u32[]{:S(2)}, u32[]{:S(2)}) collective-permute-start(bf16[512,2048]{1,0:T(8,128)(2,1)} %convolution_convert_fusion.4), channel_id=1, source_target_pairs={{0,1},{1,0},{2,3},{3,2},{4,5},{5,4},{6,7},{7,6},{8,9},{9,8},{10,11... | collective-permute-start | bytes 6291464 | tf_op jit(solution)/shard_map/ppermute | solution.py:48
  606.8 32.4 %collective-permute-start.51 = (bf16[2,128,2048]{2,1,0:T(8,128)(2,1)}, bf16[2,128,2048]{2,1,0:T(8,128)(2,1)}, u32[]{:S(2)}, u32[]{:S(2)}) collective-permute-start(bf16[2,128,2048]{2,1,0:T(8,128)(2,1)} %bitcast.57), channel_id=1, source_target_pairs={{0,4},{4,0},{1,5},{5,1},{2,6},{6,2},{3,7},{7,3},{8,12},{12,8},{9,1... | collective-permute-start | bytes 3145736 | tf_op jit(solution)/shard_map/ppermute | solution.py:48
  607.4 33.1 %collective-permute-start.55 = (bf16[2,128,2048]{2,1,0:T(8,128)(2,1)}, bf16[2,128,2048]{2,1,0:T(8,128)(2,1)}, u32[]{:S(2)}, u32[]{:S(2)}) collective-permute-start(bf16[2,128,2048]{2,1,0:T(8,128)(2,1)} %bitcast.69), channel_id=1, source_target_pairs={{0,2},{2,0},{1,3},{3,1},{4,6},{6,4},{5,7},{7,5},{8,10},{10,8},{9,1... | collective-permute-start | bytes 3145736 | tf_op jit(solution)/shard_map/ppermute | solution.py:48
  644.2 41.2 %collective-permute-start.60 = (bf16[2,128,2048]{2,1,0:T(8,128)(2,1)S(1)}, bf16[2,128,2048]{2,1,0:T(8,128)(2,1)S(1)}, u32[]{:S(2)}, u32[]{:S(2)}) collective-permute-start(bf16[2,128,2048]{2,1,0:T(8,128)(2,1)S(1)} %bitcast.477), channel_id=1, source_target_pairs={{0,2},{2,0},{1,3},{3,1},{4,6},{6,4},{5,7},{7,5},{8,10},{10,8},{9,1... | collective-permute-start | bytes 3145736 | tf_op jit(solution)/shard_map/ppermute | solution.py:48
  645.8 34.4 %collective-permute-start.53 = (bf16[128,2048]{1,0:T(8,128)(2,1)S(1)}, bf16[128,2048]{1,0:T(8,128)(2,1)S(1)}, u32[]{:S(2)}, u32[]{:S(2)}) collective-permute-start(bf16[128,2048]{1,0:T(8,128)(2,1)S(1)} %fusion.102), channel_id=1, source_target_pairs={{0,2},{2,0},{1,3},{3,1},{4,6},{6,4},{5,7},{7,5},{8,10},{10,8},{9,1... | collective-permute-start | bytes 1572872 | tf_op jit(solution)/shard_map/ppermute | solution.py:48
  648.5 38.0 %collective-permute-start.58 = (bf16[2,128,2048]{2,1,0:T(8,128)(2,1)S(1)}, bf16[2,128,2048]{2,1,0:T(8,128)(2,1)S(1)}, u32[]{:S(2)}, u32[]{:S(2)}) collective-permute-start(bf16[2,128,2048]{2,1,0:T(8,128)(2,1)S(1)} %bitcast.479), channel_id=1, source_target_pairs={{0,4},{4,0},{1,5},{5,1},{2,6},{6,2},{3,7},{7,3},{8,12},{12,8},{9,1... | collective-permute-start | bytes 3145736 | tf_op jit(solution)/shard_map/ppermute | solution.py:48
  650.1 34.0 %collective-permute-start.56 = (bf16[128,2048]{1,0:T(8,128)(2,1)S(1)}, bf16[128,2048]{1,0:T(8,128)(2,1)S(1)}, u32[]{:S(2)}, u32[]{:S(2)}) collective-permute-start(bf16[128,2048]{1,0:T(8,128)(2,1)S(1)} %fusion.103), channel_id=1, source_target_pairs={{0,4},{4,0},{1,5},{5,1},{2,6},{6,2},{3,7},{7,3},{8,12},{12,8},{9,1... | collective-permute-start | bytes 1572872 | tf_op jit(solution)/shard_map/ppermute | solution.py:48
  690.6 32.4 %collective-permute-start.63 = (bf16[256,1536]{1,0:T(8,128)(2,1)}, bf16[256,1536]{1,0:T(8,128)(2,1)}, u32[]{:S(2)}, u32[]{:S(2)}) collective-permute-start(bf16[256,1536]{1,0:T(8,128)(2,1)} %constant_dynamic-slice_fusion.4), channel_id=1, source_target_pairs={{0,4},{4,0},{1,5},{5,1},{2,6},{6,2},{3,7},{7,3},{8,12},{12,8},{9,1... | collective-permute-start | bytes 2359304 | tf_op jit(solution)/shard_map/ppermute | solution.py:48
  692.1 27.7 %collective-permute-start.61 = (bf16[128,2048]{1,0:T(8,128)(2,1)}, bf16[128,2048]{1,0:T(8,128)(2,1)S(1)}, u32[]{:S(2)}, u32[]{:S(2)}) collective-permute-start(bf16[128,2048]{1,0:T(8,128)(2,1)} %fusion.105), channel_id=1, source_target_pairs={{0,4},{4,0},{1,5},{5,1},{2,6},{6,2},{3,7},{7,3},{8,12},{12,8},{9,1... | collective-permute-start | bytes 1572872 | tf_op jit(solution)/shard_map/ppermute | solution.py:48
  692.6 27.1 %collective-permute-start.59 = (bf16[128,2048]{1,0:T(8,128)(2,1)}, bf16[128,2048]{1,0:T(8,128)(2,1)}, u32[]{:S(2)}, u32[]{:S(2)}) collective-permute-start(bf16[128,2048]{1,0:T(8,128)(2,1)} %fusion.104), channel_id=1, source_target_pairs={{0,2},{2,0},{1,3},{3,1},{4,6},{6,4},{5,7},{7,5},{8,10},{10,8},{9,1... | collective-permute-start | bytes 1572872 | tf_op jit(solution)/shard_map/ppermute | solution.py:48
  (186 other events, 2473.5 us)
Sparse Core Ops, SparseCore 0:
  25.2 82.2 all-gather.3
  109.7 113.9 all-gather.5
  225.8 113.5 all-gather.7
  341.6 108.9 reduce-scatter.3
  452.8 111.2 reduce-scatter.5
  598.1 77.1 reduce-scatter.7

commit v4 on v3

--- a/solution.py
+++ b/solution.py
@@ -77,9 +77,9 @@
     return mine[:2].astype(F32) + came[:2].astype(F32), send
 
 
-def scatter_outer(state, outer):
+def scatter_outer(state, outer, *later):
     keep, send = state
-    came = swap(send, outer)
+    came = tie(swap(send, outer), *later)
     send = (keep[1] + came[1].astype(F32)).astype(BF)
     return keep[0] + came[0].astype(F32), send
 
@@ -305,7 +305,7 @@
         out_shape=jax.ShapeDtypeStruct(out_shape, BF),
         compiler_params=pltpu.CompilerParams(vmem_limit_bytes=VMEM_LIMIT),
         cost_estimate=pl.CostEstimate(
-            flops=400_000_000, bytes_accessed=3_000_000, transcendentals=0
+            flops=7_600_000_000, bytes_accessed=3_000_000, transcendentals=0
         ),
         name="attention_forward",
     )(projected, mask, cols, gate_rows)
@@ -334,7 +334,7 @@
         ],
         compiler_params=pltpu.CompilerParams(vmem_limit_bytes=VMEM_LIMIT),
         cost_estimate=pl.CostEstimate(
-            flops=1_000_000_000, bytes_accessed=5_000_000, transcendentals=0
+            flops=14_400_000_000, bytes_accessed=5_000_000, transcendentals=0
         ),
         name="attention_backward",
     )(projected, d_combined, mask, cols, gate_rows)
@@ -395,11 +395,57 @@
         out_shape=[act, act, grad, grad],
         compiler_params=pltpu.CompilerParams(vmem_limit_bytes=VMEM_LIMIT),
         cost_estimate=pl.CostEstimate(
-            flops=tokens * D * width, bytes_accessed=tokens * D, transcendentals=0
+            flops=26 * tokens * D * width, bytes_accessed=tokens * D, transcendentals=0
         ),
         name="feed_forward",
     )(*rows, *grads, weights)
     return (out[0], out[1]), (out[2], out[3])
+
+
+def down_kernel(count, half, *refs):
+    step = pl.program_id(0)
+    mine, other, weights = (refs[k * count : (k + 1) * count] for k in range(3))
+
+    def tile(rows, out_ref):
+        terms = [mm(a[...], w[...], NT) for a, w in zip(rows, weights)]
+        out_ref[...] = sum(terms[1:], terms[0]).astype(BF)
+
+    @pl.when(step < half)
+    def first():
+        tile(mine, refs[3 * count])
+
+    @pl.when(step >= half)
+    def second():
+        tile(other, refs[3 * count + 1])
+
+
+def down_product(active, weights):
+    count = len(active)
+    tokens, width = active[0][0].shape
+    tile = 256
+    half = tokens // tile
+
+    def first(columns):
+        return pl.BlockSpec((tile, columns), lambda i: (jnp.minimum(i, half - 1), 0))
+
+    def second(columns):
+        return pl.BlockSpec((tile, columns), lambda i: (jnp.maximum(i - half, 0), 0))
+
+    down = pl.BlockSpec((D, width), lambda i: (0, 2), pipeline_mode=pl.Buffered(1))
+    return pl.pallas_call(
+        functools.partial(down_kernel, count, half),
+        grid=(2 * half,),
+        in_specs=[first(width)] * count + [second(width)] * count + [down] * count,
+        out_specs=[first(D), second(D)],
+        out_shape=[jax.ShapeDtypeStruct((tokens, D), BF)] * 2,
+        compiler_params=pltpu.CompilerParams(vmem_limit_bytes=VMEM_LIMIT),
+        cost_estimate=pl.CostEstimate(
+            flops=4 * count * tokens * D * width,
+            bytes_accessed=2 * D * (count * width + 2 * tokens),
+            transcendentals=0,
+        ),
+        name="down_product",
+    )(*[a for a, _ in active], *[b for _, b in active], *weights)
 
 
 def grads_kernel(count, *refs):
@@ -447,7 +493,7 @@
         out_shape=jax.ShapeDtypeStruct((D, first + second), BF),
         compiler_params=pltpu.CompilerParams(vmem_limit_bytes=VMEM_LIMIT),
         cost_estimate=pl.CostEstimate(
-            flops=2 * count * tokens * D * (first + second),
+            flops=3 * count * tokens * D * (first + second),
             bytes_accessed=2 * (2 * count * tokens * D + (count * tokens + D) * (first + second)),
             transcendentals=0,
         ),
@@ -630,18 +676,19 @@
         tie(inputs[m, 0], send_att).reshape(own_tokens, D).astype(F32) for m in micros
     ]
     back_low = [cotangent[m, 0].reshape(own_tokens, D) for m in micros]
+    all_ids = doc_ids[:, 0]
+    for axis in ("y", "c", "x"):
+        all_ids = jnp.stack([all_ids, swap(all_ids, axis)], axis=0)
     normed_att = [rms_norm(t, norm_gains[0]).astype(BF) for t in token_rows]
-    att_pairs = [gather_tokens(normed_att[m], *orders[m], shard_att) for m in micros]
-    att_rows = [jnp.concatenate(pair, axis=0) for pair in att_pairs]
-    all_ids = doc_ids[:, 0]
-    for axis in ("y", "x", "c"):
-        all_ids = jnp.stack([all_ids, swap(all_ids, axis)], axis=0)
+    att_rows = [
+        gather_tokens(normed_att[m], *orders[m], shard_att, all_ids) for m in micros
+    ]
 
     shard_ff = []
     full_ff = []
     for k in range(CHUNKS):
         columns_for = functools.partial(ff_columns, k)
-        earlier = [p[0] for p in att_pairs] if k == 0 else [shard_ff[-1]]
+        earlier = [p[0] for p in att_rows] if k == 0 else [shard_ff[-1]]
         shard_ff.append(exchange_rows(columns_for, columns_for(1 - x_place), *earlier))
         full_ff.append(fetch(shard_ff[-1]))
 
@@ -652,7 +699,7 @@
     masks = []
     columns = []
     for m in micros:
-        ids = jnp.transpose(all_ids[:, :, :, m], (1, 3, 0, 2, 4)).reshape(2, seg_count, -1)
+        ids = jnp.transpose(all_ids[:, :, :, m], (0, 3, 1, 2, 4)).reshape(2, seg_count, -1)
         same = ids[:, :, :, None] == ids[:, :, None, :]
         masks.append((same & causal).astype(F32))
         last = jnp.max(ids, axis=2)
@@ -669,14 +716,14 @@
     hidden = []
     mlp_rows = []
     back_states = [
-        gather_start(tie(back_low[m], *[p[0] for p in att_pairs]), *orders[m], shard_ff[0])
+        gather_start(tie(back_low[m], *[p[0] for p in att_rows]), *orders[m])
         for m in micros
     ]
     for m in micros:
-        rows_in = att_rows[m]
+        mine, other = att_rows[m]
         if m == 0:
-            rows_in = tie(rows_in, *[t for state in back_states for t in state])
-        proj = mm(rows_in, full_qkv, NN).astype(BF)
+            mine = tie(mine, *[t for state in back_states for t in state])
+        proj = jnp.concatenate([mm(p, full_qkv, NN).astype(BF) for p in (mine, other)], axis=0)
         projected.append(proj.reshape(slots + (3 * width_att,)))
         comb = attention_fwd(projected[m], masks[m], columns[m], gate_rows, wheres[m])
         combined.append(comb.reshape(tokens, width_att))
@@ -694,6 +741,15 @@
         normed_mlp = rms_norm(hidden[m], norm_gains[1]).astype(BF)
         mlp_rows.append(gather_tokens(normed_mlp, *orders[m]))
 
+    def exchange_grad(grad):
+        mine = lax.dynamic_slice_in_dim(grad, x_place * rows, rows, axis=0)
+        theirs = swap(lax.dynamic_slice_in_dim(grad, (1 - x_place) * rows, rows, axis=0), "x")
+        return mine, theirs
+
+    def squares_of(grad):
+        wide = grad.astype(F32)
+        return jnp.sum(wide * wide)
+
     def reduce_rows(partial):
         return lax.psum_scatter(partial, "z", scatter_dimension=0, tiled=True)
 
@@ -707,7 +763,6 @@
     d_gate_up = []
     own_ff = []
     d_total = [None] * micro_count
-    out_total = [None] * micro_count
     states = [None] * micro_count
     for k in range(CHUNKS):
         active.append([])
@@ -726,40 +781,51 @@
             d_total[m] = products(grad, full_ff[k][:, : 2 * width], d_total[m], dtype)
             if last:
                 states[m] = scatter_core(*d_total[m], own_tokens)
-            else:
-                out_total[m] = products(act, full_ff[k][:, 2 * width :], out_total[m], F32)
         if not last:
             grad_ff = weight_grads(mlp_rows, back_rows, d_gate_up[k], active[k])
             own_ff.append(reduce_rows(grad_ff))
-            terms = [t for pair in d_total + out_total for t in pair]
+            terms = [t for pair in d_total for t in pair]
             full_ff[k + 1] = tie(full_ff[k + 1], grad_ff, *terms)
 
-    last_active = [(active[-1][m][0], tie(active[-1][m][1], states[-1][1])) for m in micros]
+    outer_states = [scatter_outer(states[m], orders[m][0]) for m in micros]
+    last_active = [
+        (active[-1][m][0], tie(active[-1][m][1], *[t[1] for t in outer_states])) for m in micros
+    ]
     grad_ff = weight_grads(mlp_rows, back_rows, d_gate_up[-1], last_active)
     own_ff.append(reduce_rows(grad_ff))
 
     gain_grad_att = jnp.zeros((D,), F32)
     gain_grad_mlp = jnp.zeros((D,), F32)
     d_hidden = []
-    att_grads = []
+    grad_states = []
     for m in micros:
-        state = tie_send(scatter_outer(states[m], orders[m][0]), grad_ff)
-        d_normed = scatter_inner(state, orders[m][1])
+        keep, send = outer_states[m]
+        d_normed = scatter_inner((tie(keep, grad_ff), send), orders[m][1])
         ignored, norm_back = jax.vjp(rms_norm, hidden[m], norm_gains[1])
         d_norm, d_gain = norm_back(d_normed)
         gain_grad_mlp = gain_grad_mlp + d_gain
         d_hidden.append(back_low[m].astype(F32) + d_norm)
-        att_grads.append(gather_tokens(d_hidden[m].astype(BF), *orders[m]))
+        state = gather_start(d_hidden[m].astype(BF), *orders[m])
+        grad_states.append(gather_across(state, orders[m][0]))
 
     gate_sum = jnp.zeros((heads,), F32)
     d_projs = []
     out_states = []
     for m in micros:
-        act = (last_active[m][0], tie(last_active[m][1], d_hidden[m]))
-        out_total[m] = products(act, full_ff[-1][:, 2 * width :], out_total[m], BF)
-        other = att_grads[m][1] if m > 0 else tie(att_grads[m][1], own_ff[0])
+        act = [active[k][m] for k in range(CHUNKS)]
+        act[-1] = (last_active[m][0], tie(last_active[m][1], *d_hidden))
+        mine, other = down_product(act, full_ff)
+        out_states.append(scatter_core(mine, other, own_tokens))
+    sends = [t[1] for t in out_states]
+    out_states = [tie_send(t, *[g[-1] for g in grad_states]) for t in out_states]
+    att_grads = [gather_core((tie(g[0], *sends),) + g[1:]) for g in grad_states]
+    ff_pairs = [exchange_grad(own_ff[0])]
+    for m in micros:
+        mine, other = att_grads[m]
+        if m == 0:
+            other = tie(other, own_ff[0])
         d_combined = jnp.concatenate(
-            [mm(att_grads[m][0], full_out, NN), mm(other, full_out, NN)], axis=0
+            [mm(mine, full_out, NN), mm(other, full_out, NN)], axis=0
         )
         d_proj, gate_part = attention_bwd(
             projected[m],
@@ -771,27 +837,19 @@
         )
         gate_sum = gate_sum + jnp.sum(gate_part, axis=(0, 2))
         d_projs.append(d_proj.reshape(tokens, 3 * width_att))
-    for m in micros:
-        mine, other = out_total[m]
-        other = tie(other, *[pair[1] for pair in att_grads])
-        out_states.append(tie_send(scatter_core(mine, other, own_tokens), d_projs[0]))
-    grad_att = weight_grads(att_rows, att_grads, d_projs, combined)
+    out_states = [scatter_outer(out_states[m], orders[m][0], *d_projs) for m in micros]
+    by_rows = [d_projs[0], tie(d_projs[-1], *[t[1] for t in out_states])]
+    grad_att = weight_grads(att_rows, att_grads, by_rows, combined)
     own_att = reduce_rows(grad_att)
-
-    def exchange_grad(grad):
-        mine = lax.dynamic_slice_in_dim(grad, x_place * rows, rows, axis=0)
-        theirs = swap(lax.dynamic_slice_in_dim(grad, (1 - x_place) * rows, rows, axis=0), "x")
-        return mine, theirs
-
-    def squares_of(grad):
-        wide = grad.astype(F32)
-        return jnp.sum(wide * wide)
-
-    pairs = [exchange_grad(g) for g in own_ff]
+    mlp_out = [scatter_inner(out_states[m], orders[m][1]) for m in micros]
+    block_out = [(hidden[m] + mlp_out[m]).astype(BF) for m in micros]
+
+    ff_pairs += [exchange_grad(g) for g in own_ff[1:]]
 
     def ff_part(start, stop):
-        low = jnp.concatenate([p[0][:, start * width : stop * width] for p in pairs], axis=1)
-        high = jnp.concatenate([p[1][:, start * width : stop * width] for p in pairs], axis=1)
+        cols = slice(start * width, stop * width)
+        low = jnp.concatenate([p[0][:, cols] for p in ff_pairs], axis=1)
+        high = jnp.concatenate([p[1][:, cols] for p in ff_pairs], axis=1)
         return by_place(low, high, 1)
 
     grad_mlp = mlp_view(jnp.stack([ff_part(0, 1), ff_part(1, 2)], axis=1))
@@ -799,23 +857,20 @@
     ff_owned = sum(squares_of(g) for g in own_ff)
 
     grad_rows = []
-    block_out = []
     in_states = []
     for m in micros:
-        d_proj = tie(d_projs[m], grad_att)
+        d_proj = tie(d_projs[m], grad_att, *block_out, own_ff[-1], ff_pairs[0][1])
         other = mm(d_proj[half:], full_qkv, NT).astype(BF)
         mine = mm(d_proj[:half], full_qkv, NT).astype(BF)
         in_states.append(scatter_core(mine, other, own_tokens))
     for m in micros:
-        state = tie_send(scatter_outer(in_states[m], orders[m][0]), own_ff[-1])
+        state = scatter_outer(in_states[m], orders[m][0])
+        state = tie_send(state, ff_pairs[-1][1], *([grad_mlp, grad_down] if m > 0 else []))
         d_normed = scatter_inner(state, orders[m][1])
         ignored, norm_first = jax.vjp(rms_norm, token_rows[m], norm_gains[0])
         d_norm, d_gain = norm_first(d_normed)
         gain_grad_att = gain_grad_att + d_gain
         grad_rows.append((d_hidden[m] + d_norm).astype(BF))
-    for m in micros:
-        state = tie_send(scatter_outer(out_states[m], orders[m][0]), in_states[-1][1])
-        block_out.append((hidden[m] + scatter_inner(state, orders[m][1])).astype(BF))
 
     att_mine, att_theirs = exchange_grad(own_att)
 

time: 809 us -> 772 us (0.954)
  matrix products: 108 us -> 79.7 us
  Pallas kernels: 162 us -> 179 us
  starting transfers between devices: 70.5 us -> 59.1 us
  local copies, waits for them, and re-layouts: 87.4 us -> 78 us
    dot_general x30 -> x24, matrix products: 108 us -> 79.7 us  [mm(): return lax.dot_general(a, b, (dims, ((), ())), preferred_element_type=F32)]
    pallas_call x0 -> x2, Pallas kernels: none -> 18.3 us  [down_product(): pl.pallas_call(functools.partial(down_kernel, count, half), grid=(2 * hal...]
    ppermute x68, starting transfers between devices: 65.5 us -> 54 us  [swap(): return lax.ppermute(tensor, axis, [(0, 1), (1, 0)])]
    unnamed x306 -> x300, local copies, waits for them, and re-layouts: 38.3 us -> 27.6 us
    ppermute x68, waiting for transfers between devices: 272 us -> 263 us  [swap(): return lax.ppermute(tensor, axis, [(0, 1), (1, 0)])]
  transfers between devices with their start and end apart: 76 -> 76, of which waited for: 37 -> 39; matrix products, arithmetic and copies ran while one was open for 31% -> 29% of each run, Pallas kernels for 17% -> 20%
where the time goes in v4:
time: 772 us; the launch traced here: 764 us
  waiting for transfers between devices  266 us (34%)
  Pallas kernels  179 us (23%)
  other arithmetic  81.8 us (11%)
  matrix products  79.7 us (10%)
  local copies, waits for them, and re-layouts  78 us (10%)
  starting transfers between devices  59.1 us (8%)
  between operations  20.6 us (3%)
    ppermute x68, waiting for transfers between devices, swap(): return lax.ppermute(tensor, axis, [(0, 1), (1, 0)])  263 us
    dot_general x24, matrix products, mm(): return lax.dot_general(a, b, (dims, ((), ())), preferred_element_type=F32)  79.7 us
    ppermute x68, starting transfers between devices, swap(): return lax.ppermute(tensor, axis, [(0, 1), (1, 0)])  54 us
    pallas_call x4, Pallas kernels, feed_forward(): pl.pallas_call(functools.partial(ff_kernel, width, half), grid=(2 * half,...  50 us
    pallas_call x3, Pallas kernels, weight_grads(): pl.pallas_call(functools.partial(grads_kernel, count), grid=(D // tile,),...  49.2 us
    unnamed x300, local copies, waits for them, and re-layouts  27.6 us
    pallas_call x2, Pallas kernels, attention_bwd(): pl.pallas_call(functools.partial(attention_bwd_kernel, heads), grid=(seqs...  24.8 us
    pallas_call x1, Pallas kernels, adam_all(): pl.pallas_call(adam_kernel, grid=(steps,), in_specs=[pl.BlockSpec(memory_...  23.5 us
  transfers between devices with their start and end apart: 76, of which 39 were waited for; matrix products, arithmetic and copies ran while one was open for 29% of the time, Pallas kernels for 20%

profile of v4, /device:TPU:0, one launch (start us, length us, event | category | flops | bytes accessed | tf_op | source)
XLA Modules:
  0.0 763.7 jit_solution(14647837007527505351)
XLA Ops:
  19.6 7.7 %collective-permute-done.1 = bf16[256,1024]{0,1:T(8,128)(2,1)S(1)} collective-permute-done((bf16[256,1024]{0,1:T(8,128)(2,1)S(1)}, bf16[256,1024]{0,1:T(8,128)(2,1)S(1)}, u32[]{:S(2)}, u32[]{:S(2)}) %collective-permute-start.1) | collective-permute-done | bytes 524320 | tf_op jit(solution)/shard_map/ppermute | solution.py:48
  52.8 8.5 %collective-permute-done.7 = bf16[128,2048]{1,0:T(8,128)(2,1)} collective-permute-done((bf16[128,2048]{1,0:T(8,128)(2,1)S(1)}, bf16[128,2048]{1,0:T(8,128)(2,1)}, u32[]{:S(2)}, u32[]{:S(2)}) %collective-permute-start.7) | collective-permute-done | bytes 524320 | tf_op jit(solution)/shard_map/ppermute | solution.py:48
  61.8 10.8 %collective-permute-done.5 = bf16[128,2048]{1,0:T(8,128)(2,1)} collective-permute-done((bf16[128,2048]{1,0:T(8,128)(2,1)}, bf16[128,2048]{1,0:T(8,128)(2,1)}, u32[]{:S(2)}, u32[]{:S(2)}) %collective-permute-start.5) | collective-permute-done | bytes 524320 | tf_op jit(solution)/shard_map/ppermute | solution.py:48
  72.5 9.6 %collective-permute-done.6 = bf16[128,2048]{1,0:T(8,128)(2,1)} collective-permute-done((bf16[128,2048]{1,0:T(8,128)(2,1)}, bf16[128,2048]{1,0:T(8,128)(2,1)}, u32[]{:S(2)}, u32[]{:S(2)}) %collective-permute-start.6) | collective-permute-done | bytes 524320 | tf_op jit(solution)/shard_map/ppermute | solution.py:48
  95.4 13.6 %collective-permute-done.24 = bf16[256,1536]{1,0:T(8,128)(2,1)} collective-permute-done((bf16[256,1536]{1,0:T(8,128)(2,1)}, bf16[256,1536]{1,0:T(8,128)(2,1)}, u32[]{:S(2)}, u32[]{:S(2)}) %collective-permute-start.24) | collective-permute-done | bytes 786464 | tf_op jit(solution)/shard_map/ppermute | solution.py:48
  128.2 17.6 %collective-permute-done.11 = bf16[128,2048]{1,0:T(8,128)(2,1)} collective-permute-done((bf16[128,2048]{1,0:T(8,128)(2,1)}, bf16[128,2048]{1,0:T(8,128)(2,1)}, u32[]{:S(2)}, u32[]{:S(2)}) %collective-permute-start.11) | collective-permute-done | bytes 524320 | tf_op jit(solution)/shard_map/ppermute | solution.py:48
  187.7 20.5 %collective-permute-done.29 = bf16[2,128,2048]{2,1,0:T(8,128)(2,1)S(1)} collective-permute-done((bf16[2,128,2048]{2,1,0:T(8,128)(2,1)S(1)}, bf16[2,128,2048]{2,1,0:T(8,128)(2,1)S(1)}, u32[]{:S(2)}, u32[]{:S(2)}) %collective-permute-start.29) | collective-permute-done | bytes 1048608 | tf_op jit(solution)/shard_map/ppermute | solution.py:48
  216.5 7.7 %collective-permute-done.30 = bf16[128,2048]{1,0:T(8,128)(2,1)} collective-permute-done((bf16[128,2048]{1,0:T(8,128)(2,1)}, bf16[128,2048]{1,0:T(8,128)(2,1)}, u32[]{:S(2)}, u32[]{:S(2)}) %collective-permute-start.30) | collective-permute-done | bytes 524320 | tf_op jit(solution)/shard_map/ppermute | solution.py:48
  233.0 8.8 %collective-permute-done.18 = bf16[128,2048]{1,0:T(8,128)(2,1)S(1)} collective-permute-done((bf16[128,2048]{1,0:T(8,128)(2,1)S(1)}, bf16[128,2048]{1,0:T(8,128)(2,1)S(1)}, u32[]{:S(2)}, u32[]{:S(2)}) %collective-permute-start.18) | collective-permute-done | bytes 524320 | tf_op jit(solution)/shard_map/ppermute | solution.py:48
  247.3 10.7 %collective-permute-done.20 = bf16[128,2048]{1,0:T(8,128)(2,1)S(1)} collective-permute-done((bf16[128,2048]{1,0:T(8,128)(2,1)S(1)}, bf16[128,2048]{1,0:T(8,128)(2,1)S(1)}, u32[]{:S(2)}, u32[]{:S(2)}) %collective-permute-start.20) | collective-permute-done | bytes 524320 | tf_op jit(solution)/shard_map/ppermute | solution.py:48
  275.3 10.4 %collective-permute-done.33 = bf16[128,2048]{1,0:T(8,128)(2,1)S(1)} collective-permute-done((bf16[128,2048]{1,0:T(8,128)(2,1)S(1)}, bf16[128,2048]{1,0:T(8,128)(2,1)S(1)}, u32[]{:S(2)}, u32[]{:S(2)}) %collective-permute-start.33) | collective-permute-done | bytes 524320 | tf_op jit(solution)/shard_map/ppermute | solution.py:48
  287.3 12.2 %feed_forward.4 = (bf16[512,512]{1,0:T(8,128)(2,1)S(1)}, bf16[512,512]{1,0:T(8,128)(2,1)S(1)}, bf16[512,1024]{1,0:T(8,128)(2,1)S(1)}, bf16[512,1024]{1,0:T(8,128)(2,1)S(1)}) custom-call(bf16[512,2048]{1,0:T(8,128)(2,1)S(1)} %pad_maximum_fusion.2.x_mine.refs_0_, bf16[512,2048]{1,0:T(8,128)(2,1)} %collective-permute-done.21.x_other.refs_1_, ...), custom_call_target="tpu_custom_call" | custom-call | flops 13958643712 | bytes 1048576 | tf_op jit(solution)/shard_map/feed_forward/pallas_call | solution.py:390
  299.5 13.1 %feed_forward.5 = (bf16[512,512]{1,0:T(8,128)(2,1)S(1)}, bf16[512,512]{1,0:T(8,128)(2,1)S(1)}, bf16[512,1024]{1,0:T(8,128)(2,1)S(1)}, bf16[512,1024]{1,0:T(8,128)(2,1)S(1)}) custom-call(bf16[512,2048]{1,0:T(8,128)(2,1)} %pad_maximum_fusion.3.x_mine.refs_2_, bf16[512,2048]{1,0:T(8,128)(2,1)} %collective-permute-done.34.x_other.refs_3_, ...), custom_call_target="tpu_custom_call" | custom-call | flops 13958643712 | bytes 1048576 | tf_op jit(solution)/shard_map/feed_forward/pallas_call | solution.py:390
  313.6 18.1 %weight_grads.3 = bf16[2048,1536]{1,0:T(8,128)(2,1)} custom-call(bf16[512,2048]{1,0:T(8,128)(2,1)} %copy-done.1, bf16[512,2048]{1,0:T(8,128)(2,1)} %collective-permute-done.21.x_other.refs_1_, bf16[512,2048]{1,0:T(8,128)(2,1)} %pad_maximum_fusion.3.x_mine.refs_2_, bf16[512,2048]{1,0:T(8,128)(2,1)} %collective-permute-done.34.x_other.refs_3_, ...), custom_call_target="tpu_custom_call" | custom-call | flops 19327352832 | bytes 29360128 | tf_op jit(solution)/shard_map/weight_grads/pallas_call | solution.py:486
  338.8 6.7 fusion
  345.5 6.7 fusion.4
  356.6 12.4 %feed_forward.6 = (bf16[512,512]{1,0:T(8,128)(2,1)S(1)}, bf16[512,512]{1,0:T(8,128)(2,1)S(1)}, bf16[512,1024]{1,0:T(8,128)(2,1)S(1)}, bf16[512,1024]{1,0:T(8,128)(2,1)S(1)}) custom-call(bf16[512,2048]{1,0:T(8,128)(2,1)S(1)} %copy-done.2, bf16[512,2048]{1,0:T(8,128)(2,1)} %collective-permute-done.21.x_other.refs_1_, bf16[512,2048]{1,0:T(8,128)(2,1)} %copy-done.95, ...), custom_call_target="tpu_custom_call" | custom-call | flops 13958643712 | bytes 1048576 | tf_op jit(solution)/shard_map/feed_forward/pallas_call | solution.py:390
  378.3 12.4 %feed_forward.7 = (bf16[512,512]{1,0:T(8,128)(2,1)S(1)}, bf16[512,512]{1,0:T(8,128)(2,1)S(1)}, bf16[512,1024]{1,0:T(8,128)(2,1)S(1)}, bf16[512,1024]{1,0:T(8,128)(2,1)S(1)}) custom-call(bf16[512,2048]{1,0:T(8,128)(2,1)} %pad_maximum_fusion.3.x_mine.refs_2_, bf16[512,2048]{1,0:T(8,128)(2,1)} %collective-permute-done.34.x_other.refs_3_, ...), custom_call_target="tpu_custom_call" | custom-call | flops 13958643712 | bytes 1048576 | tf_op jit(solution)/shard_map/feed_forward/pallas_call | solution.py:390
  403.4 22.8 %collective-permute-done.37 = bf16[2,128,2048]{2,1,0:T(8,128)(2,1)S(1)} collective-permute-done((bf16[2,128,2048]{2,1,0:T(8,128)(2,1)S(1)}, bf16[2,128,2048]{2,1,0:T(8,128)(2,1)S(1)}, u32[]{:S(2)}, u32[]{:S(2)}) %collective-permute-start.37) | collective-permute-done | bytes 1048608 | tf_op jit(solution)/shard_map/ppermute | solution.py:48
  430.4 18.2 %weight_grads.4 = bf16[2048,1536]{1,0:T(8,128)(2,1)} custom-call(bf16[512,2048]{1,0:T(8,128)(2,1)} %copy-done.1, bf16[512,2048]{1,0:T(8,128)(2,1)} %collective-permute-done.21.x_other.refs_1_, bf16[512,2048]{1,0:T(8,128)(2,1)} %pad_maximum_fusion.3.x_mine.refs_2_, bf16[512,2048]{1,0:T(8,128)(2,1)} %collective-permute-done.34.x_other.refs_3_, ...), custom_call_target="tpu_custom_call" | custom-call | flops 19327352832 | bytes 29360128 | tf_op jit(solution)/shard_map/weight_grads/pallas_call | solution.py:486
  456.8 8.9 %down_product.2 = (bf16[512,2048]{1,0:T(8,128)(2,1)S(1)}, bf16[512,2048]{1,0:T(8,128)(2,1)}) custom-call(bf16[512,512]{1,0:T(8,128)(2,1)S(1)} %copy-done.27, bf16[512,512]{1,0:T(8,128)(2,1)S(1)} %copy-done.31, bf16[512,512]{1,0:T(8,128)(2,1)S(1)} %copy-done.29, bf16[512,512]{1,0:T(8,128)(2,1)S(1)} %copy-done.33, ...), custom_call_target="tpu_custom_call" | custom-call | flops 4294967296 | bytes 8388608 | tf_op jit(solution)/shard_map/down_product/pallas_call | solution.py:435
  465.7 9.4 %down_product.3 = (bf16[512,2048]{1,0:T(8,128)(2,1)S(1)}, bf16[512,2048]{1,0:T(8,128)(2,1)}) custom-call(bf16[512,512]{1,0:T(8,128)(2,1)S(1)} %get-tuple-element.106.refs_14_.refs_0_, bf16[512,512]{1,0:T(8,128)(2,1)S(1)} %get-tuple-element.118.refs_14_.refs_1_, bf16[512,512]{1,0:T(8,128)(2,1)S(1)} %get-tuple-element.107.refs_15_.refs_2_, ...), custom_call_target="tpu_custom_call" | custom-call | flops 4294967296 | bytes 8388608 | tf_op jit(solution)/shard_map/down_product/pallas_call | solution.py:435
  479.0 10.3 %collective-permute-done.45 = bf16[128,2048]{1,0:T(8,128)(2,1)S(1)} collective-permute-done((bf16[128,2048]{1,0:T(8,128)(2,1)S(1)}, bf16[128,2048]{1,0:T(8,128)(2,1)S(1)}, u32[]{:S(2)}, u32[]{:S(2)}) %collective-permute-start.45) | collective-permute-done | bytes 524320 | tf_op jit(solution)/shard_map/ppermute | solution.py:48
  503.1 10.1 %collective-permute-done.46 = bf16[128,2048]{1,0:T(8,128)(2,1)S(1)} collective-permute-done((bf16[128,2048]{1,0:T(8,128)(2,1)S(1)}, bf16[128,2048]{1,0:T(8,128)(2,1)S(1)}, u32[]{:S(2)}, u32[]{:S(2)}) %collective-permute-start.46) | collective-permute-done | bytes 524320 | tf_op jit(solution)/shard_map/ppermute | solution.py:48
  516.9 11.2 %collective-permute-done.49 = bf16[128,2048]{1,0:T(8,128)(2,1)S(1)} collective-permute-done((bf16[128,2048]{1,0:T(8,128)(2,1)S(1)}, bf16[128,2048]{1,0:T(8,128)(2,1)S(1)}, u32[]{:S(2)}, u32[]{:S(2)}) %collective-permute-start.49) | collective-permute-done | bytes 524320 | tf_op jit(solution)/shard_map/ppermute | solution.py:48
  533.5 12.5 %attention_backward.3 = (bf16[2,2,2,4,32,768]{5,4,3,2,1,0:T(8,128)(2,1)S(1)}, f32[2,2,128]{2,1,0:T(2,128)S(1)}) custom-call(bf16[2,2,2,4,32,768]{5,4,3,2,1,0:T(8,128)(2,1)S(1)} %bitcast.394, f32[2,2,2,4,32,256]{5,4,3,2,1,0:T(8,128)S(1)} %bitcast.398, f32[2,4,128,128]{3,2,1,0:T(8,128)S(1)} %copy-done.19, f32[2,4,128,3]{3,2,1,0:T(8,128)S(1)} %copy-done.15, ...), custom_call_target="tpu_custom_call" | custom-call | flops 14400000000 | bytes 5000000 | tf_op jit(solution)/shard_map/attention_backward/pallas_call | solution.py:317
  550.3 12.3 %attention_backward.2 = (bf16[2,2,2,4,32,768]{5,4,3,2,1,0:T(8,128)(2,1)S(1)}, f32[2,2,128]{2,1,0:T(2,128)S(1)}) custom-call(bf16[2,2,2,4,32,768]{5,4,3,2,1,0:T(8,128)(2,1)S(1)} %bitcast.396, f32[2,2,2,4,32,256]{5,4,3,2,1,0:T(8,128)S(1)} %bitcast.397, f32[2,4,128,128]{3,2,1,0:T(8,128)S(1)} %copy-done.17, f32[2,4,128,3]{3,2,1,0:T(8,128)S(1)} %copy-done.13, ...), custom_call_target="tpu_custom_call" | custom-call | flops 14400000000 | bytes 5000000 | tf_op jit(solution)/shard_map/attention_backward/pallas_call | solution.py:317
  566.8 12.9 %weight_grads.5 = bf16[2048,1024]{1,0:T(8,128)(2,1)} custom-call(bf16[512,2048]{1,0:T(8,128)(2,1)} %pad_maximum_fusion.refs_0_, bf16[512,2048]{1,0:T(8,128)(2,1)} %collective-permute-done.14.refs_1_, bf16[512,2048]{1,0:T(8,128)(2,1)} %pad_maximum_fusion.1.refs_2_, bf16[512,2048]{1,0:T(8,128)(2,1)} %collective-permute-done.26.refs_3_, ...), custom_call_target="tpu_custom_call" | custom-call | flops 12884901888 | bytes 25165824 | tf_op jit(solution)/shard_map/weight_grads/pallas_call | solution.py:486
  599.8 11.5 %collective-permute-done.56 = bf16[256,1536]{1,0:T(8,128)(2,1)} collective-permute-done((bf16[256,1536]{1,0:T(8,128)(2,1)}, bf16[256,1536]{1,0:T(8,128)(2,1)}, u32[]{:S(2)}, u32[]{:S(2)}) %collective-permute-start.56) | collective-permute-done | bytes 786464 | tf_op jit(solution)/shard_map/ppermute | solution.py:48
  637.9 12.7 %collective-permute-done.59 = bf16[256,1536]{1,0:T(8,128)(2,1)S(1)} collective-permute-done((bf16[256,1536]{1,0:T(8,128)(2,1)S(1)}, bf16[256,1536]{1,0:T(8,128)(2,1)S(1)}, u32[]{:S(2)}, u32[]{:S(2)}) %collective-permute-start.59) | collective-permute-done | bytes 786464 | tf_op jit(solution)/shard_map/ppermute | solution.py:48
  669.3 13.2 %collective-permute-done.62 = bf16[2,128,2048]{2,1,0:T(8,128)(2,1)S(1)} collective-permute-done((bf16[2,128,2048]{2,1,0:T(8,128)(2,1)S(1)}, bf16[2,128,2048]{2,1,0:T(8,128)(2,1)S(1)}, u32[]{:S(2)}, u32[]{:S(2)}) %collective-permute-start.62) | collective-permute-done | bytes 1048608 | tf_op jit(solution)/shard_map/ppermute | solution.py:48
  731.8 23.5 %adam.1 = (f32[3,256,512]{2,1,0:T(8,128)}, f32[3,256,512]{2,1,0:T(8,128)}, f32[3,256,512]{2,1,0:T(8,128)}, f32[256,512]{1,0:T(8,128)}, f32[256,512]{1,0:T(8,128)...) custom-call(s32[1]{0:T(128)} %bitcast.89.place_ref, ...), custom_call_target="tpu_custom_call" | custom-call | flops 41943040 | bytes 50331648 | tf_op jit(solution)/shard_map/adam/pallas_call | solution.py:568
  (611 shorter events, 346.1 us)
Async XLA Ops:
  7.2 142.6 %all-gather.4.cloned.1.call-start = ((), (), s32[]{:S(2)}) async-start(), calls=%async_computation.3 | async-start | bytes 5242880 | tf_op jit(solution)/shard_map/all_gather | solution.py:644
  7.2 33.4 %collective-permute-start.2 = (s32[2,4,32]{2,1,0:T(4,128)}, s32[2,4,32]{2,1,0:T(4,128)}, u32[]{:S(2)}, u32[]{:S(2)}) collective-permute-start(s32[2,4,32]{2,1,0:T(4,128)} %bitcast.446), channel_id=1, source_target_pairs={{0,2},{2,0},{1,3},{3,1},{4,6},{6,4},{5,7},{7,5},{8,10},{10,8},{9,1... | collective-permute-start | bytes 3080 | tf_op jit(solution)/shard_map/ppermute | solution.py:48
  28.3 258.9 %all-gather.6.cloned.1.call-start = ((), (), s32[]{:S(2)}) async-start(), calls=%async_computation.4 | async-start | bytes 7864320 | tf_op jit(solution)/shard_map/all_gather | solution.py:644
  30.4 54.8 %collective-permute-start.8 = (bf16[128,2048]{1,0:T(8,128)(2,1)S(1)}, bf16[128,2048]{1,0:T(8,128)(2,1)}, u32[]{:S(2)}, u32[]{:S(2)}) collective-permute-start(bf16[128,2048]{1,0:T(8,128)(2,1)S(1)} %get-tuple-element.93), channel_id=1, source_target_pairs={{0,2},{2,0},{1,3},{3,1},{4,6},{6,4},{5,7},{7,5},{8,10},{10,8},{9,1... | collective-permute-start | bytes 1572872 | tf_op jit(solution)/shard_map/ppermute | solution.py:48
  47.9 24.7 %collective-permute-start.5 = (bf16[128,2048]{1,0:T(8,128)(2,1)}, bf16[128,2048]{1,0:T(8,128)(2,1)}, u32[]{:S(2)}, u32[]{:S(2)}) collective-permute-start(bf16[128,2048]{1,0:T(8,128)(2,1)} %get-tuple-element.91), channel_id=1, source_target_pairs={{0,4},{4,0},{1,5},{5,1},{2,6},{6,2},{3,7},{7,3},{8,12},{12,8},{9,1... | collective-permute-start | bytes 1572872 | tf_op jit(solution)/shard_map/ppermute | solution.py:48
  48.4 33.7 %collective-permute-start.6 = (bf16[128,2048]{1,0:T(8,128)(2,1)}, bf16[128,2048]{1,0:T(8,128)(2,1)}, u32[]{:S(2)}, u32[]{:S(2)}) collective-permute-start(bf16[128,2048]{1,0:T(8,128)(2,1)} %collective-permute-done), channel_id=1, source_target_pairs={{0,4},{4,0},{1,5},{5,1},{2,6},{6,2},{3,7},{7,3},{8,12},{12,8},{9,1... | collective-permute-start | bytes 1572872 | tf_op jit(solution)/shard_map/ppermute | solution.py:48
  61.3 24.0 %collective-permute-start.9 = (bf16[128,2048]{1,0:T(8,128)(2,1)}, bf16[128,2048]{1,0:T(8,128)(2,1)S(1)}, u32[]{:S(2)}, u32[]{:S(2)}) collective-permute-start(bf16[128,2048]{1,0:T(8,128)(2,1)} %collective-permute-done.7), channel_id=1, source_target_pairs={{0,2},{2,0},{1,3},{3,1},{4,6},{6,4},{5,7},{7,5},{8,10},{10,8},{9,1... | collective-permute-start | bytes 1572872 | tf_op jit(solution)/shard_map/ppermute | solution.py:48
  91.5 62.9 %collective-permute-start.26 = (bf16[512,2048]{1,0:T(8,128)(2,1)}, bf16[512,2048]{1,0:T(8,128)(2,1)}, u32[]{:S(2)}, u32[]{:S(2)}) collective-permute-start(bf16[512,2048]{1,0:T(8,128)(2,1)} %pad_maximum_fusion.1.refs_2_), channel_id=1, source_target_pairs={{0,1},{1,0},{2,3},{3,2},{4,5},{5,4},{6,7},{7,6},{8,9},{9,8},{10,11... | collective-permute-start | bytes 6291464 | tf_op jit(solution)/shard_map/ppermute | solution.py:48
  91.5 28.8 %collective-permute-start.12 = (bf16[128,2048]{1,0:T(8,128)(2,1)}, bf16[128,2048]{1,0:T(8,128)(2,1)}, u32[]{:S(2)}, u32[]{:S(2)}) collective-permute-start(bf16[128,2048]{1,0:T(8,128)(2,1)} %bitcast.15), channel_id=1, source_target_pairs={{0,4},{4,0},{1,5},{5,1},{2,6},{6,2},{3,7},{7,3},{8,12},{12,8},{9,1... | collective-permute-start | bytes 1572872 | tf_op jit(solution)/shard_map/ppermute | solution.py:48
  110.3 37.5 %collective-permute-start.25 = (bf16[256,1536]{1,0:T(8,128)(2,1)}, bf16[256,1536]{1,0:T(8,128)(2,1)}, u32[]{:S(2)}, u32[]{:S(2)}) collective-permute-start(bf16[256,1536]{1,0:T(8,128)(2,1)} %pad_maximum_fusion.11), channel_id=1, source_target_pairs={{0,4},{4,0},{1,5},{5,1},{2,6},{6,2},{3,7},{7,3},{8,12},{12,8},{9,1... | collective-permute-start | bytes 2359304 | tf_op jit(solution)/shard_map/ppermute | solution.py:48
  114.2 31.6 %collective-permute-start.10 = (bf16[128,2048]{1,0:T(8,128)(2,1)}, bf16[128,2048]{1,0:T(8,128)(2,1)}, u32[]{:S(2)}, u32[]{:S(2)}) collective-permute-start(bf16[128,2048]{1,0:T(8,128)(2,1)} %bitcast.12), channel_id=1, source_target_pairs={{0,2},{2,0},{1,3},{3,1},{4,6},{6,4},{5,7},{7,5},{8,10},{10,8},{9,1... | collective-permute-start | bytes 1572872 | tf_op jit(solution)/shard_map/ppermute | solution.py:48
  115.8 240.8 %all-gather.8.cloned.1.call-start = ((), (), s32[]{:S(2)}) async-start(), calls=%async_computation.5 | async-start | bytes 7864320 | tf_op jit(solution)/shard_map/all_gather | solution.py:644
  120.3 25.5 %collective-permute-start.11 = (bf16[128,2048]{1,0:T(8,128)(2,1)}, bf16[128,2048]{1,0:T(8,128)(2,1)}, u32[]{:S(2)}, u32[]{:S(2)}) collective-permute-start(bf16[128,2048]{1,0:T(8,128)(2,1)} %bitcast.12), channel_id=1, source_target_pairs={{0,4},{4,0},{1,5},{5,1},{2,6},{6,2},{3,7},{7,3},{8,12},{12,8},{9,1... | collective-permute-start | bytes 1572872 | tf_op jit(solution)/shard_map/ppermute | solution.py:48
  128.2 41.3 %collective-permute-start.14 = (bf16[512,2048]{1,0:T(8,128)(2,1)}, bf16[512,2048]{1,0:T(8,128)(2,1)}, u32[]{:S(2)}, u32[]{:S(2)}) collective-permute-start(bf16[512,2048]{1,0:T(8,128)(2,1)} %pad_maximum_fusion.refs_0_), channel_id=1, source_target_pairs={{0,1},{1,0},{2,3},{3,2},{4,5},{5,4},{6,7},{7,6},{8,9},{9,8},{10,11... | collective-permute-start | bytes 6291464 | tf_op jit(solution)/shard_map/ppermute | solution.py:48
  183.1 25.1 %collective-permute-start.29 = (bf16[2,128,2048]{2,1,0:T(8,128)(2,1)S(1)}, bf16[2,128,2048]{2,1,0:T(8,128)(2,1)S(1)}, u32[]{:S(2)}, u32[]{:S(2)}) collective-permute-start(bf16[2,128,2048]{2,1,0:T(8,128)(2,1)S(1)} %bitcast.430), channel_id=1, source_target_pairs={{0,2},{2,0},{1,3},{3,1},{4,6},{6,4},{5,7},{7,5},{8,10},{10,8},{9,1... | collective-permute-start | bytes 3145736 | tf_op jit(solution)/shard_map/ppermute | solution.py:48
  187.2 26.2 %collective-permute-start.16 = (bf16[2,128,2048]{2,1,0:T(8,128)(2,1)}, bf16[2,128,2048]{2,1,0:T(8,128)(2,1)}, u32[]{:S(2)}, u32[]{:S(2)}) collective-permute-start(bf16[2,128,2048]{2,1,0:T(8,128)(2,1)} %bitcast.23), channel_id=1, source_target_pairs={{0,4},{4,0},{1,5},{5,1},{2,6},{6,2},{3,7},{7,3},{8,12},{12,8},{9,1... | collective-permute-start | bytes 3145736 | tf_op jit(solution)/shard_map/ppermute | solution.py:48
  210.6 335.5 %reduce-scatter.4.cloned.1.call-start = ((), (), s32[]{:S(2)}) async-start(), calls=%async_computation.6 | async-start | bytes 7864320 | tf_op jit(solution)/shard_map/reduce_scatter | solution.py:754
  245.5 41.8 %collective-permute-start.23 = (bf16[512,2048]{1,0:T(8,128)(2,1)S(1)}, bf16[512,2048]{1,0:T(8,128)(2,1)}, u32[]{:S(2)}, u32[]{:S(2)}) collective-permute-start(bf16[512,2048]{1,0:T(8,128)(2,1)S(1)} %constant_dynamic-update-slice_fusion.g_mine.refs_4_), channel_id=1, source_target_pairs={{0,1},{1,0},{2,3},{3,2},{4,5},{5,4},{6,7},{7,6},{8,9},{9,8},{10,11... | collective-permute-start | bytes 6291464 | tf_op jit(solution)/shard_map/ppermute | solution.py:48
  258.1 29.1 %collective-permute-start.21 = (bf16[512,2048]{1,0:T(8,128)(2,1)S(1)}, bf16[512,2048]{1,0:T(8,128)(2,1)}, u32[]{:S(2)}, u32[]{:S(2)}) collective-permute-start(bf16[512,2048]{1,0:T(8,128)(2,1)S(1)} %pad_maximum_fusion.2.x_mine.refs_0_), channel_id=1, source_target_pairs={{0,1},{1,0},{2,3},{3,2},{4,5},{5,4},{6,7},{7,6},{8,9},{9,8},{10,11... | collective-permute-start | bytes 6291464 | tf_op jit(solution)/shard_map/ppermute | solution.py:48
  272.8 26.7 %collective-permute-start.35 = (bf16[512,2048]{1,0:T(8,128)(2,1)}, bf16[512,2048]{1,0:T(8,128)(2,1)}, u32[]{:S(2)}, u32[]{:S(2)}) collective-permute-start(bf16[512,2048]{1,0:T(8,128)(2,1)} %constant_dynamic-update-slice_fusion.4.g_mine.refs_6_), channel_id=1, source_target_pairs={{0,1},{1,0},{2,3},{3,2},{4,5},{5,4},{6,7},{7,6},{8,9},{9,8},{10,11... | collective-permute-start | bytes 6291464 | tf_op jit(solution)/shard_map/ppermute | solution.py:48
  331.8 285.0 %reduce-scatter.6.cloned.1.call-start = ((), (), s32[]{:S(2)}) async-start(), calls=%async_computation.7 | async-start | bytes 7864320 | tf_op jit(solution)/shard_map/reduce_scatter | solution.py:754
  400.7 25.6 %collective-permute-start.37 = (bf16[2,128,2048]{2,1,0:T(8,128)(2,1)S(1)}, bf16[2,128,2048]{2,1,0:T(8,128)(2,1)S(1)}, u32[]{:S(2)}, u32[]{:S(2)}) collective-permute-start(bf16[2,128,2048]{2,1,0:T(8,128)(2,1)S(1)} %bitcast.428), channel_id=1, source_target_pairs={{0,4},{4,0},{1,5},{5,1},{2,6},{6,2},{3,7},{7,3},{8,12},{12,8},{9,1... | collective-permute-start | bytes 3145736 | tf_op jit(solution)/shard_map/ppermute | solution.py:48
  403.1 25.3 %collective-permute-start.39 = (bf16[2,128,2048]{2,1,0:T(8,128)(2,1)S(1)}, bf16[2,128,2048]{2,1,0:T(8,128)(2,1)S(1)}, u32[]{:S(2)}, u32[]{:S(2)}) collective-permute-start(bf16[2,128,2048]{2,1,0:T(8,128)(2,1)S(1)} %bitcast.429), channel_id=1, source_target_pairs={{0,2},{2,0},{1,3},{3,1},{4,6},{6,4},{5,7},{7,5},{8,10},{10,8},{9,1... | collective-permute-start | bytes 3145736 | tf_op jit(solution)/shard_map/ppermute | solution.py:48
  448.8 244.4 %reduce-scatter.8.cloned.1.call-start = ((), (), s32[]{:S(2)}) async-start(), calls=%async_computation.8 | async-start | bytes 5242880 | tf_op jit(solution)/shard_map/reduce_scatter | solution.py:754
  465.7 26.7 %collective-permute-start.42 = (bf16[512,2048]{1,0:T(8,128)(2,1)}, bf16[512,2048]{1,0:T(8,128)(2,1)S(1)}, u32[]{:S(2)}, u32[]{:S(2)}) collective-permute-start(bf16[512,2048]{1,0:T(8,128)(2,1)} %get-tuple-element.125), channel_id=1, source_target_pairs={{0,1},{1,0},{2,3},{3,2},{4,5},{5,4},{6,7},{7,6},{8,9},{9,8},{10,11... | collective-permute-start | bytes 6291464 | tf_op jit(solution)/shard_map/ppermute | solution.py:48
  478.5 24.6 %collective-permute-start.51 = (bf16[128,2048]{1,0:T(8,128)(2,1)S(1)}, bf16[128,2048]{1,0:T(8,128)(2,1)S(1)}, u32[]{:S(2)}, u32[]{:S(2)}) collective-permute-start(bf16[128,2048]{1,0:T(8,128)(2,1)S(1)} %get-tuple-element.133), channel_id=1, source_target_pairs={{0,2},{2,0},{1,3},{3,1},{4,6},{6,4},{5,7},{7,5},{8,10},{10,8},{9,1... | collective-permute-start | bytes 1572872 | tf_op jit(solution)/shard_map/ppermute | solution.py:48
  513.8 48.9 %collective-permute-start.47 = (bf16[2,128,2048]{2,1,0:T(8,128)(2,1)}, bf16[2,128,2048]{2,1,0:T(8,128)(2,1)}, u32[]{:S(2)}, u32[]{:S(2)}) collective-permute-start(bf16[2,128,2048]{2,1,0:T(8,128)(2,1)} %bitcast.57), channel_id=1, source_target_pairs={{0,4},{4,0},{1,5},{5,1},{2,6},{6,2},{3,7},{7,3},{8,12},{12,8},{9,1... | collective-permute-start | bytes 3145736 | tf_op jit(solution)/shard_map/ppermute | solution.py:48
  515.4 47.3 %collective-permute-start.54 = (bf16[2,128,2048]{2,1,0:T(8,128)(2,1)}, bf16[2,128,2048]{2,1,0:T(8,128)(2,1)}, u32[]{:S(2)}, u32[]{:S(2)}) collective-permute-start(bf16[2,128,2048]{2,1,0:T(8,128)(2,1)} %bitcast.58), channel_id=1, source_target_pairs={{0,2},{2,0},{1,3},{3,1},{4,6},{6,4},{5,7},{7,5},{8,10},{10,8},{9,1... | collective-permute-start | bytes 3145736 | tf_op jit(solution)/shard_map/ppermute | solution.py:48
  627.4 28.2 %collective-permute-start.61 = (bf16[512,2048]{1,0:T(8,128)(2,1)}, bf16[512,2048]{1,0:T(8,128)(2,1)}, u32[]{:S(2)}, u32[]{:S(2)}) collective-permute-start(bf16[512,2048]{1,0:T(8,128)(2,1)} %convolution_convert_fusion.4), channel_id=1, source_target_pairs={{0,1},{1,0},{2,3},{3,2},{4,5},{5,4},{6,7},{7,6},{8,9},{9,8},{10,11... | collective-permute-start | bytes 6291464 | tf_op jit(solution)/shard_map/ppermute | solution.py:48
  630.5 29.1 %collective-permute-start.57 = (bf16[512,2048]{1,0:T(8,128)(2,1)}, bf16[512,2048]{1,0:T(8,128)(2,1)}, u32[]{:S(2)}, u32[]{:S(2)}) collective-permute-start(bf16[512,2048]{1,0:T(8,128)(2,1)} %convolution_convert_fusion.6), channel_id=1, source_target_pairs={{0,1},{1,0},{2,3},{3,2},{4,5},{5,4},{6,7},{7,6},{8,9},{9,8},{10,11... | collective-permute-start | bytes 6291464 | tf_op jit(solution)/shard_map/ppermute | solution.py:48
  658.2 24.3 %collective-permute-start.62 = (bf16[2,128,2048]{2,1,0:T(8,128)(2,1)S(1)}, bf16[2,128,2048]{2,1,0:T(8,128)(2,1)S(1)}, u32[]{:S(2)}, u32[]{:S(2)}) collective-permute-start(bf16[2,128,2048]{2,1,0:T(8,128)(2,1)S(1)} %bitcast.426), channel_id=1, source_target_pairs={{0,2},{2,0},{1,3},{3,1},{4,6},{6,4},{5,7},{7,5},{8,10},{10,8},{9,1... | collective-permute-start | bytes 3145736 | tf_op jit(solution)/shard_map/ppermute | solution.py:48
  661.9 25.5 %collective-permute-start.58 = (bf16[2,128,2048]{2,1,0:T(8,128)(2,1)S(1)}, bf16[2,128,2048]{2,1,0:T(8,128)(2,1)S(1)}, u32[]{:S(2)}, u32[]{:S(2)}) collective-permute-start(bf16[2,128,2048]{2,1,0:T(8,128)(2,1)S(1)} %bitcast.427), channel_id=1, source_target_pairs={{0,4},{4,0},{1,5},{5,1},{2,6},{6,2},{3,7},{7,3},{8,12},{12,8},{9,1... | collective-permute-start | bytes 3145736 | tf_op jit(solution)/shard_map/ppermute | solution.py:48
  (184 other events, 2272.0 us)
Sparse Core Ops, SparseCore 0:
  28.5 81.0 all-gather.3
  115.9 114.7 all-gather.5
  232.8 113.5 all-gather.7
  348.6 108.9 reduce-scatter.3
  459.8 111.2 reduce-scatter.5
  579.8 77.0 reduce-scatter.7

commit v5 on v4

--- a/solution.py
+++ b/solution.py
@@ -515,28 +515,48 @@
     return grad_norm, jnp.minimum(1.0, CLIP / (grad_norm + 1e-06))
 
 
-def adam_kernel(place_ref, small_ref, *refs):
-    ins, grads, outs = refs[:12], refs[12:16], refs[16:]
+def adam_kernel(steps, chunks, place_ref, small_ref, *refs):
+    ins, refs = refs[:15], refs[15:]
+    grads, refs = refs[: 2 + 2 * chunks], refs[2 + 2 * chunks :]
+    outs, scratch = refs[:15], refs[15]
     factor = clip_factor(small_ref[...])[1]
     is_low = place_ref[0] == 0
-
-    def put(number, place, gradient, rate):
+    everything = slice(None)
+
+    def put(number, place, gradient, rate, decay=DECAY):
         weight, moment, second = (r[place] for r in ins[3 * number : 3 * number + 3])
-        new = adam_update(weight, moment, second, gradient.astype(F32), factor, rate, DECAY)
+        new = adam_update(weight, moment, second, gradient.astype(F32), factor, rate, decay)
         for ref, value in zip(outs[3 * number : 3 * number + 3], new):
             ref[place] = value
 
-    mine, theirs = grads[0][...], grads[1][...]
-    sides = (jnp.where(is_low, mine, theirs), jnp.where(is_low, theirs, mine))
-    width = mine.shape[1] // 4
-    everything = slice(None)
-    for s, side in enumerate(sides):
+    def sides_of(mine, theirs):
+        mine, theirs = mine[...], theirs[...]
+        return jnp.where(is_low, mine, theirs), jnp.where(is_low, theirs, mine)
+
+    for s, side in enumerate(sides_of(*grads[:2])):
+        width = side.shape[1] // 4
         cols = slice(s * width, (s + 1) * width)
         for part in range(3):
             put(0, (part, everything, cols), side[:, part * width : (part + 1) * width], RATE_QKV)
         put(1, (everything, cols), side[:, 3 * width :], RATE_OUT)
-    put(2, (everything, everything), grads[2][...], RATE_QKV)
-    put(2 + 1, (everything, everything), grads[3][...], RATE_DOWN)
+    rows, width_ff = ins[9].shape
+    lanes = width_ff // 128
+    for k in range(chunks):
+        for s, side in enumerate(sides_of(*grads[2 + 2 * k : 4 + 2 * k])):
+            side = side.astype(F32)
+            width = side.shape[1] // 3
+            start = s * (width_ff // 2) + k * width
+            put(3, (everything, slice(start, start + width)), side[:, 2 * width :], RATE_DOWN)
+            for part in range(2):
+                for lane in range(width // 128):
+                    place = pl.ds((start // 128 + lane) * 2 + part, rows, stride=2 * lanes)
+                    first = part * width + lane * 128
+                    scratch[place, :] = side[:, first : first + 128]
+    put(2, (everything, everything), scratch[...], RATE_QKV)
+
+    @pl.when(pl.program_id(0) == 0)
+    def gains():
+        put(4, (everything, everything), small_ref[: ins[12].shape[0]], 0.5, 0.0)
 
 
 def mlp_view(t):
@@ -544,37 +564,48 @@
     return t.reshape(rows, 2, width_ff // 128, 128).transpose(0, 2, 1, 3).reshape(-1, 128)
 
 
-def adam_all(small, x_place, arrays, att_mine, att_theirs, grad_mlp, grad_down):
+def adam_all(small, x_place, arrays, att_sides, ff_sides):
     rows, _, width_ff = arrays[6].shape
-    lanes = width_ff // 128
+    steps = 4
 
     def qkv_view(t):
         return jnp.transpose(t, (1, 0, 2))
 
-    def mlp_back(t):
-        return t.reshape(rows, lanes, 2, 128).transpose(0, 2, 1, 3).reshape(rows, 2, width_ff)
+    def mlp_back(t, shape):
+        rows, _, width_ff = shape
+        t = t.reshape(rows, width_ff // 128, 2, 128).transpose(0, 2, 1, 3)
+        return t.reshape(shape)
 
     views = [qkv_view(t) for t in arrays[:3]] + list(arrays[3:6])
-    views += [mlp_view(t) for t in arrays[6:9]] + list(arrays[9:])
-    grads = [att_mine, att_theirs, grad_mlp, grad_down]
-    steps = 8
+    views += [mlp_view(t) for t in arrays[6:9]] + list(arrays[9:12])
+    gains = [mlp_view(t[None]) for t in arrays[12:]]
+    grads = list(att_sides) + [t for pair in ff_sides for t in pair]
 
     def spec(t):
         axis = t.ndim - 2
         block = list(t.shape)
         block[axis] //= steps
-        return pl.BlockSpec(tuple(block), lambda i: (0,) * axis + (i, 0))
-
+        return pl.BlockSpec(tuple(block), lambda i, place: (0,) * axis + (i, 0))
+
+    def whole(t):
+        return pl.BlockSpec(t.shape, lambda i, place: (0, 0))
+
+    def mine(t):
+        return pl.BlockSpec((rows // steps, t.shape[1]), lambda i, place: (place[0] * steps + i, 0))
+
+    specs = [spec(t) for t in views] + [whole(t) for t in gains]
     new = pl.pallas_call(
-        adam_kernel,
-        grid=(steps,),
-        in_specs=[
-            pl.BlockSpec(memory_space=pltpu.SMEM),
-            pl.BlockSpec(small.shape, lambda i: (0, 0)),
-        ]
-        + [spec(t) for t in views + grads],
-        out_specs=[spec(t) for t in views],
-        out_shape=[jax.ShapeDtypeStruct(t.shape, F32) for t in views],
+        functools.partial(adam_kernel, steps, len(ff_sides)),
+        grid_spec=pltpu.PrefetchScalarGridSpec(
+            num_scalar_prefetch=1,
+            grid=(steps,),
+            in_specs=[whole(small)]
+            + specs
+            + [spec(t) if k % 2 else mine(t) for k, t in enumerate(grads)],
+            out_specs=specs,
+            scratch_shapes=[pltpu.VMEM((views[6].shape[0] // steps, 128), F32)],
+        ),
+        out_shape=[jax.ShapeDtypeStruct(t.shape, F32) for t in views + gains],
         compiler_params=pltpu.CompilerParams(vmem_limit_bytes=VMEM_LIMIT),
         cost_estimate=pl.CostEstimate(
             flops=20 * sum(t.size for t in views) // 3,
@@ -582,10 +613,14 @@
             transcendentals=0,
         ),
         name="adam",
-    )(x_place[None], small, *views, *grads)
+    )(x_place[None], small, *views, *gains, *grads)
     new = list(new)
     return (
-        [qkv_view(t) for t in new[:3]] + new[3:6] + [mlp_back(t) for t in new[6:9]] + new[9:]
+        [qkv_view(t) for t in new[:3]]
+        + new[3:6]
+        + [mlp_back(t, arrays[6].shape) for t in new[6:9]]
+        + new[9:12]
+        + [mlp_back(t, (1,) + arrays[12].shape)[0] for t in new[12:]]
     )
 
 
@@ -676,12 +711,12 @@
         tie(inputs[m, 0], send_att).reshape(own_tokens, D).astype(F32) for m in micros
     ]
     back_low = [cotangent[m, 0].reshape(own_tokens, D) for m in micros]
-    all_ids = doc_ids[:, 0]
+    all_ids = tie(doc_ids[:, 0], shard_att)
     for axis in ("y", "c", "x"):
         all_ids = jnp.stack([all_ids, swap(all_ids, axis)], axis=0)
     normed_att = [rms_norm(t, norm_gains[0]).astype(BF) for t in token_rows]
     att_rows = [
-        gather_tokens(normed_att[m], *orders[m], shard_att, all_ids) for m in micros
+        gather_tokens(normed_att[m], *orders[m], shard_att) for m in micros
     ]
 
     shard_ff = []
@@ -716,7 +751,7 @@
     hidden = []
     mlp_rows = []
     back_states = [
-        gather_start(tie(back_low[m], *[p[0] for p in att_rows]), *orders[m])
+        gather_start(tie(back_low[m], all_ids, *[p[0] for p in att_rows]), *orders[m])
         for m in micros
     ]
     for m in micros:
@@ -742,9 +777,7 @@
         mlp_rows.append(gather_tokens(normed_mlp, *orders[m]))
 
     def exchange_grad(grad):
-        mine = lax.dynamic_slice_in_dim(grad, x_place * rows, rows, axis=0)
-        theirs = swap(lax.dynamic_slice_in_dim(grad, (1 - x_place) * rows, rows, axis=0), "x")
-        return mine, theirs
+        return grad, swap(lax.dynamic_slice_in_dim(grad, (1 - x_place) * rows, rows, axis=0), "x")
 
     def squares_of(grad):
         wide = grad.astype(F32)
@@ -837,8 +870,8 @@
         )
         gate_sum = gate_sum + jnp.sum(gate_part, axis=(0, 2))
         d_projs.append(d_proj.reshape(tokens, 3 * width_att))
-    out_states = [scatter_outer(out_states[m], orders[m][0], *d_projs) for m in micros]
-    by_rows = [d_projs[0], tie(d_projs[-1], *[t[1] for t in out_states])]
+    out_states = [scatter_outer(out_states[m], orders[m][0], d_projs[0]) for m in micros]
+    by_rows = [d_projs[0], tie(d_projs[-1], ff_pairs[0][1], *[t[1] for t in out_states])]
     grad_att = weight_grads(att_rows, att_grads, by_rows, combined)
     own_att = reduce_rows(grad_att)
     mlp_out = [scatter_inner(out_states[m], orders[m][1]) for m in micros]
@@ -846,26 +879,19 @@
 
     ff_pairs += [exchange_grad(g) for g in own_ff[1:]]
 
-    def ff_part(start, stop):
-        cols = slice(start * width, stop * width)
-        low = jnp.concatenate([p[0][:, cols] for p in ff_pairs], axis=1)
-        high = jnp.concatenate([p[1][:, cols] for p in ff_pairs], axis=1)
-        return by_place(low, high, 1)
-
-    grad_mlp = mlp_view(jnp.stack([ff_part(0, 1), ff_part(1, 2)], axis=1))
-    grad_down = ff_part(2, 3)
     ff_owned = sum(squares_of(g) for g in own_ff)
 
     grad_rows = []
     in_states = []
     for m in micros:
-        d_proj = tie(d_projs[m], grad_att, *block_out, own_ff[-1], ff_pairs[0][1])
+        d_proj = tie(d_projs[m], grad_att)
         other = mm(d_proj[half:], full_qkv, NT).astype(BF)
         mine = mm(d_proj[:half], full_qkv, NT).astype(BF)
         in_states.append(scatter_core(mine, other, own_tokens))
     for m in micros:
         state = scatter_outer(in_states[m], orders[m][0])
-        state = tie_send(state, ff_pairs[-1][1], *([grad_mlp, grad_down] if m > 0 else []))
+        if m > 0:
+            state = tie_send(state, ff_pairs[-1][1])
         d_normed = scatter_inner(state, orders[m][1])
         ignored, norm_first = jax.vjp(rms_norm, token_rows[m], norm_gains[0])
         d_norm, d_gain = norm_first(d_normed)
@@ -878,16 +904,11 @@
     gate_padded = lax.dynamic_update_slice(
         jnp.zeros(gate_logit.shape, F32), gate_grad, (head_start,)
     )
-    ff_owned = tie(ff_owned, grad_mlp, grad_down)
     owned = squares_of(own_att) + ff_owned
-    small = jnp.concatenate(
-        [gain_grad_att, gain_grad_mlp, gate_padded, owned[None], jnp.zeros((111,), F32)]
-    ).reshape(-1, 128)
+    gain_grad = mlp_view(jnp.stack([gain_grad_att, gain_grad_mlp], axis=0)[None])
+    last_row = jnp.concatenate([gate_padded, owned[None], jnp.zeros((127 - HEADS,), F32)])
+    small = jnp.concatenate([gain_grad, last_row[None]], axis=0)
     small = sum_everywhere(small, z_count, att_theirs)
-    grad_norm, factor = (t.reshape(()) for t in clip_factor(small))
-    flat = small.reshape(-1)
-    gains_total = flat[: 2 * D].reshape(2, D)
-    gate_total = flat[2 * D : 2 * D + HEADS]
     arrays = [
         weight_qkv,
         moment_qkv,
@@ -901,9 +922,14 @@
         weight_down,
         moment_down,
         second_down,
+        norm_gains,
+        moment_gains,
+        second_gains,
     ]
-    new = adam_all(small, x_place, arrays, att_mine, att_theirs, grad_mlp, grad_down)
-    gains_new = adam_update(norm_gains, moment_gains, second_gains, gains_total, factor, 0.5, 0.0)
+    new = adam_all(small, x_place, arrays, (att_mine, att_theirs), ff_pairs)
+    new = [new[3 * n + k] for n in range(5) for k in (0, 1, 2)]
+    grad_norm, factor = (t.reshape(()) for t in clip_factor(tie(small, new[0])))
+    gate_total = small[-1, :HEADS]
     gate_new = adam_update(gate_logit, moment_gate, second_gate, gate_total, factor, 1.0, 0.0)
     shape = (micro_count, 1, seg_count, own_len, D)
     return (
@@ -911,7 +937,6 @@
         jnp.stack(grad_rows, axis=0).reshape(shape),
         grad_norm,
         *new,
-        *gains_new,
         *gate_new,
     )
 

time: 772 us -> 731 us (0.947)
  local copies, waits for them, and re-layouts: 78 us -> 55 us
  waiting for transfers between devices: 266 us -> 250 us
    ppermute x68, waiting for transfers between devices: 263 us -> 248 us  [swap(): return lax.ppermute(tensor, axis, [(0, 1), (1, 0)])]
    concatenate x9 -> x0, local copies, waits for them, and re-layouts: 13.2 us -> none  [the longest x8 13.1 us: by_place(): jnp.concatenate([own, other], axis=axis)]
    unnamed x300 -> x264, local copies, waits for them, and re-layouts: 27.6 us -> 26.2 us
  transfers between devices with their start and end apart: 76 -> 76, of which waited for: 39 -> 35; matrix products, arithmetic and copies ran while one was open for 29% -> 27% of each run, Pallas kernels for 20% -> 21%
where the time goes in v5:
time: 731 us; the launch traced here: 723 us
  waiting for transfers between devices  250 us (34%)
  Pallas kernels  178 us (24%)
  other arithmetic  81.1 us (11%)
  matrix products  79.4 us (11%)
  starting transfers between devices  59.5 us (8%)
  local copies, waits for them, and re-layouts  55 us (8%)
  between operations  20.5 us (3%)
    ppermute x68, waiting for transfers between devices, swap(): return lax.ppermute(tensor, axis, [(0, 1), (1, 0)])  248 us
    dot_general x24, matrix products, mm(): return lax.dot_general(a, b, (dims, ((), ())), preferred_element_type=F32)  79.4 us
    ppermute x68, starting transfers between devices, swap(): return lax.ppermute(tensor, axis, [(0, 1), (1, 0)])  54.1 us
    pallas_call x4, Pallas kernels, feed_forward(): pl.pallas_call(functools.partial(ff_kernel, width, half), grid=(2 * half,...  50 us
    pallas_call x3, Pallas kernels, weight_grads(): pl.pallas_call(functools.partial(grads_kernel, count), grid=(D // tile,),...  49.3 us
    unnamed x264, local copies, waits for them, and re-layouts  26.2 us
    pallas_call x2, Pallas kernels, attention_bwd(): pl.pallas_call(functools.partial(attention_bwd_kernel, heads), grid=(seqs...  24.8 us
    pallas_call x1, Pallas kernels, adam_all(): pl.pallas_call(functools.partial(adam_kernel, steps, len(ff_sides)), grid...  22.7 us
  transfers between devices with their start and end apart: 76, of which 35 were waited for; matrix products, arithmetic and copies ran while one was open for 27% of the time, Pallas kernels for 21%

profile of v5, /device:TPU:0, one launch (start us, length us, event | category | flops | bytes accessed | tf_op | source)
XLA Modules:
  0.0 723.3 jit_solution(782672523552911440)
XLA Ops:
  18.0 7.7 %collective-permute-done.1 = bf16[256,1024]{0,1:T(8,128)(2,1)S(1)} collective-permute-done((bf16[256,1024]{0,1:T(8,128)(2,1)S(1)}, bf16[256,1024]{0,1:T(8,128)(2,1)S(1)}, u32[]{:S(2)}, u32[]{:S(2)}) %collective-permute-start.1) | collective-permute-done | bytes 524320 | tf_op jit(solution)/shard_map/ppermute | solution.py:48
  48.4 8.0 %collective-permute-done.7 = bf16[128,2048]{1,0:T(8,128)(2,1)} collective-permute-done((bf16[128,2048]{1,0:T(8,128)(2,1)S(1)}, bf16[128,2048]{1,0:T(8,128)(2,1)}, u32[]{:S(2)}, u32[]{:S(2)}) %collective-permute-start.7) | collective-permute-done | bytes 524320 | tf_op jit(solution)/shard_map/ppermute | solution.py:48
  58.7 8.9 %collective-permute-done.2 = bf16[128,2048]{1,0:T(8,128)(2,1)} collective-permute-done((bf16[128,2048]{1,0:T(8,128)(2,1)}, bf16[128,2048]{1,0:T(8,128)(2,1)}, u32[]{:S(2)}, u32[]{:S(2)}) %collective-permute-start.2) | collective-permute-done | bytes 524320 | tf_op jit(solution)/shard_map/ppermute | solution.py:48
  67.6 8.7 %collective-permute-done.3 = bf16[128,2048]{1,0:T(8,128)(2,1)} collective-permute-done((bf16[128,2048]{1,0:T(8,128)(2,1)}, bf16[128,2048]{1,0:T(8,128)(2,1)}, u32[]{:S(2)}, u32[]{:S(2)}) %collective-permute-start.3) | collective-permute-done | bytes 524320 | tf_op jit(solution)/shard_map/ppermute | solution.py:48
  86.4 13.6 %collective-permute-done.6 = s32[2,2,2,4,32]{4,3,2,1,0:T(4,128)S(1)} collective-permute-done((s32[2,2,2,4,32]{4,3,2,1,0:T(4,128)S(1)}, s32[2,2,2,4,32]{4,3,2,1,0:T(4,128)S(1)}, u32[]{:S(2)}, u32[]{:S(2)}) %collective-permute-start.6) | collective-permute-done | bytes 4128 | tf_op jit(solution)/shard_map/ppermute | solution.py:48
  123.8 19.0 %collective-permute-done.11 = bf16[128,2048]{1,0:T(8,128)(2,1)} collective-permute-done((bf16[128,2048]{1,0:T(8,128)(2,1)}, bf16[128,2048]{1,0:T(8,128)(2,1)}, u32[]{:S(2)}, u32[]{:S(2)}) %collective-permute-start.11) | collective-permute-done | bytes 524320 | tf_op jit(solution)/shard_map/ppermute | solution.py:48
  185.4 20.5 %collective-permute-done.29 = bf16[2,128,2048]{2,1,0:T(8,128)(2,1)S(1)} collective-permute-done((bf16[2,128,2048]{2,1,0:T(8,128)(2,1)S(1)}, bf16[2,128,2048]{2,1,0:T(8,128)(2,1)S(1)}, u32[]{:S(2)}, u32[]{:S(2)}) %collective-permute-start.29) | collective-permute-done | bytes 1048608 | tf_op jit(solution)/shard_map/ppermute | solution.py:48
  213.1 8.7 %collective-permute-done.30 = bf16[128,2048]{1,0:T(8,128)(2,1)} collective-permute-done((bf16[128,2048]{1,0:T(8,128)(2,1)}, bf16[128,2048]{1,0:T(8,128)(2,1)}, u32[]{:S(2)}, u32[]{:S(2)}) %collective-permute-start.30) | collective-permute-done | bytes 524320 | tf_op jit(solution)/shard_map/ppermute | solution.py:48
  230.0 9.5 %collective-permute-done.18 = bf16[128,2048]{1,0:T(8,128)(2,1)S(1)} collective-permute-done((bf16[128,2048]{1,0:T(8,128)(2,1)S(1)}, bf16[128,2048]{1,0:T(8,128)(2,1)S(1)}, u32[]{:S(2)}, u32[]{:S(2)}) %collective-permute-start.18) | collective-permute-done | bytes 524320 | tf_op jit(solution)/shard_map/ppermute | solution.py:48
  244.9 9.4 %collective-permute-done.20 = bf16[128,2048]{1,0:T(8,128)(2,1)S(1)} collective-permute-done((bf16[128,2048]{1,0:T(8,128)(2,1)S(1)}, bf16[128,2048]{1,0:T(8,128)(2,1)S(1)}, u32[]{:S(2)}, u32[]{:S(2)}) %collective-permute-start.20) | collective-permute-done | bytes 524320 | tf_op jit(solution)/shard_map/ppermute | solution.py:48
  271.6 10.4 %collective-permute-done.33 = bf16[128,2048]{1,0:T(8,128)(2,1)S(1)} collective-permute-done((bf16[128,2048]{1,0:T(8,128)(2,1)S(1)}, bf16[128,2048]{1,0:T(8,128)(2,1)S(1)}, u32[]{:S(2)}, u32[]{:S(2)}) %collective-permute-start.33) | collective-permute-done | bytes 524320 | tf_op jit(solution)/shard_map/ppermute | solution.py:48
  283.6 12.2 %feed_forward.4 = (bf16[512,512]{1,0:T(8,128)(2,1)S(1)}, bf16[512,512]{1,0:T(8,128)(2,1)S(1)}, bf16[512,1024]{1,0:T(8,128)(2,1)S(1)}, bf16[512,1024]{1,0:T(8,128)(2,1)S(1)}) custom-call(bf16[512,2048]{1,0:T(8,128)(2,1)S(1)} %pad_maximum_fusion.2.x_mine.refs_0_, bf16[512,2048]{1,0:T(8,128)(2,1)} %collective-permute-done.21.x_other.refs_1_, ...), custom_call_target="tpu_custom_call" | custom-call | flops 13958643712 | bytes 1048576 | tf_op jit(solution)/shard_map/feed_forward/pallas_call | solution.py:390
  295.8 13.1 %feed_forward.5 = (bf16[512,512]{1,0:T(8,128)(2,1)S(1)}, bf16[512,512]{1,0:T(8,128)(2,1)S(1)}, bf16[512,1024]{1,0:T(8,128)(2,1)S(1)}, bf16[512,1024]{1,0:T(8,128)(2,1)S(1)}) custom-call(bf16[512,2048]{1,0:T(8,128)(2,1)} %pad_maximum_fusion.3.x_mine.refs_2_, bf16[512,2048]{1,0:T(8,128)(2,1)} %collective-permute-done.34.x_other.refs_3_, ...), custom_call_target="tpu_custom_call" | custom-call | flops 13958643712 | bytes 1048576 | tf_op jit(solution)/shard_map/feed_forward/pallas_call | solution.py:390
  310.0 18.1 %weight_grads.3 = bf16[2048,1536]{1,0:T(8,128)(2,1)} custom-call(bf16[512,2048]{1,0:T(8,128)(2,1)} %copy-done.1, bf16[512,2048]{1,0:T(8,128)(2,1)} %collective-permute-done.21.x_other.refs_1_, bf16[512,2048]{1,0:T(8,128)(2,1)} %pad_maximum_fusion.3.x_mine.refs_2_, bf16[512,2048]{1,0:T(8,128)(2,1)} %collective-permute-done.34.x_other.refs_3_, ...), custom_call_target="tpu_custom_call" | custom-call | flops 19327352832 | bytes 29360128 | tf_op jit(solution)/shard_map/weight_grads/pallas_call | solution.py:486
  328.4 6.7 fusion.2
  335.1 6.7 fusion
  351.0 12.4 %feed_forward.6 = (bf16[512,512]{1,0:T(8,128)(2,1)S(1)}, bf16[512,512]{1,0:T(8,128)(2,1)S(1)}, bf16[512,1024]{1,0:T(8,128)(2,1)S(1)}, bf16[512,1024]{1,0:T(8,128)(2,1)S(1)}) custom-call(bf16[512,2048]{1,0:T(8,128)(2,1)S(1)} %copy-done.2, bf16[512,2048]{1,0:T(8,128)(2,1)} %collective-permute-done.21.x_other.refs_1_, bf16[512,2048]{1,0:T(8,128)(2,1)} %copy-done.82, ...), custom_call_target="tpu_custom_call" | custom-call | flops 13958643712 | bytes 1048576 | tf_op jit(solution)/shard_map/feed_forward/pallas_call | solution.py:390
  372.5 12.3 %feed_forward.7 = (bf16[512,512]{1,0:T(8,128)(2,1)S(1)}, bf16[512,512]{1,0:T(8,128)(2,1)S(1)}, bf16[512,1024]{1,0:T(8,128)(2,1)S(1)}, bf16[512,1024]{1,0:T(8,128)(2,1)S(1)}) custom-call(bf16[512,2048]{1,0:T(8,128)(2,1)} %pad_maximum_fusion.3.x_mine.refs_2_, bf16[512,2048]{1,0:T(8,128)(2,1)} %collective-permute-done.34.x_other.refs_3_, ...), custom_call_target="tpu_custom_call" | custom-call | flops 13958643712 | bytes 1048576 | tf_op jit(solution)/shard_map/feed_forward/pallas_call | solution.py:390
  399.1 21.4 %collective-permute-done.37 = bf16[2,128,2048]{2,1,0:T(8,128)(2,1)S(1)} collective-permute-done((bf16[2,128,2048]{2,1,0:T(8,128)(2,1)S(1)}, bf16[2,128,2048]{2,1,0:T(8,128)(2,1)S(1)}, u32[]{:S(2)}, u32[]{:S(2)}) %collective-permute-start.37) | collective-permute-done | bytes 1048608 | tf_op jit(solution)/shard_map/ppermute | solution.py:48
  425.5 18.1 %weight_grads.4 = bf16[2048,1536]{1,0:T(8,128)(2,1)} custom-call(bf16[512,2048]{1,0:T(8,128)(2,1)} %copy-done.1, bf16[512,2048]{1,0:T(8,128)(2,1)} %collective-permute-done.21.x_other.refs_1_, bf16[512,2048]{1,0:T(8,128)(2,1)} %pad_maximum_fusion.3.x_mine.refs_2_, bf16[512,2048]{1,0:T(8,128)(2,1)} %collective-permute-done.34.x_other.refs_3_, ...), custom_call_target="tpu_custom_call" | custom-call | flops 19327352832 | bytes 29360128 | tf_op jit(solution)/shard_map/weight_grads/pallas_call | solution.py:486
  451.8 9.1 %down_product.2 = (bf16[512,2048]{1,0:T(8,128)(2,1)S(1)}, bf16[512,2048]{1,0:T(8,128)(2,1)}) custom-call(bf16[512,512]{1,0:T(8,128)(2,1)S(1)} %copy-done.30, bf16[512,512]{1,0:T(8,128)(2,1)S(1)} %copy-done.34, bf16[512,512]{1,0:T(8,128)(2,1)S(1)} %copy-done.32, bf16[512,512]{1,0:T(8,128)(2,1)S(1)} %copy-done.36, ...), custom_call_target="tpu_custom_call" | custom-call | flops 4294967296 | bytes 8388608 | tf_op jit(solution)/shard_map/down_product/pallas_call | solution.py:435
  460.8 8.9 %down_product.3 = (bf16[512,2048]{1,0:T(8,128)(2,1)S(1)}, bf16[512,2048]{1,0:T(8,128)(2,1)}) custom-call(bf16[512,512]{1,0:T(8,128)(2,1)S(1)} %get-tuple-element.110.refs_14_.refs_0_, bf16[512,512]{1,0:T(8,128)(2,1)S(1)} %get-tuple-element.122.refs_14_.refs_1_, bf16[512,512]{1,0:T(8,128)(2,1)S(1)} %get-tuple-element.111.refs_15_.refs_2_, ...), custom_call_target="tpu_custom_call" | custom-call | flops 4294967296 | bytes 8388608 | tf_op jit(solution)/shard_map/down_product/pallas_call | solution.py:435
  473.9 10.4 %collective-permute-done.45 = bf16[128,2048]{1,0:T(8,128)(2,1)S(1)} collective-permute-done((bf16[128,2048]{1,0:T(8,128)(2,1)S(1)}, bf16[128,2048]{1,0:T(8,128)(2,1)S(1)}, u32[]{:S(2)}, u32[]{:S(2)}) %collective-permute-start.45) | collective-permute-done | bytes 524320 | tf_op jit(solution)/shard_map/ppermute | solution.py:48
  498.0 9.9 %collective-permute-done.46 = bf16[128,2048]{1,0:T(8,128)(2,1)S(1)} collective-permute-done((bf16[128,2048]{1,0:T(8,128)(2,1)S(1)}, bf16[128,2048]{1,0:T(8,128)(2,1)S(1)}, u32[]{:S(2)}, u32[]{:S(2)}) %collective-permute-start.46) | collective-permute-done | bytes 524320 | tf_op jit(solution)/shard_map/ppermute | solution.py:48
  512.1 10.7 %collective-permute-done.49 = bf16[128,2048]{1,0:T(8,128)(2,1)S(1)} collective-permute-done((bf16[128,2048]{1,0:T(8,128)(2,1)S(1)}, bf16[128,2048]{1,0:T(8,128)(2,1)S(1)}, u32[]{:S(2)}, u32[]{:S(2)}) %collective-permute-start.49) | collective-permute-done | bytes 524320 | tf_op jit(solution)/shard_map/ppermute | solution.py:48
  532.2 12.5 %attention_backward.3 = (bf16[2,2,2,4,32,768]{5,4,3,2,1,0:T(8,128)(2,1)S(1)}, f32[2,2,128]{2,1,0:T(2,128)S(1)}) custom-call(bf16[2,2,2,4,32,768]{5,4,3,2,1,0:T(8,128)(2,1)S(1)} %bitcast.432, f32[2,2,2,4,32,256]{5,4,3,2,1,0:T(8,128)S(1)} %bitcast.434, f32[2,4,128,128]{3,2,1,0:T(8,128)S(1)} %copy-done.17, f32[2,4,128,3]{3,2,1,0:T(8,128)S(1)} %copy-done.13, ...), custom_call_target="tpu_custom_call" | custom-call | flops 14400000000 | bytes 5000000 | tf_op jit(solution)/shard_map/attention_backward/pallas_call | solution.py:317
  550.7 12.3 %attention_backward.2 = (bf16[2,2,2,4,32,768]{5,4,3,2,1,0:T(8,128)(2,1)S(1)}, f32[2,2,128]{2,1,0:T(2,128)S(1)}) custom-call(bf16[2,2,2,4,32,768]{5,4,3,2,1,0:T(8,128)(2,1)S(1)} %bitcast.430, f32[2,2,2,4,32,256]{5,4,3,2,1,0:T(8,128)S(1)} %bitcast.433, f32[2,4,128,128]{3,2,1,0:T(8,128)S(1)} %copy-done.15, f32[2,4,128,3]{3,2,1,0:T(8,128)S(1)} %copy-done.11, ...), custom_call_target="tpu_custom_call" | custom-call | flops 14400000000 | bytes 5000000 | tf_op jit(solution)/shard_map/attention_backward/pallas_call | solution.py:317
  566.9 13.1 %weight_grads.5 = bf16[2048,1024]{1,0:T(8,128)(2,1)} custom-call(bf16[512,2048]{1,0:T(8,128)(2,1)} %pad_maximum_fusion.refs_0_, bf16[512,2048]{1,0:T(8,128)(2,1)} %collective-permute-done.14.refs_1_, bf16[512,2048]{1,0:T(8,128)(2,1)} %pad_maximum_fusion.1.refs_2_, bf16[512,2048]{1,0:T(8,128)(2,1)} %collective-permute-done.26.refs_3_, ...), custom_call_target="tpu_custom_call" | custom-call | flops 12884901888 | bytes 25165824 | tf_op jit(solution)/shard_map/weight_grads/pallas_call | solution.py:486
  611.6 17.0 %collective-permute-done.58 = bf16[2,128,2048]{2,1,0:T(8,128)(2,1)S(1)} collective-permute-done((bf16[2,128,2048]{2,1,0:T(8,128)(2,1)S(1)}, bf16[2,128,2048]{2,1,0:T(8,128)(2,1)S(1)}, u32[]{:S(2)}, u32[]{:S(2)}) %collective-permute-start.58) | collective-permute-done | bytes 1048608 | tf_op jit(solution)/shard_map/ppermute | solution.py:48
  637.0 11.6 %collective-permute-done.62.refs_20_ = bf16[256,1536]{1,0:T(8,128)(2,1)S(1)} collective-permute-done((bf16[256,1536]{1,0:T(8,128)(2,1)S(1)}, bf16[256,1536]{1,0:T(8,128)(2,1)S(1)}, u32[]{:S(2)}, u32[]{:S(2)}) %collective-permute-start.62) | collective-permute-done | bytes 786464 | tf_op jit(solution)/shard_map/ppermute | solution.py:48
  654.3 6.6 collective-permute-done.63
  690.2 22.7 %adam.1 = (f32[3,256,512]{2,1,0:T(8,128)}, f32[3,256,512]{2,1,0:T(8,128)}, f32[3,256,512]{2,1,0:T(8,128)}, f32[256,512]{1,0:T(8,128)}, f32[256,512]{1,0:T(8,128)...) custom-call(s32[1]{0:T(128)} %bitcast.91.place_ref, ...), custom_call_target="tpu_custom_call" | custom-call | flops 41943040 | bytes 50331648 | tf_op jit(solution)/shard_map/adam/pallas_call | solution.py:597
  (558 shorter events, 312.3 us)
Async XLA Ops:
  7.2 140.3 %all-gather.4.cloned.1.call-start = ((), (), s32[]{:S(2)}) async-start(), calls=%async_computation.3 | async-start | bytes 5242880 | tf_op jit(solution)/shard_map/all_gather | solution.py:679
  26.8 256.8 %all-gather.6.cloned.1.call-start = ((), (), s32[]{:S(2)}) async-start(), calls=%async_computation.4 | async-start | bytes 7864320 | tf_op jit(solution)/shard_map/all_gather | solution.py:679
  30.9 48.6 %collective-permute-start.8 = (bf16[128,2048]{1,0:T(8,128)(2,1)S(1)}, bf16[128,2048]{1,0:T(8,128)(2,1)}, u32[]{:S(2)}, u32[]{:S(2)}) collective-permute-start(bf16[128,2048]{1,0:T(8,128)(2,1)S(1)} %get-tuple-element.97), channel_id=1, source_target_pairs={{0,2},{2,0},{1,3},{3,1},{4,6},{6,4},{5,7},{7,5},{8,10},{10,8},{9,1... | collective-permute-start | bytes 1572872 | tf_op jit(solution)/shard_map/ppermute | solution.py:48
  43.2 24.4 %collective-permute-start.2 = (bf16[128,2048]{1,0:T(8,128)(2,1)}, bf16[128,2048]{1,0:T(8,128)(2,1)}, u32[]{:S(2)}, u32[]{:S(2)}) collective-permute-start(bf16[128,2048]{1,0:T(8,128)(2,1)} %get-tuple-element.94), channel_id=1, source_target_pairs={{0,4},{4,0},{1,5},{5,1},{2,6},{6,2},{3,7},{7,3},{8,12},{12,8},{9,1... | collective-permute-start | bytes 1572872 | tf_op jit(solution)/shard_map/ppermute | solution.py:48
  44.3 32.1 %collective-permute-start.3 = (bf16[128,2048]{1,0:T(8,128)(2,1)}, bf16[128,2048]{1,0:T(8,128)(2,1)}, u32[]{:S(2)}, u32[]{:S(2)}) collective-permute-start(bf16[128,2048]{1,0:T(8,128)(2,1)} %collective-permute-done), channel_id=1, source_target_pairs={{0,4},{4,0},{1,5},{5,1},{2,6},{6,2},{3,7},{7,3},{8,12},{12,8},{9,1... | collective-permute-start | bytes 1572872 | tf_op jit(solution)/shard_map/ppermute | solution.py:48
  56.4 23.1 %collective-permute-start.9 = (bf16[128,2048]{1,0:T(8,128)(2,1)}, bf16[128,2048]{1,0:T(8,128)(2,1)S(1)}, u32[]{:S(2)}, u32[]{:S(2)}) collective-permute-start(bf16[128,2048]{1,0:T(8,128)(2,1)} %collective-permute-done.7), channel_id=1, source_target_pairs={{0,2},{2,0},{1,3},{3,1},{4,6},{6,4},{5,7},{7,5},{8,10},{10,8},{9,1... | collective-permute-start | bytes 1572872 | tf_op jit(solution)/shard_map/ppermute | solution.py:48
  58.4 25.5 %collective-permute-start.4 = (s32[2,4,32]{2,1,0:T(4,128)S(1)}, s32[2,4,32]{2,1,0:T(4,128)S(1)}, u32[]{:S(2)}, u32[]{:S(2)}) collective-permute-start(s32[2,4,32]{2,1,0:T(4,128)S(1)} %bitcast.487), channel_id=1, source_target_pairs={{0,2},{2,0},{1,3},{3,1},{4,6},{6,4},{5,7},{7,5},{8,10},{10,8},{9,1... | collective-permute-start | bytes 3080 | tf_op jit(solution)/shard_map/ppermute | solution.py:48
  82.4 22.1 %collective-permute-start.24 = (bf16[256,1536]{1,0:T(8,128)(2,1)}, bf16[256,1536]{1,0:T(8,128)(2,1)}, u32[]{:S(2)}, u32[]{:S(2)}) collective-permute-start(bf16[256,1536]{1,0:T(8,128)(2,1)} %pad_maximum_fusion.10), channel_id=1, source_target_pairs={{0,4},{4,0},{1,5},{5,1},{2,6},{6,2},{3,7},{7,3},{8,12},{12,8},{9,1... | collective-permute-start | bytes 2359304 | tf_op jit(solution)/shard_map/ppermute | solution.py:48
  100.0 52.0 %collective-permute-start.26 = (bf16[512,2048]{1,0:T(8,128)(2,1)}, bf16[512,2048]{1,0:T(8,128)(2,1)}, u32[]{:S(2)}, u32[]{:S(2)}) collective-permute-start(bf16[512,2048]{1,0:T(8,128)(2,1)} %pad_maximum_fusion.1.refs_2_), channel_id=1, source_target_pairs={{0,1},{1,0},{2,3},{3,2},{4,5},{5,4},{6,7},{7,6},{8,9},{9,8},{10,11... | collective-permute-start | bytes 6291464 | tf_op jit(solution)/shard_map/ppermute | solution.py:48
  105.8 39.7 %collective-permute-start.25 = (bf16[256,1536]{1,0:T(8,128)(2,1)}, bf16[256,1536]{1,0:T(8,128)(2,1)}, u32[]{:S(2)}, u32[]{:S(2)}) collective-permute-start(bf16[256,1536]{1,0:T(8,128)(2,1)} %pad_maximum_fusion.11), channel_id=1, source_target_pairs={{0,4},{4,0},{1,5},{5,1},{2,6},{6,2},{3,7},{7,3},{8,12},{12,8},{9,1... | collective-permute-start | bytes 2359304 | tf_op jit(solution)/shard_map/ppermute | solution.py:48
  109.8 33.0 %collective-permute-start.10 = (bf16[128,2048]{1,0:T(8,128)(2,1)}, bf16[128,2048]{1,0:T(8,128)(2,1)}, u32[]{:S(2)}, u32[]{:S(2)}) collective-permute-start(bf16[128,2048]{1,0:T(8,128)(2,1)} %bitcast.5), channel_id=1, source_target_pairs={{0,2},{2,0},{1,3},{3,1},{4,6},{6,4},{5,7},{7,5},{8,10},{10,8},{9,1... | collective-permute-start | bytes 1572872 | tf_op jit(solution)/shard_map/ppermute | solution.py:48
  110.7 240.3 %all-gather.8.cloned.1.call-start = ((), (), s32[]{:S(2)}) async-start(), calls=%async_computation.5 | async-start | bytes 7864320 | tf_op jit(solution)/shard_map/all_gather | solution.py:679
  115.1 27.7 %collective-permute-start.11 = (bf16[128,2048]{1,0:T(8,128)(2,1)}, bf16[128,2048]{1,0:T(8,128)(2,1)}, u32[]{:S(2)}, u32[]{:S(2)}) collective-permute-start(bf16[128,2048]{1,0:T(8,128)(2,1)} %bitcast.5), channel_id=1, source_target_pairs={{0,4},{4,0},{1,5},{5,1},{2,6},{6,2},{3,7},{7,3},{8,12},{12,8},{9,1... | collective-permute-start | bytes 1572872 | tf_op jit(solution)/shard_map/ppermute | solution.py:48
  123.7 43.3 %collective-permute-start.14 = (bf16[512,2048]{1,0:T(8,128)(2,1)}, bf16[512,2048]{1,0:T(8,128)(2,1)}, u32[]{:S(2)}, u32[]{:S(2)}) collective-permute-start(bf16[512,2048]{1,0:T(8,128)(2,1)} %pad_maximum_fusion.refs_0_), channel_id=1, source_target_pairs={{0,1},{1,0},{2,3},{3,2},{4,5},{5,4},{6,7},{7,6},{8,9},{9,8},{10,11... | collective-permute-start | bytes 6291464 | tf_op jit(solution)/shard_map/ppermute | solution.py:48
  180.8 25.2 %collective-permute-start.29 = (bf16[2,128,2048]{2,1,0:T(8,128)(2,1)S(1)}, bf16[2,128,2048]{2,1,0:T(8,128)(2,1)S(1)}, u32[]{:S(2)}, u32[]{:S(2)}) collective-permute-start(bf16[2,128,2048]{2,1,0:T(8,128)(2,1)S(1)} %bitcast.468), channel_id=1, source_target_pairs={{0,2},{2,0},{1,3},{3,1},{4,6},{6,4},{5,7},{7,5},{8,10},{10,8},{9,1... | collective-permute-start | bytes 3145736 | tf_op jit(solution)/shard_map/ppermute | solution.py:48
  184.8 26.2 %collective-permute-start.16 = (bf16[2,128,2048]{2,1,0:T(8,128)(2,1)}, bf16[2,128,2048]{2,1,0:T(8,128)(2,1)}, u32[]{:S(2)}, u32[]{:S(2)}) collective-permute-start(bf16[2,128,2048]{2,1,0:T(8,128)(2,1)} %bitcast.23), channel_id=1, source_target_pairs={{0,4},{4,0},{1,5},{5,1},{2,6},{6,2},{3,7},{7,3},{8,12},{12,8},{9,1... | collective-permute-start | bytes 3145736 | tf_op jit(solution)/shard_map/ppermute | solution.py:48
  208.4 336.3 %reduce-scatter.4.cloned.1.call-start = ((), (), s32[]{:S(2)}) async-start(), calls=%async_computation.6 | async-start | bytes 7864320 | tf_op jit(solution)/shard_map/reduce_scatter | solution.py:787
  243.3 40.3 %collective-permute-start.23 = (bf16[512,2048]{1,0:T(8,128)(2,1)S(1)}, bf16[512,2048]{1,0:T(8,128)(2,1)}, u32[]{:S(2)}, u32[]{:S(2)}) collective-permute-start(bf16[512,2048]{1,0:T(8,128)(2,1)S(1)} %constant_dynamic-update-slice_fusion.g_mine.refs_4_), channel_id=1, source_target_pairs={{0,1},{1,0},{2,3},{3,2},{4,5},{5,4},{6,7},{7,6},{8,9},{9,8},{10,11... | collective-permute-start | bytes 6291464 | tf_op jit(solution)/shard_map/ppermute | solution.py:48
  254.5 29.1 %collective-permute-start.21 = (bf16[512,2048]{1,0:T(8,128)(2,1)S(1)}, bf16[512,2048]{1,0:T(8,128)(2,1)}, u32[]{:S(2)}, u32[]{:S(2)}) collective-permute-start(bf16[512,2048]{1,0:T(8,128)(2,1)S(1)} %pad_maximum_fusion.2.x_mine.refs_0_), channel_id=1, source_target_pairs={{0,1},{1,0},{2,3},{3,2},{4,5},{5,4},{6,7},{7,6},{8,9},{9,8},{10,11... | collective-permute-start | bytes 6291464 | tf_op jit(solution)/shard_map/ppermute | solution.py:48
  270.5 25.3 %collective-permute-start.35 = (bf16[512,2048]{1,0:T(8,128)(2,1)}, bf16[512,2048]{1,0:T(8,128)(2,1)}, u32[]{:S(2)}, u32[]{:S(2)}) collective-permute-start(bf16[512,2048]{1,0:T(8,128)(2,1)} %constant_dynamic-update-slice_fusion.4.g_mine.refs_6_), channel_id=1, source_target_pairs={{0,1},{1,0},{2,3},{3,2},{4,5},{5,4},{6,7},{7,6},{8,9},{9,8},{10,11... | collective-permute-start | bytes 6291464 | tf_op jit(solution)/shard_map/ppermute | solution.py:48
  328.1 300.4 %reduce-scatter.6.cloned.1.call-start = ((), (), s32[]{:S(2)}) async-start(), calls=%async_computation.7 | async-start | bytes 7864320 | tf_op jit(solution)/shard_map/reduce_scatter | solution.py:787
  395.0 25.5 %collective-permute-start.37 = (bf16[2,128,2048]{2,1,0:T(8,128)(2,1)S(1)}, bf16[2,128,2048]{2,1,0:T(8,128)(2,1)S(1)}, u32[]{:S(2)}, u32[]{:S(2)}) collective-permute-start(bf16[2,128,2048]{2,1,0:T(8,128)(2,1)S(1)} %bitcast.466), channel_id=1, source_target_pairs={{0,4},{4,0},{1,5},{5,1},{2,6},{6,2},{3,7},{7,3},{8,12},{12,8},{9,1... | collective-permute-start | bytes 3145736 | tf_op jit(solution)/shard_map/ppermute | solution.py:48
  397.3 26.3 %collective-permute-start.39 = (bf16[2,128,2048]{2,1,0:T(8,128)(2,1)S(1)}, bf16[2,128,2048]{2,1,0:T(8,128)(2,1)S(1)}, u32[]{:S(2)}, u32[]{:S(2)}) collective-permute-start(bf16[2,128,2048]{2,1,0:T(8,128)(2,1)S(1)} %bitcast.467), channel_id=1, source_target_pairs={{0,2},{2,0},{1,3},{3,1},{4,6},{6,4},{5,7},{7,5},{8,10},{10,8},{9,1... | collective-permute-start | bytes 3145736 | tf_op jit(solution)/shard_map/ppermute | solution.py:48
  443.7 220.6 %reduce-scatter.8.cloned.1.call-start = ((), (), s32[]{:S(2)}) async-start(), calls=%async_computation.8 | async-start | bytes 5242880 | tf_op jit(solution)/shard_map/reduce_scatter | solution.py:787
  460.8 26.5 %collective-permute-start.42 = (bf16[512,2048]{1,0:T(8,128)(2,1)}, bf16[512,2048]{1,0:T(8,128)(2,1)S(1)}, u32[]{:S(2)}, u32[]{:S(2)}) collective-permute-start(bf16[512,2048]{1,0:T(8,128)(2,1)} %get-tuple-element.129), channel_id=1, source_target_pairs={{0,1},{1,0},{2,3},{3,2},{4,5},{5,4},{6,7},{7,6},{8,9},{9,8},{10,11... | collective-permute-start | bytes 6291464 | tf_op jit(solution)/shard_map/ppermute | solution.py:48
  472.0 26.0 %collective-permute-start.54 = (bf16[128,2048]{1,0:T(8,128)(2,1)S(1)}, bf16[128,2048]{1,0:T(8,128)(2,1)S(1)}, u32[]{:S(2)}, u32[]{:S(2)}) collective-permute-start(bf16[128,2048]{1,0:T(8,128)(2,1)S(1)} %get-tuple-element.140), channel_id=1, source_target_pairs={{0,2},{2,0},{1,3},{3,1},{4,6},{6,4},{5,7},{7,5},{8,10},{10,8},{9,1... | collective-permute-start | bytes 1572872 | tf_op jit(solution)/shard_map/ppermute | solution.py:48
  484.3 23.6 %collective-permute-start.46 = (bf16[128,2048]{1,0:T(8,128)(2,1)S(1)}, bf16[128,2048]{1,0:T(8,128)(2,1)S(1)}, u32[]{:S(2)}, u32[]{:S(2)}) collective-permute-start(bf16[128,2048]{1,0:T(8,128)(2,1)S(1)} %collective-permute-done.45), channel_id=1, source_target_pairs={{0,2},{2,0},{1,3},{3,1},{4,6},{6,4},{5,7},{7,5},{8,10},{10,8},{9,1... | collective-permute-start | bytes 1572872 | tf_op jit(solution)/shard_map/ppermute | solution.py:48
  508.7 54.4 %collective-permute-start.47 = (bf16[2,128,2048]{2,1,0:T(8,128)(2,1)S(1)}, bf16[2,128,2048]{2,1,0:T(8,128)(2,1)}, u32[]{:S(2)}, u32[]{:S(2)}) collective-permute-start(bf16[2,128,2048]{2,1,0:T(8,128)(2,1)S(1)} %bitcast.464), channel_id=1, source_target_pairs={{0,4},{4,0},{1,5},{5,1},{2,6},{6,2},{3,7},{7,3},{8,12},{12,8},{9,1... | collective-permute-start | bytes 3145736 | tf_op jit(solution)/shard_map/ppermute | solution.py:48
  510.1 53.0 %collective-permute-start.52 = (bf16[2,128,2048]{2,1,0:T(8,128)(2,1)}, bf16[2,128,2048]{2,1,0:T(8,128)(2,1)}, u32[]{:S(2)}, u32[]{:S(2)}) collective-permute-start(bf16[2,128,2048]{2,1,0:T(8,128)(2,1)} %bitcast.58), channel_id=1, source_target_pairs={{0,2},{2,0},{1,3},{3,1},{4,6},{6,4},{5,7},{7,5},{8,10},{10,8},{9,1... | collective-permute-start | bytes 3145736 | tf_op jit(solution)/shard_map/ppermute | solution.py:48
  590.8 58.2 %collective-permute-start.51 = (bf16[128,2048]{1,0:T(8,128)(2,1)}, bf16[128,2048]{1,0:T(8,128)(2,1)}, u32[]{:S(2)}, u32[]{:S(2)}) collective-permute-start(bf16[128,2048]{1,0:T(8,128)(2,1)} %fusion.90), channel_id=1, source_target_pairs={{0,2},{2,0},{1,3},{3,1},{4,6},{6,4},{5,7},{7,5},{8,10},{10,8},{9,1... | collective-permute-start | bytes 1572872 | tf_op jit(solution)/shard_map/ppermute | solution.py:48
  603.7 24.8 %collective-permute-start.58 = (bf16[2,128,2048]{2,1,0:T(8,128)(2,1)S(1)}, bf16[2,128,2048]{2,1,0:T(8,128)(2,1)S(1)}, u32[]{:S(2)}, u32[]{:S(2)}) collective-permute-start(bf16[2,128,2048]{2,1,0:T(8,128)(2,1)S(1)} %bitcast.465), channel_id=1, source_target_pairs={{0,4},{4,0},{1,5},{5,1},{2,6},{6,2},{3,7},{7,3},{8,12},{12,8},{9,1... | collective-permute-start | bytes 3145736 | tf_op jit(solution)/shard_map/ppermute | solution.py:48
  608.6 26.1 %collective-permute-start.61 = (bf16[2,128,2048]{2,1,0:T(8,128)(2,1)}, bf16[2,128,2048]{2,1,0:T(8,128)(2,1)}, u32[]{:S(2)}, u32[]{:S(2)}) collective-permute-start(bf16[2,128,2048]{2,1,0:T(8,128)(2,1)} %bitcast.80), channel_id=1, source_target_pairs={{0,2},{2,0},{1,3},{3,1},{4,6},{6,4},{5,7},{7,5},{8,10},{10,8},{9,1... | collective-permute-start | bytes 3145736 | tf_op jit(solution)/shard_map/ppermute | solution.py:48
  (166 other events, 2168.2 us)
Sparse Core Ops, SparseCore 0:
  26.9 82.2 all-gather.3
  111.4 115.7 all-gather.5
  229.3 113.5 all-gather.7
  345.0 108.9 reduce-scatter.3
  456.2 111.2 reduce-scatter.5
  580.2 77.2 reduce-scatter.7

commit v6 on v5

--- a/solution.py
+++ b/solution.py
@@ -89,19 +89,25 @@
     return keep + swap(send, inner).astype(F32)
 
 
+def tie_pair(pair, *earlier):
+    return pair[0], tie(pair[1], *earlier)
+
+
 def tie_send(state, *earlier):
     return state[0], tie(state[1], *earlier)
 
 
 def sum_everywhere(tensor, z_count, beside):
+    def add(tensor, axis, pairs):
+        return tensor + lax.ppermute(tensor, axis, pairs)
+
+    tensor = add(tensor, "x", [(0, 1), (1, 0)])
     reach = 1
     while reach < z_count:
-        tensor = tensor + lax.ppermute(tensor, "z", [(i, i ^ reach) for i in range(z_count)])
+        tensor = add(tensor, "z", [(i, i ^ reach) for i in range(z_count)])
         reach *= 2
-    tensor = tie(tensor + swap(tensor, "c"), beside)
-    for axis in ("y", "x"):
-        tensor = tensor + swap(tensor, axis)
-    return tensor
+    tensor = add(tensor, "c", [(0, 1), (1, 0)])
+    return add(tie(tensor, beside), "y", [(0, 1), (1, 0)])
 
 
 def mm(a, b, dims):
@@ -516,10 +522,10 @@
 
 
 def adam_kernel(steps, chunks, place_ref, small_ref, *refs):
-    ins, refs = refs[:15], refs[15:]
+    ins, refs = refs[:18], refs[18:]
     grads, refs = refs[: 2 + 2 * chunks], refs[2 + 2 * chunks :]
-    outs, scratch = refs[:15], refs[15]
-    factor = clip_factor(small_ref[...])[1]
+    outs, norm_ref, scratch = refs[:18], refs[18], refs[19]
+    grad_norm, factor = clip_factor(small_ref[...])
     is_low = place_ref[0] == 0
     everything = slice(None)
 
@@ -555,8 +561,11 @@
     put(2, (everything, everything), scratch[...], RATE_QKV)
 
     @pl.when(pl.program_id(0) == 0)
-    def gains():
-        put(4, (everything, everything), small_ref[: ins[12].shape[0]], 0.5, 0.0)
+    def small_ones():
+        last = ins[12].shape[0]
+        put(4, (everything, everything), small_ref[:last], 0.5, 0.0)
+        put(5, (everything, everything), small_ref[last:, :HEADS], 1.0, 0.0)
+        norm_ref[...] = grad_norm
 
 
 def mlp_view(t):
@@ -578,7 +587,7 @@
 
     views = [qkv_view(t) for t in arrays[:3]] + list(arrays[3:6])
     views += [mlp_view(t) for t in arrays[6:9]] + list(arrays[9:12])
-    gains = [mlp_view(t[None]) for t in arrays[12:]]
+    gains = [mlp_view(t[None]) for t in arrays[12:15]] + [t[None] for t in arrays[15:]]
     grads = list(att_sides) + [t for pair in ff_sides for t in pair]
 
     def spec(t):
@@ -602,10 +611,11 @@
             in_specs=[whole(small)]
             + specs
             + [spec(t) if k % 2 else mine(t) for k, t in enumerate(grads)],
-            out_specs=specs,
+            out_specs=specs + [pl.BlockSpec((1, 1), lambda i, place: (0, 0))],
             scratch_shapes=[pltpu.VMEM((views[6].shape[0] // steps, 128), F32)],
         ),
-        out_shape=[jax.ShapeDtypeStruct(t.shape, F32) for t in views + gains],
+        out_shape=[jax.ShapeDtypeStruct(t.shape, F32) for t in views + gains]
+        + [jax.ShapeDtypeStruct((1, 1), F32)],
         compiler_params=pltpu.CompilerParams(vmem_limit_bytes=VMEM_LIMIT),
         cost_estimate=pl.CostEstimate(
             flops=20 * sum(t.size for t in views) // 3,
@@ -620,7 +630,9 @@
         + new[3:6]
         + [mlp_back(t, arrays[6].shape) for t in new[6:9]]
         + new[9:12]
-        + [mlp_back(t, (1,) + arrays[12].shape)[0] for t in new[12:]]
+        + [mlp_back(t, (1,) + arrays[12].shape)[0] for t in new[12:15]]
+        + [t[0] for t in new[15:18]]
+        + [new[18].reshape(())]
     )
 
 
@@ -652,7 +664,6 @@
     x_place = lax.axis_index("x")
     y_place = lax.axis_index("y")
     c_place = lax.axis_index("c")
-    is_low = x_place == 0
     orders = [("x", "y") if m % 2 == 0 else ("y", "x") for m in range(micro_count)]
 
     z_count = D // (2 * weight_qkv.shape[0])
@@ -661,16 +672,7 @@
         width = weight.shape[-1] // 2
         return lax.dynamic_slice_in_dim(weight, which * width, width, axis=weight.ndim - 1)
 
-    def by_place(own, other, axis):
-        return jnp.where(
-            is_low,
-            jnp.concatenate([own, other], axis=axis),
-            jnp.concatenate([other, own], axis=axis),
-        )
-
-    def exchange_rows(columns_for, send, *earlier):
-        theirs = swap(tie(send, *earlier), "x")
-        mine = columns_for(x_place)
+    def join_rows(mine, theirs):
         both = jnp.zeros((2 * rows, mine.shape[1]), BF)
         both = lax.dynamic_update_slice_in_dim(both, mine, x_place * rows, axis=0)
         return lax.dynamic_update_slice_in_dim(both, theirs, (1 - x_place) * rows, axis=0)
@@ -684,21 +686,23 @@
     width_ff = weight_down.shape[1] // 2
     width = width_ff // CHUNKS
 
-    def att_columns(which):
-        qkv = half_columns(weight_qkv, which).astype(BF).reshape(rows, -1)
-        return jnp.concatenate([qkv, half_columns(weight_out, which).astype(BF)], axis=1)
+    def qkv_columns(which):
+        return half_columns(weight_qkv, which).astype(BF).reshape(rows, -1)
 
     def ff_columns(k, which):
         start = which * width_ff + k * width
-        mlp = lax.dynamic_slice_in_dim(weight_mlp, start, width, axis=2).astype(BF)
-        down = lax.dynamic_slice_in_dim(weight_down, start, width, axis=1).astype(BF)
+        mlp = lax.dynamic_slice_in_dim(mlp_later, start, width, axis=2).astype(BF)
+        down = lax.dynamic_slice_in_dim(down_later, start, width, axis=1).astype(BF)
         return jnp.concatenate([mlp[:, 0], mlp[:, 1], down], axis=1)
 
-    send_att = att_columns(1 - x_place)
-    shard_att = exchange_rows(att_columns, send_att)
-    full_att = fetch(shard_att)
-    full_qkv = full_att[:, : 3 * width_att]
-    full_out = full_att[:, 3 * width_att :]
+    send_qkv = qkv_columns(1 - x_place)
+    all_out = fetch(weight_out.astype(BF))
+    all_ids = doc_ids[:, 0]
+    for axis in ("y", "c"):
+        all_ids = jnp.stack([all_ids, swap(all_ids, axis)], axis=0)
+    their_qkv = swap(send_qkv, "x")
+    shard_qkv = join_rows(qkv_columns(x_place), tie(their_qkv, all_ids))
+    full_qkv = fetch(shard_qkv)
 
     head_start = (y_place * 2 + c_place) * (2 * heads) + x_place * heads
     gate_local = lax.dynamic_slice_in_dim(gate_logit, head_start, heads)
@@ -708,24 +712,42 @@
     micros = range(micro_count)
     tokens = 8 * own_tokens
     token_rows = [
-        tie(inputs[m, 0], send_att).reshape(own_tokens, D).astype(F32) for m in micros
+        tie(inputs[m, 0], send_qkv).reshape(own_tokens, D).astype(F32) for m in micros
     ]
     back_low = [cotangent[m, 0].reshape(own_tokens, D) for m in micros]
-    all_ids = tie(doc_ids[:, 0], shard_att)
-    for axis in ("y", "c", "x"):
-        all_ids = jnp.stack([all_ids, swap(all_ids, axis)], axis=0)
+    all_ids = jnp.stack([all_ids, swap(all_ids, "x")], axis=0)
     normed_att = [rms_norm(t, norm_gains[0]).astype(BF) for t in token_rows]
-    att_rows = [
-        gather_tokens(normed_att[m], *orders[m], shard_att) for m in micros
-    ]
-
+    att_states = [gather_start(normed_att[m], *orders[m], their_qkv, all_ids) for m in micros]
+    mlp_later = tie(weight_mlp, *[t for state in att_states for t in state[1:]])
+    down_later = tie(weight_down, *[t for state in att_states for t in state[1:]])
+    att_states = [gather_across(att_states[m], orders[m][0]) for m in micros]
+    att_rows = [gather_core(state) for state in att_states]
+
+    att_last = [state[-1] for state in att_states]
+    back_states = [gather_start(tie(back_low[m], *att_last), *orders[m]) for m in micros]
+    back_first = [t for state in back_states for t in state[1:]]
     shard_ff = []
     full_ff = []
+    earlier = back_first
     for k in range(CHUNKS):
-        columns_for = functools.partial(ff_columns, k)
-        earlier = [p[0] for p in att_rows] if k == 0 else [shard_ff[-1]]
-        shard_ff.append(exchange_rows(columns_for, columns_for(1 - x_place), *earlier))
-        full_ff.append(fetch(shard_ff[-1]))
+        theirs = swap(tie(ff_columns(k, 1 - x_place), *earlier), "x")
+        shard_ff.append(join_rows(ff_columns(k, x_place), theirs))
+        full_ff.append(fetch(shard_ff[k]))
+        if k == 0:
+            their_out = swap(tie(half_columns(all_out, 1 - x_place), theirs), "x")
+            both_out = jnp.zeros((z_count, 2, rows, width_att), BF)
+            for part, place in ((half_columns(all_out, x_place), x_place), (their_out, 1 - x_place)):
+                part = part.reshape(z_count, 1, rows, width_att)
+                both_out = lax.dynamic_update_slice_in_dim(both_out, part, place, axis=1)
+            full_out = both_out.reshape(D, width_att)
+            back_states = [
+                gather_across((state[0], tie(state[1], their_out), state[2]), orders[m][0])
+                for m, state in enumerate(back_states)
+            ]
+            earlier = [state[-1] for state in back_states]
+        else:
+            earlier = [theirs]
+    back_rows = [gather_core(state) for state in back_states]
 
     rel_c = jnp.arange(2)[:, None, None] ^ c_place
     rel_y = jnp.arange(2)[None, :, None] ^ y_place
@@ -750,21 +772,15 @@
     combined = []
     hidden = []
     mlp_rows = []
-    back_states = [
-        gather_start(tie(back_low[m], all_ids, *[p[0] for p in att_rows]), *orders[m])
-        for m in micros
-    ]
     for m in micros:
         mine, other = att_rows[m]
         if m == 0:
-            mine = tie(mine, *[t for state in back_states for t in state])
+            mine = tie(mine, *back_first, shard_ff[0])
         proj = jnp.concatenate([mm(p, full_qkv, NN).astype(BF) for p in (mine, other)], axis=0)
         projected.append(proj.reshape(slots + (3 * width_att,)))
         comb = attention_fwd(projected[m], masks[m], columns[m], gate_rows, wheres[m])
         combined.append(comb.reshape(tokens, width_att))
     half = tokens // 2
-    back_states = [gather_across(back_states[m], orders[m][0]) for m in micros]
-    back_rows = [gather_core(state) for state in back_states]
     for m in micros:
         ready = combined[m]
         if m > 0:
@@ -820,7 +836,13 @@
             terms = [t for pair in d_total for t in pair]
             full_ff[k + 1] = tie(full_ff[k + 1], grad_ff, *terms)
 
-    outer_states = [scatter_outer(states[m], orders[m][0]) for m in micros]
+    out_pairs = []
+    for m in micros:
+        act = [active[k][m] for k in range(CHUNKS)]
+        act[-1] = (act[-1][0], tie(act[-1][1], states[-1][1]))
+        out_pairs.append(down_product(act, full_ff))
+    products_done = [t for pair in out_pairs for t in pair]
+    outer_states = [scatter_outer(states[m], orders[m][0], *products_done) for m in micros]
     last_active = [
         (active[-1][m][0], tie(active[-1][m][1], *[t[1] for t in outer_states])) for m in micros
     ]
@@ -843,12 +865,7 @@
 
     gate_sum = jnp.zeros((heads,), F32)
     d_projs = []
-    out_states = []
-    for m in micros:
-        act = [active[k][m] for k in range(CHUNKS)]
-        act[-1] = (last_active[m][0], tie(last_active[m][1], *d_hidden))
-        mine, other = down_product(act, full_ff)
-        out_states.append(scatter_core(mine, other, own_tokens))
+    out_states = [scatter_core(*tie_pair(out_pairs[m], *d_hidden), own_tokens) for m in micros]
     sends = [t[1] for t in out_states]
     out_states = [tie_send(t, *[g[-1] for g in grad_states]) for t in out_states]
     att_grads = [gather_core((tie(g[0], *sends),) + g[1:]) for g in grad_states]
@@ -925,19 +942,17 @@
         norm_gains,
         moment_gains,
         second_gains,
+        gate_logit,
+        moment_gate,
+        second_gate,
     ]
     new = adam_all(small, x_place, arrays, (att_mine, att_theirs), ff_pairs)
-    new = [new[3 * n + k] for n in range(5) for k in (0, 1, 2)]
-    grad_norm, factor = (t.reshape(()) for t in clip_factor(tie(small, new[0])))
-    gate_total = small[-1, :HEADS]
-    gate_new = adam_update(gate_logit, moment_gate, second_gate, gate_total, factor, 1.0, 0.0)
     shape = (micro_count, 1, seg_count, own_len, D)
     return (
         jnp.stack(block_out, axis=0).reshape(shape),
         jnp.stack(grad_rows, axis=0).reshape(shape),
-        grad_norm,
-        *new,
-        *gate_new,
+        new[-1],
+        *new[:-1],
     )
 
 

time: 731 us -> 737 us (level)
  waiting for transfers between devices: 250 us -> 258 us
    unnamed x264 -> x310, local copies, waits for them, and re-layouts: 26.2 us -> 17.5 us
    reduce_scatter x3, starting transfers between devices: 0.7 us -> 8.72 us  [reduce_rows(): return lax.psum_scatter(partial, 'z', scatter_dimension=0, tiled=True)]
    convert_element_type x7 -> x5, other arithmetic: 14.8 us -> 13.4 us  [scatter_core(): send = (mine[2:].astype(F32) + came[2:].astype(F32)).astype(BF)]
    ppermute x68 -> x66, waiting for transfers between devices: 248 us -> 248 us  [swap(): return lax.ppermute(tensor, axis, [(0, 1), (1, 0)])]
    ppermute x68 -> x66, starting transfers between devices: 54.1 us -> 53.4 us  [swap(): return lax.ppermute(tensor, axis, [(0, 1), (1, 0)])]
  transfers between devices with their start and end apart: 76 -> 78, of which waited for: 35 -> 39; matrix products, arithmetic and copies ran while one was open for 27% -> 27% of each run, Pallas kernels for 21% -> 21%
where the time goes in v6:
time: 737 us; the launch traced here: 729 us
  waiting for transfers between devices  258 us (35%)
  Pallas kernels  178 us (24%)
  other arithmetic  82 us (11%)
  matrix products  78.2 us (11%)
  starting transfers between devices  65.4 us (9%)
  local copies, waits for them, and re-layouts  48.7 us (7%)
  between operations  18.6 us (3%)
    ppermute x66, waiting for transfers between devices, swap(): return lax.ppermute(tensor, axis, [(0, 1), (1, 0)])  248 us
    dot_general x24, matrix products, mm(): return lax.dot_general(a, b, (dims, ((), ())), preferred_element_type=F32)  78.2 us
    ppermute x66, starting transfers between devices, swap(): return lax.ppermute(tensor, axis, [(0, 1), (1, 0)])  53.4 us
    pallas_call x4, Pallas kernels, feed_forward(): pl.pallas_call(functools.partial(ff_kernel, width, half), grid=(2 * half,...  49.8 us
    pallas_call x3, Pallas kernels, weight_grads(): pl.pallas_call(functools.partial(grads_kernel, count), grid=(D // tile,),...  49.7 us
    pallas_call x2, Pallas kernels, attention_bwd(): pl.pallas_call(functools.partial(attention_bwd_kernel, heads), grid=(seqs...  25.1 us
    pallas_call x1, Pallas kernels, adam_all(): pl.pallas_call(functools.partial(adam_kernel, steps, len(ff_sides)), grid...  22.7 us
    pallas_call x2, Pallas kernels, down_product(): pl.pallas_call(functools.partial(down_kernel, count, half), grid=(2 * hal...  17.7 us
  transfers between devices with their start and end apart: 78, of which 39 were waited for; matrix products, arithmetic and copies ran while one was open for 27% of the time, Pallas kernels for 21%

profile of v6, /device:TPU:0, one launch (start us, length us, event | category | flops | bytes accessed | tf_op | source)
XLA Modules:
  0.0 729.2 jit_solution(11587255694218630845)
XLA Ops:
  33.8 8.8 %collective-permute-done.7 = bf16[128,2048]{1,0:T(8,128)(2,1)S(1)} collective-permute-done((bf16[128,2048]{1,0:T(8,128)(2,1)S(1)}, bf16[128,2048]{1,0:T(8,128)(2,1)S(1)}, u32[]{:S(2)}, u32[]{:S(2)}) %collective-permute-start.7) | collective-permute-done | bytes 524320 | tf_op jit(solution)/shard_map/ppermute | solution.py:48
  44.5 9.4 %collective-permute-done.5 = bf16[128,2048]{1,0:T(8,128)(2,1)} collective-permute-done((bf16[128,2048]{1,0:T(8,128)(2,1)S(1)}, bf16[128,2048]{1,0:T(8,128)(2,1)}, u32[]{:S(2)}, u32[]{:S(2)}) %collective-permute-start.5) | collective-permute-done | bytes 524320 | tf_op jit(solution)/shard_map/ppermute | solution.py:48
  69.4 10.0 %collective-permute-done.11 = bf16[128,2048]{1,0:T(8,128)(2,1)S(1)} collective-permute-done((bf16[128,2048]{1,0:T(8,128)(2,1)S(1)}, bf16[128,2048]{1,0:T(8,128)(2,1)S(1)}, u32[]{:S(2)}, u32[]{:S(2)}) %collective-permute-start.11) | collective-permute-done | bytes 524320 | tf_op jit(solution)/shard_map/ppermute | solution.py:48
  79.4 8.1 %collective-permute-done.10 = bf16[128,2048]{1,0:T(8,128)(2,1)S(1)} collective-permute-done((bf16[128,2048]{1,0:T(8,128)(2,1)S(1)}, bf16[128,2048]{1,0:T(8,128)(2,1)S(1)}, u32[]{:S(2)}, u32[]{:S(2)}) %collective-permute-start.10) | collective-permute-done | bytes 524320 | tf_op jit(solution)/shard_map/ppermute | solution.py:48
  93.8 11.3 %collective-permute-done.14 = bf16[256,1536]{1,0:T(8,128)(2,1)S(1)} collective-permute-done((bf16[256,1536]{1,0:T(8,128)(2,1)}, bf16[256,1536]{1,0:T(8,128)(2,1)S(1)}, u32[]{:S(2)}, u32[]{:S(2)}) %collective-permute-start.14) | collective-permute-done | bytes 786464 | tf_op jit(solution)/shard_map/ppermute | solution.py:48
  110.1 7.1 collective-permute-done.16
  136.1 9.5 %collective-permute-done.27 = bf16[256,1536]{1,0:T(8,128)(2,1)} collective-permute-done((bf16[256,1536]{1,0:T(8,128)(2,1)}, bf16[256,1536]{1,0:T(8,128)(2,1)}, u32[]{:S(2)}, u32[]{:S(2)}) %collective-permute-start.27) | collective-permute-done | bytes 786464 | tf_op jit(solution)/shard_map/ppermute | solution.py:48
  186.8 19.8 %collective-permute-done.18 = bf16[2,128,2048]{2,1,0:T(8,128)(2,1)S(1)} collective-permute-done((bf16[2,128,2048]{2,1,0:T(8,128)(2,1)S(1)}, bf16[2,128,2048]{2,1,0:T(8,128)(2,1)S(1)}, u32[]{:S(2)}, u32[]{:S(2)}) %collective-permute-start.18) | collective-permute-done | bytes 1048608 | tf_op jit(solution)/shard_map/ppermute | solution.py:48
  210.1 8.4 %reduce-scatter.4.cloned.1.call-start = ((), (), s32[]{:S(2)}) async-start(), calls=%async_computation.7 | async-start | bytes 7864320 | tf_op jit(solution)/shard_map/reduce_scatter | solution.py:803
  222.8 10.7 %collective-permute-done.31 = bf16[128,2048]{1,0:T(8,128)(2,1)S(1)} collective-permute-done((bf16[128,2048]{1,0:T(8,128)(2,1)S(1)}, bf16[128,2048]{1,0:T(8,128)(2,1)S(1)}, u32[]{:S(2)}, u32[]{:S(2)}) %collective-permute-start.31) | collective-permute-done | bytes 524320 | tf_op jit(solution)/shard_map/ppermute | solution.py:48
  237.1 10.9 %collective-permute-done.20 = bf16[128,2048]{1,0:T(8,128)(2,1)S(1)} collective-permute-done((bf16[128,2048]{1,0:T(8,128)(2,1)S(1)}, bf16[128,2048]{1,0:T(8,128)(2,1)S(1)}, u32[]{:S(2)}, u32[]{:S(2)}) %collective-permute-start.20) | collective-permute-done | bytes 524320 | tf_op jit(solution)/shard_map/ppermute | solution.py:48
  251.4 11.5 %collective-permute-done.22 = bf16[128,2048]{1,0:T(8,128)(2,1)S(1)} collective-permute-done((bf16[128,2048]{1,0:T(8,128)(2,1)S(1)}, bf16[128,2048]{1,0:T(8,128)(2,1)S(1)}, u32[]{:S(2)}, u32[]{:S(2)}) %collective-permute-start.22) | collective-permute-done | bytes 524320 | tf_op jit(solution)/shard_map/ppermute | solution.py:48
  264.4 7.2 collective-permute-done.32
  278.7 10.8 %collective-permute-done.34 = bf16[128,2048]{1,0:T(8,128)(2,1)S(1)} collective-permute-done((bf16[128,2048]{1,0:T(8,128)(2,1)S(1)}, bf16[128,2048]{1,0:T(8,128)(2,1)S(1)}, u32[]{:S(2)}, u32[]{:S(2)}) %collective-permute-start.34) | collective-permute-done | bytes 524320 | tf_op jit(solution)/shard_map/ppermute | solution.py:48
  292.4 12.1 %feed_forward.4 = (bf16[512,512]{1,0:T(8,128)(2,1)S(1)}, bf16[512,512]{1,0:T(8,128)(2,1)S(1)}, bf16[512,1024]{1,0:T(8,128)(2,1)S(1)}, bf16[512,1024]{1,0:T(8,128)(2,1)S(1)}) custom-call(bf16[512,2048]{1,0:T(8,128)(2,1)S(1)} %pad_maximum_fusion.1.x_mine.refs_0_, bf16[512,2048]{1,0:T(8,128)(2,1)} %collective-permute-done.23.x_other.refs_1_, ...), custom_call_target="tpu_custom_call" | custom-call | flops 13958643712 | bytes 1048576 | tf_op jit(solution)/shard_map/feed_forward/pallas_call | solution.py:396
  304.6 12.8 %feed_forward.5 = (bf16[512,512]{1,0:T(8,128)(2,1)S(1)}, bf16[512,512]{1,0:T(8,128)(2,1)S(1)}, bf16[512,1024]{1,0:T(8,128)(2,1)S(1)}, bf16[512,1024]{1,0:T(8,128)(2,1)S(1)}) custom-call(bf16[512,2048]{1,0:T(8,128)(2,1)} %pad_maximum_fusion.3.x_mine.refs_2_, bf16[512,2048]{1,0:T(8,128)(2,1)} %collective-permute-done.35.x_other.refs_3_, ...), custom_call_target="tpu_custom_call" | custom-call | flops 13958643712 | bytes 1048576 | tf_op jit(solution)/shard_map/feed_forward/pallas_call | solution.py:396
  318.4 18.1 %weight_grads.3 = bf16[2048,1536]{1,0:T(8,128)(2,1)} custom-call(bf16[512,2048]{1,0:T(8,128)(2,1)} %copy-done.4, bf16[512,2048]{1,0:T(8,128)(2,1)} %collective-permute-done.23.x_other.refs_1_, bf16[512,2048]{1,0:T(8,128)(2,1)} %pad_maximum_fusion.3.x_mine.refs_2_, bf16[512,2048]{1,0:T(8,128)(2,1)} %collective-permute-done.35.x_other.refs_3_, ...), custom_call_target="tpu_custom_call" | custom-call | flops 19327352832 | bytes 29360128 | tf_op jit(solution)/shard_map/weight_grads/pallas_call | solution.py:492
  361.2 12.6 %feed_forward.6 = (bf16[512,512]{1,0:T(8,128)(2,1)S(1)}, bf16[512,512]{1,0:T(8,128)(2,1)S(1)}, bf16[512,1024]{1,0:T(8,128)(2,1)S(1)}, bf16[512,1024]{1,0:T(8,128)(2,1)S(1)}) custom-call(bf16[512,2048]{1,0:T(8,128)(2,1)S(1)} %copy-done.5, bf16[512,2048]{1,0:T(8,128)(2,1)} %collective-permute-done.23.x_other.refs_1_, bf16[512,2048]{1,0:T(8,128)(2,1)} %copy-done.109, ...), custom_call_target="tpu_custom_call" | custom-call | flops 13958643712 | bytes 1048576 | tf_op jit(solution)/shard_map/feed_forward/pallas_call | solution.py:396
  382.8 12.2 %feed_forward.7 = (bf16[512,512]{1,0:T(8,128)(2,1)S(1)}, bf16[512,512]{1,0:T(8,128)(2,1)S(1)}, bf16[512,1024]{1,0:T(8,128)(2,1)S(1)}, bf16[512,1024]{1,0:T(8,128)(2,1)S(1)}) custom-call(bf16[512,2048]{1,0:T(8,128)(2,1)} %pad_maximum_fusion.3.x_mine.refs_2_, bf16[512,2048]{1,0:T(8,128)(2,1)} %collective-permute-done.35.x_other.refs_3_, ...), custom_call_target="tpu_custom_call" | custom-call | flops 13958643712 | bytes 1048576 | tf_op jit(solution)/shard_map/feed_forward/pallas_call | solution.py:396
  412.5 8.5 %down_product.2 = (bf16[512,2048]{1,0:T(8,128)(2,1)S(1)}, bf16[512,2048]{1,0:T(8,128)(2,1)}) custom-call(bf16[512,512]{1,0:T(8,128)(2,1)S(1)} %get-tuple-element.118.refs_12_.refs_0_, bf16[512,512]{1,0:T(8,128)(2,1)S(1)} %get-tuple-element.130.refs_1_.refs_12_, bf16[512,512]{1,0:T(8,128)(2,1)S(1)} %get-tuple-element.126.refs_13_.refs_2_, ...), custom_call_target="tpu_custom_call" | custom-call | flops 4294967296 | bytes 8388608 | tf_op jit(solution)/shard_map/down_product/pallas_call | solution.py:441
  421.1 9.2 %down_product.3 = (bf16[512,2048]{1,0:T(8,128)(2,1)S(1)}, bf16[512,2048]{1,0:T(8,128)(2,1)}) custom-call(bf16[512,512]{1,0:T(8,128)(2,1)S(1)} %copy-done.36, bf16[512,512]{1,0:T(8,128)(2,1)S(1)} %get-tuple-element.141.refs_1_.refs_14_, bf16[512,512]{1,0:T(8,128)(2,1)S(1)} %copy-done.38, bf16[512,512]{1,0:T(8,128)(2,1)S(1)} %get-tuple-element.149.refs_3_.refs_15_, ...), custom_call_target="tpu_custom_call" | custom-call | flops 4294967296 | bytes 8388608 | tf_op jit(solution)/shard_map/down_product/pallas_call | solution.py:441
  440.4 18.3 %weight_grads.4 = bf16[2048,1536]{1,0:T(8,128)(2,1)} custom-call(bf16[512,2048]{1,0:T(8,128)(2,1)} %copy-done.4, bf16[512,2048]{1,0:T(8,128)(2,1)} %collective-permute-done.23.x_other.refs_1_, bf16[512,2048]{1,0:T(8,128)(2,1)} %pad_maximum_fusion.3.x_mine.refs_2_, bf16[512,2048]{1,0:T(8,128)(2,1)} %collective-permute-done.35.x_other.refs_3_, ...), custom_call_target="tpu_custom_call" | custom-call | flops 19327352832 | bytes 29360128 | tf_op jit(solution)/shard_map/weight_grads/pallas_call | solution.py:492
  469.9 11.4 %collective-permute-done.46 = bf16[128,2048]{1,0:T(8,128)(2,1)S(1)} collective-permute-done((bf16[128,2048]{1,0:T(8,128)(2,1)S(1)}, bf16[128,2048]{1,0:T(8,128)(2,1)S(1)}, u32[]{:S(2)}, u32[]{:S(2)}) %collective-permute-start.46) | collective-permute-done | bytes 524320 | tf_op jit(solution)/shard_map/ppermute | solution.py:48
  486.7 17.3 %collective-permute-done.47 = bf16[128,2048]{1,0:T(8,128)(2,1)S(1)} collective-permute-done((bf16[128,2048]{1,0:T(8,128)(2,1)S(1)}, bf16[128,2048]{1,0:T(8,128)(2,1)S(1)}, u32[]{:S(2)}, u32[]{:S(2)}) %collective-permute-start.47) | collective-permute-done | bytes 524320 | tf_op jit(solution)/shard_map/ppermute | solution.py:48
  507.9 11.0 %collective-permute-done.50 = bf16[128,2048]{1,0:T(8,128)(2,1)S(1)} collective-permute-done((bf16[128,2048]{1,0:T(8,128)(2,1)S(1)}, bf16[128,2048]{1,0:T(8,128)(2,1)S(1)}, u32[]{:S(2)}, u32[]{:S(2)}) %collective-permute-start.50) | collective-permute-done | bytes 524320 | tf_op jit(solution)/shard_map/ppermute | solution.py:48
  519.8 9.9 %collective-permute-done.45 = bf16[128,2048]{1,0:T(8,128)(2,1)S(1)} collective-permute-done((bf16[128,2048]{1,0:T(8,128)(2,1)S(1)}, bf16[128,2048]{1,0:T(8,128)(2,1)S(1)}, u32[]{:S(2)}, u32[]{:S(2)}) %collective-permute-start.45) | collective-permute-done | bytes 524320 | tf_op jit(solution)/shard_map/ppermute | solution.py:48
  537.9 12.8 %attention_backward.3 = (bf16[2,2,2,4,32,768]{5,4,3,2,1,0:T(8,128)(2,1)S(1)}, f32[2,2,128]{2,1,0:T(2,128)S(1)}) custom-call(bf16[2,2,2,4,32,768]{5,4,3,2,1,0:T(8,128)(2,1)S(1)} %bitcast.450, f32[2,2,2,4,32,256]{5,4,3,2,1,0:T(8,128)S(1)} %bitcast.452, f32[2,4,128,128]{3,2,1,0:T(8,128)S(1)} %copy-done.19, f32[2,4,128,3]{3,2,1,0:T(8,128)S(1)} %copy-done.13, ...), custom_call_target="tpu_custom_call" | custom-call | flops 14400000000 | bytes 5000000 | tf_op jit(solution)/shard_map/attention_backward/pallas_call | solution.py:323
  555.5 12.4 %attention_backward.2 = (bf16[2,2,2,4,32,768]{5,4,3,2,1,0:T(8,128)(2,1)S(1)}, f32[2,2,128]{2,1,0:T(2,128)S(1)}) custom-call(bf16[2,2,2,4,32,768]{5,4,3,2,1,0:T(8,128)(2,1)S(1)} %bitcast.448, f32[2,2,2,4,32,256]{5,4,3,2,1,0:T(8,128)S(1)} %bitcast.451, f32[2,4,128,128]{3,2,1,0:T(8,128)S(1)} %copy-done.17, f32[2,4,128,3]{3,2,1,0:T(8,128)S(1)} %copy-done.15, ...), custom_call_target="tpu_custom_call" | custom-call | flops 14400000000 | bytes 5000000 | tf_op jit(solution)/shard_map/attention_backward/pallas_call | solution.py:323
  577.1 13.2 %weight_grads.5 = bf16[2048,1024]{1,0:T(8,128)(2,1)} custom-call(bf16[512,2048]{1,0:T(8,128)(2,1)} %pad_maximum_fusion.refs_0_, bf16[512,2048]{1,0:T(8,128)(2,1)} %collective-permute-done.15.refs_1_, bf16[512,2048]{1,0:T(8,128)(2,1)} %pad_maximum_fusion.2.refs_2_, bf16[512,2048]{1,0:T(8,128)(2,1)} %collective-permute-done.28.refs_3_, ...), custom_call_target="tpu_custom_call" | custom-call | flops 12884901888 | bytes 25165824 | tf_op jit(solution)/shard_map/weight_grads/pallas_call | solution.py:492
  623.0 16.0 %collective-permute-done.59 = bf16[2,128,2048]{2,1,0:T(8,128)(2,1)} collective-permute-done((bf16[2,128,2048]{2,1,0:T(8,128)(2,1)S(1)}, bf16[2,128,2048]{2,1,0:T(8,128)(2,1)}, u32[]{:S(2)}, u32[]{:S(2)}) %collective-permute-start.59) | collective-permute-done | bytes 1048608 | tf_op jit(solution)/shard_map/ppermute | solution.py:48
  646.9 11.4 %collective-permute-done.63.refs_23_ = bf16[256,1536]{1,0:T(8,128)(2,1)S(1)} collective-permute-done((bf16[256,1536]{1,0:T(8,128)(2,1)S(1)}, bf16[256,1536]{1,0:T(8,128)(2,1)S(1)}, u32[]{:S(2)}, u32[]{:S(2)}) %collective-permute-start.63) | collective-permute-done | bytes 786464 | tf_op jit(solution)/shard_map/ppermute | solution.py:48
  699.4 22.7 %adam.1 = (f32[3,256,512]{2,1,0:T(8,128)}, f32[3,256,512]{2,1,0:T(8,128)}, f32[3,256,512]{2,1,0:T(8,128)}, f32[256,512]{1,0:T(8,128)}, f32[256,512]{1,0:T(8,128)...) custom-call(s32[1]{0:T(128)} %bitcast.88.place_ref, ...), custom_call_target="tpu_custom_call" | custom-call | flops 41943040 | bytes 50331648 | tf_op jit(solution)/shard_map/adam/pallas_call | solution.py:606
  (607 shorter events, 325.0 us)
Async XLA Ops:
  7.2 84.2 %all-gather.7.cloned.1.call-start = ((), (), s32[]{:S(2)}) async-start(), calls=%async_computation.4 | async-start | bytes 1310720 | tf_op jit(solution)/shard_map/all_gather | solution.py:681
  12.1 135.6 %all-gather.5.cloned.1.call-start = ((), (), s32[]{:S(2)}) async-start(), calls=%async_computation.3 | async-start | bytes 3932160 | tf_op jit(solution)/shard_map/all_gather | solution.py:681
  18.8 25.7 %collective-permute-start.13 = (bf16[128,2048]{1,0:T(8,128)(2,1)S(1)}, bf16[128,2048]{1,0:T(8,128)(2,1)}, u32[]{:S(2)}, u32[]{:S(2)}) collective-permute-start(bf16[128,2048]{1,0:T(8,128)(2,1)S(1)} %get-tuple-element.108), channel_id=1, source_target_pairs={{0,2},{2,0},{1,3},{3,1},{4,6},{6,4},{5,7},{7,5},{8,10},{10,8},{9,1... | collective-permute-start | bytes 1572872 | tf_op jit(solution)/shard_map/ppermute | solution.py:48
  27.5 264.9 %all-gather.9.cloned.1.call-start = ((), (), s32[]{:S(2)}) async-start(), calls=%async_computation.5 | async-start | bytes 7864320 | tf_op jit(solution)/shard_map/all_gather | solution.py:681
  29.4 24.5 %collective-permute-start.5 = (bf16[128,2048]{1,0:T(8,128)(2,1)S(1)}, bf16[128,2048]{1,0:T(8,128)(2,1)}, u32[]{:S(2)}, u32[]{:S(2)}) collective-permute-start(bf16[128,2048]{1,0:T(8,128)(2,1)S(1)} %get-tuple-element.106), channel_id=1, source_target_pairs={{0,4},{4,0},{1,5},{5,1},{2,6},{6,2},{3,7},{7,3},{8,12},{12,8},{9,1... | collective-permute-start | bytes 1572872 | tf_op jit(solution)/shard_map/ppermute | solution.py:48
  33.2 29.2 %collective-permute-start.6 = (bf16[128,2048]{1,0:T(8,128)(2,1)}, bf16[128,2048]{1,0:T(8,128)(2,1)S(1)}, u32[]{:S(2)}, u32[]{:S(2)}) collective-permute-start(bf16[128,2048]{1,0:T(8,128)(2,1)} %collective-permute-done), channel_id=1, source_target_pairs={{0,4},{4,0},{1,5},{5,1},{2,6},{6,2},{3,7},{7,3},{8,12},{12,8},{9,1... | collective-permute-start | bytes 1572872 | tf_op jit(solution)/shard_map/ppermute | solution.py:48
  63.2 24.3 %collective-permute-start.9 = (bf16[128,2048]{1,0:T(8,128)(2,1)S(1)}, bf16[128,2048]{1,0:T(8,128)(2,1)S(1)}, u32[]{:S(2)}, u32[]{:S(2)}) collective-permute-start(bf16[128,2048]{1,0:T(8,128)(2,1)S(1)} %bitcast.485), channel_id=1, source_target_pairs={{0,2},{2,0},{1,3},{3,1},{4,6},{6,4},{5,7},{7,5},{8,10},{10,8},{9,1... | collective-permute-start | bytes 1572872 | tf_op jit(solution)/shard_map/ppermute | solution.py:48
  122.2 30.1 %collective-permute-start.15 = (bf16[512,2048]{1,0:T(8,128)(2,1)}, bf16[512,2048]{1,0:T(8,128)(2,1)}, u32[]{:S(2)}, u32[]{:S(2)}) collective-permute-start(bf16[512,2048]{1,0:T(8,128)(2,1)} %pad_maximum_fusion.refs_0_), channel_id=1, source_target_pairs={{0,1},{1,0},{2,3},{3,2},{4,5},{5,4},{6,7},{7,6},{8,9},{9,8},{10,11... | collective-permute-start | bytes 6291464 | tf_op jit(solution)/shard_map/ppermute | solution.py:48
  129.7 231.4 %all-gather.11.cloned.1.call-start = ((), (), s32[]{:S(2)}) async-start(), calls=%async_computation.6 | async-start | bytes 7864320 | tf_op jit(solution)/shard_map/all_gather | solution.py:681
  134.9 28.5 %collective-permute-start.28 = (bf16[512,2048]{1,0:T(8,128)(2,1)}, bf16[512,2048]{1,0:T(8,128)(2,1)}, u32[]{:S(2)}, u32[]{:S(2)}) collective-permute-start(bf16[512,2048]{1,0:T(8,128)(2,1)} %pad_maximum_fusion.2.refs_2_), channel_id=1, source_target_pairs={{0,1},{1,0},{2,3},{3,2},{4,5},{5,4},{6,7},{7,6},{8,9},{9,8},{10,11... | collective-permute-start | bytes 6291464 | tf_op jit(solution)/shard_map/ppermute | solution.py:48
  181.0 25.6 %collective-permute-start.18 = (bf16[2,128,2048]{2,1,0:T(8,128)(2,1)S(1)}, bf16[2,128,2048]{2,1,0:T(8,128)(2,1)S(1)}, u32[]{:S(2)}, u32[]{:S(2)}) collective-permute-start(bf16[2,128,2048]{2,1,0:T(8,128)(2,1)S(1)} %bitcast.501), channel_id=1, source_target_pairs={{0,4},{4,0},{1,5},{5,1},{2,6},{6,2},{3,7},{7,3},{8,12},{12,8},{9,1... | collective-permute-start | bytes 3145736 | tf_op jit(solution)/shard_map/ppermute | solution.py:48
  185.3 33.2 %collective-permute-start.30 = (bf16[2,128,2048]{2,1,0:T(8,128)(2,1)}, bf16[2,128,2048]{2,1,0:T(8,128)(2,1)}, u32[]{:S(2)}, u32[]{:S(2)}) collective-permute-start(bf16[2,128,2048]{2,1,0:T(8,128)(2,1)} %bitcast.45), channel_id=1, source_target_pairs={{0,2},{2,0},{1,3},{3,1},{4,6},{6,4},{5,7},{7,5},{8,10},{10,8},{9,1... | collective-permute-start | bytes 3145736 | tf_op jit(solution)/shard_map/ppermute | solution.py:48
  210.1 340.6 %reduce-scatter.4.cloned.1.call-start = ((), (), s32[]{:S(2)}) async-start(), calls=%async_computation.7 | async-start | bytes 7864320 | tf_op jit(solution)/shard_map/reduce_scatter | solution.py:803
  249.7 41.4 %collective-permute-start.25 = (bf16[512,2048]{1,0:T(8,128)(2,1)S(1)}, bf16[512,2048]{1,0:T(8,128)(2,1)S(1)}, u32[]{:S(2)}, u32[]{:S(2)}) collective-permute-start(bf16[512,2048]{1,0:T(8,128)(2,1)S(1)} %constant_dynamic-update-slice_fusion.g_mine.refs_4_), channel_id=1, source_target_pairs={{0,1},{1,0},{2,3},{3,2},{4,5},{5,4},{6,7},{7,6},{8,9},{9,8},{10,11... | collective-permute-start | bytes 6291464 | tf_op jit(solution)/shard_map/ppermute | solution.py:48
  263.0 29.4 %collective-permute-start.23 = (bf16[512,2048]{1,0:T(8,128)(2,1)S(1)}, bf16[512,2048]{1,0:T(8,128)(2,1)}, u32[]{:S(2)}, u32[]{:S(2)}) collective-permute-start(bf16[512,2048]{1,0:T(8,128)(2,1)S(1)} %pad_maximum_fusion.1.x_mine.refs_0_), channel_id=1, source_target_pairs={{0,1},{1,0},{2,3},{3,2},{4,5},{5,4},{6,7},{7,6},{8,9},{9,8},{10,11... | collective-permute-start | bytes 6291464 | tf_op jit(solution)/shard_map/ppermute | solution.py:48
  275.9 28.7 %collective-permute-start.36 = (bf16[512,2048]{1,0:T(8,128)(2,1)}, bf16[512,2048]{1,0:T(8,128)(2,1)}, u32[]{:S(2)}, u32[]{:S(2)}) collective-permute-start(bf16[512,2048]{1,0:T(8,128)(2,1)} %constant_dynamic-update-slice_fusion.4.g_mine.refs_6_), channel_id=1, source_target_pairs={{0,1},{1,0},{2,3},{3,2},{4,5},{5,4},{6,7},{7,6},{8,9},{9,8},{10,11... | collective-permute-start | bytes 6291464 | tf_op jit(solution)/shard_map/ppermute | solution.py:48
  338.1 300.8 %reduce-scatter.6.cloned.1.call-start = ((), (), s32[]{:S(2)}) async-start(), calls=%async_computation.8 | async-start | bytes 7864320 | tf_op jit(solution)/shard_map/reduce_scatter | solution.py:803
  407.4 25.8 %collective-permute-start.39 = (bf16[2,128,2048]{2,1,0:T(8,128)(2,1)}, bf16[2,128,2048]{2,1,0:T(8,128)(2,1)}, u32[]{:S(2)}, u32[]{:S(2)}) collective-permute-start(bf16[2,128,2048]{2,1,0:T(8,128)(2,1)} %bitcast.49), channel_id=1, source_target_pairs={{0,4},{4,0},{1,5},{5,1},{2,6},{6,2},{3,7},{7,3},{8,12},{12,8},{9,1... | collective-permute-start | bytes 3145736 | tf_op jit(solution)/shard_map/ppermute | solution.py:48
  411.0 26.4 %collective-permute-start.40 = (bf16[2,128,2048]{2,1,0:T(8,128)(2,1)S(1)}, bf16[2,128,2048]{2,1,0:T(8,128)(2,1)S(1)}, u32[]{:S(2)}, u32[]{:S(2)}) collective-permute-start(bf16[2,128,2048]{2,1,0:T(8,128)(2,1)S(1)} %bitcast.499), channel_id=1, source_target_pairs={{0,2},{2,0},{1,3},{3,1},{4,6},{6,4},{5,7},{7,5},{8,10},{10,8},{9,1... | collective-permute-start | bytes 3145736 | tf_op jit(solution)/shard_map/ppermute | solution.py:48
  436.0 22.9 %collective-permute-start.41 = (bf16[128,2048]{1,0:T(8,128)(2,1)}, bf16[128,2048]{1,0:T(8,128)(2,1)}, u32[]{:S(2)}, u32[]{:S(2)}) collective-permute-start(bf16[128,2048]{1,0:T(8,128)(2,1)} %get-tuple-element.227), channel_id=1, source_target_pairs={{0,2},{2,0},{1,3},{3,1},{4,6},{6,4},{5,7},{7,5},{8,10},{10,8},{9,1... | collective-permute-start | bytes 1572872 | tf_op jit(solution)/shard_map/ppermute | solution.py:48
  458.8 214.8 %reduce-scatter.8.cloned.1.call-start = ((), (), s32[]{:S(2)}) async-start(), calls=%async_computation.9 | async-start | bytes 5242880 | tf_op jit(solution)/shard_map/reduce_scatter | solution.py:803
  468.5 37.3 %collective-permute-start.44 = (bf16[128,2048]{1,0:T(8,128)(2,1)S(1)}, bf16[128,2048]{1,0:T(8,128)(2,1)S(1)}, u32[]{:S(2)}, u32[]{:S(2)}) collective-permute-start(bf16[128,2048]{1,0:T(8,128)(2,1)S(1)} %get-tuple-element.155), channel_id=1, source_target_pairs={{0,2},{2,0},{1,3},{3,1},{4,6},{6,4},{5,7},{7,5},{8,10},{10,8},{9,1... | collective-permute-start | bytes 1572872 | tf_op jit(solution)/shard_map/ppermute | solution.py:48
  481.3 22.7 %collective-permute-start.47 = (bf16[128,2048]{1,0:T(8,128)(2,1)S(1)}, bf16[128,2048]{1,0:T(8,128)(2,1)S(1)}, u32[]{:S(2)}, u32[]{:S(2)}) collective-permute-start(bf16[128,2048]{1,0:T(8,128)(2,1)S(1)} %collective-permute-done.46), channel_id=1, source_target_pairs={{0,2},{2,0},{1,3},{3,1},{4,6},{6,4},{5,7},{7,5},{8,10},{10,8},{9,1... | collective-permute-start | bytes 1572872 | tf_op jit(solution)/shard_map/ppermute | solution.py:48
  504.1 32.5 %collective-permute-start.56 = (bf16[512,2048]{1,0:T(8,128)(2,1)S(1)}, bf16[512,2048]{1,0:T(8,128)(2,1)S(1)}, u32[]{:S(2)}, u32[]{:S(2)}) collective-permute-start(bf16[512,2048]{1,0:T(8,128)(2,1)S(1)} %constant_dynamic-update-slice_fusion.12.refs_6_), channel_id=1, source_target_pairs={{0,1},{1,0},{2,3},{3,2},{4,5},{5,4},{6,7},{7,6},{8,9},{9,8},{10,11... | collective-permute-start | bytes 6291464 | tf_op jit(solution)/shard_map/ppermute | solution.py:48
  505.7 24.0 %collective-permute-start.45 = (bf16[128,2048]{1,0:T(8,128)(2,1)S(1)}, bf16[128,2048]{1,0:T(8,128)(2,1)S(1)}, u32[]{:S(2)}, u32[]{:S(2)}) collective-permute-start(bf16[128,2048]{1,0:T(8,128)(2,1)S(1)} %collective-permute-done.44), channel_id=1, source_target_pairs={{0,4},{4,0},{1,5},{5,1},{2,6},{6,2},{3,7},{7,3},{8,12},{12,8},{9,1... | collective-permute-start | bytes 1572872 | tf_op jit(solution)/shard_map/ppermute | solution.py:48
  530.6 22.0 %collective-permute-start.51 = (bf16[512,2048]{1,0:T(8,128)(2,1)}, bf16[512,2048]{1,0:T(8,128)(2,1)}, u32[]{:S(2)}, u32[]{:S(2)}) collective-permute-start(bf16[512,2048]{1,0:T(8,128)(2,1)} %constant_dynamic-update-slice_fusion.8.refs_4_), channel_id=1, source_target_pairs={{0,1},{1,0},{2,3},{3,2},{4,5},{5,4},{6,7},{7,6},{8,9},{9,8},{10,11... | collective-permute-start | bytes 6291464 | tf_op jit(solution)/shard_map/ppermute | solution.py:48
  534.4 33.5 %collective-permute-start.48 = (bf16[2,128,2048]{2,1,0:T(8,128)(2,1)}, bf16[2,128,2048]{2,1,0:T(8,128)(2,1)}, u32[]{:S(2)}, u32[]{:S(2)}) collective-permute-start(bf16[2,128,2048]{2,1,0:T(8,128)(2,1)} %bitcast.60), channel_id=1, source_target_pairs={{0,4},{4,0},{1,5},{5,1},{2,6},{6,2},{3,7},{7,3},{8,12},{12,8},{9,1... | collective-permute-start | bytes 3145736 | tf_op jit(solution)/shard_map/ppermute | solution.py:48
  536.0 31.9 %collective-permute-start.53 = (bf16[2,128,2048]{2,1,0:T(8,128)(2,1)}, bf16[2,128,2048]{2,1,0:T(8,128)(2,1)}, u32[]{:S(2)}, u32[]{:S(2)}) collective-permute-start(bf16[2,128,2048]{2,1,0:T(8,128)(2,1)} %bitcast.61), channel_id=1, source_target_pairs={{0,2},{2,0},{1,3},{3,1},{4,6},{6,4},{5,7},{7,5},{8,10},{10,8},{9,1... | collective-permute-start | bytes 3145736 | tf_op jit(solution)/shard_map/ppermute | solution.py:48
  551.9 25.2 %collective-permute-start.57 = (bf16[256,1536]{1,0:T(8,128)(2,1)S(1)}, bf16[256,1536]{1,0:T(8,128)(2,1)S(1)}, u32[]{:S(2)}, u32[]{:S(2)}) collective-permute-start(bf16[256,1536]{1,0:T(8,128)(2,1)S(1)} %constant_dynamic-slice_fusion.2), channel_id=1, source_target_pairs={{0,4},{4,0},{1,5},{5,1},{2,6},{6,2},{3,7},{7,3},{8,12},{12,8},{9,1... | collective-permute-start | bytes 2359304 | tf_op jit(solution)/shard_map/ppermute | solution.py:48
  601.1 57.9 %collective-permute-start.52 = (bf16[128,2048]{1,0:T(8,128)(2,1)}, bf16[128,2048]{1,0:T(8,128)(2,1)}, u32[]{:S(2)}, u32[]{:S(2)}) collective-permute-start(bf16[128,2048]{1,0:T(8,128)(2,1)} %fusion.82), channel_id=1, source_target_pairs={{0,2},{2,0},{1,3},{3,1},{4,6},{6,4},{5,7},{7,5},{8,10},{10,8},{9,1... | collective-permute-start | bytes 1572872 | tf_op jit(solution)/shard_map/ppermute | solution.py:48
  614.3 24.6 %collective-permute-start.59 = (bf16[2,128,2048]{2,1,0:T(8,128)(2,1)S(1)}, bf16[2,128,2048]{2,1,0:T(8,128)(2,1)}, u32[]{:S(2)}, u32[]{:S(2)}) collective-permute-start(bf16[2,128,2048]{2,1,0:T(8,128)(2,1)S(1)} %bitcast.500), channel_id=1, source_target_pairs={{0,4},{4,0},{1,5},{5,1},{2,6},{6,2},{3,7},{7,3},{8,12},{12,8},{9,1... | collective-permute-start | bytes 3145736 | tf_op jit(solution)/shard_map/ppermute | solution.py:48
  619.2 25.7 %collective-permute-start.62 = (bf16[2,128,2048]{2,1,0:T(8,128)(2,1)}, bf16[2,128,2048]{2,1,0:T(8,128)(2,1)}, u32[]{:S(2)}, u32[]{:S(2)}) collective-permute-start(bf16[2,128,2048]{2,1,0:T(8,128)(2,1)} %bitcast.83), channel_id=1, source_target_pairs={{0,2},{2,0},{1,3},{3,1},{4,6},{6,4},{5,7},{7,5},{8,10},{10,8},{9,1... | collective-permute-start | bytes 3145736 | tf_op jit(solution)/shard_map/ppermute | solution.py:48
  (194 other events, 2285.6 us)
Sparse Core Ops, SparseCore 0:
  12.2 28.5 all-gather.6
  43.0 62.9 all-gather.4
  129.9 115.6 all-gather.8
  247.5 113.5 all-gather.10
  363.3 108.9 reduce-scatter.3
  474.5 111.2 reduce-scatter.5
  590.5 75.8 reduce-scatter.7

commit v7 on v6

--- a/solution.py
+++ b/solution.py
@@ -52,13 +52,25 @@
     return lax.optimization_barrier((tensor,) + earlier)[0]
 
 
-def gather_start(own, outer, inner, *before_x):
-    start = {"x": tie(own, *before_x), "y": own}
+def gather_start(own, outer, inner, x_after=(), y_after=()):
+    start = {"x": tie(own, *x_after), "y": tie(own, *y_after)}
     return own, swap(start[inner], inner), swap(start[outer], outer)
 
 
-def gather_across(state, outer):
-    return state + (swap(state[1], outer),)
+def gather_across(state, outer, inner, last):
+    own, by_inner, by_outer = state
+    return state + (swap(by_inner if last == outer else by_outer, last),)
+
+
+def gather_steps(owns, orders):
+    starts = [gather_start(own, *order) for own, order in zip(owns, orders)]
+    firsts = [t for state in starts for t in state[1:]]
+    ready = []
+    for state, order in zip(starts, orders):
+        by_inner = tie(state[1], *firsts)
+        ready.append((state[0], by_inner, state[2], swap(by_inner, order[0])))
+    lasts = [state[-1] for state in ready]
+    return [(tie(state[0], *lasts),) + state[1:] for state in ready]
 
 
 def gather_core(state):
@@ -66,27 +78,29 @@
     return mine, swap(mine, "c")
 
 
-def gather_tokens(own, outer, inner, *before_x):
-    return gather_core(gather_across(gather_start(own, outer, inner, *before_x), outer))
-
-
-def scatter_core(mine, other, units):
-    came = swap(other, "c").reshape(4, units, -1)
-    mine = mine.reshape(4, units, -1)
-    send = (mine[2:].astype(F32) + came[2:].astype(F32)).astype(BF)
-    return mine[:2].astype(F32) + came[:2].astype(F32), send
-
-
-def scatter_outer(state, outer, *later):
+def scatter_core(mine, other, units, outer, first):
+    came = swap(other, "c").reshape(2, 2, units, -1)
+    mine = mine.reshape(2, 2, units, -1)
+    parts = []
+    for p in range(2):
+        index = (p,) if first == outer else (slice(None), p)
+        parts.append(mine[index].astype(F32) + came[index].astype(F32))
+    return parts[0], parts[1].astype(BF)
+
+
+def scatter_outer(state, axis, *later):
     keep, send = state
-    came = tie(swap(send, outer), *later)
+    return scatter_add(keep, tie(swap(send, axis), *later))
+
+
+def scatter_add(keep, came):
     send = (keep[1] + came[1].astype(F32)).astype(BF)
     return keep[0] + came[0].astype(F32), send
 
 
-def scatter_inner(state, inner):
+def scatter_inner(state, axis):
     keep, send = state
-    return keep + swap(send, inner).astype(F32)
+    return keep + swap(send, axis).astype(F32)
 
 
 def tie_pair(pair, *earlier):
@@ -717,37 +731,34 @@
     back_low = [cotangent[m, 0].reshape(own_tokens, D) for m in micros]
     all_ids = jnp.stack([all_ids, swap(all_ids, "x")], axis=0)
     normed_att = [rms_norm(t, norm_gains[0]).astype(BF) for t in token_rows]
-    att_states = [gather_start(normed_att[m], *orders[m], their_qkv, all_ids) for m in micros]
-    mlp_later = tie(weight_mlp, *[t for state in att_states for t in state[1:]])
-    down_later = tie(weight_down, *[t for state in att_states for t in state[1:]])
-    att_states = [gather_across(att_states[m], orders[m][0]) for m in micros]
+    att_states = [
+        gather_start(normed_att[m], *orders[m], (their_qkv, all_ids)) for m in micros
+    ]
+    att_by_x = [state[1 + orders[m].index("y")] for m, state in enumerate(att_states)]
+    mlp_later = tie(weight_mlp, *att_by_x)
+    down_later = tie(weight_down, *att_by_x)
+    att_states = [gather_across(state, *orders[m], "y") for m, state in enumerate(att_states)]
     att_rows = [gather_core(state) for state in att_states]
 
+    def their_ff(k, *earlier):
+        return swap(tie(ff_columns(k, 1 - x_place), *earlier), "x")
+
+    theirs = their_ff(0, *att_by_x)
+    shard_ff = [join_rows(ff_columns(0, x_place), theirs)]
+    full_ff = [fetch(shard_ff[0])]
+    their_out = swap(tie(half_columns(all_out, 1 - x_place), shard_ff[0]), "x")
+    both_out = jnp.zeros((z_count, 2, rows, width_att), BF)
+    for part, place in ((half_columns(all_out, x_place), x_place), (their_out, 1 - x_place)):
+        part = part.reshape(z_count, 1, rows, width_att)
+        both_out = lax.dynamic_update_slice_in_dim(both_out, part, place, axis=1)
+    full_out = both_out.reshape(D, width_att)
     att_last = [state[-1] for state in att_states]
-    back_states = [gather_start(tie(back_low[m], *att_last), *orders[m]) for m in micros]
+    back_states = [
+        gather_start(back_low[m], *orders[m], (their_out,), att_last) for m in micros
+    ]
     back_first = [t for state in back_states for t in state[1:]]
-    shard_ff = []
-    full_ff = []
+    back_states = [gather_across(state, *orders[m], "y") for m, state in enumerate(back_states)]
     earlier = back_first
-    for k in range(CHUNKS):
-        theirs = swap(tie(ff_columns(k, 1 - x_place), *earlier), "x")
-        shard_ff.append(join_rows(ff_columns(k, x_place), theirs))
-        full_ff.append(fetch(shard_ff[k]))
-        if k == 0:
-            their_out = swap(tie(half_columns(all_out, 1 - x_place), theirs), "x")
-            both_out = jnp.zeros((z_count, 2, rows, width_att), BF)
-            for part, place in ((half_columns(all_out, x_place), x_place), (their_out, 1 - x_place)):
-                part = part.reshape(z_count, 1, rows, width_att)
-                both_out = lax.dynamic_update_slice_in_dim(both_out, part, place, axis=1)
-            full_out = both_out.reshape(D, width_att)
-            back_states = [
-                gather_across((state[0], tie(state[1], their_out), state[2]), orders[m][0])
-                for m, state in enumerate(back_states)
-            ]
-            earlier = [state[-1] for state in back_states]
-        else:
-            earlier = [theirs]
-    back_rows = [gather_core(state) for state in back_states]
 
     rel_c = jnp.arange(2)[:, None, None] ^ c_place
     rel_y = jnp.arange(2)[None, :, None] ^ y_place
@@ -771,26 +782,34 @@
     projected = []
     combined = []
     hidden = []
-    mlp_rows = []
+    normed_mlp = []
     for m in micros:
         mine, other = att_rows[m]
         if m == 0:
-            mine = tie(mine, *back_first, shard_ff[0])
+            mine = tie(mine, *back_first)
         proj = jnp.concatenate([mm(p, full_qkv, NN).astype(BF) for p in (mine, other)], axis=0)
         projected.append(proj.reshape(slots + (3 * width_att,)))
         comb = attention_fwd(projected[m], masks[m], columns[m], gate_rows, wheres[m])
         combined.append(comb.reshape(tokens, width_att))
     half = tokens // 2
+    for k in range(1, CHUNKS):
+        theirs = their_ff(k, *earlier)
+        shard_ff.append(join_rows(ff_columns(k, x_place), tie(theirs, combined[0])))
+        full_ff.append(fetch(shard_ff[k]))
+        earlier = [theirs]
+    back_states = [(tie(state[0], combined[0]),) + state[1:] for state in back_states]
+    back_rows = [gather_core(state) for state in back_states]
     for m in micros:
         ready = combined[m]
         if m > 0:
             ready = tie(ready, *shard_ff, *[state[-1] for state in back_states])
         other = mm(ready[half:], full_out, NT).astype(BF)
         mine = mm(ready[:half], full_out, NT).astype(BF)
-        state = scatter_outer(scatter_core(mine, other, own_tokens), orders[m][0])
+        state = scatter_core(mine, other, own_tokens, orders[m][0], orders[m][0])
+        state = scatter_outer(state, orders[m][0])
         hidden.append(token_rows[m] + scatter_inner(state, orders[m][1]))
-        normed_mlp = rms_norm(hidden[m], norm_gains[1]).astype(BF)
-        mlp_rows.append(gather_tokens(normed_mlp, *orders[m]))
+        normed_mlp.append(rms_norm(hidden[m], norm_gains[1]).astype(BF))
+    mlp_rows = [gather_core(state) for state in gather_steps(normed_mlp, orders)]
 
     def exchange_grad(grad):
         return grad, swap(lax.dynamic_slice_in_dim(grad, (1 - x_place) * rows, rows, axis=0), "x")
@@ -829,7 +848,7 @@
             dtype = BF if last else F32
             d_total[m] = products(grad, full_ff[k][:, : 2 * width], d_total[m], dtype)
             if last:
-                states[m] = scatter_core(*d_total[m], own_tokens)
+                states[m] = scatter_core(*d_total[m], own_tokens, orders[m][0], orders[m][0])
         if not last:
             grad_ff = weight_grads(mlp_rows, back_rows, d_gate_up[k], active[k])
             own_ff.append(reduce_rows(grad_ff))
@@ -852,7 +871,6 @@
     gain_grad_att = jnp.zeros((D,), F32)
     gain_grad_mlp = jnp.zeros((D,), F32)
     d_hidden = []
-    grad_states = []
     for m in micros:
         keep, send = outer_states[m]
         d_normed = scatter_inner((tie(keep, grad_ff), send), orders[m][1])
@@ -860,12 +878,14 @@
         d_norm, d_gain = norm_back(d_normed)
         gain_grad_mlp = gain_grad_mlp + d_gain
         d_hidden.append(back_low[m].astype(F32) + d_norm)
-        state = gather_start(d_hidden[m].astype(BF), *orders[m])
-        grad_states.append(gather_across(state, orders[m][0]))
 
     gate_sum = jnp.zeros((heads,), F32)
     d_projs = []
-    out_states = [scatter_core(*tie_pair(out_pairs[m], *d_hidden), own_tokens) for m in micros]
+    out_states = [
+        scatter_core(*tie_pair(out_pairs[m], *d_hidden), own_tokens, orders[m][0], orders[m][0])
+        for m in micros
+    ]
+    grad_states = gather_steps([t.astype(BF) for t in d_hidden], orders)
     sends = [t[1] for t in out_states]
     out_states = [tie_send(t, *[g[-1] for g in grad_states]) for t in out_states]
     att_grads = [gather_core((tie(g[0], *sends),) + g[1:]) for g in grad_states]
@@ -887,11 +907,14 @@
         )
         gate_sum = gate_sum + jnp.sum(gate_part, axis=(0, 2))
         d_projs.append(d_proj.reshape(tokens, 3 * width_att))
-    out_states = [scatter_outer(out_states[m], orders[m][0], d_projs[0]) for m in micros]
-    by_rows = [d_projs[0], tie(d_projs[-1], ff_pairs[0][1], *[t[1] for t in out_states])]
+    out_came = [swap(out_states[m][1], orders[m][0]) for m in micros]
+    by_rows = [d_projs[0], tie(d_projs[-1], ff_pairs[0][1], *out_came)]
     grad_att = weight_grads(att_rows, att_grads, by_rows, combined)
     own_att = reduce_rows(grad_att)
-    mlp_out = [scatter_inner(out_states[m], orders[m][1]) for m in micros]
+    mlp_out = []
+    for m in micros:
+        state = scatter_add(out_states[m][0], tie(out_came[m], grad_att))
+        mlp_out.append(scatter_inner(state, orders[m][1]))
     block_out = [(hidden[m] + mlp_out[m]).astype(BF) for m in micros]
 
     ff_pairs += [exchange_grad(g) for g in own_ff[1:]]
@@ -904,7 +927,7 @@
         d_proj = tie(d_projs[m], grad_att)
         other = mm(d_proj[half:], full_qkv, NT).astype(BF)
         mine = mm(d_proj[:half], full_qkv, NT).astype(BF)
-        in_states.append(scatter_core(mine, other, own_tokens))
+        in_states.append(scatter_core(mine, other, own_tokens, orders[m][0], orders[m][0]))
     for m in micros:
         state = scatter_outer(in_states[m], orders[m][0])
         if m > 0:

time: 737 us -> 707 us (0.959)
  waiting for transfers between devices: 258 us -> 215 us
  starting transfers between devices: 65.4 us -> 75.3 us
    ppermute x66, waiting for transfers between devices: 248 us -> 182 us  [swap(): return lax.ppermute(tensor, axis, [(0, 1), (1, 0)])]
    reduce_scatter x3, waiting for transfers between devices: 0.04 us -> 18.3 us  [reduce_rows(): return lax.psum_scatter(partial, 'z', scatter_dimension=0, tiled=True)]
    unnamed x310 -> x274, local copies, waits for them, and re-layouts: 17.5 us -> 20.9 us
  transfers between devices with their start and end apart: 78 -> 78, of which waited for: 39 -> 35; matrix products, arithmetic and copies ran while one was open for 27% -> 28% of each run, Pallas kernels for 21% -> 22%
where the time goes in v7:
time: 707 us; the launch traced here: 698 us
  waiting for transfers between devices  215 us (30%)
  Pallas kernels  178 us (25%)
  matrix products  81.3 us (11%)
  other arithmetic  76.5 us (11%)
  starting transfers between devices  75.3 us (11%)
  local copies, waits for them, and re-layouts  53.6 us (8%)
  between operations  18.6 us (3%)
    ppermute x66, waiting for transfers between devices, swap(): return lax.ppermute(tensor, axis, [(0, 1), (1, 0)])  182 us
    dot_general x24, matrix products, mm(): return lax.dot_general(a, b, (dims, ((), ())), preferred_element_type=F32)  81.3 us
    ppermute x66, starting transfers between devices, swap(): return lax.ppermute(tensor, axis, [(0, 1), (1, 0)])  58.7 us
    pallas_call x4, Pallas kernels, feed_forward(): pl.pallas_call(functools.partial(ff_kernel, width, half), grid=(2 * half,...  50.2 us
    pallas_call x3, Pallas kernels, weight_grads(): pl.pallas_call(functools.partial(grads_kernel, count), grid=(D // tile,),...  49.5 us
    pallas_call x2, Pallas kernels, attention_bwd(): pl.pallas_call(functools.partial(attention_bwd_kernel, heads), grid=(seqs...  25.1 us
    pallas_call x1, Pallas kernels, adam_all(): pl.pallas_call(functools.partial(adam_kernel, steps, len(ff_sides)), grid...  22.5 us
    unnamed x274, local copies, waits for them, and re-layouts  20.9 us
  transfers between devices with their start and end apart: 78, of which 35 were waited for; matrix products, arithmetic and copies ran while one was open for 28% of the time, Pallas kernels for 22%

profile of v7, /device:TPU:0, one launch (start us, length us, event | category | flops | bytes accessed | tf_op | source)
XLA Modules:
  0.0 698.5 jit_solution(14063760268258054919)
XLA Ops:
  35.8 12.2 %collective-permute-done.7 = bf16[128,2048]{1,0:T(8,128)(2,1)} collective-permute-done((bf16[128,2048]{1,0:T(8,128)(2,1)}, bf16[128,2048]{1,0:T(8,128)(2,1)}, u32[]{:S(2)}, u32[]{:S(2)}) %collective-permute-start.7) | collective-permute-done | bytes 524320 | tf_op jit(solution)/shard_map/ppermute | solution.py:48
  48.1 8.1 %collective-permute-done.5 = bf16[128,2048]{1,0:T(8,128)(2,1)S(1)} collective-permute-done((bf16[128,2048]{1,0:T(8,128)(2,1)}, bf16[128,2048]{1,0:T(8,128)(2,1)S(1)}, u32[]{:S(2)}, u32[]{:S(2)}) %collective-permute-start.5) | collective-permute-done | bytes 524320 | tf_op jit(solution)/shard_map/ppermute | solution.py:48
  106.1 6.2 collective-permute-done.9
  112.3 9.2 %collective-permute-done.13 = bf16[128,2048]{1,0:T(8,128)(2,1)} collective-permute-done((bf16[128,2048]{1,0:T(8,128)(2,1)S(1)}, bf16[128,2048]{1,0:T(8,128)(2,1)}, u32[]{:S(2)}, u32[]{:S(2)}) %collective-permute-start.13) | collective-permute-done | bytes 524320 | tf_op jit(solution)/shard_map/ppermute | solution.py:48
  133.5 6.5 attention_forward.2
  149.3 6.5 attention_forward.3
  168.9 21.7 %collective-permute-done.27 = bf16[2,128,2048]{2,1,0:T(8,128)(2,1)S(1)} collective-permute-done((bf16[2,128,2048]{2,1,0:T(8,128)(2,1)S(1)}, bf16[2,128,2048]{2,1,0:T(8,128)(2,1)S(1)}, u32[]{:S(2)}, u32[]{:S(2)}) %collective-permute-start.27) | collective-permute-done | bytes 1048608 | tf_op jit(solution)/shard_map/ppermute | solution.py:48
  193.1 8.4 %reduce-scatter.4.cloned.1.call-start = ((), (), s32[]{:S(2)}) async-start(), calls=%async_computation.7 | async-start | bytes 7864320 | tf_op jit(solution)/shard_map/reduce_scatter | solution.py:822
  206.6 9.5 %collective-permute-done.18 = bf16[128,2048]{1,0:T(8,128)(2,1)S(1)} collective-permute-done((bf16[128,2048]{1,0:T(8,128)(2,1)S(1)}, bf16[128,2048]{1,0:T(8,128)(2,1)S(1)}, u32[]{:S(2)}, u32[]{:S(2)}) %collective-permute-start.18) | collective-permute-done | bytes 524320 | tf_op jit(solution)/shard_map/ppermute | solution.py:48
  223.2 9.6 %collective-permute-done.30 = bf16[128,2048]{1,0:T(8,128)(2,1)S(1)} collective-permute-done((bf16[128,2048]{1,0:T(8,128)(2,1)S(1)}, bf16[128,2048]{1,0:T(8,128)(2,1)S(1)}, u32[]{:S(2)}, u32[]{:S(2)}) %collective-permute-start.30) | collective-permute-done | bytes 524320 | tf_op jit(solution)/shard_map/ppermute | solution.py:48
  233.4 8.4 %collective-permute-done.20 = bf16[128,2048]{1,0:T(8,128)(2,1)S(1)} collective-permute-done((bf16[128,2048]{1,0:T(8,128)(2,1)S(1)}, bf16[128,2048]{1,0:T(8,128)(2,1)S(1)}, u32[]{:S(2)}, u32[]{:S(2)}) %collective-permute-start.20) | collective-permute-done | bytes 524320 | tf_op jit(solution)/shard_map/ppermute | solution.py:48
  261.8 12.2 %feed_forward.4 = (bf16[512,512]{1,0:T(8,128)(2,1)S(1)}, bf16[512,512]{1,0:T(8,128)(2,1)S(1)}, bf16[512,1024]{1,0:T(8,128)(2,1)S(1)}, bf16[512,1024]{1,0:T(8,128)(2,1)S(1)}) custom-call(bf16[512,2048]{1,0:T(8,128)(2,1)S(1)} %constant_dynamic-update-slice_fusion.x_mine.refs_0_, bf16[512,2048]{1,0:T(8,128)(2,1)} %collective-permute-done.33.x_other.refs_1_, ...), custom_call_target="tpu_custom_call" | custom-call | flops 13958643712 | bytes 1048576 | tf_op jit(solution)/shard_map/feed_forward/pallas_call | solution.py:410
  274.1 13.1 %feed_forward.5 = (bf16[512,512]{1,0:T(8,128)(2,1)S(1)}, bf16[512,512]{1,0:T(8,128)(2,1)S(1)}, bf16[512,1024]{1,0:T(8,128)(2,1)S(1)}, bf16[512,1024]{1,0:T(8,128)(2,1)S(1)}) custom-call(bf16[512,2048]{1,0:T(8,128)(2,1)} %constant_dynamic-update-slice_fusion.8.x_mine.refs_2_, bf16[512,2048]{1,0:T(8,128)(2,1)} %collective-permute-done.35.x_other.refs_3_, ...), custom_call_target="tpu_custom_call" | custom-call | flops 13958643712 | bytes 1048576 | tf_op jit(solution)/shard_map/feed_forward/pallas_call | solution.py:410
  288.2 18.2 %weight_grads.3 = bf16[2048,1536]{1,0:T(8,128)(2,1)} custom-call(bf16[512,2048]{1,0:T(8,128)(2,1)} %copy-done.18, bf16[512,2048]{1,0:T(8,128)(2,1)} %collective-permute-done.33.x_other.refs_1_, bf16[512,2048]{1,0:T(8,128)(2,1)} %constant_dynamic-update-slice_fusion.8.x_mine.refs_2_, bf16[512,2048]{1,0:T(8,128)(2,1)} %collective-permute-done.35.x_other.refs_3_, ...), custom_call_target="tpu_custom_call" | custom-call | flops 19327352832 | bytes 29360128 | tf_op jit(solution)/shard_map/weight_grads/pallas_call | solution.py:506
  308.3 6.8 fusion.2
  315.0 6.8 fusion
  330.6 7.2 %all-gather.11.cloned.1.call-done.w_ref.refs_5_ = bf16[2048,1536]{1,0:T(8,128)(2,1)} async-done(((bf16[512,1536]{1,0:T(8,128)(2,1)}), bf16[2048,1536]{1,0:T(8,128)(2,1)}) %all-gather.11.cloned.1.call-update) | async-done | bytes 6291472 | tf_op jit(solution)/shard_map/all_gather | solution.py:695
  337.8 12.6 %feed_forward.6 = (bf16[512,512]{1,0:T(8,128)(2,1)S(1)}, bf16[512,512]{1,0:T(8,128)(2,1)S(1)}, bf16[512,1024]{1,0:T(8,128)(2,1)S(1)}, bf16[512,1024]{1,0:T(8,128)(2,1)S(1)}) custom-call(bf16[512,2048]{1,0:T(8,128)(2,1)S(1)} %copy-done.19, bf16[512,2048]{1,0:T(8,128)(2,1)} %collective-permute-done.33.x_other.refs_1_, bf16[512,2048]{1,0:T(8,128)(2,1)} %copy-done.93, ...), custom_call_target="tpu_custom_call" | custom-call | flops 13958643712 | bytes 1048576 | tf_op jit(solution)/shard_map/feed_forward/pallas_call | solution.py:410
  359.0 12.2 %feed_forward.7 = (bf16[512,512]{1,0:T(8,128)(2,1)S(1)}, bf16[512,512]{1,0:T(8,128)(2,1)S(1)}, bf16[512,1024]{1,0:T(8,128)(2,1)S(1)}, bf16[512,1024]{1,0:T(8,128)(2,1)S(1)}) custom-call(bf16[512,2048]{1,0:T(8,128)(2,1)} %constant_dynamic-update-slice_fusion.8.x_mine.refs_2_, bf16[512,2048]{1,0:T(8,128)(2,1)} %collective-permute-done.35.x_other.refs_3_, ...), custom_call_target="tpu_custom_call" | custom-call | flops 13958643712 | bytes 1048576 | tf_op jit(solution)/shard_map/feed_forward/pallas_call | solution.py:410
  388.4 8.6 %down_product.2 = (bf16[512,2048]{1,0:T(8,128)(2,1)S(1)}, bf16[512,2048]{1,0:T(8,128)(2,1)}) custom-call(bf16[512,512]{1,0:T(8,128)(2,1)S(1)} %copy-done.34, bf16[512,512]{1,0:T(8,128)(2,1)S(1)} %get-tuple-element.148.refs_1_.refs_12_, bf16[512,512]{1,0:T(8,128)(2,1)S(1)} %copy-done.36, bf16[512,512]{1,0:T(8,128)(2,1)S(1)} %get-tuple-element.166.refs_3_.refs_13_, ...), custom_call_target="tpu_custom_call" | custom-call | flops 4294967296 | bytes 8388608 | tf_op jit(solution)/shard_map/down_product/pallas_call | solution.py:455
  396.9 9.2 %down_product.3 = (bf16[512,2048]{1,0:T(8,128)(2,1)S(1)}, bf16[512,2048]{1,0:T(8,128)(2,1)}) custom-call(bf16[512,512]{1,0:T(8,128)(2,1)S(1)} %copy-done.38, bf16[512,512]{1,0:T(8,128)(2,1)S(1)} %get-tuple-element.159.refs_1_.refs_14_, bf16[512,512]{1,0:T(8,128)(2,1)S(1)} %copy-done.40, bf16[512,512]{1,0:T(8,128)(2,1)S(1)} %get-tuple-element.167.refs_3_.refs_15_, ...), custom_call_target="tpu_custom_call" | custom-call | flops 4294967296 | bytes 8388608 | tf_op jit(solution)/shard_map/down_product/pallas_call | solution.py:455
  416.6 18.3 %weight_grads.4 = bf16[2048,1536]{1,0:T(8,128)(2,1)} custom-call(bf16[512,2048]{1,0:T(8,128)(2,1)} %copy-done.18, bf16[512,2048]{1,0:T(8,128)(2,1)} %collective-permute-done.33.x_other.refs_1_, bf16[512,2048]{1,0:T(8,128)(2,1)} %constant_dynamic-update-slice_fusion.8.x_mine.refs_2_, bf16[512,2048]{1,0:T(8,128)(2,1)} %collective-permute-done.35.x_other.refs_3_, ...), custom_call_target="tpu_custom_call" | custom-call | flops 19327352832 | bytes 29360128 | tf_op jit(solution)/shard_map/weight_grads/pallas_call | solution.py:506
  445.7 11.5 %collective-permute-done.45 = bf16[128,2048]{1,0:T(8,128)(2,1)S(1)} collective-permute-done((bf16[128,2048]{1,0:T(8,128)(2,1)S(1)}, bf16[128,2048]{1,0:T(8,128)(2,1)S(1)}, u32[]{:S(2)}, u32[]{:S(2)}) %collective-permute-start.45) | collective-permute-done | bytes 524320 | tf_op jit(solution)/shard_map/ppermute | solution.py:48
  458.4 10.6 %collective-permute-done.47 = bf16[128,2048]{1,0:T(8,128)(2,1)S(1)} collective-permute-done((bf16[128,2048]{1,0:T(8,128)(2,1)S(1)}, bf16[128,2048]{1,0:T(8,128)(2,1)S(1)}, u32[]{:S(2)}, u32[]{:S(2)}) %collective-permute-start.47) | collective-permute-done | bytes 524320 | tf_op jit(solution)/shard_map/ppermute | solution.py:48
  472.7 10.8 %collective-permute-done.48 = bf16[128,2048]{1,0:T(8,128)(2,1)S(1)} collective-permute-done((bf16[128,2048]{1,0:T(8,128)(2,1)S(1)}, bf16[128,2048]{1,0:T(8,128)(2,1)S(1)}, u32[]{:S(2)}, u32[]{:S(2)}) %collective-permute-start.48) | collective-permute-done | bytes 524320 | tf_op jit(solution)/shard_map/ppermute | solution.py:48
  503.0 12.8 %attention_backward.3 = (bf16[2,2,2,4,32,768]{5,4,3,2,1,0:T(8,128)(2,1)S(1)}, f32[2,2,128]{2,1,0:T(2,128)S(1)}) custom-call(bf16[2,2,2,4,32,768]{5,4,3,2,1,0:T(8,128)(2,1)S(1)} %bitcast.450, f32[2,2,2,4,32,256]{5,4,3,2,1,0:T(8,128)S(1)} %bitcast.452, f32[2,4,128,128]{3,2,1,0:T(8,128)S(1)} %get-tuple-element.286.mask_ref, f32[2,4,128,3]{3,2,1,0:T(8,128)S(1)} %copy-done.11, ...), custom_call_target="tpu_custom_call" | custom-call | flops 14400000000 | bytes 5000000 | tf_op jit(solution)/shard_map/attention_backward/pallas_call | solution.py:337
  521.7 12.3 %attention_backward.2 = (bf16[2,2,2,4,32,768]{5,4,3,2,1,0:T(8,128)(2,1)S(1)}, f32[2,2,128]{2,1,0:T(2,128)S(1)}) custom-call(bf16[2,2,2,4,32,768]{5,4,3,2,1,0:T(8,128)(2,1)S(1)} %bitcast.448, f32[2,2,2,4,32,256]{5,4,3,2,1,0:T(8,128)S(1)} %bitcast.451, f32[2,4,128,128]{3,2,1,0:T(8,128)S(1)} %copy-done.15, f32[2,4,128,3]{3,2,1,0:T(8,128)S(1)} %copy-done.13, ...), custom_call_target="tpu_custom_call" | custom-call | flops 14400000000 | bytes 5000000 | tf_op jit(solution)/shard_map/attention_backward/pallas_call | solution.py:337
  539.5 13.0 %weight_grads.5 = bf16[2048,1024]{1,0:T(8,128)(2,1)} custom-call(bf16[512,2048]{1,0:T(8,128)(2,1)} %pad_maximum_fusion.refs_0_, bf16[512,2048]{1,0:T(8,128)(2,1)} %collective-permute-done.15.refs_1_, bf16[512,2048]{1,0:T(8,128)(2,1)} %pad_maximum_fusion.1.refs_2_, bf16[512,2048]{1,0:T(8,128)(2,1)} %collective-permute-done.22.refs_3_, ...), custom_call_target="tpu_custom_call" | custom-call | flops 12884901888 | bytes 25165824 | tf_op jit(solution)/shard_map/weight_grads/pallas_call | solution.py:506
  582.1 18.2 %collective-permute-done.59 = bf16[2,128,2048]{2,1,0:T(8,128)(2,1)S(1)} collective-permute-done((bf16[2,128,2048]{2,1,0:T(8,128)(2,1)S(1)}, bf16[2,128,2048]{2,1,0:T(8,128)(2,1)S(1)}, u32[]{:S(2)}, u32[]{:S(2)}) %collective-permute-start.59) | collective-permute-done | bytes 1048608 | tf_op jit(solution)/shard_map/ppermute | solution.py:48
  608.4 11.8 %collective-permute-done.63.refs_23_ = bf16[256,1536]{1,0:T(8,128)(2,1)S(1)} collective-permute-done((bf16[256,1536]{1,0:T(8,128)(2,1)S(1)}, bf16[256,1536]{1,0:T(8,128)(2,1)S(1)}, u32[]{:S(2)}, u32[]{:S(2)}) %collective-permute-start.63) | collective-permute-done | bytes 786464 | tf_op jit(solution)/shard_map/ppermute | solution.py:48
  624.3 18.3 %reduce-scatter.8.cloned.1.call-done.refs_18_ = bf16[512,1024]{1,0:T(8,128)(2,1)} async-done(((bf16[2048,1024]{1,0:T(8,128)(2,1)}), bf16[512,1024]{1,0:T(8,128)(2,1)}) %reduce-scatter.8.cloned.1.call-update) | async-done | bytes 1048592 | tf_op jit(solution)/shard_map/reduce_scatter | solution.py:822
  668.9 22.5 %adam.1 = (f32[3,256,512]{2,1,0:T(8,128)}, f32[3,256,512]{2,1,0:T(8,128)}, f32[3,256,512]{2,1,0:T(8,128)}, f32[256,512]{1,0:T(8,128)}, f32[256,512]{1,0:T(8,128)...) custom-call(s32[1]{0:T(128)} %bitcast.88.place_ref, ...), custom_call_target="tpu_custom_call" | custom-call | flops 41943040 | bytes 50331648 | tf_op jit(solution)/shard_map/adam/pallas_call | solution.py:620
  (571 shorter events, 306.3 us)
Async XLA Ops:
  7.2 71.0 %all-gather.5.cloned.1.call-start = ((), (), s32[]{:S(2)}) async-start(), calls=%async_computation.3 | async-start | bytes 1310720 | tf_op jit(solution)/shard_map/all_gather | solution.py:695
  12.1 113.2 %all-gather.7.cloned.1.call-start = ((), (), s32[]{:S(2)}) async-start(), calls=%async_computation.4 | async-start | bytes 3932160 | tf_op jit(solution)/shard_map/all_gather | solution.py:695
  18.4 80.3 %collective-permute-start.21 = (bf16[128,2048]{1,0:T(8,128)(2,1)}, bf16[128,2048]{1,0:T(8,128)(2,1)}, u32[]{:S(2)}, u32[]{:S(2)}) collective-permute-start(bf16[128,2048]{1,0:T(8,128)(2,1)} %get-tuple-element.119), channel_id=1, source_target_pairs={{0,2},{2,0},{1,3},{3,1},{4,6},{6,4},{5,7},{7,5},{8,10},{10,8},{9,1... | collective-permute-start | bytes 1572872 | tf_op jit(solution)/shard_map/ppermute | solution.py:48
  18.9 51.0 %collective-permute-start = (bf16[128,2048]{1,0:T(8,128)(2,1)}, bf16[128,2048]{1,0:T(8,128)(2,1)}, u32[]{:S(2)}, u32[]{:S(2)}) collective-permute-start(bf16[128,2048]{1,0:T(8,128)(2,1)} %get-tuple-element.117), channel_id=1, source_target_pairs={{0,2},{2,0},{1,3},{3,1},{4,6},{6,4},{5,7},{7,5},{8,10},{10,8},{9,1... | collective-permute-start | bytes 1572872 | tf_op jit(solution)/shard_map/ppermute | solution.py:48
  25.4 236.4 %all-gather.9.cloned.1.call-start = ((), (), s32[]{:S(2)}) async-start(), calls=%async_computation.5 | async-start | bytes 7864320 | tf_op jit(solution)/shard_map/all_gather | solution.py:695
  34.4 21.8 %collective-permute-start.5 = (bf16[128,2048]{1,0:T(8,128)(2,1)}, bf16[128,2048]{1,0:T(8,128)(2,1)S(1)}, u32[]{:S(2)}, u32[]{:S(2)}) collective-permute-start(bf16[128,2048]{1,0:T(8,128)(2,1)} %get-tuple-element.117), channel_id=1, source_target_pairs={{0,4},{4,0},{1,5},{5,1},{2,6},{6,2},{3,7},{7,3},{8,12},{12,8},{9,1... | collective-permute-start | bytes 1572872 | tf_op jit(solution)/shard_map/ppermute | solution.py:48
  78.2 51.6 %collective-permute-start.15 = (bf16[512,2048]{1,0:T(8,128)(2,1)}, bf16[512,2048]{1,0:T(8,128)(2,1)}, u32[]{:S(2)}, u32[]{:S(2)}) collective-permute-start(bf16[512,2048]{1,0:T(8,128)(2,1)} %pad_maximum_fusion.refs_0_), channel_id=1, source_target_pairs={{0,1},{1,0},{2,3},{3,2},{4,5},{5,4},{6,7},{7,6},{8,9},{9,8},{10,11... | collective-permute-start | bytes 6291464 | tf_op jit(solution)/shard_map/ppermute | solution.py:48
  88.8 249.0 %all-gather.11.cloned.1.call-start = ((), (), s32[]{:S(2)}) async-start(), calls=%async_computation.6 | async-start | bytes 7864320 | tf_op jit(solution)/shard_map/all_gather | solution.py:695
  98.7 22.8 %collective-permute-start.13 = (bf16[128,2048]{1,0:T(8,128)(2,1)S(1)}, bf16[128,2048]{1,0:T(8,128)(2,1)}, u32[]{:S(2)}, u32[]{:S(2)}) collective-permute-start(bf16[128,2048]{1,0:T(8,128)(2,1)S(1)} %bitcast.475), channel_id=1, source_target_pairs={{0,4},{4,0},{1,5},{5,1},{2,6},{6,2},{3,7},{7,3},{8,12},{12,8},{9,1... | collective-permute-start | bytes 1572872 | tf_op jit(solution)/shard_map/ppermute | solution.py:48
  102.3 37.7 %collective-permute-start.22 = (bf16[512,2048]{1,0:T(8,128)(2,1)}, bf16[512,2048]{1,0:T(8,128)(2,1)}, u32[]{:S(2)}, u32[]{:S(2)}) collective-permute-start(bf16[512,2048]{1,0:T(8,128)(2,1)} %pad_maximum_fusion.1.refs_2_), channel_id=1, source_target_pairs={{0,1},{1,0},{2,3},{3,2},{4,5},{5,4},{6,7},{7,6},{8,9},{9,8},{10,11... | collective-permute-start | bytes 6291464 | tf_op jit(solution)/shard_map/ppermute | solution.py:48
  123.2 32.6 %collective-permute-start.24 = (bf16[128,2048]{1,0:T(8,128)(2,1)}, bf16[128,2048]{1,0:T(8,128)(2,1)}, u32[]{:S(2)}, u32[]{:S(2)}) collective-permute-start(bf16[128,2048]{1,0:T(8,128)(2,1)} %collective-permute-done.12), channel_id=1, source_target_pairs={{0,2},{2,0},{1,3},{3,1},{4,6},{6,4},{5,7},{7,5},{8,10},{10,8},{9,1... | collective-permute-start | bytes 1572872 | tf_op jit(solution)/shard_map/ppermute | solution.py:48
  123.3 32.6 %collective-permute-start.25 = (bf16[128,2048]{1,0:T(8,128)(2,1)}, bf16[128,2048]{1,0:T(8,128)(2,1)}, u32[]{:S(2)}, u32[]{:S(2)}) collective-permute-start(bf16[128,2048]{1,0:T(8,128)(2,1)} %collective-permute-done.13), channel_id=1, source_target_pairs={{0,2},{2,0},{1,3},{3,1},{4,6},{6,4},{5,7},{7,5},{8,10},{10,8},{9,1... | collective-permute-start | bytes 1572872 | tf_op jit(solution)/shard_map/ppermute | solution.py:48
  165.5 25.2 %collective-permute-start.27 = (bf16[2,128,2048]{2,1,0:T(8,128)(2,1)S(1)}, bf16[2,128,2048]{2,1,0:T(8,128)(2,1)S(1)}, u32[]{:S(2)}, u32[]{:S(2)}) collective-permute-start(bf16[2,128,2048]{2,1,0:T(8,128)(2,1)S(1)} %bitcast.494), channel_id=1, source_target_pairs={{0,2},{2,0},{1,3},{3,1},{4,6},{6,4},{5,7},{7,5},{8,10},{10,8},{9,1... | collective-permute-start | bytes 3145736 | tf_op jit(solution)/shard_map/ppermute | solution.py:48
  167.6 33.9 %collective-permute-start.17 = (bf16[2,128,2048]{2,1,0:T(8,128)(2,1)S(1)}, bf16[2,128,2048]{2,1,0:T(8,128)(2,1)}, u32[]{:S(2)}, u32[]{:S(2)}) collective-permute-start(bf16[2,128,2048]{2,1,0:T(8,128)(2,1)S(1)} %bitcast.493), channel_id=1, source_target_pairs={{0,4},{4,0},{1,5},{5,1},{2,6},{6,2},{3,7},{7,3},{8,12},{12,8},{9,1... | collective-permute-start | bytes 3145736 | tf_op jit(solution)/shard_map/ppermute | solution.py:48
  193.1 323.8 %reduce-scatter.4.cloned.1.call-start = ((), (), s32[]{:S(2)}) async-start(), calls=%async_computation.7 | async-start | bytes 7864320 | tf_op jit(solution)/shard_map/reduce_scatter | solution.py:822
  219.3 22.6 %collective-permute-start.20 = (bf16[128,2048]{1,0:T(8,128)(2,1)S(1)}, bf16[128,2048]{1,0:T(8,128)(2,1)S(1)}, u32[]{:S(2)}, u32[]{:S(2)}) collective-permute-start(bf16[128,2048]{1,0:T(8,128)(2,1)S(1)} %get-tuple-element.135), channel_id=1, source_target_pairs={{0,4},{4,0},{1,5},{5,1},{2,6},{6,2},{3,7},{7,3},{8,12},{12,8},{9,1... | collective-permute-start | bytes 1572872 | tf_op jit(solution)/shard_map/ppermute | solution.py:48
  308.0 292.3 %reduce-scatter.6.cloned.1.call-start = ((), (), s32[]{:S(2)}) async-start(), calls=%async_computation.8 | async-start | bytes 7864320 | tf_op jit(solution)/shard_map/reduce_scatter | solution.py:822
  383.0 25.3 %collective-permute-start.39 = (bf16[2,128,2048]{2,1,0:T(8,128)(2,1)S(1)}, bf16[2,128,2048]{2,1,0:T(8,128)(2,1)}, u32[]{:S(2)}, u32[]{:S(2)}) collective-permute-start(bf16[2,128,2048]{2,1,0:T(8,128)(2,1)S(1)} %bitcast.491), channel_id=1, source_target_pairs={{0,4},{4,0},{1,5},{5,1},{2,6},{6,2},{3,7},{7,3},{8,12},{12,8},{9,1... | collective-permute-start | bytes 3145736 | tf_op jit(solution)/shard_map/ppermute | solution.py:48
  386.9 25.6 %collective-permute-start.40 = (bf16[2,128,2048]{2,1,0:T(8,128)(2,1)}, bf16[2,128,2048]{2,1,0:T(8,128)(2,1)}, u32[]{:S(2)}, u32[]{:S(2)}) collective-permute-start(bf16[2,128,2048]{2,1,0:T(8,128)(2,1)} %bitcast.51), channel_id=1, source_target_pairs={{0,2},{2,0},{1,3},{3,1},{4,6},{6,4},{5,7},{7,5},{8,10},{10,8},{9,1... | collective-permute-start | bytes 3145736 | tf_op jit(solution)/shard_map/ppermute | solution.py:48
  411.0 24.1 %collective-permute-start.41 = (bf16[128,2048]{1,0:T(8,128)(2,1)}, bf16[128,2048]{1,0:T(8,128)(2,1)}, u32[]{:S(2)}, u32[]{:S(2)}) collective-permute-start(bf16[128,2048]{1,0:T(8,128)(2,1)} %get-tuple-element.249), channel_id=1, source_target_pairs={{0,2},{2,0},{1,3},{3,1},{4,6},{6,4},{5,7},{7,5},{8,10},{10,8},{9,1... | collective-permute-start | bytes 1572872 | tf_op jit(solution)/shard_map/ppermute | solution.py:48
  435.1 207.5 %reduce-scatter.8.cloned.1.call-start = ((), (), s32[]{:S(2)}) async-start(), calls=%async_computation.9 | async-start | bytes 5242880 | tf_op jit(solution)/shard_map/reduce_scatter | solution.py:822
  442.9 40.9 %collective-permute-start.43 = (bf16[512,2048]{1,0:T(8,128)(2,1)S(1)}, bf16[512,2048]{1,0:T(8,128)(2,1)S(1)}, u32[]{:S(2)}, u32[]{:S(2)}) collective-permute-start(bf16[512,2048]{1,0:T(8,128)(2,1)S(1)} %copy-done.119), channel_id=1, source_target_pairs={{0,1},{1,0},{2,3},{3,2},{4,5},{5,4},{6,7},{7,6},{8,9},{9,8},{10,11... | collective-permute-start | bytes 6291464 | tf_op jit(solution)/shard_map/ppermute | solution.py:48
  443.4 42.8 %collective-permute-start.51 = (bf16[512,2048]{1,0:T(8,128)(2,1)S(1)}, bf16[512,2048]{1,0:T(8,128)(2,1)S(1)}, u32[]{:S(2)}, u32[]{:S(2)}) collective-permute-start(bf16[512,2048]{1,0:T(8,128)(2,1)S(1)} %copy-done.118), channel_id=1, source_target_pairs={{0,1},{1,0},{2,3},{3,2},{4,5},{5,4},{6,7},{7,6},{8,9},{9,8},{10,11... | collective-permute-start | bytes 6291464 | tf_op jit(solution)/shard_map/ppermute | solution.py:48
  445.1 23.9 %collective-permute-start.47 = (bf16[128,2048]{1,0:T(8,128)(2,1)S(1)}, bf16[128,2048]{1,0:T(8,128)(2,1)S(1)}, u32[]{:S(2)}, u32[]{:S(2)}) collective-permute-start(bf16[128,2048]{1,0:T(8,128)(2,1)S(1)} %get-tuple-element.178), channel_id=1, source_target_pairs={{0,2},{2,0},{1,3},{3,1},{4,6},{6,4},{5,7},{7,5},{8,10},{10,8},{9,1... | collective-permute-start | bytes 1572872 | tf_op jit(solution)/shard_map/ppermute | solution.py:48
  492.2 26.5 %collective-permute-start.52 = (bf16[512,2048]{1,0:T(8,128)(2,1)}, bf16[512,2048]{1,0:T(8,128)(2,1)}, u32[]{:S(2)}, u32[]{:S(2)}) collective-permute-start(bf16[512,2048]{1,0:T(8,128)(2,1)} %constant_dynamic-update-slice_fusion.16.refs_4_), channel_id=1, source_target_pairs={{0,1},{1,0},{2,3},{3,2},{4,5},{5,4},{6,7},{7,6},{8,9},{9,8},{10,11... | collective-permute-start | bytes 6291464 | tf_op jit(solution)/shard_map/ppermute | solution.py:48
  497.2 36.9 %collective-permute-start.50 = (bf16[2,128,2048]{2,1,0:T(8,128)(2,1)}, bf16[2,128,2048]{2,1,0:T(8,128)(2,1)S(1)}, u32[]{:S(2)}, u32[]{:S(2)}) collective-permute-start(bf16[2,128,2048]{2,1,0:T(8,128)(2,1)} %bitcast.61), channel_id=1, source_target_pairs={{0,4},{4,0},{1,5},{5,1},{2,6},{6,2},{3,7},{7,3},{8,12},{12,8},{9,1... | collective-permute-start | bytes 3145736 | tf_op jit(solution)/shard_map/ppermute | solution.py:48
  498.7 35.3 %collective-permute-start.55 = (bf16[2,128,2048]{2,1,0:T(8,128)(2,1)}, bf16[2,128,2048]{2,1,0:T(8,128)(2,1)}, u32[]{:S(2)}, u32[]{:S(2)}) collective-permute-start(bf16[2,128,2048]{2,1,0:T(8,128)(2,1)} %bitcast.62), channel_id=1, source_target_pairs={{0,2},{2,0},{1,3},{3,1},{4,6},{6,4},{5,7},{7,5},{8,10},{10,8},{9,1... | collective-permute-start | bytes 3145736 | tf_op jit(solution)/shard_map/ppermute | solution.py:48
  518.2 21.3 %collective-permute-start.54 = (bf16[256,1536]{1,0:T(8,128)(2,1)S(1)}, bf16[256,1536]{1,0:T(8,128)(2,1)S(1)}, u32[]{:S(2)}, u32[]{:S(2)}) collective-permute-start(bf16[256,1536]{1,0:T(8,128)(2,1)S(1)} %constant_dynamic-slice_fusion.2), channel_id=1, source_target_pairs={{0,4},{4,0},{1,5},{5,1},{2,6},{6,2},{3,7},{7,3},{8,12},{12,8},{9,1... | collective-permute-start | bytes 2359304 | tf_op jit(solution)/shard_map/ppermute | solution.py:48
  575.7 24.7 %collective-permute-start.59 = (bf16[2,128,2048]{2,1,0:T(8,128)(2,1)S(1)}, bf16[2,128,2048]{2,1,0:T(8,128)(2,1)S(1)}, u32[]{:S(2)}, u32[]{:S(2)}) collective-permute-start(bf16[2,128,2048]{2,1,0:T(8,128)(2,1)S(1)} %bitcast.492), channel_id=1, source_target_pairs={{0,4},{4,0},{1,5},{5,1},{2,6},{6,2},{3,7},{7,3},{8,12},{12,8},{9,1... | collective-permute-start | bytes 3145736 | tf_op jit(solution)/shard_map/ppermute | solution.py:48
  579.6 26.3 %collective-permute-start.62 = (bf16[2,128,2048]{2,1,0:T(8,128)(2,1)}, bf16[2,128,2048]{2,1,0:T(8,128)(2,1)}, u32[]{:S(2)}, u32[]{:S(2)}) collective-permute-start(bf16[2,128,2048]{2,1,0:T(8,128)(2,1)} %bitcast.83), channel_id=1, source_target_pairs={{0,2},{2,0},{1,3},{3,1},{4,6},{6,4},{5,7},{7,5},{8,10},{10,8},{9,1... | collective-permute-start | bytes 3145736 | tf_op jit(solution)/shard_map/ppermute | solution.py:48
  604.9 40.8 %collective-permute-start.60 = (bf16[128,2048]{1,0:T(8,128)(2,1)}, bf16[128,2048]{1,0:T(8,128)(2,1)}, u32[]{:S(2)}, u32[]{:S(2)}) collective-permute-start(bf16[128,2048]{1,0:T(8,128)(2,1)} %fusion.84), channel_id=1, source_target_pairs={{0,2},{2,0},{1,3},{3,1},{4,6},{6,4},{5,7},{7,5},{8,10},{10,8},{9,1... | collective-permute-start | bytes 1572872 | tf_op jit(solution)/shard_map/ppermute | solution.py:48
  620.2 25.5 %collective-permute-start.64 = (bf16[128,2048]{1,0:T(8,128)(2,1)}, bf16[128,2048]{1,0:T(8,128)(2,1)}, u32[]{:S(2)}, u32[]{:S(2)}) collective-permute-start(bf16[128,2048]{1,0:T(8,128)(2,1)} %fusion.85), channel_id=1, source_target_pairs={{0,4},{4,0},{1,5},{5,1},{2,6},{6,2},{3,7},{7,3},{8,12},{12,8},{9,1... | collective-permute-start | bytes 1572872 | tf_op jit(solution)/shard_map/ppermute | solution.py:48
  (173 other events, 2159.3 us)
Sparse Core Ops, SparseCore 0:
  12.2 28.5 all-gather.4
  43.0 62.9 all-gather.6
  108.1 114.0 all-gather.8
  224.2 113.5 all-gather.10
  340.0 108.9 reduce-scatter.3
  451.1 111.2 reduce-scatter.5
  565.3 77.2 reduce-scatter.7

commit v8 on v7

--- a/solution.py
+++ b/solution.py
@@ -109,6 +109,18 @@
 
 def tie_send(state, *earlier):
     return state[0], tie(state[1], *earlier)
+
+
+def ring_gather(block, z_count):
+    rows = block.shape[0]
+    place = lax.axis_index("z")
+    full = jnp.zeros((z_count * rows, block.shape[1]), block.dtype)
+    for step in range(z_count):
+        slot = lax.rem(place + z_count - step, z_count)
+        full = lax.dynamic_update_slice_in_dim(full, block, slot * rows, axis=0)
+        if step < z_count - 1:
+            block = lax.ppermute(block, "z", [(i, (i + 1) % z_count) for i in range(z_count)])
+    return full
 
 
 def sum_everywhere(tensor, z_count, beside):
@@ -710,8 +722,8 @@
         return jnp.concatenate([mlp[:, 0], mlp[:, 1], down], axis=1)
 
     send_qkv = qkv_columns(1 - x_place)
-    all_out = fetch(weight_out.astype(BF))
-    all_ids = doc_ids[:, 0]
+    all_out = ring_gather(tie(weight_out, send_qkv).astype(BF), z_count)
+    all_ids = tie(doc_ids[:, 0], send_qkv)
     for axis in ("y", "c"):
         all_ids = jnp.stack([all_ids, swap(all_ids, axis)], axis=0)
     their_qkv = swap(send_qkv, "x")

time: 707 us -> 701 us (level)
  waiting for transfers between devices: 215 us -> 207 us
    ppermute x66, waiting for transfers between devices: 182 us -> 158 us  [swap(): return lax.ppermute(tensor, axis, [(0, 1), (1, 0)])]
    ppermute x0 -> x3, waiting for transfers between devices: none -> 20.2 us  [ring_gather(): lax.ppermute(block, 'z', [(i, (i + 1) % z_count) for i in range(z_count)])]
    unnamed x274 -> x284, local copies, waits for them, and re-layouts: 20.9 us -> 19.3 us
  transfers between devices with their start and end apart: 78 -> 80, of which waited for: 35 -> 36; matrix products, arithmetic and copies ran while one was open for 28% -> 28% of each run, Pallas kernels for 22% -> 22%
where the time goes in v8:
time: 701 us; the launch traced here: 692 us
  waiting for transfers between devices  207 us (30%)
  Pallas kernels  178 us (25%)
  matrix products  80.3 us (11%)
  starting transfers between devices  80.1 us (11%)
  other arithmetic  78.2 us (11%)
  local copies, waits for them, and re-layouts  50.1 us (7%)
  between operations  18.6 us (3%)
    ppermute x66, waiting for transfers between devices, swap(): return lax.ppermute(tensor, axis, [(0, 1), (1, 0)])  158 us
    dot_general x24, matrix products, mm(): return lax.dot_general(a, b, (dims, ((), ())), preferred_element_type=F32)  80.3 us
    ppermute x66, starting transfers between devices, swap(): return lax.ppermute(tensor, axis, [(0, 1), (1, 0)])  56.9 us
    pallas_call x4, Pallas kernels, feed_forward(): pl.pallas_call(functools.partial(ff_kernel, width, half), grid=(2 * half,...  50.2 us
    pallas_call x3, Pallas kernels, weight_grads(): pl.pallas_call(functools.partial(grads_kernel, count), grid=(D // tile,),...  49.3 us
    pallas_call x2, Pallas kernels, attention_bwd(): pl.pallas_call(functools.partial(attention_bwd_kernel, heads), grid=(seqs...  25.1 us
    pallas_call x1, Pallas kernels, adam_all(): pl.pallas_call(functools.partial(adam_kernel, steps, len(ff_sides)), grid...  22.5 us
    ppermute x3, waiting for transfers between devices, ring_gather(): lax.ppermute(block, 'z', [(i, (i + 1) % z_count) for i in range(z_count)])  20.2 us
  transfers between devices with their start and end apart: 80, of which 36 were waited for; matrix products, arithmetic and copies ran while one was open for 28% of the time, Pallas kernels for 22%

profile of v8, /device:TPU:0, one launch (start us, length us, event | category | flops | bytes accessed | tf_op | source)
XLA Modules:
  0.0 692.1 jit_solution(531573941420994199)
XLA Ops:
  38.4 12.3 %collective-permute-done.11 = bf16[256,512]{1,0:T(8,128)(2,1)S(1)} collective-permute-done((bf16[256,512]{1,0:T(8,128)(2,1)}, bf16[256,512]{1,0:T(8,128)(2,1)S(1)}, u32[]{:S(2)}, u32[]{:S(2)}) %collective-permute-start.11) | collective-permute-done | bytes 262176 | tf_op jit(solution)/shard_map/ppermute | solution.py:122
  63.0 7.9 %collective-permute-done.12 = bf16[256,512]{1,0:T(8,128)(2,1)S(1)} collective-permute-done((bf16[256,512]{1,0:T(8,128)(2,1)S(1)}, bf16[256,512]{1,0:T(8,128)(2,1)S(1)}, u32[]{:S(2)}, u32[]{:S(2)}) %collective-permute-start.12) | collective-permute-done | bytes 262176 | tf_op jit(solution)/shard_map/ppermute | solution.py:122
  85.0 6.5 collective-permute-done.8
  110.6 5.8 collective-permute-done.9
  131.0 6.6 attention_forward.2
  147.6 6.5 attention_forward.3
  167.9 21.1 %collective-permute-done.30 = bf16[2,128,2048]{2,1,0:T(8,128)(2,1)S(1)} collective-permute-done((bf16[2,128,2048]{2,1,0:T(8,128)(2,1)S(1)}, bf16[2,128,2048]{2,1,0:T(8,128)(2,1)S(1)}, u32[]{:S(2)}, u32[]{:S(2)}) %collective-permute-start.30) | collective-permute-done | bytes 1048608 | tf_op jit(solution)/shard_map/ppermute | solution.py:48
  191.4 8.4 %reduce-scatter.4.cloned.1.call-start = ((), (), s32[]{:S(2)}) async-start(), calls=%async_computation.6 | async-start | bytes 7864320 | tf_op jit(solution)/shard_map/reduce_scatter | solution.py:834
  205.0 9.3 %collective-permute-done.21 = bf16[128,2048]{1,0:T(8,128)(2,1)S(1)} collective-permute-done((bf16[128,2048]{1,0:T(8,128)(2,1)S(1)}, bf16[128,2048]{1,0:T(8,128)(2,1)S(1)}, u32[]{:S(2)}, u32[]{:S(2)}) %collective-permute-start.21) | collective-permute-done | bytes 524320 | tf_op jit(solution)/shard_map/ppermute | solution.py:48
  221.5 9.6 %collective-permute-done.33 = bf16[128,2048]{1,0:T(8,128)(2,1)S(1)} collective-permute-done((bf16[128,2048]{1,0:T(8,128)(2,1)S(1)}, bf16[128,2048]{1,0:T(8,128)(2,1)S(1)}, u32[]{:S(2)}, u32[]{:S(2)}) %collective-permute-start.33) | collective-permute-done | bytes 524320 | tf_op jit(solution)/shard_map/ppermute | solution.py:48
  231.9 8.4 %collective-permute-done.23 = bf16[128,2048]{1,0:T(8,128)(2,1)S(1)} collective-permute-done((bf16[128,2048]{1,0:T(8,128)(2,1)S(1)}, bf16[128,2048]{1,0:T(8,128)(2,1)S(1)}, u32[]{:S(2)}, u32[]{:S(2)}) %collective-permute-start.23) | collective-permute-done | bytes 524320 | tf_op jit(solution)/shard_map/ppermute | solution.py:48
  260.1 12.1 %feed_forward.4 = (bf16[512,512]{1,0:T(8,128)(2,1)S(1)}, bf16[512,512]{1,0:T(8,128)(2,1)S(1)}, bf16[512,1024]{1,0:T(8,128)(2,1)S(1)}, bf16[512,1024]{1,0:T(8,128)(2,1)S(1)}) custom-call(bf16[512,2048]{1,0:T(8,128)(2,1)S(1)} %constant_dynamic-update-slice_fusion.x_mine.refs_0_, bf16[512,2048]{1,0:T(8,128)(2,1)} %collective-permute-done.36.x_other.refs_1_, ...), custom_call_target="tpu_custom_call" | custom-call | flops 13958643712 | bytes 1048576 | tf_op jit(solution)/shard_map/feed_forward/pallas_call | solution.py:422
  272.3 13.2 %feed_forward.5 = (bf16[512,512]{1,0:T(8,128)(2,1)S(1)}, bf16[512,512]{1,0:T(8,128)(2,1)S(1)}, bf16[512,1024]{1,0:T(8,128)(2,1)S(1)}, bf16[512,1024]{1,0:T(8,128)(2,1)S(1)}) custom-call(bf16[512,2048]{1,0:T(8,128)(2,1)} %constant_dynamic-update-slice_fusion.8.x_mine.refs_2_, bf16[512,2048]{1,0:T(8,128)(2,1)} %collective-permute-done.38.x_other.refs_3_, ...), custom_call_target="tpu_custom_call" | custom-call | flops 13958643712 | bytes 1048576 | tf_op jit(solution)/shard_map/feed_forward/pallas_call | solution.py:422
  286.5 18.1 %weight_grads.3 = bf16[2048,1536]{1,0:T(8,128)(2,1)} custom-call(bf16[512,2048]{1,0:T(8,128)(2,1)} %copy-done.21, bf16[512,2048]{1,0:T(8,128)(2,1)} %collective-permute-done.36.x_other.refs_1_, bf16[512,2048]{1,0:T(8,128)(2,1)} %constant_dynamic-update-slice_fusion.8.x_mine.refs_2_, bf16[512,2048]{1,0:T(8,128)(2,1)} %collective-permute-done.38.x_other.refs_3_, ...), custom_call_target="tpu_custom_call" | custom-call | flops 19327352832 | bytes 29360128 | tf_op jit(solution)/shard_map/weight_grads/pallas_call | solution.py:518
  306.5 6.8 fusion.2
  313.3 6.8 fusion
  331.2 12.6 %feed_forward.6 = (bf16[512,512]{1,0:T(8,128)(2,1)S(1)}, bf16[512,512]{1,0:T(8,128)(2,1)S(1)}, bf16[512,1024]{1,0:T(8,128)(2,1)S(1)}, bf16[512,1024]{1,0:T(8,128)(2,1)S(1)}) custom-call(bf16[512,2048]{1,0:T(8,128)(2,1)S(1)} %copy-done.22, bf16[512,2048]{1,0:T(8,128)(2,1)} %collective-permute-done.36.x_other.refs_1_, bf16[512,2048]{1,0:T(8,128)(2,1)} %copy-done.98, ...), custom_call_target="tpu_custom_call" | custom-call | flops 13958643712 | bytes 1048576 | tf_op jit(solution)/shard_map/feed_forward/pallas_call | solution.py:422
  352.4 12.2 %feed_forward.7 = (bf16[512,512]{1,0:T(8,128)(2,1)S(1)}, bf16[512,512]{1,0:T(8,128)(2,1)S(1)}, bf16[512,1024]{1,0:T(8,128)(2,1)S(1)}, bf16[512,1024]{1,0:T(8,128)(2,1)S(1)}) custom-call(bf16[512,2048]{1,0:T(8,128)(2,1)} %constant_dynamic-update-slice_fusion.8.x_mine.refs_2_, bf16[512,2048]{1,0:T(8,128)(2,1)} %collective-permute-done.38.x_other.refs_3_, ...), custom_call_target="tpu_custom_call" | custom-call | flops 13958643712 | bytes 1048576 | tf_op jit(solution)/shard_map/feed_forward/pallas_call | solution.py:422
  367.4 6.0 add_convert_fusion
  381.8 8.6 %down_product.2 = (bf16[512,2048]{1,0:T(8,128)(2,1)S(1)}, bf16[512,2048]{1,0:T(8,128)(2,1)}) custom-call(bf16[512,512]{1,0:T(8,128)(2,1)S(1)} %copy-done.37, bf16[512,512]{1,0:T(8,128)(2,1)S(1)} %get-tuple-element.152.refs_1_.refs_12_, bf16[512,512]{1,0:T(8,128)(2,1)S(1)} %copy-done.39, bf16[512,512]{1,0:T(8,128)(2,1)S(1)} %get-tuple-element.170.refs_3_.refs_13_, ...), custom_call_target="tpu_custom_call" | custom-call | flops 4294967296 | bytes 8388608 | tf_op jit(solution)/shard_map/down_product/pallas_call | solution.py:467
  390.3 9.2 %down_product.3 = (bf16[512,2048]{1,0:T(8,128)(2,1)S(1)}, bf16[512,2048]{1,0:T(8,128)(2,1)}) custom-call(bf16[512,512]{1,0:T(8,128)(2,1)S(1)} %copy-done.41, bf16[512,512]{1,0:T(8,128)(2,1)S(1)} %get-tuple-element.163.refs_1_.refs_14_, bf16[512,512]{1,0:T(8,128)(2,1)S(1)} %copy-done.43, bf16[512,512]{1,0:T(8,128)(2,1)S(1)} %get-tuple-element.171.refs_3_.refs_15_, ...), custom_call_target="tpu_custom_call" | custom-call | flops 4294967296 | bytes 8388608 | tf_op jit(solution)/shard_map/down_product/pallas_call | solution.py:467
  410.0 18.3 %weight_grads.4 = bf16[2048,1536]{1,0:T(8,128)(2,1)} custom-call(bf16[512,2048]{1,0:T(8,128)(2,1)} %copy-done.21, bf16[512,2048]{1,0:T(8,128)(2,1)} %collective-permute-done.36.x_other.refs_1_, bf16[512,2048]{1,0:T(8,128)(2,1)} %constant_dynamic-update-slice_fusion.8.x_mine.refs_2_, bf16[512,2048]{1,0:T(8,128)(2,1)} %collective-permute-done.38.x_other.refs_3_, ...), custom_call_target="tpu_custom_call" | custom-call | flops 19327352832 | bytes 29360128 | tf_op jit(solution)/shard_map/weight_grads/pallas_call | solution.py:518
  439.0 11.5 %collective-permute-done.48 = bf16[128,2048]{1,0:T(8,128)(2,1)S(1)} collective-permute-done((bf16[128,2048]{1,0:T(8,128)(2,1)S(1)}, bf16[128,2048]{1,0:T(8,128)(2,1)S(1)}, u32[]{:S(2)}, u32[]{:S(2)}) %collective-permute-start.48) | collective-permute-done | bytes 524320 | tf_op jit(solution)/shard_map/ppermute | solution.py:48
  451.8 10.6 %collective-permute-done.50 = bf16[128,2048]{1,0:T(8,128)(2,1)S(1)} collective-permute-done((bf16[128,2048]{1,0:T(8,128)(2,1)S(1)}, bf16[128,2048]{1,0:T(8,128)(2,1)S(1)}, u32[]{:S(2)}, u32[]{:S(2)}) %collective-permute-start.50) | collective-permute-done | bytes 524320 | tf_op jit(solution)/shard_map/ppermute | solution.py:48
  466.1 10.8 %collective-permute-done.51 = bf16[128,2048]{1,0:T(8,128)(2,1)S(1)} collective-permute-done((bf16[128,2048]{1,0:T(8,128)(2,1)S(1)}, bf16[128,2048]{1,0:T(8,128)(2,1)S(1)}, u32[]{:S(2)}, u32[]{:S(2)}) %collective-permute-start.51) | collective-permute-done | bytes 524320 | tf_op jit(solution)/shard_map/ppermute | solution.py:48
  497.2 12.8 %attention_backward.3 = (bf16[2,2,2,4,32,768]{5,4,3,2,1,0:T(8,128)(2,1)S(1)}, f32[2,2,128]{2,1,0:T(2,128)S(1)}) custom-call(bf16[2,2,2,4,32,768]{5,4,3,2,1,0:T(8,128)(2,1)S(1)} %bitcast.450, f32[2,2,2,4,32,256]{5,4,3,2,1,0:T(8,128)S(1)} %bitcast.452, f32[2,4,128,128]{3,2,1,0:T(8,128)S(1)} %get-tuple-element.292.mask_ref, f32[2,4,128,3]{3,2,1,0:T(8,128)S(1)} %copy-done.13, ...), custom_call_target="tpu_custom_call" | custom-call | flops 14400000000 | bytes 5000000 | tf_op jit(solution)/shard_map/attention_backward/pallas_call | solution.py:349
  516.0 12.4 %attention_backward.2 = (bf16[2,2,2,4,32,768]{5,4,3,2,1,0:T(8,128)(2,1)S(1)}, f32[2,2,128]{2,1,0:T(2,128)S(1)}) custom-call(bf16[2,2,2,4,32,768]{5,4,3,2,1,0:T(8,128)(2,1)S(1)} %bitcast.448, f32[2,2,2,4,32,256]{5,4,3,2,1,0:T(8,128)S(1)} %bitcast.451, f32[2,4,128,128]{3,2,1,0:T(8,128)S(1)} %copy-done.15, f32[2,4,128,3]{3,2,1,0:T(8,128)S(1)} %copy-done.11, ...), custom_call_target="tpu_custom_call" | custom-call | flops 14400000000 | bytes 5000000 | tf_op jit(solution)/shard_map/attention_backward/pallas_call | solution.py:349
  533.7 12.9 %weight_grads.5 = bf16[2048,1024]{1,0:T(8,128)(2,1)} custom-call(bf16[512,2048]{1,0:T(8,128)(2,1)} %pad_maximum_fusion.refs_0_, bf16[512,2048]{1,0:T(8,128)(2,1)} %collective-permute-done.18.refs_1_, bf16[512,2048]{1,0:T(8,128)(2,1)} %pad_maximum_fusion.1.refs_2_, bf16[512,2048]{1,0:T(8,128)(2,1)} %collective-permute-done.25.refs_3_, ...), custom_call_target="tpu_custom_call" | custom-call | flops 12884901888 | bytes 25165824 | tf_op jit(solution)/shard_map/weight_grads/pallas_call | solution.py:518
  577.0 16.2 %collective-permute-done.62 = bf16[2,128,2048]{2,1,0:T(8,128)(2,1)} collective-permute-done((bf16[2,128,2048]{2,1,0:T(8,128)(2,1)S(1)}, bf16[2,128,2048]{2,1,0:T(8,128)(2,1)}, u32[]{:S(2)}, u32[]{:S(2)}) %collective-permute-start.62) | collective-permute-done | bytes 1048608 | tf_op jit(solution)/shard_map/ppermute | solution.py:48
  602.0 9.8 %collective-permute-done.66.refs_23_ = bf16[256,1536]{1,0:T(8,128)(2,1)S(1)} collective-permute-done((bf16[256,1536]{1,0:T(8,128)(2,1)S(1)}, bf16[256,1536]{1,0:T(8,128)(2,1)S(1)}, u32[]{:S(2)}, u32[]{:S(2)}) %collective-permute-start.66) | collective-permute-done | bytes 786464 | tf_op jit(solution)/shard_map/ppermute | solution.py:48
  617.0 18.9 %reduce-scatter.8.cloned.1.call-done.refs_18_ = bf16[512,1024]{1,0:T(8,128)(2,1)} async-done(((bf16[2048,1024]{1,0:T(8,128)(2,1)}), bf16[512,1024]{1,0:T(8,128)(2,1)}) %reduce-scatter.8.cloned.1.call-update) | async-done | bytes 1048592 | tf_op jit(solution)/shard_map/reduce_scatter | solution.py:834
  662.5 22.5 %adam.1 = (f32[3,256,512]{2,1,0:T(8,128)}, f32[3,256,512]{2,1,0:T(8,128)}, f32[3,256,512]{2,1,0:T(8,128)}, f32[256,512]{1,0:T(8,128)}, f32[256,512]{1,0:T(8,128)...) custom-call(s32[1]{0:T(128)} %bitcast.88.place_ref, ...), custom_call_target="tpu_custom_call" | custom-call | flops 41943040 | bytes 50331648 | tf_op jit(solution)/shard_map/adam/pallas_call | solution.py:632
  (588 shorter events, 308.8 us)
Async XLA Ops:
  7.2 115.6 %all-gather.4.cloned.1.call-start = ((), (), s32[]{:S(2)}) async-start(), calls=%async_computation.3 | async-start | bytes 3932160 | tf_op jit(solution)/shard_map/all_gather | solution.py:707
  18.6 77.6 %collective-permute-start.24 = (bf16[128,2048]{1,0:T(8,128)(2,1)}, bf16[128,2048]{1,0:T(8,128)(2,1)}, u32[]{:S(2)}, u32[]{:S(2)}) collective-permute-start(bf16[128,2048]{1,0:T(8,128)(2,1)} %get-tuple-element.122), channel_id=1, source_target_pairs={{0,2},{2,0},{1,3},{3,1},{4,6},{6,4},{5,7},{7,5},{8,10},{10,8},{9,1... | collective-permute-start | bytes 1572872 | tf_op jit(solution)/shard_map/ppermute | solution.py:48
  19.1 52.9 %collective-permute-start = (bf16[128,2048]{1,0:T(8,128)(2,1)}, bf16[128,2048]{1,0:T(8,128)(2,1)}, u32[]{:S(2)}, u32[]{:S(2)}) collective-permute-start(bf16[128,2048]{1,0:T(8,128)(2,1)} %get-tuple-element.120), channel_id=1, source_target_pairs={{0,2},{2,0},{1,3},{3,1},{4,6},{6,4},{5,7},{7,5},{8,10},{10,8},{9,1... | collective-permute-start | bytes 1572872 | tf_op jit(solution)/shard_map/ppermute | solution.py:48
  24.1 236.0 %all-gather.6.cloned.1.call-start = ((), (), s32[]{:S(2)}) async-start(), calls=%async_computation.4 | async-start | bytes 7864320 | tf_op jit(solution)/shard_map/all_gather | solution.py:707
  32.5 21.6 %collective-permute-start.7 = (bf16[128,2048]{1,0:T(8,128)(2,1)}, bf16[128,2048]{1,0:T(8,128)(2,1)}, u32[]{:S(2)}, u32[]{:S(2)}) collective-permute-start(bf16[128,2048]{1,0:T(8,128)(2,1)} %get-tuple-element.122), channel_id=1, source_target_pairs={{0,4},{4,0},{1,5},{5,1},{2,6},{6,2},{3,7},{7,3},{8,12},{12,8},{9,1... | collective-permute-start | bytes 1572872 | tf_op jit(solution)/shard_map/ppermute | solution.py:48
  33.5 23.8 %collective-permute-start.5 = (bf16[128,2048]{1,0:T(8,128)(2,1)}, bf16[128,2048]{1,0:T(8,128)(2,1)S(1)}, u32[]{:S(2)}, u32[]{:S(2)}) collective-permute-start(bf16[128,2048]{1,0:T(8,128)(2,1)} %get-tuple-element.120), channel_id=1, source_target_pairs={{0,4},{4,0},{1,5},{5,1},{2,6},{6,2},{3,7},{7,3},{8,12},{12,8},{9,1... | collective-permute-start | bytes 1572872 | tf_op jit(solution)/shard_map/ppermute | solution.py:48
  74.7 52.7 %collective-permute-start.18 = (bf16[512,2048]{1,0:T(8,128)(2,1)}, bf16[512,2048]{1,0:T(8,128)(2,1)}, u32[]{:S(2)}, u32[]{:S(2)}) collective-permute-start(bf16[512,2048]{1,0:T(8,128)(2,1)} %pad_maximum_fusion.refs_0_), channel_id=1, source_target_pairs={{0,1},{1,0},{2,3},{3,2},{4,5},{5,4},{6,7},{7,6},{8,9},{9,8},{10,11... | collective-permute-start | bytes 6291464 | tf_op jit(solution)/shard_map/ppermute | solution.py:48
  91.9 239.3 %all-gather.8.cloned.1.call-start = ((), (), s32[]{:S(2)}) async-start(), calls=%async_computation.5 | async-start | bytes 7864320 | tf_op jit(solution)/shard_map/all_gather | solution.py:707
  94.2 22.1 %collective-permute-start.9 = (bf16[128,2048]{1,0:T(8,128)(2,1)}, bf16[128,2048]{1,0:T(8,128)(2,1)S(1)}, u32[]{:S(2)}, u32[]{:S(2)}) collective-permute-start(bf16[128,2048]{1,0:T(8,128)(2,1)} %bitcast.477), channel_id=1, source_target_pairs={{0,2},{2,0},{1,3},{3,1},{4,6},{6,4},{5,7},{7,5},{8,10},{10,8},{9,1... | collective-permute-start | bytes 1572872 | tf_op jit(solution)/shard_map/ppermute | solution.py:48
  96.2 24.3 %collective-permute-start.16 = (bf16[128,2048]{1,0:T(8,128)(2,1)S(1)}, bf16[128,2048]{1,0:T(8,128)(2,1)}, u32[]{:S(2)}, u32[]{:S(2)}) collective-permute-start(bf16[128,2048]{1,0:T(8,128)(2,1)S(1)} %bitcast.475), channel_id=1, source_target_pairs={{0,4},{4,0},{1,5},{5,1},{2,6},{6,2},{3,7},{7,3},{8,12},{12,8},{9,1... | collective-permute-start | bytes 1572872 | tf_op jit(solution)/shard_map/ppermute | solution.py:48
  106.5 31.9 %collective-permute-start.25 = (bf16[512,2048]{1,0:T(8,128)(2,1)}, bf16[512,2048]{1,0:T(8,128)(2,1)}, u32[]{:S(2)}, u32[]{:S(2)}) collective-permute-start(bf16[512,2048]{1,0:T(8,128)(2,1)} %pad_maximum_fusion.1.refs_2_), channel_id=1, source_target_pairs={{0,1},{1,0},{2,3},{3,2},{4,5},{5,4},{6,7},{7,6},{8,9},{9,8},{10,11... | collective-permute-start | bytes 6291464 | tf_op jit(solution)/shard_map/ppermute | solution.py:48
  120.8 33.4 %collective-permute-start.27 = (bf16[128,2048]{1,0:T(8,128)(2,1)}, bf16[128,2048]{1,0:T(8,128)(2,1)}, u32[]{:S(2)}, u32[]{:S(2)}) collective-permute-start(bf16[128,2048]{1,0:T(8,128)(2,1)} %collective-permute-done.15), channel_id=1, source_target_pairs={{0,2},{2,0},{1,3},{3,1},{4,6},{6,4},{5,7},{7,5},{8,10},{10,8},{9,1... | collective-permute-start | bytes 1572872 | tf_op jit(solution)/shard_map/ppermute | solution.py:48
  122.4 31.8 %collective-permute-start.28 = (bf16[128,2048]{1,0:T(8,128)(2,1)}, bf16[128,2048]{1,0:T(8,128)(2,1)}, u32[]{:S(2)}, u32[]{:S(2)}) collective-permute-start(bf16[128,2048]{1,0:T(8,128)(2,1)} %collective-permute-done.16), channel_id=1, source_target_pairs={{0,2},{2,0},{1,3},{3,1},{4,6},{6,4},{5,7},{7,5},{8,10},{10,8},{9,1... | collective-permute-start | bytes 1572872 | tf_op jit(solution)/shard_map/ppermute | solution.py:48
  163.9 25.2 %collective-permute-start.30 = (bf16[2,128,2048]{2,1,0:T(8,128)(2,1)S(1)}, bf16[2,128,2048]{2,1,0:T(8,128)(2,1)S(1)}, u32[]{:S(2)}, u32[]{:S(2)}) collective-permute-start(bf16[2,128,2048]{2,1,0:T(8,128)(2,1)S(1)} %bitcast.494), channel_id=1, source_target_pairs={{0,2},{2,0},{1,3},{3,1},{4,6},{6,4},{5,7},{7,5},{8,10},{10,8},{9,1... | collective-permute-start | bytes 3145736 | tf_op jit(solution)/shard_map/ppermute | solution.py:48
  167.0 32.8 %collective-permute-start.20 = (bf16[2,128,2048]{2,1,0:T(8,128)(2,1)S(1)}, bf16[2,128,2048]{2,1,0:T(8,128)(2,1)}, u32[]{:S(2)}, u32[]{:S(2)}) collective-permute-start(bf16[2,128,2048]{2,1,0:T(8,128)(2,1)S(1)} %bitcast.493), channel_id=1, source_target_pairs={{0,4},{4,0},{1,5},{5,1},{2,6},{6,2},{3,7},{7,3},{8,12},{12,8},{9,1... | collective-permute-start | bytes 3145736 | tf_op jit(solution)/shard_map/ppermute | solution.py:48
  191.4 319.8 %reduce-scatter.4.cloned.1.call-start = ((), (), s32[]{:S(2)}) async-start(), calls=%async_computation.6 | async-start | bytes 7864320 | tf_op jit(solution)/shard_map/reduce_scatter | solution.py:834
  218.1 22.1 %collective-permute-start.23 = (bf16[128,2048]{1,0:T(8,128)(2,1)S(1)}, bf16[128,2048]{1,0:T(8,128)(2,1)S(1)}, u32[]{:S(2)}, u32[]{:S(2)}) collective-permute-start(bf16[128,2048]{1,0:T(8,128)(2,1)S(1)} %get-tuple-element.139), channel_id=1, source_target_pairs={{0,4},{4,0},{1,5},{5,1},{2,6},{6,2},{3,7},{7,3},{8,12},{12,8},{9,1... | collective-permute-start | bytes 1572872 | tf_op jit(solution)/shard_map/ppermute | solution.py:48
  306.2 287.0 %reduce-scatter.6.cloned.1.call-start = ((), (), s32[]{:S(2)}) async-start(), calls=%async_computation.7 | async-start | bytes 7864320 | tf_op jit(solution)/shard_map/reduce_scatter | solution.py:834
  376.4 25.3 %collective-permute-start.42 = (bf16[2,128,2048]{2,1,0:T(8,128)(2,1)S(1)}, bf16[2,128,2048]{2,1,0:T(8,128)(2,1)}, u32[]{:S(2)}, u32[]{:S(2)}) collective-permute-start(bf16[2,128,2048]{2,1,0:T(8,128)(2,1)S(1)} %bitcast.491), channel_id=1, source_target_pairs={{0,4},{4,0},{1,5},{5,1},{2,6},{6,2},{3,7},{7,3},{8,12},{12,8},{9,1... | collective-permute-start | bytes 3145736 | tf_op jit(solution)/shard_map/ppermute | solution.py:48
  380.3 25.6 %collective-permute-start.43 = (bf16[2,128,2048]{2,1,0:T(8,128)(2,1)}, bf16[2,128,2048]{2,1,0:T(8,128)(2,1)}, u32[]{:S(2)}, u32[]{:S(2)}) collective-permute-start(bf16[2,128,2048]{2,1,0:T(8,128)(2,1)} %bitcast.51), channel_id=1, source_target_pairs={{0,2},{2,0},{1,3},{3,1},{4,6},{6,4},{5,7},{7,5},{8,10},{10,8},{9,1... | collective-permute-start | bytes 3145736 | tf_op jit(solution)/shard_map/ppermute | solution.py:48
  404.4 24.1 %collective-permute-start.44 = (bf16[128,2048]{1,0:T(8,128)(2,1)}, bf16[128,2048]{1,0:T(8,128)(2,1)}, u32[]{:S(2)}, u32[]{:S(2)}) collective-permute-start(bf16[128,2048]{1,0:T(8,128)(2,1)} %get-tuple-element.255), channel_id=1, source_target_pairs={{0,2},{2,0},{1,3},{3,1},{4,6},{6,4},{5,7},{7,5},{8,10},{10,8},{9,1... | collective-permute-start | bytes 1572872 | tf_op jit(solution)/shard_map/ppermute | solution.py:48
  428.5 207.4 %reduce-scatter.8.cloned.1.call-start = ((), (), s32[]{:S(2)}) async-start(), calls=%async_computation.8 | async-start | bytes 5242880 | tf_op jit(solution)/shard_map/reduce_scatter | solution.py:834
  436.2 40.9 %collective-permute-start.46 = (bf16[512,2048]{1,0:T(8,128)(2,1)S(1)}, bf16[512,2048]{1,0:T(8,128)(2,1)S(1)}, u32[]{:S(2)}, u32[]{:S(2)}) collective-permute-start(bf16[512,2048]{1,0:T(8,128)(2,1)S(1)} %copy-done.124), channel_id=1, source_target_pairs={{0,1},{1,0},{2,3},{3,2},{4,5},{5,4},{6,7},{7,6},{8,9},{9,8},{10,11... | collective-permute-start | bytes 6291464 | tf_op jit(solution)/shard_map/ppermute | solution.py:48
  436.8 42.8 %collective-permute-start.54 = (bf16[512,2048]{1,0:T(8,128)(2,1)S(1)}, bf16[512,2048]{1,0:T(8,128)(2,1)S(1)}, u32[]{:S(2)}, u32[]{:S(2)}) collective-permute-start(bf16[512,2048]{1,0:T(8,128)(2,1)S(1)} %copy-done.123), channel_id=1, source_target_pairs={{0,1},{1,0},{2,3},{3,2},{4,5},{5,4},{6,7},{7,6},{8,9},{9,8},{10,11... | collective-permute-start | bytes 6291464 | tf_op jit(solution)/shard_map/ppermute | solution.py:48
  438.5 23.9 %collective-permute-start.50 = (bf16[128,2048]{1,0:T(8,128)(2,1)S(1)}, bf16[128,2048]{1,0:T(8,128)(2,1)S(1)}, u32[]{:S(2)}, u32[]{:S(2)}) collective-permute-start(bf16[128,2048]{1,0:T(8,128)(2,1)S(1)} %get-tuple-element.182), channel_id=1, source_target_pairs={{0,2},{2,0},{1,3},{3,1},{4,6},{6,4},{5,7},{7,5},{8,10},{10,8},{9,1... | collective-permute-start | bytes 1572872 | tf_op jit(solution)/shard_map/ppermute | solution.py:48
  485.6 27.4 %collective-permute-start.55 = (bf16[512,2048]{1,0:T(8,128)(2,1)}, bf16[512,2048]{1,0:T(8,128)(2,1)}, u32[]{:S(2)}, u32[]{:S(2)}) collective-permute-start(bf16[512,2048]{1,0:T(8,128)(2,1)} %constant_dynamic-update-slice_fusion.16.refs_4_), channel_id=1, source_target_pairs={{0,1},{1,0},{2,3},{3,2},{4,5},{5,4},{6,7},{7,6},{8,9},{9,8},{10,11... | collective-permute-start | bytes 6291464 | tf_op jit(solution)/shard_map/ppermute | solution.py:48
  491.3 37.1 %collective-permute-start.53 = (bf16[2,128,2048]{2,1,0:T(8,128)(2,1)}, bf16[2,128,2048]{2,1,0:T(8,128)(2,1)}, u32[]{:S(2)}, u32[]{:S(2)}) collective-permute-start(bf16[2,128,2048]{2,1,0:T(8,128)(2,1)} %bitcast.61), channel_id=1, source_target_pairs={{0,4},{4,0},{1,5},{5,1},{2,6},{6,2},{3,7},{7,3},{8,12},{12,8},{9,1... | collective-permute-start | bytes 3145736 | tf_op jit(solution)/shard_map/ppermute | solution.py:48
  492.9 35.5 %collective-permute-start.58 = (bf16[2,128,2048]{2,1,0:T(8,128)(2,1)}, bf16[2,128,2048]{2,1,0:T(8,128)(2,1)}, u32[]{:S(2)}, u32[]{:S(2)}) collective-permute-start(bf16[2,128,2048]{2,1,0:T(8,128)(2,1)} %bitcast.62), channel_id=1, source_target_pairs={{0,2},{2,0},{1,3},{3,1},{4,6},{6,4},{5,7},{7,5},{8,10},{10,8},{9,1... | collective-permute-start | bytes 3145736 | tf_op jit(solution)/shard_map/ppermute | solution.py:48
  569.5 23.7 %collective-permute-start.62 = (bf16[2,128,2048]{2,1,0:T(8,128)(2,1)S(1)}, bf16[2,128,2048]{2,1,0:T(8,128)(2,1)}, u32[]{:S(2)}, u32[]{:S(2)}) collective-permute-start(bf16[2,128,2048]{2,1,0:T(8,128)(2,1)S(1)} %bitcast.492), channel_id=1, source_target_pairs={{0,4},{4,0},{1,5},{5,1},{2,6},{6,2},{3,7},{7,3},{8,12},{12,8},{9,1... | collective-permute-start | bytes 3145736 | tf_op jit(solution)/shard_map/ppermute | solution.py:48
  573.4 26.2 %collective-permute-start.65 = (bf16[2,128,2048]{2,1,0:T(8,128)(2,1)}, bf16[2,128,2048]{2,1,0:T(8,128)(2,1)}, u32[]{:S(2)}, u32[]{:S(2)}) collective-permute-start(bf16[2,128,2048]{2,1,0:T(8,128)(2,1)} %bitcast.83), channel_id=1, source_target_pairs={{0,2},{2,0},{1,3},{3,1},{4,6},{6,4},{5,7},{7,5},{8,10},{10,8},{9,1... | collective-permute-start | bytes 3145736 | tf_op jit(solution)/shard_map/ppermute | solution.py:48
  598.1 40.8 %collective-permute-start.63 = (bf16[128,2048]{1,0:T(8,128)(2,1)}, bf16[128,2048]{1,0:T(8,128)(2,1)}, u32[]{:S(2)}, u32[]{:S(2)}) collective-permute-start(bf16[128,2048]{1,0:T(8,128)(2,1)} %fusion.84), channel_id=1, source_target_pairs={{0,2},{2,0},{1,3},{3,1},{4,6},{6,4},{5,7},{7,5},{8,10},{10,8},{9,1... | collective-permute-start | bytes 1572872 | tf_op jit(solution)/shard_map/ppermute | solution.py:48
  611.8 27.1 %collective-permute-start.67 = (bf16[128,2048]{1,0:T(8,128)(2,1)}, bf16[128,2048]{1,0:T(8,128)(2,1)}, u32[]{:S(2)}, u32[]{:S(2)}) collective-permute-start(bf16[128,2048]{1,0:T(8,128)(2,1)} %fusion.85), channel_id=1, source_target_pairs={{0,4},{4,0},{1,5},{5,1},{2,6},{6,2},{3,7},{7,3},{8,12},{12,8},{9,1... | collective-permute-start | bytes 1572872 | tf_op jit(solution)/shard_map/ppermute | solution.py:48
  (180 other events, 2558.7 us)
Sparse Core Ops, SparseCore 0:
  24.2 75.2 all-gather.3
  101.6 113.7 all-gather.5
  217.6 113.5 all-gather.7
  333.4 108.9 reduce-scatter.3
  444.5 111.2 reduce-scatter.5
  558.6 77.2 reduce-scatter.7

commit v9 on v8

--- a/solution.py
+++ b/solution.py
@@ -111,15 +111,17 @@
     return state[0], tie(state[1], *earlier)
 
 
-def ring_gather(block, z_count):
+def direct_gather(block, z_count):
     rows = block.shape[0]
     place = lax.axis_index("z")
+    pieces = [block]
+    for step in range(1, z_count):
+        pairs = [(i, (i + step) % z_count) for i in range(z_count)]
+        pieces.append(lax.ppermute(block, "z", pairs))
     full = jnp.zeros((z_count * rows, block.shape[1]), block.dtype)
-    for step in range(z_count):
+    for step, piece in enumerate(pieces):
         slot = lax.rem(place + z_count - step, z_count)
-        full = lax.dynamic_update_slice_in_dim(full, block, slot * rows, axis=0)
-        if step < z_count - 1:
-            block = lax.ppermute(block, "z", [(i, (i + 1) % z_count) for i in range(z_count)])
+        full = lax.dynamic_update_slice_in_dim(full, piece, slot * rows, axis=0)
     return full
 
 
@@ -538,6 +540,31 @@
 RATE_DOWN = FF ** (-0.5)
 
 
+def small_kernel(owned_ref, att_ref, gains_ref, gate_ref, out_ref):
+    wide = att_ref[...].astype(F32)
+    squares = jnp.sum(wide * wide, axis=(0, 1), keepdims=True) + owned_ref[0]
+    count = gains_ref.shape[0]
+    out_ref[:count] = gains_ref[...]
+    lane = lax.broadcasted_iota(jnp.int32, gate_ref.shape, 1)
+    out_ref[count:] = jnp.where(lane == HEADS, squares, gate_ref[...])
+
+
+def small_sums(owned, own_att, gains, gate_row):
+    return pl.pallas_call(
+        small_kernel,
+        in_specs=[
+            pl.BlockSpec(memory_space=pltpu.SMEM),
+            pl.BlockSpec(memory_space=pltpu.VMEM),
+            pl.BlockSpec(memory_space=pltpu.VMEM),
+            pl.BlockSpec(memory_space=pltpu.VMEM),
+        ],
+        out_specs=pl.BlockSpec(memory_space=pltpu.VMEM),
+        out_shape=jax.ShapeDtypeStruct((gains.shape[0] + 1, 128), F32),
+        compiler_params=pltpu.CompilerParams(vmem_limit_bytes=16 * 1024 * 1024),
+        name="small_sums",
+    )(owned[None], own_att, gains, gate_row)
+
+
 def clip_factor(small):
     row = lax.broadcasted_iota(jnp.int32, small.shape, 0)
     lane = lax.broadcasted_iota(jnp.int32, small.shape, 1)
@@ -722,7 +749,7 @@
         return jnp.concatenate([mlp[:, 0], mlp[:, 1], down], axis=1)
 
     send_qkv = qkv_columns(1 - x_place)
-    all_out = ring_gather(tie(weight_out, send_qkv).astype(BF), z_count)
+    all_out = direct_gather(tie(weight_out, send_qkv).astype(BF), z_count)
     all_ids = tie(doc_ids[:, 0], send_qkv)
     for axis in ("y", "c"):
         all_ids = jnp.stack([all_ids, swap(all_ids, axis)], axis=0)
@@ -956,10 +983,9 @@
     gate_padded = lax.dynamic_update_slice(
         jnp.zeros(gate_logit.shape, F32), gate_grad, (head_start,)
     )
-    owned = squares_of(own_att) + ff_owned
     gain_grad = mlp_view(jnp.stack([gain_grad_att, gain_grad_mlp], axis=0)[None])
-    last_row = jnp.concatenate([gate_padded, owned[None], jnp.zeros((127 - HEADS,), F32)])
-    small = jnp.concatenate([gain_grad, last_row[None]], axis=0)
+    gate_row = jnp.concatenate([gate_padded, jnp.zeros((128 - HEADS,), F32)])[None]
+    small = small_sums(ff_owned, own_att, gain_grad, gate_row)
     small = sum_everywhere(small, z_count, att_theirs)
     arrays = [
         weight_qkv,

time: 701 us -> 709 us (1.011)
  local copies, waits for them, and re-layouts: 50.1 us -> 63.2 us
    ppermute x66, waiting for transfers between devices: 158 us -> 191 us  [swap(): return lax.ppermute(tensor, axis, [(0, 1), (1, 0)])]
    ppermute x3, waiting for transfers between devices: 20.2 us -> 0.01 us  [direct_gather(): pieces.append(lax.ppermute(block, 'z', pairs))]
    reduce_scatter x3, waiting for transfers between devices: 18.9 us -> 5.56 us  [reduce_rows(): return lax.psum_scatter(partial, 'z', scatter_dimension=0, tiled=True)]
  transfers between devices with their start and end apart: 80 -> 80, of which waited for: 36 -> 37; matrix products, arithmetic and copies ran while one was open for 28% -> 29% of each run, Pallas kernels for 22% -> 22%
where the time goes in v9:
time: 709 us; the launch traced here: 701 us
  waiting for transfers between devices  208 us (29%)
  Pallas kernels  179 us (25%)
  matrix products  81.7 us (12%)
  starting transfers between devices  78.7 us (11%)
  other arithmetic  72.5 us (10%)
  local copies, waits for them, and re-layouts  63.2 us (9%)
  between operations  17.8 us (3%)
    ppermute x66, waiting for transfers between devices, swap(): return lax.ppermute(tensor, axis, [(0, 1), (1, 0)])  191 us
    dot_general x24, matrix products, mm(): return lax.dot_general(a, b, (dims, ((), ())), preferred_element_type=F32)  81.7 us
    ppermute x66, starting transfers between devices, swap(): return lax.ppermute(tensor, axis, [(0, 1), (1, 0)])  54.1 us
    pallas_call x4, Pallas kernels, feed_forward(): pl.pallas_call(functools.partial(ff_kernel, width, half), grid=(2 * half,...  50.3 us
    pallas_call x3, Pallas kernels, weight_grads(): pl.pallas_call(functools.partial(grads_kernel, count), grid=(D // tile,),...  49.5 us
    pallas_call x2, Pallas kernels, attention_bwd(): pl.pallas_call(functools.partial(attention_bwd_kernel, heads), grid=(seqs...  25.1 us
    unnamed x284, local copies, waits for them, and re-layouts  24.2 us
    pallas_call x1, Pallas kernels, adam_all(): pl.pallas_call(functools.partial(adam_kernel, steps, len(ff_sides)), grid...  22.5 us
  transfers between devices with their start and end apart: 80, of which 37 were waited for; matrix products, arithmetic and copies ran while one was open for 29% of the time, Pallas kernels for 22%

profile of v9, /device:TPU:0, one launch (start us, length us, event | category | flops | bytes accessed | tf_op | source)
XLA Modules:
  0.0 701.0 jit_solution(12670323232731916389)
XLA Ops:
  42.3 9.4 %collective-permute-done.7 = bf16[128,2048]{1,0:T(8,128)(2,1)} collective-permute-done((bf16[128,2048]{1,0:T(8,128)(2,1)}, bf16[128,2048]{1,0:T(8,128)(2,1)}, u32[]{:S(2)}, u32[]{:S(2)}) %collective-permute-start.7) | collective-permute-done | bytes 524320 | tf_op jit(solution)/shard_map/ppermute | solution.py:48
  52.2 9.2 %collective-permute-done.5 = bf16[128,2048]{1,0:T(8,128)(2,1)} collective-permute-done((bf16[128,2048]{1,0:T(8,128)(2,1)}, bf16[128,2048]{1,0:T(8,128)(2,1)}, u32[]{:S(2)}, u32[]{:S(2)}) %collective-permute-start.5) | collective-permute-done | bytes 524320 | tf_op jit(solution)/shard_map/ppermute | solution.py:48
  76.3 5.9 collective-permute-done.6
  93.3 8.5 %collective-permute-done.8 = bf16[128,2048]{1,0:T(8,128)(2,1)} collective-permute-done((bf16[128,2048]{1,0:T(8,128)(2,1)}, bf16[128,2048]{1,0:T(8,128)(2,1)}, u32[]{:S(2)}, u32[]{:S(2)}) %collective-permute-start.8) | collective-permute-done | bytes 524320 | tf_op jit(solution)/shard_map/ppermute | solution.py:48
  141.4 6.6 attention_forward.2
  157.8 6.5 attention_forward.3
  177.8 21.5 %collective-permute-done.30 = bf16[2,128,2048]{2,1,0:T(8,128)(2,1)S(1)} collective-permute-done((bf16[2,128,2048]{2,1,0:T(8,128)(2,1)S(1)}, bf16[2,128,2048]{2,1,0:T(8,128)(2,1)S(1)}, u32[]{:S(2)}, u32[]{:S(2)}) %collective-permute-start.30) | collective-permute-done | bytes 1048608 | tf_op jit(solution)/shard_map/ppermute | solution.py:48
  201.5 8.4 %reduce-scatter.4.cloned.1.call-start = ((), (), s32[]{:S(2)}) async-start(), calls=%async_computation.6 | async-start | bytes 7864320 | tf_op jit(solution)/shard_map/reduce_scatter | solution.py:861
  215.3 9.3 %collective-permute-done.21 = bf16[128,2048]{1,0:T(8,128)(2,1)S(1)} collective-permute-done((bf16[128,2048]{1,0:T(8,128)(2,1)S(1)}, bf16[128,2048]{1,0:T(8,128)(2,1)S(1)}, u32[]{:S(2)}, u32[]{:S(2)}) %collective-permute-start.21) | collective-permute-done | bytes 524320 | tf_op jit(solution)/shard_map/ppermute | solution.py:48
  231.7 9.6 %collective-permute-done.33 = bf16[128,2048]{1,0:T(8,128)(2,1)S(1)} collective-permute-done((bf16[128,2048]{1,0:T(8,128)(2,1)S(1)}, bf16[128,2048]{1,0:T(8,128)(2,1)S(1)}, u32[]{:S(2)}, u32[]{:S(2)}) %collective-permute-start.33) | collective-permute-done | bytes 524320 | tf_op jit(solution)/shard_map/ppermute | solution.py:48
  241.8 8.3 %collective-permute-done.23 = bf16[128,2048]{1,0:T(8,128)(2,1)S(1)} collective-permute-done((bf16[128,2048]{1,0:T(8,128)(2,1)S(1)}, bf16[128,2048]{1,0:T(8,128)(2,1)S(1)}, u32[]{:S(2)}, u32[]{:S(2)}) %collective-permute-start.23) | collective-permute-done | bytes 524320 | tf_op jit(solution)/shard_map/ppermute | solution.py:48
  269.9 12.2 %feed_forward.4 = (bf16[512,512]{1,0:T(8,128)(2,1)S(1)}, bf16[512,512]{1,0:T(8,128)(2,1)S(1)}, bf16[512,1024]{1,0:T(8,128)(2,1)S(1)}, bf16[512,1024]{1,0:T(8,128)(2,1)S(1)}) custom-call(bf16[512,2048]{1,0:T(8,128)(2,1)S(1)} %constant_dynamic-update-slice_fusion.x_mine.refs_0_, bf16[512,2048]{1,0:T(8,128)(2,1)} %collective-permute-done.36.x_other.refs_1_, ...), custom_call_target="tpu_custom_call" | custom-call | flops 13958643712 | bytes 1048576 | tf_op jit(solution)/shard_map/feed_forward/pallas_call | solution.py:424
  282.1 13.2 %feed_forward.5 = (bf16[512,512]{1,0:T(8,128)(2,1)S(1)}, bf16[512,512]{1,0:T(8,128)(2,1)S(1)}, bf16[512,1024]{1,0:T(8,128)(2,1)S(1)}, bf16[512,1024]{1,0:T(8,128)(2,1)S(1)}) custom-call(bf16[512,2048]{1,0:T(8,128)(2,1)} %constant_dynamic-update-slice_fusion.8.x_mine.refs_2_, bf16[512,2048]{1,0:T(8,128)(2,1)} %collective-permute-done.38.x_other.refs_3_, ...), custom_call_target="tpu_custom_call" | custom-call | flops 13958643712 | bytes 1048576 | tf_op jit(solution)/shard_map/feed_forward/pallas_call | solution.py:424
  296.3 18.1 %weight_grads.3 = bf16[2048,1536]{1,0:T(8,128)(2,1)} custom-call(bf16[512,2048]{1,0:T(8,128)(2,1)} %copy-done.22, bf16[512,2048]{1,0:T(8,128)(2,1)} %collective-permute-done.36.x_other.refs_1_, bf16[512,2048]{1,0:T(8,128)(2,1)} %constant_dynamic-update-slice_fusion.8.x_mine.refs_2_, bf16[512,2048]{1,0:T(8,128)(2,1)} %collective-permute-done.38.x_other.refs_3_, ...), custom_call_target="tpu_custom_call" | custom-call | flops 19327352832 | bytes 29360128 | tf_op jit(solution)/shard_map/weight_grads/pallas_call | solution.py:520
  316.3 6.8 fusion.2
  323.1 6.8 fusion
  343.0 12.6 %feed_forward.6 = (bf16[512,512]{1,0:T(8,128)(2,1)S(1)}, bf16[512,512]{1,0:T(8,128)(2,1)S(1)}, bf16[512,1024]{1,0:T(8,128)(2,1)S(1)}, bf16[512,1024]{1,0:T(8,128)(2,1)S(1)}) custom-call(bf16[512,2048]{1,0:T(8,128)(2,1)S(1)} %copy-done.23, bf16[512,2048]{1,0:T(8,128)(2,1)} %collective-permute-done.36.x_other.refs_1_, bf16[512,2048]{1,0:T(8,128)(2,1)} %copy-done.97, ...), custom_call_target="tpu_custom_call" | custom-call | flops 13958643712 | bytes 1048576 | tf_op jit(solution)/shard_map/feed_forward/pallas_call | solution.py:424
  364.2 12.2 %feed_forward.7 = (bf16[512,512]{1,0:T(8,128)(2,1)S(1)}, bf16[512,512]{1,0:T(8,128)(2,1)S(1)}, bf16[512,1024]{1,0:T(8,128)(2,1)S(1)}, bf16[512,1024]{1,0:T(8,128)(2,1)S(1)}) custom-call(bf16[512,2048]{1,0:T(8,128)(2,1)} %constant_dynamic-update-slice_fusion.8.x_mine.refs_2_, bf16[512,2048]{1,0:T(8,128)(2,1)} %collective-permute-done.38.x_other.refs_3_, ...), custom_call_target="tpu_custom_call" | custom-call | flops 13958643712 | bytes 1048576 | tf_op jit(solution)/shard_map/feed_forward/pallas_call | solution.py:424
  379.2 6.0 add_convert_fusion
  393.5 8.6 %down_product.2 = (bf16[512,2048]{1,0:T(8,128)(2,1)S(1)}, bf16[512,2048]{1,0:T(8,128)(2,1)}) custom-call(bf16[512,512]{1,0:T(8,128)(2,1)S(1)} %copy-done.38, bf16[512,512]{1,0:T(8,128)(2,1)S(1)} %get-tuple-element.152.refs_1_.refs_12_, bf16[512,512]{1,0:T(8,128)(2,1)S(1)} %copy-done.40, bf16[512,512]{1,0:T(8,128)(2,1)S(1)} %get-tuple-element.170.refs_3_.refs_13_, ...), custom_call_target="tpu_custom_call" | custom-call | flops 4294967296 | bytes 8388608 | tf_op jit(solution)/shard_map/down_product/pallas_call | solution.py:469
  402.1 9.2 %down_product.3 = (bf16[512,2048]{1,0:T(8,128)(2,1)S(1)}, bf16[512,2048]{1,0:T(8,128)(2,1)}) custom-call(bf16[512,512]{1,0:T(8,128)(2,1)S(1)} %copy-done.42, bf16[512,512]{1,0:T(8,128)(2,1)S(1)} %get-tuple-element.163.refs_1_.refs_14_, bf16[512,512]{1,0:T(8,128)(2,1)S(1)} %copy-done.44, bf16[512,512]{1,0:T(8,128)(2,1)S(1)} %get-tuple-element.171.refs_3_.refs_15_, ...), custom_call_target="tpu_custom_call" | custom-call | flops 4294967296 | bytes 8388608 | tf_op jit(solution)/shard_map/down_product/pallas_call | solution.py:469
  421.8 18.3 %weight_grads.4 = bf16[2048,1536]{1,0:T(8,128)(2,1)} custom-call(bf16[512,2048]{1,0:T(8,128)(2,1)} %copy-done.22, bf16[512,2048]{1,0:T(8,128)(2,1)} %collective-permute-done.36.x_other.refs_1_, bf16[512,2048]{1,0:T(8,128)(2,1)} %constant_dynamic-update-slice_fusion.8.x_mine.refs_2_, bf16[512,2048]{1,0:T(8,128)(2,1)} %collective-permute-done.38.x_other.refs_3_, ...), custom_call_target="tpu_custom_call" | custom-call | flops 19327352832 | bytes 29360128 | tf_op jit(solution)/shard_map/weight_grads/pallas_call | solution.py:520
  450.8 11.5 %collective-permute-done.48 = bf16[128,2048]{1,0:T(8,128)(2,1)S(1)} collective-permute-done((bf16[128,2048]{1,0:T(8,128)(2,1)S(1)}, bf16[128,2048]{1,0:T(8,128)(2,1)S(1)}, u32[]{:S(2)}, u32[]{:S(2)}) %collective-permute-start.48) | collective-permute-done | bytes 524320 | tf_op jit(solution)/shard_map/ppermute | solution.py:48
  463.5 10.6 %collective-permute-done.50 = bf16[128,2048]{1,0:T(8,128)(2,1)S(1)} collective-permute-done((bf16[128,2048]{1,0:T(8,128)(2,1)S(1)}, bf16[128,2048]{1,0:T(8,128)(2,1)S(1)}, u32[]{:S(2)}, u32[]{:S(2)}) %collective-permute-start.50) | collective-permute-done | bytes 524320 | tf_op jit(solution)/shard_map/ppermute | solution.py:48
  477.9 10.8 %collective-permute-done.51 = bf16[128,2048]{1,0:T(8,128)(2,1)S(1)} collective-permute-done((bf16[128,2048]{1,0:T(8,128)(2,1)S(1)}, bf16[128,2048]{1,0:T(8,128)(2,1)S(1)}, u32[]{:S(2)}, u32[]{:S(2)}) %collective-permute-start.51) | collective-permute-done | bytes 524320 | tf_op jit(solution)/shard_map/ppermute | solution.py:48
  508.1 12.8 %attention_backward.3 = (bf16[2,2,2,4,32,768]{5,4,3,2,1,0:T(8,128)(2,1)S(1)}, f32[2,2,128]{2,1,0:T(2,128)S(1)}) custom-call(bf16[2,2,2,4,32,768]{5,4,3,2,1,0:T(8,128)(2,1)S(1)} %bitcast.450, f32[2,2,2,4,32,256]{5,4,3,2,1,0:T(8,128)S(1)} %bitcast.452, f32[2,4,128,128]{3,2,1,0:T(8,128)S(1)} %get-tuple-element.292.mask_ref, f32[2,4,128,3]{3,2,1,0:T(8,128)S(1)} %copy-done.14, ...), custom_call_target="tpu_custom_call" | custom-call | flops 14400000000 | bytes 5000000 | tf_op jit(solution)/shard_map/attention_backward/pallas_call | solution.py:351
  526.8 12.4 %attention_backward.2 = (bf16[2,2,2,4,32,768]{5,4,3,2,1,0:T(8,128)(2,1)S(1)}, f32[2,2,128]{2,1,0:T(2,128)S(1)}) custom-call(bf16[2,2,2,4,32,768]{5,4,3,2,1,0:T(8,128)(2,1)S(1)} %bitcast.448, f32[2,2,2,4,32,256]{5,4,3,2,1,0:T(8,128)S(1)} %bitcast.451, f32[2,4,128,128]{3,2,1,0:T(8,128)S(1)} %copy-done.16, f32[2,4,128,3]{3,2,1,0:T(8,128)S(1)} %copy-done.12, ...), custom_call_target="tpu_custom_call" | custom-call | flops 14400000000 | bytes 5000000 | tf_op jit(solution)/shard_map/attention_backward/pallas_call | solution.py:351
  544.6 13.0 %weight_grads.5 = bf16[2048,1024]{1,0:T(8,128)(2,1)} custom-call(bf16[512,2048]{1,0:T(8,128)(2,1)} %pad_maximum_fusion.refs_0_, bf16[512,2048]{1,0:T(8,128)(2,1)} %collective-permute-done.18.refs_1_, bf16[512,2048]{1,0:T(8,128)(2,1)} %pad_maximum_fusion.1.refs_2_, bf16[512,2048]{1,0:T(8,128)(2,1)} %collective-permute-done.25.refs_3_, ...), custom_call_target="tpu_custom_call" | custom-call | flops 12884901888 | bytes 25165824 | tf_op jit(solution)/shard_map/weight_grads/pallas_call | solution.py:520
  586.5 19.6 %collective-permute-done.62 = bf16[2,128,2048]{2,1,0:T(8,128)(2,1)} collective-permute-done((bf16[2,128,2048]{2,1,0:T(8,128)(2,1)S(1)}, bf16[2,128,2048]{2,1,0:T(8,128)(2,1)}, u32[]{:S(2)}, u32[]{:S(2)}) %collective-permute-start.62) | collective-permute-done | bytes 1048608 | tf_op jit(solution)/shard_map/ppermute | solution.py:48
  615.0 11.0 %collective-permute-done.66.refs_23_ = bf16[256,1536]{1,0:T(8,128)(2,1)S(1)} collective-permute-done((bf16[256,1536]{1,0:T(8,128)(2,1)S(1)}, bf16[256,1536]{1,0:T(8,128)(2,1)S(1)}, u32[]{:S(2)}, u32[]{:S(2)}) %collective-permute-start.66) | collective-permute-done | bytes 786464 | tf_op jit(solution)/shard_map/ppermute | solution.py:48
  631.7 6.9 collective-permute-done.67
  671.4 22.5 %adam.1 = (f32[3,256,512]{2,1,0:T(8,128)}, f32[3,256,512]{2,1,0:T(8,128)}, f32[3,256,512]{2,1,0:T(8,128)}, f32[256,512]{1,0:T(8,128)}, f32[256,512]{1,0:T(8,128)...) custom-call(s32[1]{0:T(128)} %bitcast.88.place_ref, ...), custom_call_target="tpu_custom_call" | custom-call | flops 41943040 | bytes 50331648 | tf_op jit(solution)/shard_map/adam/pallas_call | solution.py:659
  (586 shorter events, 324.9 us)
Async XLA Ops:
  7.2 126.0 %all-gather.4.cloned.1.call-start = ((), (), s32[]{:S(2)}) async-start(), calls=%async_computation.3 | async-start | bytes 3932160 | tf_op jit(solution)/shard_map/all_gather | solution.py:734
  14.6 55.5 %collective-permute-start.11 = (bf16[256,512]{1,0:T(8,128)(2,1)}, bf16[256,512]{1,0:T(8,128)(2,1)}, u32[]{:S(2)}, u32[]{:S(2)}) collective-permute-start(bf16[256,512]{1,0:T(8,128)(2,1)} %get-tuple-element.236), channel_id=1, source_target_pairs={{0,16},{8,24},{16,0},{24,8},{1,17},{9,25},{17,1},{25,9},{2,18},{10... | collective-permute-start | bytes 786440 | tf_op jit(solution)/shard_map/ppermute | solution.py:120
  17.2 22.9 %collective-permute-start.10 = (bf16[256,512]{1,0:T(8,128)(2,1)}, bf16[256,512]{1,0:T(8,128)(2,1)}, u32[]{:S(2)}, u32[]{:S(2)}) collective-permute-start(bf16[256,512]{1,0:T(8,128)(2,1)} %get-tuple-element.236), channel_id=1, source_target_pairs={{0,8},{8,16},{16,24},{24,0},{1,9},{9,17},{17,25},{25,1},{2,10},{10... | collective-permute-start | bytes 786440 | tf_op jit(solution)/shard_map/ppermute | solution.py:120
  18.7 53.6 %collective-permute-start.12 = (bf16[256,512]{1,0:T(8,128)(2,1)}, bf16[256,512]{1,0:T(8,128)(2,1)}, u32[]{:S(2)}, u32[]{:S(2)}) collective-permute-start(bf16[256,512]{1,0:T(8,128)(2,1)} %get-tuple-element.236), channel_id=1, source_target_pairs={{0,24},{8,0},{16,8},{24,16},{1,25},{9,1},{17,9},{25,17},{2,26},{10... | collective-permute-start | bytes 786440 | tf_op jit(solution)/shard_map/ppermute | solution.py:120
  29.4 240.4 %all-gather.6.cloned.1.call-start = ((), (), s32[]{:S(2)}) async-start(), calls=%async_computation.4 | async-start | bytes 7864320 | tf_op jit(solution)/shard_map/all_gather | solution.py:734
  37.1 24.3 %collective-permute-start.5 = (bf16[128,2048]{1,0:T(8,128)(2,1)}, bf16[128,2048]{1,0:T(8,128)(2,1)}, u32[]{:S(2)}, u32[]{:S(2)}) collective-permute-start(bf16[128,2048]{1,0:T(8,128)(2,1)} %get-tuple-element.120), channel_id=1, source_target_pairs={{0,4},{4,0},{1,5},{5,1},{2,6},{6,2},{3,7},{7,3},{8,12},{12,8},{9,1... | collective-permute-start | bytes 1572872 | tf_op jit(solution)/shard_map/ppermute | solution.py:48
  40.0 66.7 %collective-permute-start.24 = (bf16[128,2048]{1,0:T(8,128)(2,1)}, bf16[128,2048]{1,0:T(8,128)(2,1)}, u32[]{:S(2)}, u32[]{:S(2)}) collective-permute-start(bf16[128,2048]{1,0:T(8,128)(2,1)} %get-tuple-element.122), channel_id=1, source_target_pairs={{0,2},{2,0},{1,3},{3,1},{4,6},{6,4},{5,7},{7,5},{8,10},{10,8},{9,1... | collective-permute-start | bytes 1572872 | tf_op jit(solution)/shard_map/ppermute | solution.py:48
  51.7 24.5 %collective-permute-start = (bf16[128,2048]{1,0:T(8,128)(2,1)}, bf16[128,2048]{1,0:T(8,128)(2,1)S(1)}, u32[]{:S(2)}, u32[]{:S(2)}) collective-permute-start(bf16[128,2048]{1,0:T(8,128)(2,1)} %get-tuple-element.120), channel_id=1, source_target_pairs={{0,2},{2,0},{1,3},{3,1},{4,6},{6,4},{5,7},{7,5},{8,10},{10,8},{9,1... | collective-permute-start | bytes 1572872 | tf_op jit(solution)/shard_map/ppermute | solution.py:48
  84.9 52.9 %collective-permute-start.18 = (bf16[512,2048]{1,0:T(8,128)(2,1)}, bf16[512,2048]{1,0:T(8,128)(2,1)}, u32[]{:S(2)}, u32[]{:S(2)}) collective-permute-start(bf16[512,2048]{1,0:T(8,128)(2,1)} %pad_maximum_fusion.refs_0_), channel_id=1, source_target_pairs={{0,1},{1,0},{2,3},{3,2},{4,5},{5,4},{6,7},{7,6},{8,9},{9,8},{10,11... | collective-permute-start | bytes 6291464 | tf_op jit(solution)/shard_map/ppermute | solution.py:48
  102.3 240.7 %all-gather.8.cloned.1.call-start = ((), (), s32[]{:S(2)}) async-start(), calls=%async_computation.5 | async-start | bytes 7864320 | tf_op jit(solution)/shard_map/all_gather | solution.py:734
  106.7 24.0 %collective-permute-start.16 = (bf16[128,2048]{1,0:T(8,128)(2,1)S(1)}, bf16[128,2048]{1,0:T(8,128)(2,1)}, u32[]{:S(2)}, u32[]{:S(2)}) collective-permute-start(bf16[128,2048]{1,0:T(8,128)(2,1)S(1)} %bitcast.476), channel_id=1, source_target_pairs={{0,4},{4,0},{1,5},{5,1},{2,6},{6,2},{3,7},{7,3},{8,12},{12,8},{9,1... | collective-permute-start | bytes 1572872 | tf_op jit(solution)/shard_map/ppermute | solution.py:48
  116.7 31.9 %collective-permute-start.25 = (bf16[512,2048]{1,0:T(8,128)(2,1)}, bf16[512,2048]{1,0:T(8,128)(2,1)}, u32[]{:S(2)}, u32[]{:S(2)}) collective-permute-start(bf16[512,2048]{1,0:T(8,128)(2,1)} %pad_maximum_fusion.1.refs_2_), channel_id=1, source_target_pairs={{0,1},{1,0},{2,3},{3,2},{4,5},{5,4},{6,7},{7,6},{8,9},{9,8},{10,11... | collective-permute-start | bytes 6291464 | tf_op jit(solution)/shard_map/ppermute | solution.py:48
  131.2 33.2 %collective-permute-start.27 = (bf16[128,2048]{1,0:T(8,128)(2,1)}, bf16[128,2048]{1,0:T(8,128)(2,1)}, u32[]{:S(2)}, u32[]{:S(2)}) collective-permute-start(bf16[128,2048]{1,0:T(8,128)(2,1)} %collective-permute-done.15), channel_id=1, source_target_pairs={{0,2},{2,0},{1,3},{3,1},{4,6},{6,4},{5,7},{7,5},{8,10},{10,8},{9,1... | collective-permute-start | bytes 1572872 | tf_op jit(solution)/shard_map/ppermute | solution.py:48
  131.7 32.7 %collective-permute-start.28 = (bf16[128,2048]{1,0:T(8,128)(2,1)}, bf16[128,2048]{1,0:T(8,128)(2,1)}, u32[]{:S(2)}, u32[]{:S(2)}) collective-permute-start(bf16[128,2048]{1,0:T(8,128)(2,1)} %collective-permute-done.16), channel_id=1, source_target_pairs={{0,2},{2,0},{1,3},{3,1},{4,6},{6,4},{5,7},{7,5},{8,10},{10,8},{9,1... | collective-permute-start | bytes 1572872 | tf_op jit(solution)/shard_map/ppermute | solution.py:48
  174.1 25.2 %collective-permute-start.30 = (bf16[2,128,2048]{2,1,0:T(8,128)(2,1)S(1)}, bf16[2,128,2048]{2,1,0:T(8,128)(2,1)S(1)}, u32[]{:S(2)}, u32[]{:S(2)}) collective-permute-start(bf16[2,128,2048]{2,1,0:T(8,128)(2,1)S(1)} %bitcast.495), channel_id=1, source_target_pairs={{0,2},{2,0},{1,3},{3,1},{4,6},{6,4},{5,7},{7,5},{8,10},{10,8},{9,1... | collective-permute-start | bytes 3145736 | tf_op jit(solution)/shard_map/ppermute | solution.py:48
  176.7 33.3 %collective-permute-start.20 = (bf16[2,128,2048]{2,1,0:T(8,128)(2,1)S(1)}, bf16[2,128,2048]{2,1,0:T(8,128)(2,1)}, u32[]{:S(2)}, u32[]{:S(2)}) collective-permute-start(bf16[2,128,2048]{2,1,0:T(8,128)(2,1)S(1)} %bitcast.494), channel_id=1, source_target_pairs={{0,4},{4,0},{1,5},{5,1},{2,6},{6,2},{3,7},{7,3},{8,12},{12,8},{9,1... | collective-permute-start | bytes 3145736 | tf_op jit(solution)/shard_map/ppermute | solution.py:48
  201.5 320.5 %reduce-scatter.4.cloned.1.call-start = ((), (), s32[]{:S(2)}) async-start(), calls=%async_computation.6 | async-start | bytes 7864320 | tf_op jit(solution)/shard_map/reduce_scatter | solution.py:861
  227.9 22.2 %collective-permute-start.23 = (bf16[128,2048]{1,0:T(8,128)(2,1)S(1)}, bf16[128,2048]{1,0:T(8,128)(2,1)S(1)}, u32[]{:S(2)}, u32[]{:S(2)}) collective-permute-start(bf16[128,2048]{1,0:T(8,128)(2,1)S(1)} %get-tuple-element.139), channel_id=1, source_target_pairs={{0,4},{4,0},{1,5},{5,1},{2,6},{6,2},{3,7},{7,3},{8,12},{12,8},{9,1... | collective-permute-start | bytes 1572872 | tf_op jit(solution)/shard_map/ppermute | solution.py:48
  316.0 290.1 %reduce-scatter.6.cloned.1.call-start = ((), (), s32[]{:S(2)}) async-start(), calls=%async_computation.7 | async-start | bytes 7864320 | tf_op jit(solution)/shard_map/reduce_scatter | solution.py:861
  388.2 25.3 %collective-permute-start.42 = (bf16[2,128,2048]{2,1,0:T(8,128)(2,1)S(1)}, bf16[2,128,2048]{2,1,0:T(8,128)(2,1)}, u32[]{:S(2)}, u32[]{:S(2)}) collective-permute-start(bf16[2,128,2048]{2,1,0:T(8,128)(2,1)S(1)} %bitcast.492), channel_id=1, source_target_pairs={{0,4},{4,0},{1,5},{5,1},{2,6},{6,2},{3,7},{7,3},{8,12},{12,8},{9,1... | collective-permute-start | bytes 3145736 | tf_op jit(solution)/shard_map/ppermute | solution.py:48
  392.1 25.6 %collective-permute-start.43 = (bf16[2,128,2048]{2,1,0:T(8,128)(2,1)}, bf16[2,128,2048]{2,1,0:T(8,128)(2,1)}, u32[]{:S(2)}, u32[]{:S(2)}) collective-permute-start(bf16[2,128,2048]{2,1,0:T(8,128)(2,1)} %bitcast.51), channel_id=1, source_target_pairs={{0,2},{2,0},{1,3},{3,1},{4,6},{6,4},{5,7},{7,5},{8,10},{10,8},{9,1... | collective-permute-start | bytes 3145736 | tf_op jit(solution)/shard_map/ppermute | solution.py:48
  416.2 24.1 %collective-permute-start.44 = (bf16[128,2048]{1,0:T(8,128)(2,1)}, bf16[128,2048]{1,0:T(8,128)(2,1)}, u32[]{:S(2)}, u32[]{:S(2)}) collective-permute-start(bf16[128,2048]{1,0:T(8,128)(2,1)} %get-tuple-element.255), channel_id=1, source_target_pairs={{0,2},{2,0},{1,3},{3,1},{4,6},{6,4},{5,7},{7,5},{8,10},{10,8},{9,1... | collective-permute-start | bytes 1572872 | tf_op jit(solution)/shard_map/ppermute | solution.py:48
  440.2 207.5 %reduce-scatter.8.cloned.1.call-start = ((), (), s32[]{:S(2)}) async-start(), calls=%async_computation.8 | async-start | bytes 5242880 | tf_op jit(solution)/shard_map/reduce_scatter | solution.py:861
  448.0 40.9 %collective-permute-start.46 = (bf16[512,2048]{1,0:T(8,128)(2,1)S(1)}, bf16[512,2048]{1,0:T(8,128)(2,1)S(1)}, u32[]{:S(2)}, u32[]{:S(2)}) collective-permute-start(bf16[512,2048]{1,0:T(8,128)(2,1)S(1)} %copy-done.124), channel_id=1, source_target_pairs={{0,1},{1,0},{2,3},{3,2},{4,5},{5,4},{6,7},{7,6},{8,9},{9,8},{10,11... | collective-permute-start | bytes 6291464 | tf_op jit(solution)/shard_map/ppermute | solution.py:48
  448.5 42.8 %collective-permute-start.54 = (bf16[512,2048]{1,0:T(8,128)(2,1)S(1)}, bf16[512,2048]{1,0:T(8,128)(2,1)S(1)}, u32[]{:S(2)}, u32[]{:S(2)}) collective-permute-start(bf16[512,2048]{1,0:T(8,128)(2,1)S(1)} %copy-done.123), channel_id=1, source_target_pairs={{0,1},{1,0},{2,3},{3,2},{4,5},{5,4},{6,7},{7,6},{8,9},{9,8},{10,11... | collective-permute-start | bytes 6291464 | tf_op jit(solution)/shard_map/ppermute | solution.py:48
  450.2 23.9 %collective-permute-start.50 = (bf16[128,2048]{1,0:T(8,128)(2,1)S(1)}, bf16[128,2048]{1,0:T(8,128)(2,1)S(1)}, u32[]{:S(2)}, u32[]{:S(2)}) collective-permute-start(bf16[128,2048]{1,0:T(8,128)(2,1)S(1)} %get-tuple-element.182), channel_id=1, source_target_pairs={{0,2},{2,0},{1,3},{3,1},{4,6},{6,4},{5,7},{7,5},{8,10},{10,8},{9,1... | collective-permute-start | bytes 1572872 | tf_op jit(solution)/shard_map/ppermute | solution.py:48
  497.4 26.5 %collective-permute-start.55 = (bf16[512,2048]{1,0:T(8,128)(2,1)}, bf16[512,2048]{1,0:T(8,128)(2,1)}, u32[]{:S(2)}, u32[]{:S(2)}) collective-permute-start(bf16[512,2048]{1,0:T(8,128)(2,1)} %constant_dynamic-update-slice_fusion.16.refs_4_), channel_id=1, source_target_pairs={{0,1},{1,0},{2,3},{3,2},{4,5},{5,4},{6,7},{7,6},{8,9},{9,8},{10,11... | collective-permute-start | bytes 6291464 | tf_op jit(solution)/shard_map/ppermute | solution.py:48
  502.3 36.9 %collective-permute-start.53 = (bf16[2,128,2048]{2,1,0:T(8,128)(2,1)}, bf16[2,128,2048]{2,1,0:T(8,128)(2,1)S(1)}, u32[]{:S(2)}, u32[]{:S(2)}) collective-permute-start(bf16[2,128,2048]{2,1,0:T(8,128)(2,1)} %bitcast.61), channel_id=1, source_target_pairs={{0,4},{4,0},{1,5},{5,1},{2,6},{6,2},{3,7},{7,3},{8,12},{12,8},{9,1... | collective-permute-start | bytes 3145736 | tf_op jit(solution)/shard_map/ppermute | solution.py:48
  503.8 35.3 %collective-permute-start.58 = (bf16[2,128,2048]{2,1,0:T(8,128)(2,1)}, bf16[2,128,2048]{2,1,0:T(8,128)(2,1)}, u32[]{:S(2)}, u32[]{:S(2)}) collective-permute-start(bf16[2,128,2048]{2,1,0:T(8,128)(2,1)} %bitcast.62), channel_id=1, source_target_pairs={{0,2},{2,0},{1,3},{3,1},{4,6},{6,4},{5,7},{7,5},{8,10},{10,8},{9,1... | collective-permute-start | bytes 3145736 | tf_op jit(solution)/shard_map/ppermute | solution.py:48
  572.1 55.5 %collective-permute-start.59 = (bf16[128,2048]{1,0:T(8,128)(2,1)}, bf16[128,2048]{1,0:T(8,128)(2,1)S(1)}, u32[]{:S(2)}, u32[]{:S(2)}) collective-permute-start(bf16[128,2048]{1,0:T(8,128)(2,1)} %fusion.82), channel_id=1, source_target_pairs={{0,2},{2,0},{1,3},{3,1},{4,6},{6,4},{5,7},{7,5},{8,10},{10,8},{9,1... | collective-permute-start | bytes 1572872 | tf_op jit(solution)/shard_map/ppermute | solution.py:48
  579.3 26.8 %collective-permute-start.62 = (bf16[2,128,2048]{2,1,0:T(8,128)(2,1)S(1)}, bf16[2,128,2048]{2,1,0:T(8,128)(2,1)}, u32[]{:S(2)}, u32[]{:S(2)}) collective-permute-start(bf16[2,128,2048]{2,1,0:T(8,128)(2,1)S(1)} %bitcast.493), channel_id=1, source_target_pairs={{0,4},{4,0},{1,5},{5,1},{2,6},{6,2},{3,7},{7,3},{8,12},{12,8},{9,1... | collective-permute-start | bytes 3145736 | tf_op jit(solution)/shard_map/ppermute | solution.py:48
  582.3 30.5 %collective-permute-start.65 = (bf16[2,128,2048]{2,1,0:T(8,128)(2,1)}, bf16[2,128,2048]{2,1,0:T(8,128)(2,1)}, u32[]{:S(2)}, u32[]{:S(2)}) collective-permute-start(bf16[2,128,2048]{2,1,0:T(8,128)(2,1)} %bitcast.83), channel_id=1, source_target_pairs={{0,2},{2,0},{1,3},{3,1},{4,6},{6,4},{5,7},{7,5},{8,10},{10,8},{9,1... | collective-permute-start | bytes 3145736 | tf_op jit(solution)/shard_map/ppermute | solution.py:48
  (180 other events, 2154.4 us)
Sparse Core Ops, SparseCore 0:
  29.6 61.9 all-gather.3
  102.4 124.7 all-gather.5
  229.4 113.5 all-gather.7
  345.1 108.9 reduce-scatter.3
  456.3 111.2 reduce-scatter.5
  570.3 77.3 reduce-scatter.7

commit v10 on v9

--- a/solution.py
+++ b/solution.py
@@ -753,23 +753,23 @@
     all_ids = tie(doc_ids[:, 0], send_qkv)
     for axis in ("y", "c"):
         all_ids = jnp.stack([all_ids, swap(all_ids, axis)], axis=0)
-    their_qkv = swap(send_qkv, "x")
-    shard_qkv = join_rows(qkv_columns(x_place), tie(their_qkv, all_ids))
-    full_qkv = fetch(shard_qkv)
-
-    head_start = (y_place * 2 + c_place) * (2 * heads) + x_place * heads
-    gate_local = lax.dynamic_slice_in_dim(gate_logit, head_start, heads)
-    mixing = jax.nn.sigmoid(gate_local)
-    gate_rows = jnp.broadcast_to(mixing[:, None], (heads, HEAD_DIM))
-
     micros = range(micro_count)
     tokens = 8 * own_tokens
     token_rows = [
         tie(inputs[m, 0], send_qkv).reshape(own_tokens, D).astype(F32) for m in micros
     ]
+    normed_att = [rms_norm(t, norm_gains[0]).astype(BF) for t in token_rows]
+    their_qkv = swap(send_qkv, "x")
+    shard_qkv = join_rows(qkv_columns(x_place), tie(their_qkv, all_ids, *normed_att))
+    full_qkv = fetch(shard_qkv)
+
+    head_start = (y_place * 2 + c_place) * (2 * heads) + x_place * heads
+    gate_local = lax.dynamic_slice_in_dim(gate_logit, head_start, heads)
+    mixing = jax.nn.sigmoid(gate_local)
+    gate_rows = jnp.broadcast_to(mixing[:, None], (heads, HEAD_DIM))
+
     back_low = [cotangent[m, 0].reshape(own_tokens, D) for m in micros]
     all_ids = jnp.stack([all_ids, swap(all_ids, "x")], axis=0)
-    normed_att = [rms_norm(t, norm_gains[0]).astype(BF) for t in token_rows]
     att_states = [
         gather_start(normed_att[m], *orders[m], (their_qkv, all_ids)) for m in micros
     ]
@@ -791,9 +791,8 @@
         part = part.reshape(z_count, 1, rows, width_att)
         both_out = lax.dynamic_update_slice_in_dim(both_out, part, place, axis=1)
     full_out = both_out.reshape(D, width_att)
-    att_last = [state[-1] for state in att_states]
     back_states = [
-        gather_start(back_low[m], *orders[m], (their_out,), att_last) for m in micros
+        gather_start(back_low[m], *orders[m], (their_out,), (shard_ff[0],)) for m in micros
     ]
     back_first = [t for state in back_states for t in state[1:]]
     back_states = [gather_across(state, *orders[m], "y") for m, state in enumerate(back_states)]

time: 709 us -> 703 us (level)
  waiting for transfers between devices: 208 us -> 200 us
    unnamed x284 -> x286, local copies, waits for them, and re-layouts: 24.2 us -> 22.8 us
where the time goes in v10:
time: 703 us; the launch traced here: 698 us
  waiting for transfers between devices  200 us (28%)
  Pallas kernels  179 us (25%)
  starting transfers between devices  85.1 us (12%)
  matrix products  81.7 us (12%)
  other arithmetic  72 us (10%)
  local copies, waits for them, and re-layouts  61.8 us (9%)
  between operations  17.9 us (3%)
    ppermute x66, waiting for transfers between devices, swap(): return lax.ppermute(tensor, axis, [(0, 1), (1, 0)])  187 us
    dot_general x24, matrix products, mm(): return lax.dot_general(a, b, (dims, ((), ())), preferred_element_type=F32)  81.7 us
    ppermute x66, starting transfers between devices, swap(): return lax.ppermute(tensor, axis, [(0, 1), (1, 0)])  55.4 us
    pallas_call x4, Pallas kernels, feed_forward(): pl.pallas_call(functools.partial(ff_kernel, width, half), grid=(2 * half,...  50.2 us
    pallas_call x3, Pallas kernels, weight_grads(): pl.pallas_call(functools.partial(grads_kernel, count), grid=(D // tile,),...  49.5 us
    pallas_call x2, Pallas kernels, attention_bwd(): pl.pallas_call(functools.partial(attention_bwd_kernel, heads), grid=(seqs...  25.1 us
    unnamed x286, local copies, waits for them, and re-layouts  22.8 us
    pallas_call x1, Pallas kernels, adam_all(): pl.pallas_call(functools.partial(adam_kernel, steps, len(ff_sides)), grid...  22.5 us
  transfers between devices with their start and end apart: 80, of which 37 were waited for; matrix products, arithmetic and copies ran while one was open for 29% of the time, Pallas kernels for 22%

profile of v10, /device:TPU:0, one launch (start us, length us, event | category | flops | bytes accessed | tf_op | source)
XLA Modules:
  0.0 697.7 jit_solution(427760490196424248)
XLA Ops:
  41.9 9.4 %collective-permute-done.7 = bf16[128,2048]{1,0:T(8,128)(2,1)} collective-permute-done((bf16[128,2048]{1,0:T(8,128)(2,1)}, bf16[128,2048]{1,0:T(8,128)(2,1)}, u32[]{:S(2)}, u32[]{:S(2)}) %collective-permute-start.7) | collective-permute-done | bytes 524320 | tf_op jit(solution)/shard_map/ppermute | solution.py:48
  51.8 9.0 %collective-permute-done.5 = bf16[128,2048]{1,0:T(8,128)(2,1)} collective-permute-done((bf16[128,2048]{1,0:T(8,128)(2,1)}, bf16[128,2048]{1,0:T(8,128)(2,1)}, u32[]{:S(2)}, u32[]{:S(2)}) %collective-permute-start.5) | collective-permute-done | bytes 524320 | tf_op jit(solution)/shard_map/ppermute | solution.py:48
  116.8 6.7 collective-permute-done.16
  138.7 6.6 attention_forward.2
  154.7 6.5 attention_forward.3
  175.1 21.0 %collective-permute-done.30 = bf16[2,128,2048]{2,1,0:T(8,128)(2,1)S(1)} collective-permute-done((bf16[2,128,2048]{2,1,0:T(8,128)(2,1)S(1)}, bf16[2,128,2048]{2,1,0:T(8,128)(2,1)S(1)}, u32[]{:S(2)}, u32[]{:S(2)}) %collective-permute-start.30) | collective-permute-done | bytes 1048608 | tf_op jit(solution)/shard_map/ppermute | solution.py:48
  198.8 8.4 %reduce-scatter.4.cloned.1.call-start = ((), (), s32[]{:S(2)}) async-start(), calls=%async_computation.6 | async-start | bytes 7864320 | tf_op jit(solution)/shard_map/reduce_scatter | solution.py:860
  212.1 9.7 %collective-permute-done.20 = bf16[128,2048]{1,0:T(8,128)(2,1)S(1)} collective-permute-done((bf16[128,2048]{1,0:T(8,128)(2,1)S(1)}, bf16[128,2048]{1,0:T(8,128)(2,1)S(1)}, u32[]{:S(2)}, u32[]{:S(2)}) %collective-permute-start.20) | collective-permute-done | bytes 524320 | tf_op jit(solution)/shard_map/ppermute | solution.py:48
  229.0 9.6 %collective-permute-done.33 = bf16[128,2048]{1,0:T(8,128)(2,1)S(1)} collective-permute-done((bf16[128,2048]{1,0:T(8,128)(2,1)S(1)}, bf16[128,2048]{1,0:T(8,128)(2,1)S(1)}, u32[]{:S(2)}, u32[]{:S(2)}) %collective-permute-start.33) | collective-permute-done | bytes 524320 | tf_op jit(solution)/shard_map/ppermute | solution.py:48
  239.1 8.4 %collective-permute-done.22 = bf16[128,2048]{1,0:T(8,128)(2,1)S(1)} collective-permute-done((bf16[128,2048]{1,0:T(8,128)(2,1)S(1)}, bf16[128,2048]{1,0:T(8,128)(2,1)S(1)}, u32[]{:S(2)}, u32[]{:S(2)}) %collective-permute-start.22) | collective-permute-done | bytes 524320 | tf_op jit(solution)/shard_map/ppermute | solution.py:48
  265.5 12.2 %feed_forward.4 = (bf16[512,512]{1,0:T(8,128)(2,1)S(1)}, bf16[512,512]{1,0:T(8,128)(2,1)S(1)}, bf16[512,1024]{1,0:T(8,128)(2,1)S(1)}, bf16[512,1024]{1,0:T(8,128)(2,1)S(1)}) custom-call(bf16[512,2048]{1,0:T(8,128)(2,1)S(1)} %constant_dynamic-update-slice_fusion.x_mine.refs_0_, bf16[512,2048]{1,0:T(8,128)(2,1)} %collective-permute-done.36.x_other.refs_1_, ...), custom_call_target="tpu_custom_call" | custom-call | flops 13958643712 | bytes 1048576 | tf_op jit(solution)/shard_map/feed_forward/pallas_call | solution.py:424
  277.7 13.2 %feed_forward.5 = (bf16[512,512]{1,0:T(8,128)(2,1)S(1)}, bf16[512,512]{1,0:T(8,128)(2,1)S(1)}, bf16[512,1024]{1,0:T(8,128)(2,1)S(1)}, bf16[512,1024]{1,0:T(8,128)(2,1)S(1)}) custom-call(bf16[512,2048]{1,0:T(8,128)(2,1)} %constant_dynamic-update-slice_fusion.8.x_mine.refs_2_, bf16[512,2048]{1,0:T(8,128)(2,1)} %collective-permute-done.38.x_other.refs_3_, ...), custom_call_target="tpu_custom_call" | custom-call | flops 13958643712 | bytes 1048576 | tf_op jit(solution)/shard_map/feed_forward/pallas_call | solution.py:424
  291.9 18.2 %weight_grads.3 = bf16[2048,1536]{1,0:T(8,128)(2,1)} custom-call(bf16[512,2048]{1,0:T(8,128)(2,1)} %copy-done.22, bf16[512,2048]{1,0:T(8,128)(2,1)} %collective-permute-done.36.x_other.refs_1_, bf16[512,2048]{1,0:T(8,128)(2,1)} %constant_dynamic-update-slice_fusion.8.x_mine.refs_2_, bf16[512,2048]{1,0:T(8,128)(2,1)} %collective-permute-done.38.x_other.refs_3_, ...), custom_call_target="tpu_custom_call" | custom-call | flops 19327352832 | bytes 29360128 | tf_op jit(solution)/shard_map/weight_grads/pallas_call | solution.py:520
  311.9 6.8 fusion.2
  318.7 6.8 fusion
  334.4 12.6 %feed_forward.6 = (bf16[512,512]{1,0:T(8,128)(2,1)S(1)}, bf16[512,512]{1,0:T(8,128)(2,1)S(1)}, bf16[512,1024]{1,0:T(8,128)(2,1)S(1)}, bf16[512,1024]{1,0:T(8,128)(2,1)S(1)}) custom-call(bf16[512,2048]{1,0:T(8,128)(2,1)S(1)} %copy-done.23, bf16[512,2048]{1,0:T(8,128)(2,1)} %collective-permute-done.36.x_other.refs_1_, bf16[512,2048]{1,0:T(8,128)(2,1)} %copy-done.99, ...), custom_call_target="tpu_custom_call" | custom-call | flops 13958643712 | bytes 1048576 | tf_op jit(solution)/shard_map/feed_forward/pallas_call | solution.py:424
  355.9 12.2 %feed_forward.7 = (bf16[512,512]{1,0:T(8,128)(2,1)S(1)}, bf16[512,512]{1,0:T(8,128)(2,1)S(1)}, bf16[512,1024]{1,0:T(8,128)(2,1)S(1)}, bf16[512,1024]{1,0:T(8,128)(2,1)S(1)}) custom-call(bf16[512,2048]{1,0:T(8,128)(2,1)} %constant_dynamic-update-slice_fusion.8.x_mine.refs_2_, bf16[512,2048]{1,0:T(8,128)(2,1)} %collective-permute-done.38.x_other.refs_3_, ...), custom_call_target="tpu_custom_call" | custom-call | flops 13958643712 | bytes 1048576 | tf_op jit(solution)/shard_map/feed_forward/pallas_call | solution.py:424
  370.9 6.0 add_convert_fusion
  384.9 8.6 %down_product.2 = (bf16[512,2048]{1,0:T(8,128)(2,1)S(1)}, bf16[512,2048]{1,0:T(8,128)(2,1)}) custom-call(bf16[512,512]{1,0:T(8,128)(2,1)S(1)} %copy-done.38, bf16[512,512]{1,0:T(8,128)(2,1)S(1)} %get-tuple-element.152.refs_1_.refs_12_, bf16[512,512]{1,0:T(8,128)(2,1)S(1)} %copy-done.40, bf16[512,512]{1,0:T(8,128)(2,1)S(1)} %get-tuple-element.170.refs_3_.refs_13_, ...), custom_call_target="tpu_custom_call" | custom-call | flops 4294967296 | bytes 8388608 | tf_op jit(solution)/shard_map/down_product/pallas_call | solution.py:469
  393.5 9.2 %down_product.3 = (bf16[512,2048]{1,0:T(8,128)(2,1)S(1)}, bf16[512,2048]{1,0:T(8,128)(2,1)}) custom-call(bf16[512,512]{1,0:T(8,128)(2,1)S(1)} %copy-done.42, bf16[512,512]{1,0:T(8,128)(2,1)S(1)} %get-tuple-element.163.refs_1_.refs_14_, bf16[512,512]{1,0:T(8,128)(2,1)S(1)} %copy-done.44, bf16[512,512]{1,0:T(8,128)(2,1)S(1)} %get-tuple-element.171.refs_3_.refs_15_, ...), custom_call_target="tpu_custom_call" | custom-call | flops 4294967296 | bytes 8388608 | tf_op jit(solution)/shard_map/down_product/pallas_call | solution.py:469
  413.2 18.3 %weight_grads.4 = bf16[2048,1536]{1,0:T(8,128)(2,1)} custom-call(bf16[512,2048]{1,0:T(8,128)(2,1)} %copy-done.22, bf16[512,2048]{1,0:T(8,128)(2,1)} %collective-permute-done.36.x_other.refs_1_, bf16[512,2048]{1,0:T(8,128)(2,1)} %constant_dynamic-update-slice_fusion.8.x_mine.refs_2_, bf16[512,2048]{1,0:T(8,128)(2,1)} %collective-permute-done.38.x_other.refs_3_, ...), custom_call_target="tpu_custom_call" | custom-call | flops 19327352832 | bytes 29360128 | tf_op jit(solution)/shard_map/weight_grads/pallas_call | solution.py:520
  442.3 11.4 %collective-permute-done.48 = bf16[128,2048]{1,0:T(8,128)(2,1)S(1)} collective-permute-done((bf16[128,2048]{1,0:T(8,128)(2,1)S(1)}, bf16[128,2048]{1,0:T(8,128)(2,1)S(1)}, u32[]{:S(2)}, u32[]{:S(2)}) %collective-permute-start.48) | collective-permute-done | bytes 524320 | tf_op jit(solution)/shard_map/ppermute | solution.py:48
  455.1 10.6 %collective-permute-done.50 = bf16[128,2048]{1,0:T(8,128)(2,1)S(1)} collective-permute-done((bf16[128,2048]{1,0:T(8,128)(2,1)S(1)}, bf16[128,2048]{1,0:T(8,128)(2,1)S(1)}, u32[]{:S(2)}, u32[]{:S(2)}) %collective-permute-start.50) | collective-permute-done | bytes 524320 | tf_op jit(solution)/shard_map/ppermute | solution.py:48
  469.3 10.8 %collective-permute-done.51 = bf16[128,2048]{1,0:T(8,128)(2,1)S(1)} collective-permute-done((bf16[128,2048]{1,0:T(8,128)(2,1)S(1)}, bf16[128,2048]{1,0:T(8,128)(2,1)S(1)}, u32[]{:S(2)}, u32[]{:S(2)}) %collective-permute-start.51) | collective-permute-done | bytes 524320 | tf_op jit(solution)/shard_map/ppermute | solution.py:48
  499.5 12.8 %attention_backward.3 = (bf16[2,2,2,4,32,768]{5,4,3,2,1,0:T(8,128)(2,1)S(1)}, f32[2,2,128]{2,1,0:T(2,128)S(1)}) custom-call(bf16[2,2,2,4,32,768]{5,4,3,2,1,0:T(8,128)(2,1)S(1)} %bitcast.450, f32[2,2,2,4,32,256]{5,4,3,2,1,0:T(8,128)S(1)} %bitcast.452, f32[2,4,128,128]{3,2,1,0:T(8,128)S(1)} %get-tuple-element.292.mask_ref, f32[2,4,128,3]{3,2,1,0:T(8,128)S(1)} %copy-done.14, ...), custom_call_target="tpu_custom_call" | custom-call | flops 14400000000 | bytes 5000000 | tf_op jit(solution)/shard_map/attention_backward/pallas_call | solution.py:351
  518.2 12.4 %attention_backward.2 = (bf16[2,2,2,4,32,768]{5,4,3,2,1,0:T(8,128)(2,1)S(1)}, f32[2,2,128]{2,1,0:T(2,128)S(1)}) custom-call(bf16[2,2,2,4,32,768]{5,4,3,2,1,0:T(8,128)(2,1)S(1)} %bitcast.448, f32[2,2,2,4,32,256]{5,4,3,2,1,0:T(8,128)S(1)} %bitcast.451, f32[2,4,128,128]{3,2,1,0:T(8,128)S(1)} %copy-done.16, f32[2,4,128,3]{3,2,1,0:T(8,128)S(1)} %copy-done.12, ...), custom_call_target="tpu_custom_call" | custom-call | flops 14400000000 | bytes 5000000 | tf_op jit(solution)/shard_map/attention_backward/pallas_call | solution.py:351
  536.2 13.0 %weight_grads.5 = bf16[2048,1024]{1,0:T(8,128)(2,1)} custom-call(bf16[512,2048]{1,0:T(8,128)(2,1)} %pad_maximum_fusion.refs_0_, bf16[512,2048]{1,0:T(8,128)(2,1)} %collective-permute-done.17.refs_1_, bf16[512,2048]{1,0:T(8,128)(2,1)} %pad_maximum_fusion.1.refs_2_, bf16[512,2048]{1,0:T(8,128)(2,1)} %collective-permute-done.25.refs_3_, ...), custom_call_target="tpu_custom_call" | custom-call | flops 12884901888 | bytes 25165824 | tf_op jit(solution)/shard_map/weight_grads/pallas_call | solution.py:520
  578.0 19.6 %collective-permute-done.62 = bf16[2,128,2048]{2,1,0:T(8,128)(2,1)} collective-permute-done((bf16[2,128,2048]{2,1,0:T(8,128)(2,1)S(1)}, bf16[2,128,2048]{2,1,0:T(8,128)(2,1)}, u32[]{:S(2)}, u32[]{:S(2)}) %collective-permute-start.62) | collective-permute-done | bytes 1048608 | tf_op jit(solution)/shard_map/ppermute | solution.py:48
  606.4 11.2 %collective-permute-done.66.refs_23_ = bf16[256,1536]{1,0:T(8,128)(2,1)S(1)} collective-permute-done((bf16[256,1536]{1,0:T(8,128)(2,1)S(1)}, bf16[256,1536]{1,0:T(8,128)(2,1)S(1)}, u32[]{:S(2)}, u32[]{:S(2)}) %collective-permute-start.66) | collective-permute-done | bytes 786464 | tf_op jit(solution)/shard_map/ppermute | solution.py:48
  623.1 7.1 %collective-permute-done.67 = bf16[128,2048]{1,0:T(8,128)(2,1)} collective-permute-done((bf16[128,2048]{1,0:T(8,128)(2,1)}, bf16[128,2048]{1,0:T(8,128)(2,1)}, u32[]{:S(2)}, u32[]{:S(2)}) %collective-permute-start.67) | collective-permute-done | bytes 524320 | tf_op jit(solution)/shard_map/ppermute | solution.py:48
  645.0 7.1 %collective-permute-start.69 = (f32[33,128]{1,0:T(8,128)S(1)}, f32[33,128]{1,0:T(8,128)S(1)}, u32[]{:S(2)}, u32[]{:S(2)}) collective-permute-start(f32[33,128]{1,0:T(8,128)S(1)} %add.545), channel_id=1, source_target_pairs={{0,8},{8,0},{16,24},{24,16},{1,9},{9,1},{17,25},{25,17},{2,10},{10... | collective-permute-start | bytes 50696 | tf_op jit(solution)/shard_map/ppermute | solution.py:130
  668.1 22.5 %adam.1 = (f32[3,256,512]{2,1,0:T(8,128)}, f32[3,256,512]{2,1,0:T(8,128)}, f32[3,256,512]{2,1,0:T(8,128)}, f32[256,512]{1,0:T(8,128)}, f32[256,512]{1,0:T(8,128)...) custom-call(s32[1]{0:T(128)} %bitcast.88.place_ref, ...), custom_call_target="tpu_custom_call" | custom-call | flops 41943040 | bytes 50331648 | tf_op jit(solution)/shard_map/adam/pallas_call | solution.py:659
  (588 shorter events, 322.4 us)
Async XLA Ops:
  7.2 123.3 %all-gather.4.cloned.1.call-start = ((), (), s32[]{:S(2)}) async-start(), calls=%async_computation.3 | async-start | bytes 3932160 | tf_op jit(solution)/shard_map/all_gather | solution.py:734
  13.9 55.7 %collective-permute-start.11 = (bf16[256,512]{1,0:T(8,128)(2,1)}, bf16[256,512]{1,0:T(8,128)(2,1)}, u32[]{:S(2)}, u32[]{:S(2)}) collective-permute-start(bf16[256,512]{1,0:T(8,128)(2,1)} %get-tuple-element.236), channel_id=1, source_target_pairs={{0,16},{8,24},{16,0},{24,8},{1,17},{9,25},{17,1},{25,9},{2,18},{10... | collective-permute-start | bytes 786440 | tf_op jit(solution)/shard_map/ppermute | solution.py:120
  16.5 23.1 %collective-permute-start.10 = (bf16[256,512]{1,0:T(8,128)(2,1)}, bf16[256,512]{1,0:T(8,128)(2,1)}, u32[]{:S(2)}, u32[]{:S(2)}) collective-permute-start(bf16[256,512]{1,0:T(8,128)(2,1)} %get-tuple-element.236), channel_id=1, source_target_pairs={{0,8},{8,16},{16,24},{24,0},{1,9},{9,17},{17,25},{25,1},{2,10},{10... | collective-permute-start | bytes 786440 | tf_op jit(solution)/shard_map/ppermute | solution.py:120
  18.1 53.8 %collective-permute-start.12 = (bf16[256,512]{1,0:T(8,128)(2,1)}, bf16[256,512]{1,0:T(8,128)(2,1)}, u32[]{:S(2)}, u32[]{:S(2)}) collective-permute-start(bf16[256,512]{1,0:T(8,128)(2,1)} %get-tuple-element.236), channel_id=1, source_target_pairs={{0,24},{8,0},{16,8},{24,16},{1,25},{9,1},{17,9},{25,17},{2,26},{10... | collective-permute-start | bytes 786440 | tf_op jit(solution)/shard_map/ppermute | solution.py:120
  28.0 237.5 %all-gather.6.cloned.1.call-start = ((), (), s32[]{:S(2)}) async-start(), calls=%async_computation.4 | async-start | bytes 7864320 | tf_op jit(solution)/shard_map/all_gather | solution.py:734
  36.6 24.3 %collective-permute-start.5 = (bf16[128,2048]{1,0:T(8,128)(2,1)}, bf16[128,2048]{1,0:T(8,128)(2,1)}, u32[]{:S(2)}, u32[]{:S(2)}) collective-permute-start(bf16[128,2048]{1,0:T(8,128)(2,1)} %get-tuple-element.120), channel_id=1, source_target_pairs={{0,4},{4,0},{1,5},{5,1},{2,6},{6,2},{3,7},{7,3},{8,12},{12,8},{9,1... | collective-permute-start | bytes 1572872 | tf_op jit(solution)/shard_map/ppermute | solution.py:48
  39.6 64.2 %collective-permute-start.23 = (bf16[128,2048]{1,0:T(8,128)(2,1)}, bf16[128,2048]{1,0:T(8,128)(2,1)}, u32[]{:S(2)}, u32[]{:S(2)}) collective-permute-start(bf16[128,2048]{1,0:T(8,128)(2,1)} %get-tuple-element.122), channel_id=1, source_target_pairs={{0,2},{2,0},{1,3},{3,1},{4,6},{6,4},{5,7},{7,5},{8,10},{10,8},{9,1... | collective-permute-start | bytes 1572872 | tf_op jit(solution)/shard_map/ppermute | solution.py:48
  51.2 24.5 %collective-permute-start = (bf16[128,2048]{1,0:T(8,128)(2,1)}, bf16[128,2048]{1,0:T(8,128)(2,1)S(1)}, u32[]{:S(2)}, u32[]{:S(2)}) collective-permute-start(bf16[128,2048]{1,0:T(8,128)(2,1)} %get-tuple-element.120), channel_id=1, source_target_pairs={{0,2},{2,0},{1,3},{3,1},{4,6},{6,4},{5,7},{7,5},{8,10},{10,8},{9,1... | collective-permute-start | bytes 1572872 | tf_op jit(solution)/shard_map/ppermute | solution.py:48
  84.3 50.7 %collective-permute-start.17 = (bf16[512,2048]{1,0:T(8,128)(2,1)}, bf16[512,2048]{1,0:T(8,128)(2,1)}, u32[]{:S(2)}, u32[]{:S(2)}) collective-permute-start(bf16[512,2048]{1,0:T(8,128)(2,1)} %pad_maximum_fusion.refs_0_), channel_id=1, source_target_pairs={{0,1},{1,0},{2,3},{3,2},{4,5},{5,4},{6,7},{7,6},{8,9},{9,8},{10,11... | collective-permute-start | bytes 6291464 | tf_op jit(solution)/shard_map/ppermute | solution.py:48
  92.7 241.6 %all-gather.8.cloned.1.call-start = ((), (), s32[]{:S(2)}) async-start(), calls=%async_computation.5 | async-start | bytes 7864320 | tf_op jit(solution)/shard_map/all_gather | solution.py:734
  104.3 23.6 %collective-permute-start.15 = (bf16[128,2048]{1,0:T(8,128)(2,1)S(1)}, bf16[128,2048]{1,0:T(8,128)(2,1)}, u32[]{:S(2)}, u32[]{:S(2)}) collective-permute-start(bf16[128,2048]{1,0:T(8,128)(2,1)S(1)} %bitcast.476), channel_id=1, source_target_pairs={{0,4},{4,0},{1,5},{5,1},{2,6},{6,2},{3,7},{7,3},{8,12},{12,8},{9,1... | collective-permute-start | bytes 1572872 | tf_op jit(solution)/shard_map/ppermute | solution.py:48
  112.6 32.8 %collective-permute-start.25 = (bf16[512,2048]{1,0:T(8,128)(2,1)}, bf16[512,2048]{1,0:T(8,128)(2,1)}, u32[]{:S(2)}, u32[]{:S(2)}) collective-permute-start(bf16[512,2048]{1,0:T(8,128)(2,1)} %pad_maximum_fusion.1.refs_2_), channel_id=1, source_target_pairs={{0,1},{1,0},{2,3},{3,2},{4,5},{5,4},{6,7},{7,6},{8,9},{9,8},{10,11... | collective-permute-start | bytes 6291464 | tf_op jit(solution)/shard_map/ppermute | solution.py:48
  128.5 32.8 %collective-permute-start.27 = (bf16[128,2048]{1,0:T(8,128)(2,1)}, bf16[128,2048]{1,0:T(8,128)(2,1)}, u32[]{:S(2)}, u32[]{:S(2)}) collective-permute-start(bf16[128,2048]{1,0:T(8,128)(2,1)} %collective-permute-done.14), channel_id=1, source_target_pairs={{0,2},{2,0},{1,3},{3,1},{4,6},{6,4},{5,7},{7,5},{8,10},{10,8},{9,1... | collective-permute-start | bytes 1572872 | tf_op jit(solution)/shard_map/ppermute | solution.py:48
  129.1 32.3 %collective-permute-start.28 = (bf16[128,2048]{1,0:T(8,128)(2,1)}, bf16[128,2048]{1,0:T(8,128)(2,1)}, u32[]{:S(2)}, u32[]{:S(2)}) collective-permute-start(bf16[128,2048]{1,0:T(8,128)(2,1)} %collective-permute-done.15), channel_id=1, source_target_pairs={{0,2},{2,0},{1,3},{3,1},{4,6},{6,4},{5,7},{7,5},{8,10},{10,8},{9,1... | collective-permute-start | bytes 1572872 | tf_op jit(solution)/shard_map/ppermute | solution.py:48
  171.0 25.2 %collective-permute-start.30 = (bf16[2,128,2048]{2,1,0:T(8,128)(2,1)S(1)}, bf16[2,128,2048]{2,1,0:T(8,128)(2,1)S(1)}, u32[]{:S(2)}, u32[]{:S(2)}) collective-permute-start(bf16[2,128,2048]{2,1,0:T(8,128)(2,1)S(1)} %bitcast.495), channel_id=1, source_target_pairs={{0,2},{2,0},{1,3},{3,1},{4,6},{6,4},{5,7},{7,5},{8,10},{10,8},{9,1... | collective-permute-start | bytes 3145736 | tf_op jit(solution)/shard_map/ppermute | solution.py:48
  173.7 33.6 %collective-permute-start.19 = (bf16[2,128,2048]{2,1,0:T(8,128)(2,1)S(1)}, bf16[2,128,2048]{2,1,0:T(8,128)(2,1)}, u32[]{:S(2)}, u32[]{:S(2)}) collective-permute-start(bf16[2,128,2048]{2,1,0:T(8,128)(2,1)S(1)} %bitcast.494), channel_id=1, source_target_pairs={{0,4},{4,0},{1,5},{5,1},{2,6},{6,2},{3,7},{7,3},{8,12},{12,8},{9,1... | collective-permute-start | bytes 3145736 | tf_op jit(solution)/shard_map/ppermute | solution.py:48
  198.8 314.7 %reduce-scatter.4.cloned.1.call-start = ((), (), s32[]{:S(2)}) async-start(), calls=%async_computation.6 | async-start | bytes 7864320 | tf_op jit(solution)/shard_map/reduce_scatter | solution.py:860
  224.8 22.7 %collective-permute-start.22 = (bf16[128,2048]{1,0:T(8,128)(2,1)S(1)}, bf16[128,2048]{1,0:T(8,128)(2,1)S(1)}, u32[]{:S(2)}, u32[]{:S(2)}) collective-permute-start(bf16[128,2048]{1,0:T(8,128)(2,1)S(1)} %get-tuple-element.139), channel_id=1, source_target_pairs={{0,4},{4,0},{1,5},{5,1},{2,6},{6,2},{3,7},{7,3},{8,12},{12,8},{9,1... | collective-permute-start | bytes 1572872 | tf_op jit(solution)/shard_map/ppermute | solution.py:48
  311.7 286.0 %reduce-scatter.6.cloned.1.call-start = ((), (), s32[]{:S(2)}) async-start(), calls=%async_computation.7 | async-start | bytes 7864320 | tf_op jit(solution)/shard_map/reduce_scatter | solution.py:860
  379.5 25.5 %collective-permute-start.42 = (bf16[2,128,2048]{2,1,0:T(8,128)(2,1)S(1)}, bf16[2,128,2048]{2,1,0:T(8,128)(2,1)}, u32[]{:S(2)}, u32[]{:S(2)}) collective-permute-start(bf16[2,128,2048]{2,1,0:T(8,128)(2,1)S(1)} %bitcast.492), channel_id=1, source_target_pairs={{0,4},{4,0},{1,5},{5,1},{2,6},{6,2},{3,7},{7,3},{8,12},{12,8},{9,1... | collective-permute-start | bytes 3145736 | tf_op jit(solution)/shard_map/ppermute | solution.py:48
  383.4 25.8 %collective-permute-start.43 = (bf16[2,128,2048]{2,1,0:T(8,128)(2,1)}, bf16[2,128,2048]{2,1,0:T(8,128)(2,1)}, u32[]{:S(2)}, u32[]{:S(2)}) collective-permute-start(bf16[2,128,2048]{2,1,0:T(8,128)(2,1)} %bitcast.51), channel_id=1, source_target_pairs={{0,2},{2,0},{1,3},{3,1},{4,6},{6,4},{5,7},{7,5},{8,10},{10,8},{9,1... | collective-permute-start | bytes 3145736 | tf_op jit(solution)/shard_map/ppermute | solution.py:48
  407.9 23.9 %collective-permute-start.44 = (bf16[128,2048]{1,0:T(8,128)(2,1)}, bf16[128,2048]{1,0:T(8,128)(2,1)}, u32[]{:S(2)}, u32[]{:S(2)}) collective-permute-start(bf16[128,2048]{1,0:T(8,128)(2,1)} %get-tuple-element.255), channel_id=1, source_target_pairs={{0,2},{2,0},{1,3},{3,1},{4,6},{6,4},{5,7},{7,5},{8,10},{10,8},{9,1... | collective-permute-start | bytes 1572872 | tf_op jit(solution)/shard_map/ppermute | solution.py:48
  431.6 207.7 %reduce-scatter.8.cloned.1.call-start = ((), (), s32[]{:S(2)}) async-start(), calls=%async_computation.8 | async-start | bytes 5242880 | tf_op jit(solution)/shard_map/reduce_scatter | solution.py:860
  439.4 41.1 %collective-permute-start.46 = (bf16[512,2048]{1,0:T(8,128)(2,1)S(1)}, bf16[512,2048]{1,0:T(8,128)(2,1)S(1)}, u32[]{:S(2)}, u32[]{:S(2)}) collective-permute-start(bf16[512,2048]{1,0:T(8,128)(2,1)S(1)} %copy-done.125), channel_id=1, source_target_pairs={{0,1},{1,0},{2,3},{3,2},{4,5},{5,4},{6,7},{7,6},{8,9},{9,8},{10,11... | collective-permute-start | bytes 6291464 | tf_op jit(solution)/shard_map/ppermute | solution.py:48
  440.1 42.8 %collective-permute-start.54 = (bf16[512,2048]{1,0:T(8,128)(2,1)S(1)}, bf16[512,2048]{1,0:T(8,128)(2,1)S(1)}, u32[]{:S(2)}, u32[]{:S(2)}) collective-permute-start(bf16[512,2048]{1,0:T(8,128)(2,1)S(1)} %copy-done.124), channel_id=1, source_target_pairs={{0,1},{1,0},{2,3},{3,2},{4,5},{5,4},{6,7},{7,6},{8,9},{9,8},{10,11... | collective-permute-start | bytes 6291464 | tf_op jit(solution)/shard_map/ppermute | solution.py:48
  441.6 24.0 %collective-permute-start.50 = (bf16[128,2048]{1,0:T(8,128)(2,1)S(1)}, bf16[128,2048]{1,0:T(8,128)(2,1)S(1)}, u32[]{:S(2)}, u32[]{:S(2)}) collective-permute-start(bf16[128,2048]{1,0:T(8,128)(2,1)S(1)} %get-tuple-element.182), channel_id=1, source_target_pairs={{0,2},{2,0},{1,3},{3,1},{4,6},{6,4},{5,7},{7,5},{8,10},{10,8},{9,1... | collective-permute-start | bytes 1572872 | tf_op jit(solution)/shard_map/ppermute | solution.py:48
  488.9 26.4 %collective-permute-start.55 = (bf16[512,2048]{1,0:T(8,128)(2,1)}, bf16[512,2048]{1,0:T(8,128)(2,1)}, u32[]{:S(2)}, u32[]{:S(2)}) collective-permute-start(bf16[512,2048]{1,0:T(8,128)(2,1)} %constant_dynamic-update-slice_fusion.16.refs_4_), channel_id=1, source_target_pairs={{0,1},{1,0},{2,3},{3,2},{4,5},{5,4},{6,7},{7,6},{8,9},{9,8},{10,11... | collective-permute-start | bytes 6291464 | tf_op jit(solution)/shard_map/ppermute | solution.py:48
  493.8 36.7 %collective-permute-start.53 = (bf16[2,128,2048]{2,1,0:T(8,128)(2,1)}, bf16[2,128,2048]{2,1,0:T(8,128)(2,1)S(1)}, u32[]{:S(2)}, u32[]{:S(2)}) collective-permute-start(bf16[2,128,2048]{2,1,0:T(8,128)(2,1)} %bitcast.61), channel_id=1, source_target_pairs={{0,4},{4,0},{1,5},{5,1},{2,6},{6,2},{3,7},{7,3},{8,12},{12,8},{9,1... | collective-permute-start | bytes 3145736 | tf_op jit(solution)/shard_map/ppermute | solution.py:48
  495.2 35.3 %collective-permute-start.58 = (bf16[2,128,2048]{2,1,0:T(8,128)(2,1)}, bf16[2,128,2048]{2,1,0:T(8,128)(2,1)}, u32[]{:S(2)}, u32[]{:S(2)}) collective-permute-start(bf16[2,128,2048]{2,1,0:T(8,128)(2,1)} %bitcast.62), channel_id=1, source_target_pairs={{0,2},{2,0},{1,3},{3,1},{4,6},{6,4},{5,7},{7,5},{8,10},{10,8},{9,1... | collective-permute-start | bytes 3145736 | tf_op jit(solution)/shard_map/ppermute | solution.py:48
  563.5 55.5 %collective-permute-start.59 = (bf16[128,2048]{1,0:T(8,128)(2,1)}, bf16[128,2048]{1,0:T(8,128)(2,1)S(1)}, u32[]{:S(2)}, u32[]{:S(2)}) collective-permute-start(bf16[128,2048]{1,0:T(8,128)(2,1)} %fusion.82), channel_id=1, source_target_pairs={{0,2},{2,0},{1,3},{3,1},{4,6},{6,4},{5,7},{7,5},{8,10},{10,8},{9,1... | collective-permute-start | bytes 1572872 | tf_op jit(solution)/shard_map/ppermute | solution.py:48
  570.7 26.9 %collective-permute-start.62 = (bf16[2,128,2048]{2,1,0:T(8,128)(2,1)S(1)}, bf16[2,128,2048]{2,1,0:T(8,128)(2,1)}, u32[]{:S(2)}, u32[]{:S(2)}) collective-permute-start(bf16[2,128,2048]{2,1,0:T(8,128)(2,1)S(1)} %bitcast.493), channel_id=1, source_target_pairs={{0,4},{4,0},{1,5},{5,1},{2,6},{6,2},{3,7},{7,3},{8,12},{12,8},{9,1... | collective-permute-start | bytes 3145736 | tf_op jit(solution)/shard_map/ppermute | solution.py:48
  573.7 30.5 %collective-permute-start.65 = (bf16[2,128,2048]{2,1,0:T(8,128)(2,1)}, bf16[2,128,2048]{2,1,0:T(8,128)(2,1)}, u32[]{:S(2)}, u32[]{:S(2)}) collective-permute-start(bf16[2,128,2048]{2,1,0:T(8,128)(2,1)} %bitcast.83), channel_id=1, source_target_pairs={{0,2},{2,0},{1,3},{3,1},{4,6},{6,4},{5,7},{7,5},{8,10},{10,8},{9,1... | collective-permute-start | bytes 3145736 | tf_op jit(solution)/shard_map/ppermute | solution.py:48
  (181 other events, 2174.0 us)
Sparse Core Ops, SparseCore 0:
  28.1 62.6 all-gather.3
  93.0 125.5 all-gather.5
  220.7 113.5 all-gather.7
  336.5 108.9 reduce-scatter.3
  447.7 111.2 reduce-scatter.5
  561.7 77.5 reduce-scatter.7

commit v11 on v10

--- a/solution.py
+++ b/solution.py
@@ -339,7 +339,7 @@
         out_shape=jax.ShapeDtypeStruct(out_shape, BF),
         compiler_params=pltpu.CompilerParams(vmem_limit_bytes=VMEM_LIMIT),
         cost_estimate=pl.CostEstimate(
-            flops=7_600_000_000, bytes_accessed=3_000_000, transcendentals=0
+            flops=100_000_000, bytes_accessed=100_000, transcendentals=0
         ),
         name="attention_forward",
     )(projected, mask, cols, gate_rows)
@@ -743,9 +743,9 @@
         return half_columns(weight_qkv, which).astype(BF).reshape(rows, -1)
 
     def ff_columns(k, which):
-        start = which * width_ff + k * width
-        mlp = lax.dynamic_slice_in_dim(mlp_later, start, width, axis=2).astype(BF)
-        down = lax.dynamic_slice_in_dim(down_later, start, width, axis=1).astype(BF)
+        start = tie(which * width_ff + k * width, shard_qkv)
+        mlp = lax.dynamic_slice_in_dim(weight_mlp, start, width, axis=2).astype(BF)
+        down = lax.dynamic_slice_in_dim(weight_down, start, width, axis=1).astype(BF)
         return jnp.concatenate([mlp[:, 0], mlp[:, 1], down], axis=1)
 
     send_qkv = qkv_columns(1 - x_place)
@@ -770,22 +770,20 @@
 
     back_low = [cotangent[m, 0].reshape(own_tokens, D) for m in micros]
     all_ids = jnp.stack([all_ids, swap(all_ids, "x")], axis=0)
+    their_first = swap(ff_columns(0, 1 - x_place), "x")
+    shard_ff = [join_rows(ff_columns(0, x_place), their_first)]
     att_states = [
-        gather_start(normed_att[m], *orders[m], (their_qkv, all_ids)) for m in micros
+        gather_start(normed_att[m], *orders[m], (shard_ff[0], all_ids)) for m in micros
     ]
     att_by_x = [state[1 + orders[m].index("y")] for m, state in enumerate(att_states)]
-    mlp_later = tie(weight_mlp, *att_by_x)
-    down_later = tie(weight_down, *att_by_x)
     att_states = [gather_across(state, *orders[m], "y") for m, state in enumerate(att_states)]
     att_rows = [gather_core(state) for state in att_states]
 
     def their_ff(k, *earlier):
         return swap(tie(ff_columns(k, 1 - x_place), *earlier), "x")
 
-    theirs = their_ff(0, *att_by_x)
-    shard_ff = [join_rows(ff_columns(0, x_place), theirs)]
     full_ff = [fetch(shard_ff[0])]
-    their_out = swap(tie(half_columns(all_out, 1 - x_place), shard_ff[0]), "x")
+    their_out = swap(tie(half_columns(all_out, 1 - x_place), *att_by_x), "x")
     both_out = jnp.zeros((z_count, 2, rows, width_att), BF)
     for part, place in ((half_columns(all_out, x_place), x_place), (their_out, 1 - x_place)):
         part = part.reshape(z_count, 1, rows, width_att)

time: 703 us -> 703 us (level)
  starting transfers between devices: 85.1 us -> 71.7 us
  waiting for transfers between devices: 200 us -> 213 us
    ppermute x3, waiting for transfers between devices: 0.01 us -> 9.36 us  [direct_gather(): pieces.append(lax.ppermute(block, 'z', pairs))]
    ppermute x5, starting transfers between devices: 14.2 us -> 5.09 us  [add(): return tensor + lax.ppermute(tensor, axis, pairs)]
    reduce_scatter x3, starting transfers between devices: 8.73 us -> 0.34 us  [reduce_rows(): return lax.psum_scatter(partial, 'z', scatter_dimension=0, tiled=True)]
    ppermute x66, waiting for transfers between devices: 187 us -> 195 us  [swap(): return lax.ppermute(tensor, axis, [(0, 1), (1, 0)])]
    unnamed x286 -> x282, local copies, waits for them, and re-layouts: 22.8 us -> 20 us
  transfers between devices with their start and end apart: 80 -> 80, of which waited for: 37 -> 35; matrix products, arithmetic and copies ran while one was open for 29% -> 29% of each run, Pallas kernels for 22% -> 22%
where the time goes in v11:
time: 703 us; the launch traced here: 695 us
  waiting for transfers between devices  213 us (30%)
  Pallas kernels  179 us (25%)
  matrix products  81.7 us (12%)
  other arithmetic  75.8 us (11%)
  starting transfers between devices  71.7 us (10%)
  local copies, waits for them, and re-layouts  55.8 us (8%)
  between operations  17.9 us (3%)
    ppermute x66, waiting for transfers between devices, swap(): return lax.ppermute(tensor, axis, [(0, 1), (1, 0)])  195 us
    dot_general x24, matrix products, mm(): return lax.dot_general(a, b, (dims, ((), ())), preferred_element_type=F32)  81.7 us
    ppermute x66, starting transfers between devices, swap(): return lax.ppermute(tensor, axis, [(0, 1), (1, 0)])  59.4 us
    pallas_call x4, Pallas kernels, feed_forward(): pl.pallas_call(functools.partial(ff_kernel, width, half), grid=(2 * half,...  50.4 us
    pallas_call x3, Pallas kernels, weight_grads(): pl.pallas_call(functools.partial(grads_kernel, count), grid=(D // tile,),...  49.3 us
    pallas_call x2, Pallas kernels, attention_bwd(): pl.pallas_call(functools.partial(attention_bwd_kernel, heads), grid=(seqs...  24.9 us
    pallas_call x1, Pallas kernels, adam_all(): pl.pallas_call(functools.partial(adam_kernel, steps, len(ff_sides)), grid...  22.5 us
    unnamed x282, local copies, waits for them, and re-layouts  20 us
  transfers between devices with their start and end apart: 80, of which 35 were waited for; matrix products, arithmetic and copies ran while one was open for 29% of the time, Pallas kernels for 22%

profile of v11, /device:TPU:0, one launch (start us, length us, event | category | flops | bytes accessed | tf_op | source)
XLA Modules:
  0.0 695.5 jit_solution(9313911101801563991)
XLA Ops:
  45.3 14.3 %collective-permute-done.4 = bf16[256,1536]{1,0:T(8,128)(2,1)S(1)} collective-permute-done((bf16[256,1536]{1,0:T(8,128)(2,1)}, bf16[256,1536]{1,0:T(8,128)(2,1)S(1)}, u32[]{:S(2)}, u32[]{:S(2)}) %collective-permute-start.4) | collective-permute-done | bytes 786464 | tf_op jit(solution)/shard_map/ppermute | solution.py:48
  64.6 11.1 %collective-permute-done.12 = bf16[128,2048]{1,0:T(8,128)(2,1)} collective-permute-done((bf16[128,2048]{1,0:T(8,128)(2,1)}, bf16[128,2048]{1,0:T(8,128)(2,1)}, u32[]{:S(2)}, u32[]{:S(2)}) %collective-permute-start.12) | collective-permute-done | bytes 524320 | tf_op jit(solution)/shard_map/ppermute | solution.py:48
  84.9 9.4 %collective-permute-done.11 = bf16[256,512]{1,0:T(8,128)(2,1)} collective-permute-done((bf16[256,512]{1,0:T(8,128)(2,1)}, bf16[256,512]{1,0:T(8,128)(2,1)}, u32[]{:S(2)}, u32[]{:S(2)}) %collective-permute-start.11) | collective-permute-done | bytes 262176 | tf_op jit(solution)/shard_map/ppermute | solution.py:120
  110.9 7.6 %collective-permute-done.13 = bf16[1024,256]{1,0:T(8,128)(2,1)S(1)} collective-permute-done((bf16[1024,256]{1,0:T(8,128)(2,1)S(1)}, bf16[1024,256]{1,0:T(8,128)(2,1)S(1)}, u32[]{:S(2)}, u32[]{:S(2)}) %collective-permute-start.13) | collective-permute-done | bytes 524320 | tf_op jit(solution)/shard_map/ppermute | solution.py:48
  133.5 9.6 %collective-permute-done.15 = bf16[128,2048]{1,0:T(8,128)(2,1)} collective-permute-done((bf16[128,2048]{1,0:T(8,128)(2,1)S(1)}, bf16[128,2048]{1,0:T(8,128)(2,1)}, u32[]{:S(2)}, u32[]{:S(2)}) %collective-permute-start.15) | collective-permute-done | bytes 524320 | tf_op jit(solution)/shard_map/ppermute | solution.py:48
  161.5 7.1 %attention_forward.2 = bf16[2,2,2,4,32,256]{5,4,3,2,1,0:T(8,128)(2,1)S(1)} custom-call(bf16[2,2,2,4,32,768]{5,4,3,2,1,0:T(8,128)(2,1)S(1)} %bitcast.447, f32[2,4,128,128]{3,2,1,0:T(8,128)S(1)} %get-tuple-element.293.mask_ref, f32[2,4,128,3]{3,2,1,0:T(8,128)S(1)} %add_convert_fusion.12.cols_ref, f32[2,128]{1,0:T(2,128)S(1)} %broadcast_in_dim.30.gate_ref), custom_call_target="tpu_custom_call" | custom-call | flops 100000000 | bytes 100000 | tf_op jit(solution)/shard_map/attention_forward/pallas_call | solution.py:329
  168.7 6.6 attention_forward.3
  192.6 20.7 %collective-permute-done.30 = bf16[2,128,2048]{2,1,0:T(8,128)(2,1)S(1)} collective-permute-done((bf16[2,128,2048]{2,1,0:T(8,128)(2,1)S(1)}, bf16[2,128,2048]{2,1,0:T(8,128)(2,1)S(1)}, u32[]{:S(2)}, u32[]{:S(2)}) %collective-permute-start.30) | collective-permute-done | bytes 1048608 | tf_op jit(solution)/shard_map/ppermute | solution.py:48
  219.0 8.8 %collective-permute-done.31 = bf16[128,2048]{1,0:T(8,128)(2,1)S(1)} collective-permute-done((bf16[128,2048]{1,0:T(8,128)(2,1)}, bf16[128,2048]{1,0:T(8,128)(2,1)S(1)}, u32[]{:S(2)}, u32[]{:S(2)}) %collective-permute-start.31) | collective-permute-done | bytes 524320 | tf_op jit(solution)/shard_map/ppermute | solution.py:48
  238.1 9.6 %collective-permute-done.33 = bf16[128,2048]{1,0:T(8,128)(2,1)S(1)} collective-permute-done((bf16[128,2048]{1,0:T(8,128)(2,1)S(1)}, bf16[128,2048]{1,0:T(8,128)(2,1)S(1)}, u32[]{:S(2)}, u32[]{:S(2)}) %collective-permute-start.33) | collective-permute-done | bytes 524320 | tf_op jit(solution)/shard_map/ppermute | solution.py:48
  248.3 8.4 %collective-permute-done.22 = bf16[128,2048]{1,0:T(8,128)(2,1)S(1)} collective-permute-done((bf16[128,2048]{1,0:T(8,128)(2,1)S(1)}, bf16[128,2048]{1,0:T(8,128)(2,1)S(1)}, u32[]{:S(2)}, u32[]{:S(2)}) %collective-permute-start.22) | collective-permute-done | bytes 524320 | tf_op jit(solution)/shard_map/ppermute | solution.py:48
  275.0 12.3 %feed_forward.4 = (bf16[512,512]{1,0:T(8,128)(2,1)S(1)}, bf16[512,512]{1,0:T(8,128)(2,1)S(1)}, bf16[512,1024]{1,0:T(8,128)(2,1)S(1)}, bf16[512,1024]{1,0:T(8,128)(2,1)S(1)}) custom-call(bf16[512,2048]{1,0:T(8,128)(2,1)S(1)} %constant_dynamic-update-slice_fusion.x_mine.refs_0_, bf16[512,2048]{1,0:T(8,128)(2,1)} %collective-permute-done.36.x_other.refs_1_, ...), custom_call_target="tpu_custom_call" | custom-call | flops 13958643712 | bytes 1048576 | tf_op jit(solution)/shard_map/feed_forward/pallas_call | solution.py:424
  287.4 13.2 %feed_forward.5 = (bf16[512,512]{1,0:T(8,128)(2,1)S(1)}, bf16[512,512]{1,0:T(8,128)(2,1)S(1)}, bf16[512,1024]{1,0:T(8,128)(2,1)S(1)}, bf16[512,1024]{1,0:T(8,128)(2,1)S(1)}) custom-call(bf16[512,2048]{1,0:T(8,128)(2,1)} %constant_dynamic-update-slice_fusion.8.x_mine.refs_2_, bf16[512,2048]{1,0:T(8,128)(2,1)} %collective-permute-done.38.x_other.refs_3_, ...), custom_call_target="tpu_custom_call" | custom-call | flops 13958643712 | bytes 1048576 | tf_op jit(solution)/shard_map/feed_forward/pallas_call | solution.py:424
  301.5 18.1 %weight_grads.3 = bf16[2048,1536]{1,0:T(8,128)(2,1)} custom-call(bf16[512,2048]{1,0:T(8,128)(2,1)} %copy-done.21, bf16[512,2048]{1,0:T(8,128)(2,1)} %collective-permute-done.36.x_other.refs_1_, bf16[512,2048]{1,0:T(8,128)(2,1)} %constant_dynamic-update-slice_fusion.8.x_mine.refs_2_, bf16[512,2048]{1,0:T(8,128)(2,1)} %collective-permute-done.38.x_other.refs_3_, ...), custom_call_target="tpu_custom_call" | custom-call | flops 19327352832 | bytes 29360128 | tf_op jit(solution)/shard_map/weight_grads/pallas_call | solution.py:520
  321.6 6.7 fusion.2
  328.3 6.7 fusion
  344.0 12.4 %feed_forward.6 = (bf16[512,512]{1,0:T(8,128)(2,1)S(1)}, bf16[512,512]{1,0:T(8,128)(2,1)S(1)}, bf16[512,1024]{1,0:T(8,128)(2,1)S(1)}, bf16[512,1024]{1,0:T(8,128)(2,1)S(1)}) custom-call(bf16[512,2048]{1,0:T(8,128)(2,1)S(1)} %copy-done.22, bf16[512,2048]{1,0:T(8,128)(2,1)} %collective-permute-done.36.x_other.refs_1_, bf16[512,2048]{1,0:T(8,128)(2,1)} %copy-done.95, ...), custom_call_target="tpu_custom_call" | custom-call | flops 13958643712 | bytes 1048576 | tf_op jit(solution)/shard_map/feed_forward/pallas_call | solution.py:424
  365.3 12.5 %feed_forward.7 = (bf16[512,512]{1,0:T(8,128)(2,1)S(1)}, bf16[512,512]{1,0:T(8,128)(2,1)S(1)}, bf16[512,1024]{1,0:T(8,128)(2,1)S(1)}, bf16[512,1024]{1,0:T(8,128)(2,1)S(1)}) custom-call(bf16[512,2048]{1,0:T(8,128)(2,1)} %constant_dynamic-update-slice_fusion.8.x_mine.refs_2_, bf16[512,2048]{1,0:T(8,128)(2,1)} %collective-permute-done.38.x_other.refs_3_, ...), custom_call_target="tpu_custom_call" | custom-call | flops 13958643712 | bytes 1048576 | tf_op jit(solution)/shard_map/feed_forward/pallas_call | solution.py:424
  380.5 6.0 add_convert_fusion
  394.4 8.6 %down_product.2 = (bf16[512,2048]{1,0:T(8,128)(2,1)S(1)}, bf16[512,2048]{1,0:T(8,128)(2,1)}) custom-call(bf16[512,512]{1,0:T(8,128)(2,1)S(1)} %copy-done.37, bf16[512,512]{1,0:T(8,128)(2,1)S(1)} %get-tuple-element.154.refs_1_.refs_12_, bf16[512,512]{1,0:T(8,128)(2,1)S(1)} %copy-done.39, bf16[512,512]{1,0:T(8,128)(2,1)S(1)} %get-tuple-element.172.refs_3_.refs_13_, ...), custom_call_target="tpu_custom_call" | custom-call | flops 4294967296 | bytes 8388608 | tf_op jit(solution)/shard_map/down_product/pallas_call | solution.py:469
  403.0 9.2 %down_product.3 = (bf16[512,2048]{1,0:T(8,128)(2,1)S(1)}, bf16[512,2048]{1,0:T(8,128)(2,1)}) custom-call(bf16[512,512]{1,0:T(8,128)(2,1)S(1)} %copy-done.41, bf16[512,512]{1,0:T(8,128)(2,1)S(1)} %get-tuple-element.165.refs_1_.refs_14_, bf16[512,512]{1,0:T(8,128)(2,1)S(1)} %copy-done.43, bf16[512,512]{1,0:T(8,128)(2,1)S(1)} %get-tuple-element.173.refs_3_.refs_15_, ...), custom_call_target="tpu_custom_call" | custom-call | flops 4294967296 | bytes 8388608 | tf_op jit(solution)/shard_map/down_product/pallas_call | solution.py:469
  422.6 18.3 %weight_grads.4 = bf16[2048,1536]{1,0:T(8,128)(2,1)} custom-call(bf16[512,2048]{1,0:T(8,128)(2,1)} %copy-done.21, bf16[512,2048]{1,0:T(8,128)(2,1)} %collective-permute-done.36.x_other.refs_1_, bf16[512,2048]{1,0:T(8,128)(2,1)} %constant_dynamic-update-slice_fusion.8.x_mine.refs_2_, bf16[512,2048]{1,0:T(8,128)(2,1)} %collective-permute-done.38.x_other.refs_3_, ...), custom_call_target="tpu_custom_call" | custom-call | flops 19327352832 | bytes 29360128 | tf_op jit(solution)/shard_map/weight_grads/pallas_call | solution.py:520
  451.8 11.3 %collective-permute-done.48 = bf16[128,2048]{1,0:T(8,128)(2,1)S(1)} collective-permute-done((bf16[128,2048]{1,0:T(8,128)(2,1)S(1)}, bf16[128,2048]{1,0:T(8,128)(2,1)S(1)}, u32[]{:S(2)}, u32[]{:S(2)}) %collective-permute-start.48) | collective-permute-done | bytes 524320 | tf_op jit(solution)/shard_map/ppermute | solution.py:48
  464.6 10.6 %collective-permute-done.50 = bf16[128,2048]{1,0:T(8,128)(2,1)S(1)} collective-permute-done((bf16[128,2048]{1,0:T(8,128)(2,1)S(1)}, bf16[128,2048]{1,0:T(8,128)(2,1)S(1)}, u32[]{:S(2)}, u32[]{:S(2)}) %collective-permute-start.50) | collective-permute-done | bytes 524320 | tf_op jit(solution)/shard_map/ppermute | solution.py:48
  478.7 10.9 %collective-permute-done.51 = bf16[128,2048]{1,0:T(8,128)(2,1)S(1)} collective-permute-done((bf16[128,2048]{1,0:T(8,128)(2,1)S(1)}, bf16[128,2048]{1,0:T(8,128)(2,1)S(1)}, u32[]{:S(2)}, u32[]{:S(2)}) %collective-permute-start.51) | collective-permute-done | bytes 524320 | tf_op jit(solution)/shard_map/ppermute | solution.py:48
  509.7 12.6 %attention_backward.3 = (bf16[2,2,2,4,32,768]{5,4,3,2,1,0:T(8,128)(2,1)S(1)}, f32[2,2,128]{2,1,0:T(2,128)S(1)}) custom-call(bf16[2,2,2,4,32,768]{5,4,3,2,1,0:T(8,128)(2,1)S(1)} %bitcast.450, f32[2,2,2,4,32,256]{5,4,3,2,1,0:T(8,128)S(1)} %bitcast.458, f32[2,4,128,128]{3,2,1,0:T(8,128)S(1)} %copy-done.16, f32[2,4,128,3]{3,2,1,0:T(8,128)S(1)} %copy-done.12, ...), custom_call_target="tpu_custom_call" | custom-call | flops 14400000000 | bytes 5000000 | tf_op jit(solution)/shard_map/attention_backward/pallas_call | solution.py:351
  528.3 12.4 %attention_backward.2 = (bf16[2,2,2,4,32,768]{5,4,3,2,1,0:T(8,128)(2,1)S(1)}, f32[2,2,128]{2,1,0:T(2,128)S(1)}) custom-call(bf16[2,2,2,4,32,768]{5,4,3,2,1,0:T(8,128)(2,1)S(1)} %bitcast.448, f32[2,2,2,4,32,256]{5,4,3,2,1,0:T(8,128)S(1)} %bitcast.457, f32[2,4,128,128]{3,2,1,0:T(8,128)S(1)} %copy-done.14, f32[2,4,128,3]{3,2,1,0:T(8,128)S(1)} %copy-done.10, ...), custom_call_target="tpu_custom_call" | custom-call | flops 14400000000 | bytes 5000000 | tf_op jit(solution)/shard_map/attention_backward/pallas_call | solution.py:351
  540.7 6.0 collective-permute-done.57.refs_21_
  546.7 12.9 %weight_grads.5 = bf16[2048,1024]{1,0:T(8,128)(2,1)} custom-call(bf16[512,2048]{1,0:T(8,128)(2,1)} %pad_maximum_fusion.refs_0_, bf16[512,2048]{1,0:T(8,128)(2,1)} %collective-permute-done.17.refs_1_, bf16[512,2048]{1,0:T(8,128)(2,1)} %pad_maximum_fusion.1.refs_2_, bf16[512,2048]{1,0:T(8,128)(2,1)} %collective-permute-done.25.refs_3_, ...), custom_call_target="tpu_custom_call" | custom-call | flops 12884901888 | bytes 25165824 | tf_op jit(solution)/shard_map/weight_grads/pallas_call | solution.py:520
  588.6 19.4 %collective-permute-done.62 = bf16[2,128,2048]{2,1,0:T(8,128)(2,1)} collective-permute-done((bf16[2,128,2048]{2,1,0:T(8,128)(2,1)S(1)}, bf16[2,128,2048]{2,1,0:T(8,128)(2,1)}, u32[]{:S(2)}, u32[]{:S(2)}) %collective-permute-start.62) | collective-permute-done | bytes 1048608 | tf_op jit(solution)/shard_map/ppermute | solution.py:48
  616.5 11.2 %collective-permute-done.66.refs_23_ = bf16[256,1536]{1,0:T(8,128)(2,1)S(1)} collective-permute-done((bf16[256,1536]{1,0:T(8,128)(2,1)S(1)}, bf16[256,1536]{1,0:T(8,128)(2,1)S(1)}, u32[]{:S(2)}, u32[]{:S(2)}) %collective-permute-start.66) | collective-permute-done | bytes 786464 | tf_op jit(solution)/shard_map/ppermute | solution.py:48
  665.9 22.5 %adam.1 = (f32[3,256,512]{2,1,0:T(8,128)}, f32[3,256,512]{2,1,0:T(8,128)}, f32[3,256,512]{2,1,0:T(8,128)}, f32[256,512]{1,0:T(8,128)}, f32[256,512]{1,0:T(8,128)...) custom-call(s32[1]{0:T(128)} %bitcast.88.place_ref, ...), custom_call_target="tpu_custom_call" | custom-call | flops 41943040 | bytes 50331648 | tf_op jit(solution)/shard_map/adam/pallas_call | solution.py:659
  (585 shorter events, 310.8 us)
Async XLA Ops:
  7.2 139.2 %all-gather.4.cloned.1.call-start = ((), (), s32[]{:S(2)}) async-start(), calls=%async_computation.3 | async-start | bytes 3932160 | tf_op jit(solution)/shard_map/all_gather | solution.py:734
  23.1 251.8 %all-gather.6.cloned.1.call-start = ((), (), s32[]{:S(2)}) async-start(), calls=%async_computation.4 | async-start | bytes 7864320 | tf_op jit(solution)/shard_map/all_gather | solution.py:734
  25.1 56.3 %collective-permute-start.10 = (bf16[256,512]{1,0:T(8,128)(2,1)}, bf16[256,512]{1,0:T(8,128)(2,1)}, u32[]{:S(2)}, u32[]{:S(2)}) collective-permute-start(bf16[256,512]{1,0:T(8,128)(2,1)} %get-tuple-element.238), channel_id=1, source_target_pairs={{0,16},{8,24},{16,0},{24,8},{1,17},{9,25},{17,1},{25,9},{2,18},{10... | collective-permute-start | bytes 786440 | tf_op jit(solution)/shard_map/ppermute | solution.py:120
  27.9 48.8 %collective-permute-start.9 = (bf16[256,512]{1,0:T(8,128)(2,1)}, bf16[256,512]{1,0:T(8,128)(2,1)}, u32[]{:S(2)}, u32[]{:S(2)}) collective-permute-start(bf16[256,512]{1,0:T(8,128)(2,1)} %get-tuple-element.238), channel_id=1, source_target_pairs={{0,8},{8,16},{16,24},{24,0},{1,9},{9,17},{17,25},{25,1},{2,10},{10... | collective-permute-start | bytes 786440 | tf_op jit(solution)/shard_map/ppermute | solution.py:120
  29.5 68.0 %collective-permute-start.23 = (bf16[128,2048]{1,0:T(8,128)(2,1)}, bf16[128,2048]{1,0:T(8,128)(2,1)}, u32[]{:S(2)}, u32[]{:S(2)}) collective-permute-start(bf16[128,2048]{1,0:T(8,128)(2,1)} %get-tuple-element.128), channel_id=1, source_target_pairs={{0,2},{2,0},{1,3},{3,1},{4,6},{6,4},{5,7},{7,5},{8,10},{10,8},{9,1... | collective-permute-start | bytes 1572872 | tf_op jit(solution)/shard_map/ppermute | solution.py:48
  63.1 32.8 %collective-permute-start.6 = (bf16[128,2048]{1,0:T(8,128)(2,1)}, bf16[128,2048]{1,0:T(8,128)(2,1)}, u32[]{:S(2)}, u32[]{:S(2)}) collective-permute-start(bf16[128,2048]{1,0:T(8,128)(2,1)} %get-tuple-element.125), channel_id=1, source_target_pairs={{0,4},{4,0},{1,5},{5,1},{2,6},{6,2},{3,7},{7,3},{8,12},{12,8},{9,1... | collective-permute-start | bytes 1572872 | tf_op jit(solution)/shard_map/ppermute | solution.py:48
  81.1 262.9 %all-gather.8.cloned.1.call-start = ((), (), s32[]{:S(2)}) async-start(), calls=%async_computation.5 | async-start | bytes 7864320 | tf_op jit(solution)/shard_map/all_gather | solution.py:734
  81.4 24.4 %collective-permute-start = (bf16[128,2048]{1,0:T(8,128)(2,1)}, bf16[128,2048]{1,0:T(8,128)(2,1)S(1)}, u32[]{:S(2)}, u32[]{:S(2)}) collective-permute-start(bf16[128,2048]{1,0:T(8,128)(2,1)} %get-tuple-element.125), channel_id=1, source_target_pairs={{0,2},{2,0},{1,3},{3,1},{4,6},{6,4},{5,7},{7,5},{8,10},{10,8},{9,1... | collective-permute-start | bytes 1572872 | tf_op jit(solution)/shard_map/ppermute | solution.py:48
  100.6 50.4 %collective-permute-start.25 = (bf16[512,2048]{1,0:T(8,128)(2,1)}, bf16[512,2048]{1,0:T(8,128)(2,1)}, u32[]{:S(2)}, u32[]{:S(2)}) collective-permute-start(bf16[512,2048]{1,0:T(8,128)(2,1)} %pad_maximum_fusion.1.refs_2_), channel_id=1, source_target_pairs={{0,1},{1,0},{2,3},{3,2},{4,5},{5,4},{6,7},{7,6},{8,9},{9,8},{10,11... | collective-permute-start | bytes 6291464 | tf_op jit(solution)/shard_map/ppermute | solution.py:48
  108.4 46.1 %collective-permute-start.17 = (bf16[512,2048]{1,0:T(8,128)(2,1)}, bf16[512,2048]{1,0:T(8,128)(2,1)}, u32[]{:S(2)}, u32[]{:S(2)}) collective-permute-start(bf16[512,2048]{1,0:T(8,128)(2,1)} %pad_maximum_fusion.refs_0_), channel_id=1, source_target_pairs={{0,1},{1,0},{2,3},{3,2},{4,5},{5,4},{6,7},{7,6},{8,9},{9,8},{10,11... | collective-permute-start | bytes 6291464 | tf_op jit(solution)/shard_map/ppermute | solution.py:48
  119.8 23.3 %collective-permute-start.15 = (bf16[128,2048]{1,0:T(8,128)(2,1)S(1)}, bf16[128,2048]{1,0:T(8,128)(2,1)}, u32[]{:S(2)}, u32[]{:S(2)}) collective-permute-start(bf16[128,2048]{1,0:T(8,128)(2,1)S(1)} %bitcast.476), channel_id=1, source_target_pairs={{0,4},{4,0},{1,5},{5,1},{2,6},{6,2},{3,7},{7,3},{8,12},{12,8},{9,1... | collective-permute-start | bytes 1572872 | tf_op jit(solution)/shard_map/ppermute | solution.py:48
  143.1 25.4 %collective-permute-start.26 = (bf16[256,1536]{1,0:T(8,128)(2,1)}, bf16[256,1536]{1,0:T(8,128)(2,1)}, u32[]{:S(2)}, u32[]{:S(2)}) collective-permute-start(bf16[256,1536]{1,0:T(8,128)(2,1)} %pad_maximum_fusion.9), channel_id=1, source_target_pairs={{0,4},{4,0},{1,5},{5,1},{2,6},{6,2},{3,7},{7,3},{8,12},{12,8},{9,1... | collective-permute-start | bytes 2359304 | tf_op jit(solution)/shard_map/ppermute | solution.py:48
  144.4 34.3 %collective-permute-start.27 = (bf16[128,2048]{1,0:T(8,128)(2,1)}, bf16[128,2048]{1,0:T(8,128)(2,1)}, u32[]{:S(2)}, u32[]{:S(2)}) collective-permute-start(bf16[128,2048]{1,0:T(8,128)(2,1)} %collective-permute-done.14), channel_id=1, source_target_pairs={{0,2},{2,0},{1,3},{3,1},{4,6},{6,4},{5,7},{7,5},{8,10},{10,8},{9,1... | collective-permute-start | bytes 1572872 | tf_op jit(solution)/shard_map/ppermute | solution.py:48
  145.9 32.8 %collective-permute-start.28 = (bf16[128,2048]{1,0:T(8,128)(2,1)}, bf16[128,2048]{1,0:T(8,128)(2,1)}, u32[]{:S(2)}, u32[]{:S(2)}) collective-permute-start(bf16[128,2048]{1,0:T(8,128)(2,1)} %collective-permute-done.15), channel_id=1, source_target_pairs={{0,2},{2,0},{1,3},{3,1},{4,6},{6,4},{5,7},{7,5},{8,10},{10,8},{9,1... | collective-permute-start | bytes 1572872 | tf_op jit(solution)/shard_map/ppermute | solution.py:48
  188.1 25.2 %collective-permute-start.30 = (bf16[2,128,2048]{2,1,0:T(8,128)(2,1)S(1)}, bf16[2,128,2048]{2,1,0:T(8,128)(2,1)S(1)}, u32[]{:S(2)}, u32[]{:S(2)}) collective-permute-start(bf16[2,128,2048]{2,1,0:T(8,128)(2,1)S(1)} %bitcast.495), channel_id=1, source_target_pairs={{0,2},{2,0},{1,3},{3,1},{4,6},{6,4},{5,7},{7,5},{8,10},{10,8},{9,1... | collective-permute-start | bytes 3145736 | tf_op jit(solution)/shard_map/ppermute | solution.py:48
  191.8 24.9 %collective-permute-start.19 = (bf16[2,128,2048]{2,1,0:T(8,128)(2,1)S(1)}, bf16[2,128,2048]{2,1,0:T(8,128)(2,1)}, u32[]{:S(2)}, u32[]{:S(2)}) collective-permute-start(bf16[2,128,2048]{2,1,0:T(8,128)(2,1)S(1)} %bitcast.494), channel_id=1, source_target_pairs={{0,4},{4,0},{1,5},{5,1},{2,6},{6,2},{3,7},{7,3},{8,12},{12,8},{9,1... | collective-permute-start | bytes 3145736 | tf_op jit(solution)/shard_map/ppermute | solution.py:48
  215.2 308.2 %reduce-scatter.4.cloned.1.call-start = ((), (), s32[]{:S(2)}) async-start(), calls=%async_computation.6 | async-start | bytes 7864320 | tf_op jit(solution)/shard_map/reduce_scatter | solution.py:858
  234.5 22.2 %collective-permute-start.22 = (bf16[128,2048]{1,0:T(8,128)(2,1)S(1)}, bf16[128,2048]{1,0:T(8,128)(2,1)S(1)}, u32[]{:S(2)}, u32[]{:S(2)}) collective-permute-start(bf16[128,2048]{1,0:T(8,128)(2,1)S(1)} %get-tuple-element.141), channel_id=1, source_target_pairs={{0,4},{4,0},{1,5},{5,1},{2,6},{6,2},{3,7},{7,3},{8,12},{12,8},{9,1... | collective-permute-start | bytes 1572872 | tf_op jit(solution)/shard_map/ppermute | solution.py:48
  321.3 286.7 %reduce-scatter.6.cloned.1.call-start = ((), (), s32[]{:S(2)}) async-start(), calls=%async_computation.7 | async-start | bytes 7864320 | tf_op jit(solution)/shard_map/reduce_scatter | solution.py:858
  389.2 25.6 %collective-permute-start.42 = (bf16[2,128,2048]{2,1,0:T(8,128)(2,1)S(1)}, bf16[2,128,2048]{2,1,0:T(8,128)(2,1)}, u32[]{:S(2)}, u32[]{:S(2)}) collective-permute-start(bf16[2,128,2048]{2,1,0:T(8,128)(2,1)S(1)} %bitcast.492), channel_id=1, source_target_pairs={{0,4},{4,0},{1,5},{5,1},{2,6},{6,2},{3,7},{7,3},{8,12},{12,8},{9,1... | collective-permute-start | bytes 3145736 | tf_op jit(solution)/shard_map/ppermute | solution.py:48
  393.1 25.7 %collective-permute-start.43 = (bf16[2,128,2048]{2,1,0:T(8,128)(2,1)}, bf16[2,128,2048]{2,1,0:T(8,128)(2,1)}, u32[]{:S(2)}, u32[]{:S(2)}) collective-permute-start(bf16[2,128,2048]{2,1,0:T(8,128)(2,1)} %bitcast.51), channel_id=1, source_target_pairs={{0,2},{2,0},{1,3},{3,1},{4,6},{6,4},{5,7},{7,5},{8,10},{10,8},{9,1... | collective-permute-start | bytes 3145736 | tf_op jit(solution)/shard_map/ppermute | solution.py:48
  417.5 23.6 %collective-permute-start.44 = (bf16[128,2048]{1,0:T(8,128)(2,1)}, bf16[128,2048]{1,0:T(8,128)(2,1)}, u32[]{:S(2)}, u32[]{:S(2)}) collective-permute-start(bf16[128,2048]{1,0:T(8,128)(2,1)} %get-tuple-element.261), channel_id=1, source_target_pairs={{0,2},{2,0},{1,3},{3,1},{4,6},{6,4},{5,7},{7,5},{8,10},{10,8},{9,1... | collective-permute-start | bytes 1572872 | tf_op jit(solution)/shard_map/ppermute | solution.py:48
  441.0 202.6 %reduce-scatter.8.cloned.1.call-start = ((), (), s32[]{:S(2)}) async-start(), calls=%async_computation.8 | async-start | bytes 5242880 | tf_op jit(solution)/shard_map/reduce_scatter | solution.py:858
  448.7 41.4 %collective-permute-start.46 = (bf16[512,2048]{1,0:T(8,128)(2,1)S(1)}, bf16[512,2048]{1,0:T(8,128)(2,1)S(1)}, u32[]{:S(2)}, u32[]{:S(2)}) collective-permute-start(bf16[512,2048]{1,0:T(8,128)(2,1)S(1)} %copy-done.121), channel_id=1, source_target_pairs={{0,1},{1,0},{2,3},{3,2},{4,5},{5,4},{6,7},{7,6},{8,9},{9,8},{10,11... | collective-permute-start | bytes 6291464 | tf_op jit(solution)/shard_map/ppermute | solution.py:48
  449.6 43.0 %collective-permute-start.54 = (bf16[512,2048]{1,0:T(8,128)(2,1)S(1)}, bf16[512,2048]{1,0:T(8,128)(2,1)S(1)}, u32[]{:S(2)}, u32[]{:S(2)}) collective-permute-start(bf16[512,2048]{1,0:T(8,128)(2,1)S(1)} %copy-done.120), channel_id=1, source_target_pairs={{0,1},{1,0},{2,3},{3,2},{4,5},{5,4},{6,7},{7,6},{8,9},{9,8},{10,11... | collective-permute-start | bytes 6291464 | tf_op jit(solution)/shard_map/ppermute | solution.py:48
  451.0 24.2 %collective-permute-start.50 = (bf16[128,2048]{1,0:T(8,128)(2,1)S(1)}, bf16[128,2048]{1,0:T(8,128)(2,1)S(1)}, u32[]{:S(2)}, u32[]{:S(2)}) collective-permute-start(bf16[128,2048]{1,0:T(8,128)(2,1)S(1)} %get-tuple-element.184), channel_id=1, source_target_pairs={{0,2},{2,0},{1,3},{3,1},{4,6},{6,4},{5,7},{7,5},{8,10},{10,8},{9,1... | collective-permute-start | bytes 1572872 | tf_op jit(solution)/shard_map/ppermute | solution.py:48
  498.6 26.9 %collective-permute-start.55 = (bf16[512,2048]{1,0:T(8,128)(2,1)}, bf16[512,2048]{1,0:T(8,128)(2,1)}, u32[]{:S(2)}, u32[]{:S(2)}) collective-permute-start(bf16[512,2048]{1,0:T(8,128)(2,1)} %constant_dynamic-update-slice_fusion.16.refs_4_), channel_id=1, source_target_pairs={{0,1},{1,0},{2,3},{3,2},{4,5},{5,4},{6,7},{7,6},{8,9},{9,8},{10,11... | collective-permute-start | bytes 6291464 | tf_op jit(solution)/shard_map/ppermute | solution.py:48
  504.4 36.3 %collective-permute-start.53 = (bf16[2,128,2048]{2,1,0:T(8,128)(2,1)}, bf16[2,128,2048]{2,1,0:T(8,128)(2,1)}, u32[]{:S(2)}, u32[]{:S(2)}) collective-permute-start(bf16[2,128,2048]{2,1,0:T(8,128)(2,1)} %bitcast.61), channel_id=1, source_target_pairs={{0,4},{4,0},{1,5},{5,1},{2,6},{6,2},{3,7},{7,3},{8,12},{12,8},{9,1... | collective-permute-start | bytes 3145736 | tf_op jit(solution)/shard_map/ppermute | solution.py:48
  505.7 35.0 %collective-permute-start.58 = (bf16[2,128,2048]{2,1,0:T(8,128)(2,1)}, bf16[2,128,2048]{2,1,0:T(8,128)(2,1)}, u32[]{:S(2)}, u32[]{:S(2)}) collective-permute-start(bf16[2,128,2048]{2,1,0:T(8,128)(2,1)} %bitcast.62), channel_id=1, source_target_pairs={{0,2},{2,0},{1,3},{3,1},{4,6},{6,4},{5,7},{7,5},{8,10},{10,8},{9,1... | collective-permute-start | bytes 3145736 | tf_op jit(solution)/shard_map/ppermute | solution.py:48
  575.2 53.6 %collective-permute-start.59 = (bf16[128,2048]{1,0:T(8,128)(2,1)}, bf16[128,2048]{1,0:T(8,128)(2,1)}, u32[]{:S(2)}, u32[]{:S(2)}) collective-permute-start(bf16[128,2048]{1,0:T(8,128)(2,1)} %fusion.82), channel_id=1, source_target_pairs={{0,2},{2,0},{1,3},{3,1},{4,6},{6,4},{5,7},{7,5},{8,10},{10,8},{9,1... | collective-permute-start | bytes 1572872 | tf_op jit(solution)/shard_map/ppermute | solution.py:48
  582.1 25.8 %collective-permute-start.62 = (bf16[2,128,2048]{2,1,0:T(8,128)(2,1)S(1)}, bf16[2,128,2048]{2,1,0:T(8,128)(2,1)}, u32[]{:S(2)}, u32[]{:S(2)}) collective-permute-start(bf16[2,128,2048]{2,1,0:T(8,128)(2,1)S(1)} %bitcast.493), channel_id=1, source_target_pairs={{0,4},{4,0},{1,5},{5,1},{2,6},{6,2},{3,7},{7,3},{8,12},{12,8},{9,1... | collective-permute-start | bytes 3145736 | tf_op jit(solution)/shard_map/ppermute | solution.py:48
  585.3 28.8 %collective-permute-start.65 = (bf16[2,128,2048]{2,1,0:T(8,128)(2,1)}, bf16[2,128,2048]{2,1,0:T(8,128)(2,1)}, u32[]{:S(2)}, u32[]{:S(2)}) collective-permute-start(bf16[2,128,2048]{2,1,0:T(8,128)(2,1)} %bitcast.83), channel_id=1, source_target_pairs={{0,2},{2,0},{1,3},{3,1},{4,6},{6,4},{5,7},{7,5},{8,10},{10,8},{9,1... | collective-permute-start | bytes 3145736 | tf_op jit(solution)/shard_map/ppermute | solution.py:48
  (177 other events, 2120.9 us)
Sparse Core Ops, SparseCore 0:
  23.3 78.4 all-gather.3
  103.9 116.1 all-gather.5
  222.2 113.5 all-gather.7
  337.9 108.9 reduce-scatter.3
  449.1 111.2 reduce-scatter.5
  563.1 77.2 reduce-scatter.7
